TPU v7x, 32 devices: a whole 2x2x4 slice. The times are simulated.
32 devices in a mesh: groups: 2 (over y), dp: 4 (over z), mp: 2 (over x), rep: 2 (over core).
Axes of the slice: x: 2, y: 2, z: 4, core: 2. Of those that a mesh axis runs over, the one named last changes fastest.
Arguments:
- query_ids: int32 [16384], P(('groups', 'dp', 'rep')), parts along dimension 0, may hold values from 0 to 128255
- query_delta: bfloat16 [16384, 4096], P(('groups', 'dp', 'rep'), 'mp'), parts along dimension 0, may hold values from -6 to 6
- doc_lengths: int32 [16, 128], P(('groups', 'dp', 'rep')), parts along dimension 0, may hold values from 1 to 32, 1024 in all within a row
- vocab_factor: bfloat16 [128256, 64], P('mp'), may hold values from -6 to 6
- output_factor: bfloat16 [4096, 64], P('mp'), may hold values from -0.09375 to 0.09375
- train_grads: bfloat16 [4096, 4096], P(('groups', 'dp'), 'mp'), parts along dimension 0, as said below
Outputs:
- scores: bfloat16 [4096, 4, 2, 128], P(('groups', 'dp', 'mp'), None, 'rep'), parts along dimension 0
There are 2 independent parts, one for each index of `groups`. A program takes and returns all parts, laid end to end along the dimension named above; an argument that names none is the same for every part. Nothing has to cross between parts.
Inputs may be any that keep to these rules, and one draw needn't show every extreme that they name: `doc_lengths`: in each row the lengths sum to 1024. `train_grads`: coordinates ordered as 64 model-width-side indices by 64 vocabulary-side indices.
All inputs are finite; a program needn't handle non-finite values.
Results may differ from a plain program's by a relative error of at most 0.012.
The roundings to bfloat16 on the way count: a program that leaves them out, or rounds other values in their place, can miss the bound.
Values may be sent and summed in bfloat16 or wider, within the bound.
No kernel may reach another device: no remote copies, remote signals or barrier semaphores. Data moves between devices by JAX's collectives and lax.ppermute only.
A program may use at most 128 MiB of HBM per device.

v0:
```python
import jax
import jax.numpy as jnp
from jax import lax
from jax.sharding import PartitionSpec as P

FBLK = 128


damping = 0.1


def passed_along(shard, axis, by):
    size = lax.axis_size(axis)
    return lax.ppermute(shard, axis, [(i, (i + by) % size) for i in range(size)])


def doc_matrix(lengths_row, count):
    ends = jnp.cumsum(lengths_row)
    starts = ends - lengths_row
    place = jnp.arange(count, dtype=jnp.int32)
    inside = (place[None, :] >= starts[:, None]) & (place[None, :] < ends[:, None])
    return inside.astype(jnp.bfloat16)


def solve_block(factor, rhs):
    return jax.scipy.linalg.cho_solve((factor, True), rhs)


def per_device(query_ids, query_delta, doc_lengths, vocab_factor, output_factor, train_grads):
    model_count = lax.axis_size("mp")
    model_index = lax.axis_index("mp")
    vocab_rows = vocab_factor.shape[0]
    local_ids = query_ids - model_index * vocab_rows
    owned = (local_ids >= 0) & (local_ids < vocab_rows)
    looked = vocab_factor[jnp.clip(local_ids, 0, vocab_rows - 1)].astype(jnp.float32)
    vocab_part = jnp.where(owned[:, None], looked, jnp.zeros_like(looked))
    output_part = jnp.dot(query_delta, output_factor, preferred_element_type=jnp.float32)
    input_side, output_side = lax.psum((vocab_part, output_part), "mp")
    proj = output_side.shape[1]
    rows_each = proj // model_count
    mine = lax.dynamic_slice_in_dim(output_side, model_index * rows_each, rows_each, 1)
    token_count = query_ids.shape[0]
    token_grads = (
        (mine[:, :, None] * input_side[:, None, :])
        .reshape(token_count, rows_each * proj)
        .astype(jnp.bfloat16)
    )
    query_grads = jnp.dot(
        doc_matrix(doc_lengths[0], token_count), token_grads, preferred_element_type=jnp.float32
    )
    train_rows, feat_dev = train_grads.shape
    nblocks = feat_dev // FBLK
    tiled = train_grads.reshape(train_rows, nblocks, FBLK)
    local_gram = jnp.einsum("tbi,tbj->bij", tiled, tiled, preferred_element_type=jnp.float32)
    total_gram = lax.psum(local_gram, "dp")
    fisher = total_gram / (train_rows * lax.axis_size("dp"))
    shift_amount = damping * (jnp.trace(fisher, axis1=1, axis2=2) / FBLK)
    damped = fisher + shift_amount[:, None, None] * jnp.eye(FBLK, dtype=jnp.float32)[None]
    factor = jnp.linalg.cholesky(damped)
    queries = query_grads.shape[0]
    rhs = jnp.transpose(query_grads.reshape(queries, nblocks, FBLK), (1, 2, 0))
    solved = jax.vmap(solve_block)(factor, rhs)
    pre = (jnp.transpose(solved, (2, 0, 1)).reshape(queries, feat_dev) / proj).astype(jnp.bfloat16)
    cycle = lax.axis_size("dp")
    place = lax.axis_index("dp")
    half = queries // 2

    def scores_of(block):
        return lax.dot_general(
            train_grads, block, (((1,), (1,)), ((), ())), preferred_element_type=jnp.float32
        )

    def record(buffer, lower_scores, upper_scores, lower_source, upper_source):
        anchor = jnp.zeros((), jnp.int32)
        middle = jnp.full((), half, jnp.int32)
        buffer = lax.dynamic_update_slice(
            buffer, lower_scores[:, None, :], (anchor, lower_source, anchor)
        )
        buffer = lax.dynamic_update_slice(
            buffer, upper_scores[:, None, :], (anchor, upper_source, middle)
        )
        return buffer

    buffer = jnp.zeros((train_rows, cycle, queries), jnp.float32)
    block_scores = scores_of(pre)
    buffer = record(buffer, block_scores[:, :half], block_scores[:, half:], place, place)

    def advance_one(step, carry):
        buffer, visiting = carry
        visiting = passed_along(visiting, "dp", 1)
        visit_scores = scores_of(visiting)
        source = (place - step) % cycle
        buffer = record(buffer, visit_scores[:, :half], visit_scores[:, half:], source, source)
        return (buffer, visiting)

    buffer, visiting = lax.fori_loop(1, cycle, advance_one, (buffer, pre))
    summed = lax.psum_scatter(buffer.astype(jnp.bfloat16), "mp", scatter_dimension=0, tiled=True)
    return summed[:, :, None, :]


def solution(mesh):
    placed = (
        P(("groups", "dp", "rep")),
        P(("groups", "dp", "rep"), "mp"),
        P(("groups", "dp", "rep"), None),
        P("mp", None),
        P("mp", None),
        P(("groups", "dp"), "mp"),
    )
    return jax.shard_map(
        per_device,
        mesh=mesh,
        in_specs=placed,
        out_specs=P(("groups", "dp", "mp"), None, "rep", None),
        check_vma=False,
    )
```

profile of v0, /device:TPU:0, one launch (start us, length us, event | category | flops | bytes accessed | tf_op | source)
XLA Modules:
  0.0 582.6 jit_solution(6688117721106643512)
XLA Ops:
  6.5 0.7 fusion.19
  7.3 0.7 compare_and_fusion
  8.0 15.5 %copy.36 = bf16[64128,64]{1,0:T(8,128)(2,1)} copy(bf16[64128,64]{0,1:T(8,128)(2,1)} %param.11) | data formatting | bytes 16416768 | tf_op args[3]
  23.5 10.7 %gather_fusion = bf16[1024,64]{1,0:T(8,128)(2,1)S(1)} fusion(bf16[64128,64]{1,0:T(8,128)(2,1)} %copy.36, s32[1024]{0:T(1024)S(1)} %fusion.19), kind=kCustom, calls=%fused_computation | custom fusion | bytes 266240 | tf_op jit(solution)/shard_map/gather | solution.py:35
  34.1 1.0 convert_select_fusion
  35.1 4.3 fusion.21
  39.4 0.0 all-reduce.10.cloned.1.call-update
  39.5 0.0 all-reduce.6.cloned.1.call-start
  39.5 1.9 fusion.2
  41.4 0.0 all-reduce.8.cloned.1.call-start
  41.5 0.1 copy.38
  41.6 0.2 reduce-window.7
  41.8 0.1 reduce.6
  41.9 34.9 %all-reduce.10.cloned.1.call-done = (f32[1024,64]{1,0:T(8,128)}, f32[1024,64]{0,1:T(8,128)}) async-done(((f32[1024,64]{1,0:T(8,128)}, f32[1024,64]{0,1:T(8,128)}), (f32[1024,64]{1,0:T(8,128)}, f32[1024,64]{0,1:T(8,128)})) %all-reduce.10.cloned.1.call-update) | async-done | bytes 524304 | tf_op jit(solution)/shard_map/psum | solution.py:38
  76.8 1.2 copy.37
  78.0 0.9 constant_dynamic-slice_fusion
  79.0 1.3 multiply_convert_fusion
  80.2 2.4 fusion.12
  82.6 48.5 %all-reduce.6.cloned.1.call-done = f32[16,128,128]{2,1,0:T(8,128)} async-done(((f32[16,128,128]{2,1,0:T(8,128)}), f32[16,128,128]{2,1,0:T(8,128)}) %all-reduce.6.cloned.1.call-update) | async-done | bytes 1048592 | tf_op jit(solution)/shard_map/psum | solution.py:55
  131.1 1.5 select_reduce_fusion.1
  132.7 2.4 multiply_add_fusion
  135.1 2.5 copy.35
  137.6 2.4 fusion.9
  140.1 188.3 %custom-call.11 = f32[16,128,128]{2,1,0:T(8,128)S(1)} custom-call(f32[16,128,128]{2,1,0:T(8,128)} %fusion.9), custom_call_target="Cholesky" | custom-call | tf_op jit(solution)/shard_map/jit(cholesky)/cholesky | solution.py:59
  328.4 0.1 select_reduce_fusion
  328.5 0.1 compare_reduce_fusion
  328.6 1.2 select_bitcast_fusion
  329.8 157.9 %custom-call.12 = f32[16,1,128,128]{2,3,1,0:T(8,128)S(1)} custom-call(f32[16,1,128,128]{3,2,1,0:T(8,128)} %select_bitcast_fusion), custom_call_target="InvertDiagBlocksLowerTriangular" | custom-call | tf_op jit(solution)/shard_map/vmap(jit(_cho_solve))/triangular_solve | solution.py:26
  487.8 1.0 copy-done.3
  488.8 3.1 fusion.7
  491.8 2.4 fusion.5
  494.3 0.8 convolution_bitcast_fusion
  495.1 1.0 copy.40
  496.2 50.1 %while.17 = (s32[]{:T(128)}, bf16[512,4,128]{0,2,1:T(8,128)(2,1)S(1)}, bf16[128,2048]{1,0:T(8,128)(2,1)}, bf16[512,2048]{1,0:T(8,128)(2,1)S(1)}, s32[]{:T(128)},...) while((s32[]{:T(128)}, bf16[512,4,128]{0,2,1:T(8,128)(2,1)S(1)}, bf16[128,2048]{1,0:T(8,128)(2,1)}, ...), condition=%wide.region_8.9_spmd, body=%wide.region_7.8_spmd.sunk | while | flops 268435456 | bytes 6160680 | solution.py:96
  496.2 1.4 collective-permute-start
  497.6 14.6 %collective-permute-done = bf16[128,2048]{1,0:T(8,128)(2,1)S(1)} collective-permute-done((bf16[128,2048]{1,0:T(8,128)(2,1)}, bf16[128,2048]{1,0:T(8,128)(2,1)S(1)}, u32[]{:S(2)}, u32[]{:S(2)}) %collective-permute-start) | collective-permute-done | bytes 524320 | tf_op jit(solution)/shard_map/while/body/eval_jaxpr/ppermute | solution.py:14
  512.2 0.8 fusion.39
  513.1 0.8 copy.64
  513.8 15.0 %collective-permute-done = bf16[128,2048]{1,0:T(8,128)(2,1)S(1)} collective-permute-done((bf16[128,2048]{1,0:T(8,128)(2,1)}, bf16[128,2048]{1,0:T(8,128)(2,1)S(1)}, u32[]{:S(2)}, u32[]{:S(2)}) %collective-permute-start) | collective-permute-done | bytes 524320 | tf_op jit(solution)/shard_map/while/body/eval_jaxpr/ppermute | solution.py:14
  528.9 0.8 fusion.39
  529.8 0.8 copy.64
  530.5 14.1 %collective-permute-done = bf16[128,2048]{1,0:T(8,128)(2,1)S(1)} collective-permute-done((bf16[128,2048]{1,0:T(8,128)(2,1)}, bf16[128,2048]{1,0:T(8,128)(2,1)S(1)}, u32[]{:S(2)}, u32[]{:S(2)}) %collective-permute-start) | collective-permute-done | bytes 524320 | tf_op jit(solution)/shard_map/while/body/eval_jaxpr/ppermute | solution.py:14
  544.7 0.8 fusion.39
  545.5 0.8 copy.64
  546.3 1.1 copy.41
  547.4 0.6 dynamic-slice
  548.7 25.7 %all-reduce.8.cloned.1.call-done = bf16[512,4,128]{2,1,0:T(4,128)(2,1)} async-done(((bf16[512,4,128]{2,1,0:T(4,128)(2,1)}), bf16[512,4,128]{2,1,0:T(4,128)(2,1)}) %all-reduce.8.cloned.1.call-update) | async-done | bytes 524304
  574.4 1.7 dynamic-slice_bitcast_fusion
  (30 shorter events, 0.2 us)
Async XLA Ops:
  6.5 28.6 %copy-start = (bf16[2048,64]{0,1:T(8,128)(2,1)S(1)}, bf16[2048,64]{0,1:T(8,128)(2,1)}, u32[]{:S(2)}) copy-start(bf16[2048,64]{0,1:T(8,128)(2,1)} %param.12) | copy-start | bytes 786436
  6.5 70.3 %all-reduce.10.cloned.1.call-start = ((), (), s32[]{:S(2)}) async-start(), calls=%async_computation.2 | async-start | bytes 1572864 | tf_op jit(solution)/shard_map/psum | solution.py:38
  34.1 5.4 copy-start.1
  39.4 2.1 copy-start.4
  39.5 91.7 %all-reduce.6.cloned.1.call-start = ((), (), s32[]{:S(2)}) async-start(), calls=%async_computation | async-start | bytes 2097152 | tf_op jit(solution)/shard_map/psum | solution.py:55
  41.4 532.9 %all-reduce.8.cloned.1.call-start = ((), (), s32[]{:S(2)}) async-start(), calls=%async_computation.1 | async-start | bytes 1048576
  131.1 6.5 %copy-start.2 = (f32[16,128,128]{2,1,0:T(8,128)S(1)}, f32[16,128,128]{2,1,0:T(8,128)}, u32[]{:S(2)}) copy-start(f32[16,128,128]{2,1,0:T(8,128)} %all-reduce.6.cloned.1.call-done) | copy-start | bytes 3145732
  487.7 1.0 copy-start.3
  496.2 51.2 %copy-start.5 = (u32[32]{0:T(128)S(1)}, u32[32]{0:T(128)}, u32[]{:S(2)}) copy-start(u32[32]{0:T(128)} %constant.154) | copy-start | bytes 388
  496.2 15.9 %collective-permute-start = (bf16[128,2048]{1,0:T(8,128)(2,1)}, bf16[128,2048]{1,0:T(8,128)(2,1)S(1)}, u32[]{:S(2)}, u32[]{:S(2)}) collective-permute-start(bf16[128,2048]{1,0:T(8,128)(2,1)} %get-tuple-element.213), channel_id=1, source_target_pairs={{0,4},{4,8},{8,12},{12,0},{1,5},{5,9},{9,13},{13,1},{2,6},{6,10},{... | collective-permute-start | bytes 1572872 | tf_op jit(solution)/shard_map/while/body/eval_jaxpr/ppermute | solution.py:14
  513.8 15.0 %collective-permute-start = (bf16[128,2048]{1,0:T(8,128)(2,1)}, bf16[128,2048]{1,0:T(8,128)(2,1)S(1)}, u32[]{:S(2)}, u32[]{:S(2)}) collective-permute-start(bf16[128,2048]{1,0:T(8,128)(2,1)} %get-tuple-element.213), channel_id=1, source_target_pairs={{0,4},{4,8},{8,12},{12,0},{1,5},{5,9},{9,13},{13,1},{2,6},{6,10},{... | collective-permute-start | bytes 1572872 | tf_op jit(solution)/shard_map/while/body/eval_jaxpr/ppermute | solution.py:14
  530.5 14.1 %collective-permute-start = (bf16[128,2048]{1,0:T(8,128)(2,1)}, bf16[128,2048]{1,0:T(8,128)(2,1)S(1)}, u32[]{:S(2)}, u32[]{:S(2)}) collective-permute-start(bf16[128,2048]{1,0:T(8,128)(2,1)} %get-tuple-element.213), channel_id=1, source_target_pairs={{0,4},{4,8},{8,12},{12,0},{1,5},{5,9},{9,13},{13,1},{2,6},{6,10},{... | collective-permute-start | bytes 1572872 | tf_op jit(solution)/shard_map/while/body/eval_jaxpr/ppermute | solution.py:14
Sparse Core Ops, SparseCore 0:
  39.6 37.1 all-reduce.9
  79.3 51.8 all-reduce.5
  547.5 26.7 all-reduce.7
where the time goes:
time: 584 us; the launch traced here: 583 us
  other arithmetic  358 us (61%)
  waiting for transfers between devices  153 us (26%)
  local copies, waits for them, and re-layouts  38.9 us (7%)
  matrix products  17.3 us (3%)
  between operations  14 us (2%)
    another operation x4, other arithmetic, per_device(): factor = jnp.linalg.cholesky(damped)  189 us
    another operation x3, other arithmetic, solve_block(): return jax.scipy.linalg.cho_solve((factor, True), rhs)  159 us
    psum x1, waiting for transfers between devices, per_device(): total_gram = lax.psum(local_gram, 'dp')  48.5 us
    ppermute x3, waiting for transfers between devices, passed_along(): lax.ppermute(shard, axis, [(i, (i + by) % size) for i in range(size)])  43.7 us
    psum x1, waiting for transfers between devices, per_device(): input_side, output_side = lax.psum((vocab_part, output_part), 'mp')  34.9 us
    unnamed x4, waiting for transfers between devices  25.7 us
    unnamed x14, local copies, waits for them, and re-layouts  17.1 us
  transfers between devices with their start and end apart: 6, of which 6 were waited for; matrix products, arithmetic and copies ran while one was open for 1% of the time, Pallas kernels for 0%

commit v1 on v0

--- a/solution.py
+++ b/solution.py
@@ -1,17 +1,307 @@
+import functools
 import jax
 import jax.numpy as jnp
 from jax import lax
+from jax.experimental import pallas as pl
+from jax.experimental.pallas import tpu as pltpu
 from jax.sharding import PartitionSpec as P
 
 FBLK = 128
-
+SLAB = FBLK + 8
 
 damping = 0.1
+
+VMEM = pl.BlockSpec(memory_space=pltpu.VMEM)
+SMEM = pl.BlockSpec(memory_space=pltpu.SMEM)
+HBM = pl.BlockSpec(memory_space=pl.ANY)
+
+
+def call(kernel, outs, in_specs, scratch=(), vmem=48, flops=0, moved=0):
+    return pl.pallas_call(
+        kernel,
+        out_shape=outs,
+        in_specs=in_specs,
+        scratch_shapes=list(scratch),
+        compiler_params=pltpu.CompilerParams(vmem_limit_bytes=vmem << 20),
+        cost_estimate=pl.CostEstimate(flops=flops, bytes_accessed=moved, transcendentals=0),
+    )
 
 
 def passed_along(shard, axis, by):
     size = lax.axis_size(axis)
     return lax.ppermute(shard, axis, [(i, (i + by) % size) for i in range(size)])
+
+
+def square(dim):
+    return lax.broadcasted_iota(jnp.int32, (FBLK, FBLK), dim)
+
+
+def halves(value):
+    high = value.astype(jnp.bfloat16)
+    return high, (value - high.astype(jnp.float32)).astype(jnp.bfloat16)
+
+
+def pack(first, second, spare=None):
+    row, col = square(0), square(1)
+    body = jnp.where(row >= col, first, second)
+    diagonal = jnp.sum(jnp.where(row == col, second, 0.0), axis=0, keepdims=True)
+    place = lax.broadcasted_iota(jnp.int32, (8, FBLK), 0)
+    tail = jnp.where(place == 0, diagonal, 0.0)
+    if spare is not None:
+        tail = jnp.where(place == 1, spare, tail)
+    return body, tail
+
+
+def unpack(body, diagonal):
+    row, col = square(0), square(1)
+    turned = body.T
+    first = jnp.where(row >= col, body, turned)
+    second = jnp.where(row < col, body, jnp.where(row > col, turned, diagonal))
+    return first, second
+
+
+def gram_kernel(cycle, lengths, train, *slabs):
+    mine, half = lax.axis_index("dp"), lax.axis_index("rep")
+    spare = lengths[...].astype(jnp.float32)
+    for shift in range(cycle):
+        owner = half * cycle + lax.rem(mine + shift, cycle)
+        start = pl.multiple_of(owner * (2 * FBLK), 2 * FBLK)
+        part = train[:, pl.ds(start, 2 * FBLK)]
+        gram = lax.dot_general(part, part, (((0,), (0,)), ((), ())), preferred_element_type=jnp.float32)
+        body, tail = pack(gram[:FBLK, :FBLK], gram[FBLK:, FBLK:], spare)
+        slabs[shift][pl.ds(0, FBLK), :] = body
+        slabs[shift][pl.ds(FBLK, 8), :] = tail
+
+
+def inverted(block):
+    lane = square(1)
+    row8 = lax.broadcasted_iota(jnp.int32, (FBLK, FBLK), 0)
+    for k in range(FBLK):
+        column = jnp.broadcast_to(block[:, k:k + 1], (FBLK, FBLK))
+        pivot = 1.0 / column[k:k + 1, :]
+        line = jnp.where(lane[:1, :] == k, pivot, block[k:k + 1, :] * pivot)
+        rest = jnp.where(lane == k, 0.0, block) - column * line
+        block = jnp.where(row8 == k, line, rest)
+    return block
+
+
+def factor_kernel(examples, scale, *refs):
+    slabs, out = refs[:-1], refs[-1]
+    body = slabs[0][pl.ds(0, FBLK), :]
+    diagonal = slabs[0][pl.ds(FBLK, 1), :]
+    for slab in slabs[1:]:
+        body = body + slab[pl.ds(0, FBLK), :]
+        diagonal = diagonal + slab[pl.ds(FBLK, 1), :]
+    same = square(0) == square(1)
+    results = []
+    for gram in unpack(body, diagonal):
+        fisher = gram / examples
+        trace = jnp.sum(jnp.sum(jnp.where(same, fisher, 0.0), axis=0, keepdims=True), axis=1, keepdims=True)
+        results.append(inverted(fisher + jnp.where(same, damping * (trace / FBLK), 0.0)) * scale)
+    body, tail = pack(*results)
+    out[pl.ds(0, FBLK), :] = body
+    out[pl.ds(FBLK, 8), :] = tail
+
+
+def factors_kernel(ids, id_rows, delta_hbm, table_hbm, factor, sent, kept, delta, table, looked, sems):
+    model = lax.axis_index("mp")
+    vocab_rows = table.shape[1]
+    tokens, width = delta.shape
+    proj = factor.shape[0]
+    each = proj // lax.axis_size("mp")
+    get_delta = pltpu.make_async_copy(delta_hbm, delta, sems.at[0])
+    get_table = pltpu.make_async_copy(table_hbm, table, sems.at[1])
+    get_delta.start()
+    get_table.start()
+    get_delta.wait()
+    output = lax.dot_general(
+        delta[...], factor[...], (((1,), (1,)), ((), ())), preferred_element_type=jnp.float32
+    )
+    looked[pl.ds(0, proj), :] = output.T
+    mine = looked[pl.ds(pl.multiple_of(model * each, each), each), :]
+    other = looked[pl.ds(pl.multiple_of((1 - model) * each, each), each), :]
+    kept[...] = mine
+    high, low = halves(other)
+    sent[pl.ds(0, each), :] = high
+    sent[pl.ds(each, each), :] = low
+    get_table.wait()
+    lanes = lax.broadcasted_iota(jnp.int32, (proj, FBLK), 1)
+    first = model * vocab_rows
+
+    def group(g, carry):
+        gathered = jnp.zeros((proj, FBLK), jnp.bfloat16)
+        base = g * FBLK
+        for j in range(FBLK):
+            local = ids[base + j] - first
+            local = jnp.where((local >= 0) & (local < vocab_rows), local, 0)
+            block = table[:, pl.ds(pl.multiple_of((local >> 7) * FBLK, FBLK), FBLK)]
+            gathered = jnp.where(lanes == j, pltpu.roll(block, (j - local) & (FBLK - 1), 1), gathered)
+        local = id_rows[pl.ds(g, 1), :] - first
+        owned = (local >= 0) & (local < vocab_rows)
+        spread = jnp.where(owned, 1.0, 0.0)
+        gathered = (gathered.astype(jnp.float32) * spread).astype(jnp.bfloat16)
+        sent[pl.ds(2 * each, proj), pl.ds(pl.multiple_of(base, FBLK), FBLK)] = gathered
+        return carry
+
+    lax.fori_loop(0, tokens // FBLK, group, 0)
+
+
+def merge_kernel(kept, sent, got, out):
+    each = kept.shape[0]
+    received = got[pl.ds(0, each), :].astype(jnp.float32) + got[pl.ds(each, each), :].astype(jnp.float32)
+    high, low = halves(kept[...] + received)
+    out[pl.ds(0, each), :] = high
+    out[pl.ds(each, each), :] = low
+    rows = pl.ds(2 * each, out.shape[0] - 2 * each)
+    out[rows, :] = sent[rows, :] + got[rows, :]
+
+
+def queries_kernel(each, factors, slab, high_out, low_out):
+    tokens = factors.shape[1]
+    proj = factors.shape[0] - 2 * each
+    queries = high_out.shape[1]
+    lengths = slab[pl.ds(FBLK + 1, 1), :]
+    upto = jnp.where(square(0) <= square(1), 1.0, 0.0).astype(jnp.bfloat16)
+    ends = lax.dot_general(
+        jnp.broadcast_to(lengths, (8, queries)).astype(jnp.bfloat16), upto, (((1,), (0,)), ((), ())),
+        preferred_element_type=jnp.float32,
+    )[:1]
+    starts = ends - lengths
+    place = lax.broadcasted_iota(jnp.int32, (tokens, queries), 0).astype(jnp.float32)
+    inside = jnp.where((place >= starts) & (place < ends), 1.0, 0.0).astype(jnp.bfloat16)
+    output = factors[pl.ds(0, each), :].astype(jnp.float32) + factors[pl.ds(each, each), :].astype(jnp.float32)
+    inputs = factors[pl.ds(2 * each, proj), :].astype(jnp.float32)
+    step = 8
+    for start in range(0, each, step):
+        grads = jnp.concatenate(
+            [(inputs * output[r:r + 1, :]).astype(jnp.bfloat16) for r in range(start, start + step)], axis=0
+        )
+        summed = jnp.dot(grads, inside, preferred_element_type=jnp.float32)
+        high, low = halves(summed)
+        high_out[pl.ds(start * proj, step * proj), :] = high
+        low_out[pl.ds(start * proj, step * proj), :] = low
+
+
+def scores_kernel(cycle, *refs):
+    own, peers = refs[:cycle], refs[cycle:2 * cycle]
+    highs, lows = refs[2 * cycle:3 * cycle], refs[3 * cycle:4 * cycle]
+    train, sent, kept, pre = refs[4 * cycle:]
+    mine, rep, model = lax.axis_index("dp"), lax.axis_index("rep"), lax.axis_index("mp")
+    queries = highs[0].shape[1]
+    for side, slabs in enumerate((own, peers)):
+        half = rep if side == 0 else 1 - rep
+        for shift in range(cycle):
+            owner = half * cycle + lax.rem(mine + cycle - shift, cycle)
+            slab = slabs[shift]
+            blocks = unpack(slab[pl.ds(0, FBLK), :], slab[pl.ds(FBLK, 1), :])
+            for index, block in enumerate(blocks):
+                rows = pl.ds(pl.multiple_of(owner * (2 * FBLK) + index * FBLK, FBLK), FBLK)
+                high, low = halves(block)
+                right_high = jnp.concatenate([ref[rows, :] for ref in highs], axis=1)
+                right_low = jnp.concatenate([ref[rows, :] for ref in lows], axis=1)
+                solved = jnp.dot(
+                    jnp.concatenate([high, high, low], axis=1),
+                    jnp.concatenate([right_high, right_low, right_high], axis=0),
+                    preferred_element_type=jnp.float32,
+                )
+                pre[rows, :] = solved.astype(jnp.bfloat16)
+    half_rows = sent.shape[0]
+    for out, which in ((sent, 1 - model), (kept, model)):
+        rows = pl.ds(pl.multiple_of(which * half_rows, half_rows), half_rows)
+        scores = jnp.dot(train[rows, :], pre[...], preferred_element_type=jnp.float32).astype(jnp.bfloat16)
+        for shift in range(cycle):
+            source = lax.rem(mine + cycle - shift, cycle)
+            out[:, pl.ds(pl.multiple_of(source * queries, queries), queries)] = (
+                scores[:, shift * queries:(shift + 1) * queries]
+            )
+
+
+def shape(dims, dtype):
+    return jax.ShapeDtypeStruct(dims, dtype)
+
+
+def split_over_blocks(query_ids, query_delta, doc_lengths, vocab_factor, output_factor, train_grads):
+    cycle = lax.axis_size("dp")
+    tokens, width = query_delta.shape
+    proj = output_factor.shape[1]
+    each = proj // lax.axis_size("mp")
+    vocab_rows = vocab_factor.shape[0]
+    train_rows, feat = train_grads.shape
+    queries = doc_lengths.shape[1]
+    bf16, f32 = jnp.bfloat16, jnp.float32
+
+    slabs = call(
+        functools.partial(gram_kernel, cycle),
+        [shape((SLAB, FBLK), f32)] * cycle,
+        [VMEM, VMEM],
+        flops=train_rows * feat * FBLK * 2,
+        moved=2 * train_rows * feat,
+        vmem=16,
+    )(doc_lengths, train_grads)
+    parts = [slabs[0]] + [passed_along(slabs[s], "dp", s) for s in range(1, cycle)]
+
+    sent, kept = call(
+        factors_kernel,
+        [shape((2 * each + proj, tokens), bf16), shape((each, tokens), f32)],
+        [SMEM, VMEM, HBM, HBM, VMEM],
+        [
+            pltpu.VMEM((tokens, width), bf16),
+            pltpu.VMEM((proj, vocab_rows), bf16),
+            pltpu.VMEM((proj, tokens), f32),
+            pltpu.SemaphoreType.DMA((2,)),
+        ],
+        vmem=24,
+        flops=2 * tokens * width * proj,
+        moved=2 * (tokens * width + proj * vocab_rows) * 2,
+    )(query_ids, query_ids.reshape(tokens // FBLK, FBLK), query_delta, vocab_factor.T, output_factor.T)
+    got = passed_along(sent, "mp", 1)
+    factors = call(
+        merge_kernel,
+        shape(sent.shape, bf16),
+        [VMEM, VMEM, VMEM],
+        vmem=16,
+        flops=tokens * each,
+        moved=8 * tokens * each * 4,
+    )(kept, sent, got)
+    gathered = [factors] + [passed_along(factors, "dp", s) for s in range(1, cycle)]
+
+    inverse = call(
+        functools.partial(factor_kernel, train_rows * cycle, 1.0 / proj),
+        shape((SLAB, FBLK), f32),
+        [VMEM] * cycle,
+        vmem=16,
+        flops=10 ** 10,
+        moved=10 ** 6,
+    )(*parts)
+    inverses = [inverse] + [passed_along(inverse, "dp", s) for s in range(1, cycle)]
+    peers = [passed_along(slab, "rep", 1) for slab in inverses]
+
+    highs, lows = [], []
+    for s in range(cycle):
+        high, low = call(
+            functools.partial(queries_kernel, each),
+            [shape((feat, queries), bf16)] * 2,
+            [VMEM, VMEM],
+            vmem=24,
+            flops=2 * feat * tokens * queries,
+            moved=6 * feat * queries,
+        )(gathered[s], parts[s])
+        highs.append(high)
+        lows.append(low)
+
+    half_rows = train_rows // lax.axis_size("mp")
+    outgoing, own = call(
+        functools.partial(scores_kernel, cycle),
+        [shape((half_rows, cycle * queries), bf16)] * 2,
+        [VMEM] * (4 * cycle + 1),
+        [pltpu.VMEM((feat, cycle * queries), bf16)],
+        vmem=32,
+        flops=2 * train_rows * feat * cycle * queries,
+        moved=8 * feat * queries * cycle,
+    )(*inverses, *peers, *highs, *lows, train_grads)
+    incoming = passed_along(outgoing, "mp", 1)
+    total = (own.astype(f32) + incoming.astype(f32)).astype(bf16)
+    return total.reshape(half_rows, cycle, 1, queries)
 
 
 def doc_matrix(lengths_row, count):
@@ -26,7 +316,7 @@
     return jax.scipy.linalg.cho_solve((factor, True), rhs)
 
 
-def per_device(query_ids, query_delta, doc_lengths, vocab_factor, output_factor, train_grads):
+def general(query_ids, query_delta, doc_lengths, vocab_factor, output_factor, train_grads):
     model_count = lax.axis_size("mp")
     model_index = lax.axis_index("mp")
     vocab_rows = vocab_factor.shape[0]
@@ -62,40 +352,26 @@
     solved = jax.vmap(solve_block)(factor, rhs)
     pre = (jnp.transpose(solved, (2, 0, 1)).reshape(queries, feat_dev) / proj).astype(jnp.bfloat16)
     cycle = lax.axis_size("dp")
-    place = lax.axis_index("dp")
-    half = queries // 2
-
-    def scores_of(block):
-        return lax.dot_general(
-            train_grads, block, (((1,), (1,)), ((), ())), preferred_element_type=jnp.float32
-        )
-
-    def record(buffer, lower_scores, upper_scores, lower_source, upper_source):
-        anchor = jnp.zeros((), jnp.int32)
-        middle = jnp.full((), half, jnp.int32)
-        buffer = lax.dynamic_update_slice(
-            buffer, lower_scores[:, None, :], (anchor, lower_source, anchor)
-        )
-        buffer = lax.dynamic_update_slice(
-            buffer, upper_scores[:, None, :], (anchor, upper_source, middle)
-        )
-        return buffer
-
-    buffer = jnp.zeros((train_rows, cycle, queries), jnp.float32)
-    block_scores = scores_of(pre)
-    buffer = record(buffer, block_scores[:, :half], block_scores[:, half:], place, place)
-
-    def advance_one(step, carry):
-        buffer, visiting = carry
-        visiting = passed_along(visiting, "dp", 1)
-        visit_scores = scores_of(visiting)
-        source = (place - step) % cycle
-        buffer = record(buffer, visit_scores[:, :half], visit_scores[:, half:], source, source)
-        return (buffer, visiting)
-
-    buffer, visiting = lax.fori_loop(1, cycle, advance_one, (buffer, pre))
-    summed = lax.psum_scatter(buffer.astype(jnp.bfloat16), "mp", scatter_dimension=0, tiled=True)
+    everyone = lax.all_gather(pre, "dp", axis=0, tiled=True)
+    scores = lax.dot_general(
+        train_grads, everyone, (((1,), (1,)), ((), ())), preferred_element_type=jnp.float32
+    )
+    scores = scores.astype(jnp.bfloat16).reshape(train_rows, cycle, queries)
+    summed = lax.psum_scatter(scores, "mp", scatter_dimension=0, tiled=True)
     return summed[:, :, None, :]
+
+
+def per_device(query_ids, query_delta, doc_lengths, vocab_factor, output_factor, train_grads):
+    owners = lax.axis_size("dp") * lax.axis_size("rep")
+    fits = (
+        train_grads.shape[1] == 2 * FBLK * owners
+        and lax.axis_size("mp") == 2
+        and lax.axis_size("rep") == 2
+        and doc_lengths.shape[1] == FBLK
+        and vocab_factor.shape[0] % FBLK == 0
+    )
+    body = split_over_blocks if fits else general
+    return body(query_ids, query_delta, doc_lengths, vocab_factor, output_factor, train_grads)
 
 
 def solution(mesh):

time: 584 us -> 74.2 us (0.13)
  other arithmetic: 358 us -> 0.07 us
  waiting for transfers between devices: 153 us -> 7.09 us
  local copies, waits for them, and re-layouts: 38.9 us -> 7.93 us
  Pallas kernels: 0 us -> 30.9 us
  starting transfers between devices: 1.47 us -> 27.8 us
  matrix products: 17.3 us -> 0 us
  between operations: 14 us -> 0.14 us
    another operation x9 -> x0, other arithmetic: 348 us -> none  [the longest x4 189 us: per_device(): factor = jnp.linalg.cholesky(damped)]
    psum x2 -> x0, waiting for transfers between devices: 83.4 us -> none  [the longest x1 48.5 us: per_device(): total_gram = lax.psum(local_gram, 'dp')]
    ppermute x3 -> x15, waiting for transfers between devices: 43.7 us -> 7.09 us  [passed_along(): lax.ppermute(shard, axis, [(i, (i + by) % size) for i in range(size)])]
    pallas_call x0 -> x9, Pallas kernels: none -> 30.9 us  [the longest x1 13.3 us: split_over_blocks(): call(functools.partial(factor_kernel, train_rows * cycle, 1.0 / proj), sh...]
    ppermute x3 -> x15, starting transfers between devices: 1.39 us -> 27.8 us  [passed_along(): lax.ppermute(shard, axis, [(i, (i + by) % size) for i in range(size)])]
    unnamed x4 -> x0, waiting for transfers between devices: 25.7 us -> none
    dot_general x7 -> x0, matrix products: 11.8 us -> none  [the longest x1 4.29 us: per_device(): jnp.dot(query_delta, output_factor, preferred_element_type=jnp.float32)]
    gather x1 -> x0, local copies, waits for them, and re-layouts: 10.7 us -> none  [per_device(): vocab_factor[jnp.clip(local_ids, 0, vocab_rows - 1)].astype(jnp.float32)]
  transfers between devices with their start and end apart: 6 -> 15, of which waited for: 6 -> 2; matrix products, arithmetic and copies ran while one was open for 1% -> 0% of each run, Pallas kernels for 0% -> 26%
where the time goes in v1:
time: 74.2 us; the launch traced here: 74 us
  Pallas kernels  30.9 us (42%)
  starting transfers between devices  27.8 us (37%)
  local copies, waits for them, and re-layouts  7.93 us (11%)
  waiting for transfers between devices  7.09 us (10%)
    ppermute x15, starting transfers between devices, passed_along(): lax.ppermute(shard, axis, [(i, (i + by) % size) for i in range(size)])  27.8 us
    pallas_call x1, Pallas kernels, split_over_blocks(): call(functools.partial(factor_kernel, train_rows * cycle, 1.0 / proj), sh...  13.3 us
    pallas_call x1, Pallas kernels, split_over_blocks(): call(factors_kernel, [shape((2 * each + proj, tokens), bf16), shape((each...  8.88 us
    unnamed x12, local copies, waits for them, and re-layouts  7.16 us
    ppermute x15, waiting for transfers between devices, passed_along(): lax.ppermute(shard, axis, [(i, (i + by) % size) for i in range(size)])  7.09 us
    pallas_call x4, Pallas kernels, split_over_blocks(): call(functools.partial(queries_kernel, each), [shape((feat, queries), bf1...  5.63 us
    pallas_call x1, Pallas kernels, split_over_blocks(): call(functools.partial(scores_kernel, cycle), [shape((half_rows, cycle *...  2.59 us
  transfers between devices with their start and end apart: 15, of which 2 were waited for; matrix products, arithmetic and copies ran while one was open for 0% of the time, Pallas kernels for 26%

profile of v1, /device:TPU:0, one launch (start us, length us, event | category | flops | bytes accessed | tf_op | source)
XLA Modules:
  0.0 74.0 jit_solution(6029670802130982643)
XLA Ops:
  0.0 0.0 copy-start.1
  0.0 3.3 %copy-done.1 = bf16[64128,64]{0,1:T(8,128)(2,1)S(1)} copy-done((bf16[64128,64]{0,1:T(8,128)(2,1)S(1)}, bf16[64128,64]{0,1:T(8,128)(2,1)}, u32[]{:S(2)}) %copy-start.1) | copy-done | bytes 8208408
  3.3 0.0 copy-start.2
  3.3 2.2 %copy-done.2 = bf16[1024,2048]{1,0:T(8,128)(2,1)S(1)} copy-done((bf16[1024,2048]{1,0:T(8,128)(2,1)S(1)}, bf16[1024,2048]{1,0:T(8,128)(2,1)}, u32[]{:S(2)}) %copy-start.2) | copy-done | bytes 4194328
  5.5 0.9 %copy-done.3 = bf16[2048,64]{0,1:T(8,128)(2,1)S(1)} copy-done((bf16[2048,64]{0,1:T(8,128)(2,1)S(1)}, bf16[2048,64]{0,1:T(8,128)(2,1)}, u32[]{:S(2)}) %copy-start.3) | copy-done | bytes 262168
  6.5 0.7 copy-done.4
  7.2 8.9 %shard_map.66 = (bf16[128,1024]{1,0:T(8,128)(2,1)S(1)}, f32[32,1024]{1,0:T(8,128)S(1)}) custom-call(s32[1024]{0:T(1024)S(1)} %copy-done.4, s32[8,128]{1,0:T(8,128)S(1)} %bitcast.6, bf16[1024,2048]{1,0:T(8,128)(2,1)S(1)} %copy-done.2, bf16[64,64128]{1,0:T(8,128)(2,1)S(1)} %bitcast.4, bf16[64,2048]{1,0:T(8,128)(2,1)S(1)} %bitcast.5), custom_call_target="tpu_custom_call" | custom-call | flops 268435456 | bytes 24805376 | tf_op jit(solution)/shard_map/pallas_call | solution.py:243
  16.1 3.0 %collective-permute-start.10 = (bf16[128,1024]{1,0:T(8,128)(2,1)S(1)}, bf16[128,1024]{1,0:T(8,128)(2,1)S(1)}, u32[]{:S(2)}, u32[]{:S(2)}) collective-permute-start(bf16[128,1024]{1,0:T(8,128)(2,1)S(1)} %get-tuple-element.26.sent), channel_id=1, source_target_pairs={{0,2},{2,0},{1,3},{3,1},{4,6},{6,4},{5,7},{7,5},{8,10},{10,8},{9,1... | collective-permute-start | bytes 786440 | tf_op jit(solution)/shard_map/ppermute | solution.py:32
  19.1 0.0 copy-done
  19.1 0.0 copy-done.5
  19.1 0.5 shard_map.64
  19.6 1.6 %collective-permute-start = (f32[136,128]{1,0:T(8,128)S(1)}, f32[136,128]{1,0:T(8,128)S(1)}, u32[]{:S(2)}, u32[]{:S(2)}) collective-permute-start(f32[136,128]{1,0:T(8,128)S(1)} %get-tuple-element.22), channel_id=1, source_target_pairs={{0,4},{4,8},{8,12},{12,0},{1,5},{5,9},{9,13},{13,1},{2,6},{6,10},{... | collective-permute-start | bytes 208904 | tf_op jit(solution)/shard_map/ppermute | solution.py:32
  21.2 2.6 %collective-permute-start.1 = (f32[136,128]{1,0:T(8,128)S(1)}, f32[136,128]{1,0:T(8,128)S(1)}, u32[]{:S(2)}, u32[]{:S(2)}) collective-permute-start(f32[136,128]{1,0:T(8,128)S(1)} %get-tuple-element.23), channel_id=1, source_target_pairs={{0,8},{4,12},{8,0},{12,4},{1,9},{5,13},{9,1},{13,5},{2,10},{6,14},... | collective-permute-start | bytes 208904 | tf_op jit(solution)/shard_map/ppermute | solution.py:32
  23.8 1.4 %collective-permute-start.2 = (f32[136,128]{1,0:T(8,128)S(1)}, f32[136,128]{1,0:T(8,128)S(1)}, u32[]{:S(2)}, u32[]{:S(2)}) collective-permute-start(f32[136,128]{1,0:T(8,128)S(1)} %get-tuple-element.24), channel_id=1, source_target_pairs={{0,12},{4,0},{8,4},{12,8},{1,13},{5,1},{9,5},{13,9},{2,14},{6,2},{... | collective-permute-start | bytes 208904 | tf_op jit(solution)/shard_map/ppermute | solution.py:32
  25.1 0.2 collective-permute-done.10.got
  25.4 3.9 %collective-permute-start.13 = (bf16[128,1024]{1,0:T(8,128)(2,1)S(1)}, bf16[128,1024]{1,0:T(8,128)(2,1)S(1)}, u32[]{:S(2)}, u32[]{:S(2)}) collective-permute-start(bf16[128,1024]{1,0:T(8,128)(2,1)S(1)} %shard_map.67.factors), channel_id=1, source_target_pairs={{0,12},{4,0},{8,4},{12,8},{1,13},{5,1},{9,5},{13,9},{2,14},{6,2},{... | collective-permute-start | bytes 786440 | tf_op jit(solution)/shard_map/ppermute | solution.py:32
  29.3 0.0 collective-permute-start.12
  29.3 0.0 collective-permute-done.refs_1_.slab
  29.3 1.0 %collective-permute-start.11 = (bf16[128,1024]{1,0:T(8,128)(2,1)S(1)}, bf16[128,1024]{1,0:T(8,128)(2,1)S(1)}, u32[]{:S(2)}, u32[]{:S(2)}) collective-permute-start(bf16[128,1024]{1,0:T(8,128)(2,1)S(1)} %shard_map.67.factors), channel_id=1, source_target_pairs={{0,4},{4,8},{8,12},{12,0},{1,5},{5,9},{9,13},{13,1},{2,6},{6,10},{... | collective-permute-start | bytes 786440 | tf_op jit(solution)/shard_map/ppermute | solution.py:32
  30.3 0.0 collective-permute-done.1.refs_2_.slab
  30.3 0.0 collective-permute-done.2.refs_3_.slab
  30.3 13.3 %shard_map.65.refs_0_ = f32[136,128]{1,0:T(8,128)S(1)} custom-call(f32[136,128]{1,0:T(8,128)S(1)} %get-tuple-element.21.refs_0_.slab, f32[136,128]{1,0:T(8,128)S(1)} %collective-permute-done.refs_1_.slab, f32[136,128]{1,0:T(8,128)S(1)} %collective-permute-done.1.refs_2_.slab, f32[136,128]{1,0:T(8,128)S(1)} %collective-permute-done.2.refs_3_.slab), custom_call_target="tpu_custom_call" | custom-call | flops 10000000000 | bytes 1000000 | tf_op jit(solution)/shard_map/pallas_call | solution.py:268
  43.6 2.9 %collective-permute-start.5 = (f32[136,128]{1,0:T(8,128)S(1)}, f32[136,128]{1,0:T(8,128)S(1)}, u32[]{:S(2)}, u32[]{:S(2)}) collective-permute-start(f32[136,128]{1,0:T(8,128)S(1)} %shard_map.65.refs_0_), channel_id=1, source_target_pairs={{0,12},{4,0},{8,4},{12,8},{1,13},{5,1},{9,5},{13,9},{2,14},{6,2},{... | collective-permute-start | bytes 208904 | tf_op jit(solution)/shard_map/ppermute | solution.py:32
  46.5 1.1 %collective-permute-start.4 = (f32[136,128]{1,0:T(8,128)S(1)}, f32[136,128]{1,0:T(8,128)S(1)}, u32[]{:S(2)}, u32[]{:S(2)}) collective-permute-start(f32[136,128]{1,0:T(8,128)S(1)} %shard_map.65.refs_0_), channel_id=1, source_target_pairs={{0,8},{4,12},{8,0},{12,4},{1,9},{5,13},{9,1},{13,5},{2,10},{6,14},... | collective-permute-start | bytes 208904 | tf_op jit(solution)/shard_map/ppermute | solution.py:32
  47.6 0.0 collective-permute-done.11.factors
  47.6 7.7 %collective-permute-start.3 = (f32[136,128]{1,0:T(8,128)S(1)}, f32[136,128]{1,0:T(8,128)S(1)}, u32[]{:S(2)}, u32[]{:S(2)}) collective-permute-start(f32[136,128]{1,0:T(8,128)S(1)} %shard_map.65.refs_0_), channel_id=1, source_target_pairs={{0,4},{4,8},{8,12},{12,0},{1,5},{5,9},{9,13},{13,1},{2,6},{6,10},{... | collective-permute-start | bytes 208904 | tf_op jit(solution)/shard_map/ppermute | solution.py:32
  55.4 1.4 %shard_map.68 = (bf16[2048,128]{1,0:T(8,128)(2,1)S(1)}, bf16[2048,128]{1,0:T(8,128)(2,1)S(1)}) custom-call(bf16[128,1024]{1,0:T(8,128)(2,1)S(1)} %shard_map.67.factors, f32[136,128]{1,0:T(8,128)S(1)} %get-tuple-element.21.refs_0_.slab), custom_call_target="tpu_custom_call" | custom-call | flops 536870912 | bytes 1572864 | tf_op jit(solution)/shard_map/pallas_call | solution.py:281
  56.8 1.4 %shard_map.69 = (bf16[2048,128]{1,0:T(8,128)(2,1)S(1)}, bf16[2048,128]{1,0:T(8,128)(2,1)S(1)}) custom-call(bf16[128,1024]{1,0:T(8,128)(2,1)S(1)} %collective-permute-done.11.factors, f32[136,128]{1,0:T(8,128)S(1)} %collective-permute-done.refs_1_.slab), custom_call_target="tpu_custom_call" | custom-call | flops 536870912 | bytes 1572864 | tf_op jit(solution)/shard_map/pallas_call | solution.py:281
  58.2 0.0 collective-permute-done.5.refs_3_
  58.2 0.1 collective-permute-start.6
  58.3 0.0 collective-permute-done.4.refs_2_
  58.3 0.5 collective-permute-start.9
  58.8 0.0 collective-permute-done.3.refs_1_
  58.8 0.1 collective-permute-start.8
  58.9 0.0 collective-permute-done.12.factors
  58.9 0.4 collective-permute-start.7
  59.3 1.4 %shard_map.70 = (bf16[2048,128]{1,0:T(8,128)(2,1)S(1)}, bf16[2048,128]{1,0:T(8,128)(2,1)S(1)}) custom-call(bf16[128,1024]{1,0:T(8,128)(2,1)S(1)} %collective-permute-done.12.factors, f32[136,128]{1,0:T(8,128)S(1)} %collective-permute-done.1.refs_2_.slab), custom_call_target="tpu_custom_call" | custom-call | flops 536870912 | bytes 1572864 | tf_op jit(solution)/shard_map/pallas_call | solution.py:281
  60.7 0.0 collective-permute-done.13.factors
  60.7 1.4 %shard_map.71 = (bf16[2048,128]{1,0:T(8,128)(2,1)S(1)}, bf16[2048,128]{1,0:T(8,128)(2,1)S(1)}) custom-call(bf16[128,1024]{1,0:T(8,128)(2,1)S(1)} %collective-permute-done.13.factors, f32[136,128]{1,0:T(8,128)S(1)} %collective-permute-done.2.refs_3_.slab), custom_call_target="tpu_custom_call" | custom-call | flops 536870912 | bytes 1572864 | tf_op jit(solution)/shard_map/pallas_call | solution.py:281
  62.1 0.0 collective-permute-done.6.refs_4_
  62.2 0.0 collective-permute-done.9.refs_7_
  62.2 0.0 collective-permute-done.8.refs_6_
  62.2 0.0 collective-permute-done.7.refs_5_
  62.2 2.6 %shard_map.72 = (bf16[256,512]{1,0:T(8,128)(2,1)S(1)}, bf16[256,512]{1,0:T(8,128)(2,1)S(1)}) custom-call(f32[136,128]{1,0:T(8,128)S(1)} %shard_map.65.refs_0_, f32[136,128]{1,0:T(8,128)S(1)} %collective-permute-done.3.refs_1_, f32[136,128]{1,0:T(8,128)S(1)} %collective-permute-done.4.refs_2_, f32[136,128]{1,0:T(8,128)S(1)} %collective-permute-done.5.refs_3_, ...), custom_call_target="tpu_custom_call" | custom-call | flops 1073741824 | bytes 8388608 | tf_op jit(solution)/shard_map/pallas_call | solution.py:293
  64.8 1.5 %collective-permute-start.14 = (bf16[256,512]{1,0:T(8,128)(2,1)S(1)}, bf16[256,512]{1,0:T(8,128)(2,1)S(1)}, u32[]{:S(2)}, u32[]{:S(2)}) collective-permute-start(bf16[256,512]{1,0:T(8,128)(2,1)S(1)} %get-tuple-element.36), channel_id=1, source_target_pairs={{0,2},{2,0},{1,3},{3,1},{4,6},{6,4},{5,7},{7,5},{8,10},{10,8},{9,1... | collective-permute-start | bytes 786440 | tf_op jit(solution)/shard_map/ppermute | solution.py:32
  66.3 6.9 %collective-permute-done.14 = bf16[256,512]{1,0:T(8,128)(2,1)S(1)} collective-permute-done((bf16[256,512]{1,0:T(8,128)(2,1)S(1)}, bf16[256,512]{1,0:T(8,128)(2,1)S(1)}, u32[]{:S(2)}, u32[]{:S(2)}) %collective-permute-start.14) | collective-permute-done | bytes 262176 | tf_op jit(solution)/shard_map/ppermute | solution.py:32
  73.1 0.1 add_convert_fusion
  73.2 0.8 %reshape.7 = bf16[256,4,1,128]{3,1,0,2:T(4,128)(2,1)} reshape(bf16[256,512]{1,0:T(8,128)(2,1)S(1)} %add_convert_fusion) | data formatting | bytes 524288 | tf_op jit(solution)/shard_map/reshape | solution.py:304
  (5 shorter events, 0.1 us)
Async XLA Ops:
  0.0 3.3 %copy-start.1 = (bf16[64128,64]{0,1:T(8,128)(2,1)S(1)}, bf16[64128,64]{0,1:T(8,128)(2,1)}, u32[]{:S(2)}) copy-start(bf16[64128,64]{0,1:T(8,128)(2,1)} %param.9) | copy-start | bytes 24625156
  3.3 2.2 %copy-start.2 = (bf16[1024,2048]{1,0:T(8,128)(2,1)S(1)}, bf16[1024,2048]{1,0:T(8,128)(2,1)}, u32[]{:S(2)}) copy-start(bf16[1024,2048]{1,0:T(8,128)(2,1)} %delta_hbm.1) | copy-start | bytes 12582916
  5.5 0.9 %copy-start.3 = (bf16[2048,64]{0,1:T(8,128)(2,1)S(1)}, bf16[2048,64]{0,1:T(8,128)(2,1)}, u32[]{:S(2)}) copy-start(bf16[2048,64]{0,1:T(8,128)(2,1)} %param.10) | copy-start | bytes 786436
  6.5 0.7 copy-start.4
  7.2 11.9 %copy-start = (bf16[512,2048]{1,0:T(8,128)(2,1)S(1)}, bf16[512,2048]{1,0:T(8,128)(2,1)}, u32[]{:S(2)}) copy-start(bf16[512,2048]{1,0:T(8,128)(2,1)} %refs_16_.1) | copy-start | bytes 6291460
  7.2 11.9 %copy-start.5 = (s32[1,128]{1,0:T(1,128)S(1)}, s32[1,128]{1,0:T(1,128)}, u32[]{:S(2)}) copy-start(s32[1,128]{1,0:T(1,128)} %lengths.1) | copy-start | bytes 1540
  16.1 9.3 %collective-permute-start.10 = (bf16[128,1024]{1,0:T(8,128)(2,1)S(1)}, bf16[128,1024]{1,0:T(8,128)(2,1)S(1)}, u32[]{:S(2)}, u32[]{:S(2)}) collective-permute-start(bf16[128,1024]{1,0:T(8,128)(2,1)S(1)} %get-tuple-element.26.sent), channel_id=1, source_target_pairs={{0,2},{2,0},{1,3},{3,1},{4,6},{6,4},{5,7},{7,5},{8,10},{10,8},{9,1... | collective-permute-start | bytes 786440 | tf_op jit(solution)/shard_map/ppermute | solution.py:32
  19.6 9.7 %collective-permute-start = (f32[136,128]{1,0:T(8,128)S(1)}, f32[136,128]{1,0:T(8,128)S(1)}, u32[]{:S(2)}, u32[]{:S(2)}) collective-permute-start(f32[136,128]{1,0:T(8,128)S(1)} %get-tuple-element.22), channel_id=1, source_target_pairs={{0,4},{4,8},{8,12},{12,0},{1,5},{5,9},{9,13},{13,1},{2,6},{6,10},{... | collective-permute-start | bytes 208904 | tf_op jit(solution)/shard_map/ppermute | solution.py:32
  21.2 9.1 %collective-permute-start.1 = (f32[136,128]{1,0:T(8,128)S(1)}, f32[136,128]{1,0:T(8,128)S(1)}, u32[]{:S(2)}, u32[]{:S(2)}) collective-permute-start(f32[136,128]{1,0:T(8,128)S(1)} %get-tuple-element.23), channel_id=1, source_target_pairs={{0,8},{4,12},{8,0},{12,4},{1,9},{5,13},{9,1},{13,5},{2,10},{6,14},... | collective-permute-start | bytes 208904 | tf_op jit(solution)/shard_map/ppermute | solution.py:32
  23.8 6.6 %collective-permute-start.2 = (f32[136,128]{1,0:T(8,128)S(1)}, f32[136,128]{1,0:T(8,128)S(1)}, u32[]{:S(2)}, u32[]{:S(2)}) collective-permute-start(f32[136,128]{1,0:T(8,128)S(1)} %get-tuple-element.24), channel_id=1, source_target_pairs={{0,12},{4,0},{8,4},{12,8},{1,13},{5,1},{9,5},{13,9},{2,14},{6,2},{... | collective-permute-start | bytes 208904 | tf_op jit(solution)/shard_map/ppermute | solution.py:32
  25.4 35.3 %collective-permute-start.13 = (bf16[128,1024]{1,0:T(8,128)(2,1)S(1)}, bf16[128,1024]{1,0:T(8,128)(2,1)S(1)}, u32[]{:S(2)}, u32[]{:S(2)}) collective-permute-start(bf16[128,1024]{1,0:T(8,128)(2,1)S(1)} %shard_map.67.factors), channel_id=1, source_target_pairs={{0,12},{4,0},{8,4},{12,8},{1,13},{5,1},{9,5},{13,9},{2,14},{6,2},{... | collective-permute-start | bytes 786440 | tf_op jit(solution)/shard_map/ppermute | solution.py:32
  29.3 29.6 %collective-permute-start.12 = (bf16[128,1024]{1,0:T(8,128)(2,1)S(1)}, bf16[128,1024]{1,0:T(8,128)(2,1)S(1)}, u32[]{:S(2)}, u32[]{:S(2)}) collective-permute-start(bf16[128,1024]{1,0:T(8,128)(2,1)S(1)} %shard_map.67.factors), channel_id=1, source_target_pairs={{0,8},{4,12},{8,0},{12,4},{1,9},{5,13},{9,1},{13,5},{2,10},{6,14},... | collective-permute-start | bytes 786440 | tf_op jit(solution)/shard_map/ppermute | solution.py:32
  29.3 18.3 %collective-permute-start.11 = (bf16[128,1024]{1,0:T(8,128)(2,1)S(1)}, bf16[128,1024]{1,0:T(8,128)(2,1)S(1)}, u32[]{:S(2)}, u32[]{:S(2)}) collective-permute-start(bf16[128,1024]{1,0:T(8,128)(2,1)S(1)} %shard_map.67.factors), channel_id=1, source_target_pairs={{0,4},{4,8},{8,12},{12,0},{1,5},{5,9},{9,13},{13,1},{2,6},{6,10},{... | collective-permute-start | bytes 786440 | tf_op jit(solution)/shard_map/ppermute | solution.py:32
  43.6 14.6 %collective-permute-start.5 = (f32[136,128]{1,0:T(8,128)S(1)}, f32[136,128]{1,0:T(8,128)S(1)}, u32[]{:S(2)}, u32[]{:S(2)}) collective-permute-start(f32[136,128]{1,0:T(8,128)S(1)} %shard_map.65.refs_0_), channel_id=1, source_target_pairs={{0,12},{4,0},{8,4},{12,8},{1,13},{5,1},{9,5},{13,9},{2,14},{6,2},{... | collective-permute-start | bytes 208904 | tf_op jit(solution)/shard_map/ppermute | solution.py:32
  46.5 11.8 %collective-permute-start.4 = (f32[136,128]{1,0:T(8,128)S(1)}, f32[136,128]{1,0:T(8,128)S(1)}, u32[]{:S(2)}, u32[]{:S(2)}) collective-permute-start(f32[136,128]{1,0:T(8,128)S(1)} %shard_map.65.refs_0_), channel_id=1, source_target_pairs={{0,8},{4,12},{8,0},{12,4},{1,9},{5,13},{9,1},{13,5},{2,10},{6,14},... | collective-permute-start | bytes 208904 | tf_op jit(solution)/shard_map/ppermute | solution.py:32
  47.6 11.2 %collective-permute-start.3 = (f32[136,128]{1,0:T(8,128)S(1)}, f32[136,128]{1,0:T(8,128)S(1)}, u32[]{:S(2)}, u32[]{:S(2)}) collective-permute-start(f32[136,128]{1,0:T(8,128)S(1)} %shard_map.65.refs_0_), channel_id=1, source_target_pairs={{0,4},{4,8},{8,12},{12,0},{1,5},{5,9},{9,13},{13,1},{2,6},{6,10},{... | collective-permute-start | bytes 208904 | tf_op jit(solution)/shard_map/ppermute | solution.py:32
  58.2 3.9 %collective-permute-start.6 = (f32[136,128]{1,0:T(8,128)S(1)}, f32[136,128]{1,0:T(8,128)S(1)}, u32[]{:S(2)}, u32[]{:S(2)}) collective-permute-start(f32[136,128]{1,0:T(8,128)S(1)} %shard_map.65.refs_0_), channel_id=1, source_target_pairs={{0,1},{1,0},{2,3},{3,2},{4,5},{5,4},{6,7},{7,6},{8,9},{9,8},{10,11... | collective-permute-start | bytes 208904 | tf_op jit(solution)/shard_map/ppermute | solution.py:32
  58.3 3.9 %collective-permute-start.9 = (f32[136,128]{1,0:T(8,128)S(1)}, f32[136,128]{1,0:T(8,128)S(1)}, u32[]{:S(2)}, u32[]{:S(2)}) collective-permute-start(f32[136,128]{1,0:T(8,128)S(1)} %collective-permute-done.5.refs_3_), channel_id=1, source_target_pairs={{0,1},{1,0},{2,3},{3,2},{4,5},{5,4},{6,7},{7,6},{8,9},{9,8},{10,11... | collective-permute-start | bytes 208904 | tf_op jit(solution)/shard_map/ppermute | solution.py:32
  58.8 3.4 %collective-permute-start.8 = (f32[136,128]{1,0:T(8,128)S(1)}, f32[136,128]{1,0:T(8,128)S(1)}, u32[]{:S(2)}, u32[]{:S(2)}) collective-permute-start(f32[136,128]{1,0:T(8,128)S(1)} %collective-permute-done.4.refs_2_), channel_id=1, source_target_pairs={{0,1},{1,0},{2,3},{3,2},{4,5},{5,4},{6,7},{7,6},{8,9},{9,8},{10,11... | collective-permute-start | bytes 208904 | tf_op jit(solution)/shard_map/ppermute | solution.py:32
  58.9 3.3 %collective-permute-start.7 = (f32[136,128]{1,0:T(8,128)S(1)}, f32[136,128]{1,0:T(8,128)S(1)}, u32[]{:S(2)}, u32[]{:S(2)}) collective-permute-start(f32[136,128]{1,0:T(8,128)S(1)} %collective-permute-done.3.refs_1_), channel_id=1, source_target_pairs={{0,1},{1,0},{2,3},{3,2},{4,5},{5,4},{6,7},{7,6},{8,9},{9,8},{10,11... | collective-permute-start | bytes 208904 | tf_op jit(solution)/shard_map/ppermute | solution.py:32
  64.8 8.4 %collective-permute-start.14 = (bf16[256,512]{1,0:T(8,128)(2,1)S(1)}, bf16[256,512]{1,0:T(8,128)(2,1)S(1)}, u32[]{:S(2)}, u32[]{:S(2)}) collective-permute-start(bf16[256,512]{1,0:T(8,128)(2,1)S(1)} %get-tuple-element.36), channel_id=1, source_target_pairs={{0,2},{2,0},{1,3},{3,1},{4,6},{6,4},{5,7},{7,5},{8,10},{10,8},{9,1... | collective-permute-start | bytes 786440 | tf_op jit(solution)/shard_map/ppermute | solution.py:32

commit v2 on v1

--- a/solution.py
+++ b/solution.py
@@ -8,12 +8,13 @@
 
 FBLK = 128
 SLAB = FBLK + 8
+PIVOTS = 4
 
 damping = 0.1
 
 VMEM = pl.BlockSpec(memory_space=pltpu.VMEM)
 SMEM = pl.BlockSpec(memory_space=pltpu.SMEM)
-HBM = pl.BlockSpec(memory_space=pl.ANY)
+HBM = pl.BlockSpec(memory_space=pltpu.HBM)
 
 
 def call(kernel, outs, in_specs, scratch=(), vmem=48, flops=0, moved=0):
@@ -74,15 +75,46 @@
 
 
 def inverted(block):
-    lane = square(1)
-    row8 = lax.broadcasted_iota(jnp.int32, (FBLK, FBLK), 0)
-    for k in range(FBLK):
-        column = jnp.broadcast_to(block[:, k:k + 1], (FBLK, FBLK))
-        pivot = 1.0 / column[k:k + 1, :]
-        line = jnp.where(lane[:1, :] == k, pivot, block[k:k + 1, :] * pivot)
-        rest = jnp.where(lane == k, 0.0, block) - column * line
-        block = jnp.where(row8 == k, line, rest)
-    return block
+    lane = lax.broadcasted_iota(jnp.int32, (8, FBLK), 1)
+    sublane = lax.broadcasted_iota(jnp.int32, (8, FBLK), 0)
+    groups = [block[8 * g:8 * (g + 1), :] for g in range(FBLK // 8)]
+
+    def across(value, row):
+        return jnp.broadcast_to(value[row:row + 1, :], (8, FBLK))
+
+    def along(value, column):
+        return jnp.broadcast_to(value[:, column:column + 1], (8, FBLK))
+
+    for first in range(0, FBLK, PIVOTS):
+        home, top = first // 8, first % 8
+        count = range(PIVOTS)
+        within = (lane >= first) & (lane < first + PIVOTS)
+        panel = groups[home]
+        columns = [along(panel, first + j) for j in count]
+        pivots = [[across(columns[j], top + i) for j in count] for i in count]
+        lines = [
+            jnp.where(within, jnp.where(lane == first + i, 1.0, 0.0), across(panel, top + i)) for i in count
+        ]
+        for i in count:
+            scale = 1.0 / pivots[i][i]
+            lines[i] = lines[i] * scale
+            for j in range(i + 1, PIVOTS):
+                pivots[i][j] = pivots[i][j] * scale
+            for other in count:
+                if other != i:
+                    lines[other] = lines[other] - pivots[other][i] * lines[i]
+                    for j in range(i + 1, PIVOTS):
+                        pivots[other][j] = pivots[other][j] - pivots[other][i] * pivots[i][j]
+        for g in range(FBLK // 8):
+            rest = jnp.where(within, 0.0, groups[g])
+            for j in count:
+                column = columns[j] if g == home else along(groups[g], first + j)
+                rest = rest - column * lines[j]
+            if g == home:
+                for j in count:
+                    rest = jnp.where(sublane == top + j, lines[j], rest)
+            groups[g] = rest
+    return jnp.concatenate(groups, axis=0)
 
 
 def factor_kernel(examples, scale, *refs):
@@ -156,38 +188,42 @@
     out[rows, :] = sent[rows, :] + got[rows, :]
 
 
-def queries_kernel(each, factors, slab, high_out, low_out):
-    tokens = factors.shape[1]
-    proj = factors.shape[0] - 2 * each
-    queries = high_out.shape[1]
-    lengths = slab[pl.ds(FBLK + 1, 1), :]
+def queries_kernel(each, cycle, factors, *refs):
+    slabs, (high_out, low_out) = refs[:cycle], refs[cycle:]
+    mine = lax.axis_index("dp")
+    tokens = factors.shape[2]
+    proj = factors.shape[1] - 2 * each
     upto = jnp.where(square(0) <= square(1), 1.0, 0.0).astype(jnp.bfloat16)
-    ends = lax.dot_general(
-        jnp.broadcast_to(lengths, (8, queries)).astype(jnp.bfloat16), upto, (((1,), (0,)), ((), ())),
-        preferred_element_type=jnp.float32,
-    )[:1]
-    starts = ends - lengths
-    place = lax.broadcasted_iota(jnp.int32, (tokens, queries), 0).astype(jnp.float32)
-    inside = jnp.where((place >= starts) & (place < ends), 1.0, 0.0).astype(jnp.bfloat16)
-    output = factors[pl.ds(0, each), :].astype(jnp.float32) + factors[pl.ds(each, each), :].astype(jnp.float32)
-    inputs = factors[pl.ds(2 * each, proj), :].astype(jnp.float32)
-    step = 8
-    for start in range(0, each, step):
-        grads = jnp.concatenate(
-            [(inputs * output[r:r + 1, :]).astype(jnp.bfloat16) for r in range(start, start + step)], axis=0
-        )
-        summed = jnp.dot(grads, inside, preferred_element_type=jnp.float32)
-        high, low = halves(summed)
-        high_out[pl.ds(start * proj, step * proj), :] = high
-        low_out[pl.ds(start * proj, step * proj), :] = low
+    place = lax.broadcasted_iota(jnp.int32, (tokens, FBLK), 0).astype(jnp.float32)
+    for shift in range(cycle):
+        source = lax.rem(mine + cycle - shift, cycle)
+        lengths = slabs[shift][pl.ds(FBLK + 1, 1), :]
+        ends = lax.dot_general(
+            jnp.broadcast_to(lengths, (8, FBLK)).astype(jnp.bfloat16), upto, (((1,), (0,)), ((), ())),
+            preferred_element_type=jnp.float32,
+        )[:1]
+        starts = ends - lengths
+        inside = jnp.where((place >= starts) & (place < ends), 1.0, 0.0).astype(jnp.bfloat16)
+        output = factors[source, pl.ds(0, each), :].astype(jnp.float32)
+        output = output + factors[source, pl.ds(each, each), :].astype(jnp.float32)
+        inputs = factors[source, pl.ds(2 * each, proj), :].astype(jnp.float32)
+        columns = pl.ds(shift * FBLK, FBLK)
+        step = 8
+        for start in range(0, each, step):
+            grads = jnp.concatenate(
+                [(inputs * output[r:r + 1, :]).astype(jnp.bfloat16) for r in range(start, start + step)], axis=0
+            )
+            summed = jnp.dot(grads, inside, preferred_element_type=jnp.float32)
+            high, low = halves(summed)
+            high_out[pl.ds(start * proj, step * proj), columns] = high
+            low_out[pl.ds(start * proj, step * proj), columns] = low
 
 
 def scores_kernel(cycle, *refs):
     own, peers = refs[:cycle], refs[cycle:2 * cycle]
-    highs, lows = refs[2 * cycle:3 * cycle], refs[3 * cycle:4 * cycle]
-    train, sent, kept, pre = refs[4 * cycle:]
+    highs, lows, train, sent, kept, pre = refs[2 * cycle:]
     mine, rep, model = lax.axis_index("dp"), lax.axis_index("rep"), lax.axis_index("mp")
-    queries = highs[0].shape[1]
+    queries = highs.shape[1] // cycle
     for side, slabs in enumerate((own, peers)):
         half = rep if side == 0 else 1 - rep
         for shift in range(cycle):
@@ -197,8 +233,7 @@
             for index, block in enumerate(blocks):
                 rows = pl.ds(pl.multiple_of(owner * (2 * FBLK) + index * FBLK, FBLK), FBLK)
                 high, low = halves(block)
-                right_high = jnp.concatenate([ref[rows, :] for ref in highs], axis=1)
-                right_low = jnp.concatenate([ref[rows, :] for ref in lows], axis=1)
+                right_high, right_low = highs[rows, :], lows[rows, :]
                 solved = jnp.dot(
                     jnp.concatenate([high, high, low], axis=1),
                     jnp.concatenate([right_high, right_low, right_high], axis=0),
@@ -263,7 +298,7 @@
         flops=tokens * each,
         moved=8 * tokens * each * 4,
     )(kept, sent, got)
-    gathered = [factors] + [passed_along(factors, "dp", s) for s in range(1, cycle)]
+    gathered = lax.all_gather(factors, "dp", axis=0)
 
     inverse = call(
         functools.partial(factor_kernel, train_rows * cycle, 1.0 / proj),
@@ -276,29 +311,25 @@
     inverses = [inverse] + [passed_along(inverse, "dp", s) for s in range(1, cycle)]
     peers = [passed_along(slab, "rep", 1) for slab in inverses]
 
-    highs, lows = [], []
-    for s in range(cycle):
-        high, low = call(
-            functools.partial(queries_kernel, each),
-            [shape((feat, queries), bf16)] * 2,
-            [VMEM, VMEM],
-            vmem=24,
-            flops=2 * feat * tokens * queries,
-            moved=6 * feat * queries,
-        )(gathered[s], parts[s])
-        highs.append(high)
-        lows.append(low)
+    highs, lows = call(
+        functools.partial(queries_kernel, each, cycle),
+        [shape((feat, cycle * queries), bf16)] * 2,
+        [VMEM] * (1 + cycle),
+        vmem=24,
+        flops=2 * feat * tokens * queries * cycle,
+        moved=6 * feat * queries * cycle,
+    )(gathered, *parts)
 
     half_rows = train_rows // lax.axis_size("mp")
     outgoing, own = call(
         functools.partial(scores_kernel, cycle),
         [shape((half_rows, cycle * queries), bf16)] * 2,
-        [VMEM] * (4 * cycle + 1),
+        [VMEM] * (2 * cycle + 3),
         [pltpu.VMEM((feat, cycle * queries), bf16)],
         vmem=32,
         flops=2 * train_rows * feat * cycle * queries,
         moved=8 * feat * queries * cycle,
-    )(*inverses, *peers, *highs, *lows, train_grads)
+    )(*inverses, *peers, highs, lows, train_grads)
     incoming = passed_along(outgoing, "mp", 1)
     total = (own.astype(f32) + incoming.astype(f32)).astype(bf16)
     return total.reshape(half_rows, cycle, 1, queries)

time: 74.2 us -> 93.2 us (1.26)
  waiting for transfers between devices: 7.09 us -> 21.5 us
  between operations: 0.14 us -> 13.5 us
  starting transfers between devices: 27.8 us -> 14.9 us
  Pallas kernels: 30.9 us -> 33.8 us
  local copies, waits for them, and re-layouts: 7.93 us -> 9.15 us
    ppermute x15 -> x12, waiting for transfers between devices: 7.09 us -> 21.4 us  [passed_along(): lax.ppermute(shard, axis, [(i, (i + by) % size) for i in range(size)])]
    ppermute x15 -> x12, starting transfers between devices: 27.8 us -> 14.9 us  [passed_along(): lax.ppermute(shard, axis, [(i, (i + by) % size) for i in range(size)])]
    pallas_call x1, Pallas kernels: 13.3 us -> 15.8 us  [split_over_blocks(): call(functools.partial(factor_kernel, train_rows * cycle, 1.0 / proj), sh...]
    unnamed x12 -> x14, local copies, waits for them, and re-layouts: 7.16 us -> 8.39 us
    pallas_call x4 -> x1, Pallas kernels: 5.63 us -> 5.22 us  [split_over_blocks(): call(functools.partial(queries_kernel, each, cycle), [shape((feat, cycle...]
  transfers between devices with their start and end apart: 15 -> 13, of which waited for: 2 -> 7; matrix products, arithmetic and copies ran while one was open for 0% -> 0% of each run, Pallas kernels for 26% -> 23%
where the time goes in v2:
time: 93.2 us; the launch traced here: 92.8 us
  Pallas kernels  33.8 us (36%)
  waiting for transfers between devices  21.5 us (23%)
  starting transfers between devices  14.9 us (16%)
  between operations  13.5 us (14%)
  local copies, waits for them, and re-layouts  9.15 us (10%)
    ppermute x12, waiting for transfers between devices, passed_along(): lax.ppermute(shard, axis, [(i, (i + by) % size) for i in range(size)])  21.4 us
    pallas_call x1, Pallas kernels, split_over_blocks(): call(functools.partial(factor_kernel, train_rows * cycle, 1.0 / proj), sh...  15.8 us
    ppermute x12, starting transfers between devices, passed_along(): lax.ppermute(shard, axis, [(i, (i + by) % size) for i in range(size)])  14.9 us
    pallas_call x1, Pallas kernels, split_over_blocks(): call(factors_kernel, [shape((2 * each + proj, tokens), bf16), shape((each...  8.87 us
    unnamed x14, local copies, waits for them, and re-layouts  8.39 us
    pallas_call x1, Pallas kernels, split_over_blocks(): call(functools.partial(queries_kernel, each, cycle), [shape((feat, cycle...  5.22 us
    pallas_call x1, Pallas kernels, split_over_blocks(): call(functools.partial(scores_kernel, cycle), [shape((half_rows, cycle *...  2.58 us
  transfers between devices with their start and end apart: 13, of which 7 were waited for; matrix products, arithmetic and copies ran while one was open for 0% of the time, Pallas kernels for 23%

profile of v2, /device:TPU:0, one launch (start us, length us, event | category | flops | bytes accessed | tf_op | source)
XLA Modules:
  0.0 92.8 jit_solution(8272511981821488297)
XLA Ops:
  6.5 0.0 all-gather.3.cloned.1.call-start
  6.5 0.0 copy-start.1
  6.5 3.3 %copy-done.1 = bf16[64128,64]{0,1:T(8,128)(2,1)S(1)} copy-done((bf16[64128,64]{0,1:T(8,128)(2,1)S(1)}, bf16[64128,64]{0,1:T(8,128)(2,1)}, u32[]{:S(2)}) %copy-start.1) | copy-done | bytes 8208408
  9.9 0.0 copy-start.2
  9.9 2.2 %copy-done.2 = bf16[1024,2048]{1,0:T(8,128)(2,1)S(1)} copy-done((bf16[1024,2048]{1,0:T(8,128)(2,1)S(1)}, bf16[1024,2048]{1,0:T(8,128)(2,1)}, u32[]{:S(2)}) %copy-start.2) | copy-done | bytes 4194328
  12.1 0.0 copy-start.3
  12.1 0.9 %copy-done.3 = bf16[2048,64]{0,1:T(8,128)(2,1)S(1)} copy-done((bf16[2048,64]{0,1:T(8,128)(2,1)S(1)}, bf16[2048,64]{0,1:T(8,128)(2,1)}, u32[]{:S(2)}) %copy-start.3) | copy-done | bytes 262168
  13.0 0.0 copy-start.4
  13.0 0.7 copy-done.4
  13.7 0.0 copy-start
  13.7 0.0 copy-start.5
  13.7 8.9 %shard_map.66 = (bf16[128,1024]{1,0:T(8,128)(2,1)S(1)}, f32[32,1024]{1,0:T(8,128)S(1)}) custom-call(s32[1024]{0:T(1024)S(1)} %copy-done.4, s32[8,128]{1,0:T(8,128)S(1)} %bitcast.7, bf16[1024,2048]{1,0:T(8,128)(2,1)S(1)} %copy-done.2, bf16[64,64128]{1,0:T(8,128)(2,1)S(1)} %bitcast.5, bf16[64,2048]{1,0:T(8,128)(2,1)S(1)} %bitcast.6), custom_call_target="tpu_custom_call" | custom-call | flops 268435456 | bytes 24805376 | tf_op jit(solution)/shard_map/pallas_call | solution.py:278
  22.6 3.0 %collective-permute-start.10 = (bf16[128,1024]{1,0:T(8,128)(2,1)S(1)}, bf16[128,1024]{1,0:T(8,128)(2,1)S(1)}, u32[]{:S(2)}, u32[]{:S(2)}) collective-permute-start(bf16[128,1024]{1,0:T(8,128)(2,1)S(1)} %get-tuple-element.20.sent), channel_id=1, source_target_pairs={{0,2},{2,0},{1,3},{3,1},{4,6},{6,4},{5,7},{7,5},{8,10},{10,8},{9,1... | collective-permute-start | bytes 786440 | tf_op jit(solution)/shard_map/ppermute | solution.py:33
  25.6 6.3 %collective-permute-done.10.got = bf16[128,1024]{1,0:T(8,128)(2,1)S(1)} collective-permute-done((bf16[128,1024]{1,0:T(8,128)(2,1)S(1)}, bf16[128,1024]{1,0:T(8,128)(2,1)S(1)}, u32[]{:S(2)}, u32[]{:S(2)}) %collective-permute-start.10) | collective-permute-done | bytes 262176 | tf_op jit(solution)/shard_map/ppermute | solution.py:33
  31.9 0.8 shard_map.67
  32.7 0.0 all-gather.3.cloned.1.call-update
  32.7 0.0 copy-done
  32.7 0.0 copy-done.5
  32.7 0.5 shard_map.64
  33.2 1.9 %collective-permute-start = (f32[136,128]{1,0:T(8,128)S(1)}, f32[136,128]{1,0:T(8,128)S(1)}, u32[]{:S(2)}, u32[]{:S(2)}) collective-permute-start(f32[136,128]{1,0:T(8,128)S(1)} %get-tuple-element.16), channel_id=1, source_target_pairs={{0,4},{4,8},{8,12},{12,0},{1,5},{5,9},{9,13},{13,1},{2,6},{6,10},{... | collective-permute-start | bytes 208904 | tf_op jit(solution)/shard_map/ppermute | solution.py:33
  35.1 2.6 %collective-permute-start.1 = (f32[136,128]{1,0:T(8,128)S(1)}, f32[136,128]{1,0:T(8,128)S(1)}, u32[]{:S(2)}, u32[]{:S(2)}) collective-permute-start(f32[136,128]{1,0:T(8,128)S(1)} %get-tuple-element.17), channel_id=1, source_target_pairs={{0,8},{4,12},{8,0},{12,4},{1,9},{5,13},{9,1},{13,5},{2,10},{6,14},... | collective-permute-start | bytes 208904 | tf_op jit(solution)/shard_map/ppermute | solution.py:33
  37.7 1.3 %collective-permute-start.2 = (f32[136,128]{1,0:T(8,128)S(1)}, f32[136,128]{1,0:T(8,128)S(1)}, u32[]{:S(2)}, u32[]{:S(2)}) collective-permute-start(f32[136,128]{1,0:T(8,128)S(1)} %get-tuple-element.18), channel_id=1, source_target_pairs={{0,12},{4,0},{8,4},{12,8},{1,13},{5,1},{9,5},{13,9},{2,14},{6,2},{... | collective-permute-start | bytes 208904 | tf_op jit(solution)/shard_map/ppermute | solution.py:33
  39.0 1.1 %collective-permute-done.refs_1_ = f32[136,128]{1,0:T(8,128)S(1)} collective-permute-done((f32[136,128]{1,0:T(8,128)S(1)}, f32[136,128]{1,0:T(8,128)S(1)}, u32[]{:S(2)}, u32[]{:S(2)}) %collective-permute-start) | collective-permute-done | bytes 69664 | tf_op jit(solution)/shard_map/ppermute | solution.py:33
  40.1 2.1 %collective-permute-done.1.refs_2_ = f32[136,128]{1,0:T(8,128)S(1)} collective-permute-done((f32[136,128]{1,0:T(8,128)S(1)}, f32[136,128]{1,0:T(8,128)S(1)}, u32[]{:S(2)}, u32[]{:S(2)}) %collective-permute-start.1) | collective-permute-done | bytes 69664 | tf_op jit(solution)/shard_map/ppermute | solution.py:33
  42.2 0.2 collective-permute-done.2.refs_3_
  42.4 15.8 %shard_map.65.refs_0_ = f32[136,128]{1,0:T(8,128)S(1)} custom-call(f32[136,128]{1,0:T(8,128)S(1)} %get-tuple-element.15.refs_0_, f32[136,128]{1,0:T(8,128)S(1)} %collective-permute-done.refs_1_, f32[136,128]{1,0:T(8,128)S(1)} %collective-permute-done.1.refs_2_, f32[136,128]{1,0:T(8,128)S(1)} %collective-permute-done.2.refs_3_), custom_call_target="tpu_custom_call" | custom-call | flops 10000000000 | bytes 1000000 | tf_op jit(solution)/shard_map/pallas_call | solution.py:303
  58.2 1.2 %collective-permute-start.3 = (f32[136,128]{1,0:T(8,128)S(1)}, f32[136,128]{1,0:T(8,128)S(1)}, u32[]{:S(2)}, u32[]{:S(2)}) collective-permute-start(f32[136,128]{1,0:T(8,128)S(1)} %shard_map.65.refs_0_), channel_id=1, source_target_pairs={{0,4},{4,8},{8,12},{12,0},{1,5},{5,9},{9,13},{13,1},{2,6},{6,10},{... | collective-permute-start | bytes 208904 | tf_op jit(solution)/shard_map/ppermute | solution.py:33
  59.4 2.2 %collective-permute-start.4 = (f32[136,128]{1,0:T(8,128)S(1)}, f32[136,128]{1,0:T(8,128)S(1)}, u32[]{:S(2)}, u32[]{:S(2)}) collective-permute-start(f32[136,128]{1,0:T(8,128)S(1)} %shard_map.65.refs_0_), channel_id=1, source_target_pairs={{0,8},{4,12},{8,0},{12,4},{1,9},{5,13},{9,1},{13,5},{2,10},{6,14},... | collective-permute-start | bytes 208904 | tf_op jit(solution)/shard_map/ppermute | solution.py:33
  61.6 0.5 collective-permute-start.5
  62.1 0.0 collective-permute-start.6
  62.1 3.6 %collective-permute-done.3.refs_1_ = f32[136,128]{1,0:T(8,128)S(1)} collective-permute-done((f32[136,128]{1,0:T(8,128)S(1)}, f32[136,128]{1,0:T(8,128)S(1)}, u32[]{:S(2)}, u32[]{:S(2)}) %collective-permute-start.3) | collective-permute-done | bytes 69664 | tf_op jit(solution)/shard_map/ppermute | solution.py:33
  65.7 0.0 collective-permute-start.7
  65.7 1.6 %collective-permute-done.4.refs_2_ = f32[136,128]{1,0:T(8,128)S(1)} collective-permute-done((f32[136,128]{1,0:T(8,128)S(1)}, f32[136,128]{1,0:T(8,128)S(1)}, u32[]{:S(2)}, u32[]{:S(2)}) %collective-permute-start.4) | collective-permute-done | bytes 69664 | tf_op jit(solution)/shard_map/ppermute | solution.py:33
  67.3 0.0 collective-permute-start.8
  67.3 0.0 collective-permute-done.5.refs_3_
  67.3 0.5 collective-permute-start.9
  67.8 0.0 all-gather.3.cloned.1.call-done
  67.8 1.2 %copy-done.6 = bf16[512,1024]{1,0:T(8,128)(2,1)S(1)} copy-done((bf16[512,1024]{1,0:T(8,128)(2,1)S(1)}, bf16[512,1024]{1,0:T(8,128)(2,1)}, u32[]{:S(2)}) %copy-start.6) | copy-done | bytes 1048600
  69.0 5.2 %shard_map.68 = (bf16[2048,512]{1,0:T(8,128)(2,1)S(1)}, bf16[2048,512]{1,0:T(8,128)(2,1)S(1)}) custom-call(bf16[4,128,1024]{2,1,0:T(8,128)(2,1)S(1)} %bitcast.8, f32[136,128]{1,0:T(8,128)S(1)} %get-tuple-element.15.refs_0_, f32[136,128]{1,0:T(8,128)S(1)} %collective-permute-done.refs_1_, f32[136,128]{1,0:T(8,128)S(1)} %collective-permute-done.1.refs_2_, ...), custom_call_target="tpu_custom_call" | custom-call | flops 2147483648 | bytes 6291456 | tf_op jit(solution)/shard_map/pallas_call | solution.py:314
  74.2 0.0 collective-permute-done.6.refs_4_
  74.2 0.0 collective-permute-done.7.refs_5_
  74.3 0.0 collective-permute-done.8.refs_6_
  74.3 0.0 collective-permute-done.9.refs_7_
  74.3 2.6 %shard_map.69 = (bf16[256,512]{1,0:T(8,128)(2,1)S(1)}, bf16[256,512]{1,0:T(8,128)(2,1)S(1)}) custom-call(f32[136,128]{1,0:T(8,128)S(1)} %shard_map.65.refs_0_, f32[136,128]{1,0:T(8,128)S(1)} %collective-permute-done.3.refs_1_, f32[136,128]{1,0:T(8,128)S(1)} %collective-permute-done.4.refs_2_, f32[136,128]{1,0:T(8,128)S(1)} %collective-permute-done.5.refs_3_, ...), custom_call_target="tpu_custom_call" | custom-call | flops 1073741824 | bytes 8388608 | tf_op jit(solution)/shard_map/pallas_call | solution.py:324
  76.9 1.7 %collective-permute-start.11 = (bf16[256,512]{1,0:T(8,128)(2,1)S(1)}, bf16[256,512]{1,0:T(8,128)(2,1)S(1)}, u32[]{:S(2)}, u32[]{:S(2)}) collective-permute-start(bf16[256,512]{1,0:T(8,128)(2,1)S(1)} %get-tuple-element.24), channel_id=1, source_target_pairs={{0,2},{2,0},{1,3},{3,1},{4,6},{6,4},{5,7},{7,5},{8,10},{10,8},{9,1... | collective-permute-start | bytes 786440 | tf_op jit(solution)/shard_map/ppermute | solution.py:33
  78.5 6.6 %collective-permute-done.11 = bf16[256,512]{1,0:T(8,128)(2,1)S(1)} collective-permute-done((bf16[256,512]{1,0:T(8,128)(2,1)S(1)}, bf16[256,512]{1,0:T(8,128)(2,1)S(1)}, u32[]{:S(2)}, u32[]{:S(2)}) %collective-permute-start.11) | collective-permute-done | bytes 262176 | tf_op jit(solution)/shard_map/ppermute | solution.py:33
  85.2 0.1 add_convert_fusion
  85.2 0.8 reshape.7
  (1 shorter events, 0.0 us)
Async XLA Ops:
  6.5 61.2 %all-gather.3.cloned.1.call-start = ((), (), s32[]{:S(2)}) async-start(), calls=%async_computation | async-start | bytes 1310720 | tf_op jit(solution)/shard_map/all_gather | solution.py:301
  6.5 3.3 %copy-start.1 = (bf16[64128,64]{0,1:T(8,128)(2,1)S(1)}, bf16[64128,64]{0,1:T(8,128)(2,1)}, u32[]{:S(2)}) copy-start(bf16[64128,64]{0,1:T(8,128)(2,1)} %param.9) | copy-start | bytes 24625156
  9.9 2.2 %copy-start.2 = (bf16[1024,2048]{1,0:T(8,128)(2,1)S(1)}, bf16[1024,2048]{1,0:T(8,128)(2,1)}, u32[]{:S(2)}) copy-start(bf16[1024,2048]{1,0:T(8,128)(2,1)} %delta_hbm.1) | copy-start | bytes 12582916
  12.1 0.9 %copy-start.3 = (bf16[2048,64]{0,1:T(8,128)(2,1)S(1)}, bf16[2048,64]{0,1:T(8,128)(2,1)}, u32[]{:S(2)}) copy-start(bf16[2048,64]{0,1:T(8,128)(2,1)} %param.10) | copy-start | bytes 786436
  13.0 0.7 copy-start.4
  13.7 19.0 %copy-start = (bf16[512,2048]{1,0:T(8,128)(2,1)S(1)}, bf16[512,2048]{1,0:T(8,128)(2,1)}, u32[]{:S(2)}) copy-start(bf16[512,2048]{1,0:T(8,128)(2,1)} %refs_10_.1) | copy-start | bytes 6291460
  13.7 19.0 %copy-start.5 = (s32[1,128]{1,0:T(1,128)S(1)}, s32[1,128]{1,0:T(1,128)}, u32[]{:S(2)}) copy-start(s32[1,128]{1,0:T(1,128)} %lengths.1) | copy-start | bytes 1540
  22.6 9.3 %collective-permute-start.10 = (bf16[128,1024]{1,0:T(8,128)(2,1)S(1)}, bf16[128,1024]{1,0:T(8,128)(2,1)S(1)}, u32[]{:S(2)}, u32[]{:S(2)}) collective-permute-start(bf16[128,1024]{1,0:T(8,128)(2,1)S(1)} %get-tuple-element.20.sent), channel_id=1, source_target_pairs={{0,2},{2,0},{1,3},{3,1},{4,6},{6,4},{5,7},{7,5},{8,10},{10,8},{9,1... | collective-permute-start | bytes 786440 | tf_op jit(solution)/shard_map/ppermute | solution.py:33
  33.2 6.9 %collective-permute-start = (f32[136,128]{1,0:T(8,128)S(1)}, f32[136,128]{1,0:T(8,128)S(1)}, u32[]{:S(2)}, u32[]{:S(2)}) collective-permute-start(f32[136,128]{1,0:T(8,128)S(1)} %get-tuple-element.16), channel_id=1, source_target_pairs={{0,4},{4,8},{8,12},{12,0},{1,5},{5,9},{9,13},{13,1},{2,6},{6,10},{... | collective-permute-start | bytes 208904 | tf_op jit(solution)/shard_map/ppermute | solution.py:33
  35.1 7.1 %collective-permute-start.1 = (f32[136,128]{1,0:T(8,128)S(1)}, f32[136,128]{1,0:T(8,128)S(1)}, u32[]{:S(2)}, u32[]{:S(2)}) collective-permute-start(f32[136,128]{1,0:T(8,128)S(1)} %get-tuple-element.17), channel_id=1, source_target_pairs={{0,8},{4,12},{8,0},{12,4},{1,9},{5,13},{9,1},{13,5},{2,10},{6,14},... | collective-permute-start | bytes 208904 | tf_op jit(solution)/shard_map/ppermute | solution.py:33
  37.7 4.7 %collective-permute-start.2 = (f32[136,128]{1,0:T(8,128)S(1)}, f32[136,128]{1,0:T(8,128)S(1)}, u32[]{:S(2)}, u32[]{:S(2)}) collective-permute-start(f32[136,128]{1,0:T(8,128)S(1)} %get-tuple-element.18), channel_id=1, source_target_pairs={{0,12},{4,0},{8,4},{12,8},{1,13},{5,1},{9,5},{13,9},{2,14},{6,2},{... | collective-permute-start | bytes 208904 | tf_op jit(solution)/shard_map/ppermute | solution.py:33
  58.2 7.5 %collective-permute-start.3 = (f32[136,128]{1,0:T(8,128)S(1)}, f32[136,128]{1,0:T(8,128)S(1)}, u32[]{:S(2)}, u32[]{:S(2)}) collective-permute-start(f32[136,128]{1,0:T(8,128)S(1)} %shard_map.65.refs_0_), channel_id=1, source_target_pairs={{0,4},{4,8},{8,12},{12,0},{1,5},{5,9},{9,13},{13,1},{2,6},{6,10},{... | collective-permute-start | bytes 208904 | tf_op jit(solution)/shard_map/ppermute | solution.py:33
  59.4 7.9 %collective-permute-start.4 = (f32[136,128]{1,0:T(8,128)S(1)}, f32[136,128]{1,0:T(8,128)S(1)}, u32[]{:S(2)}, u32[]{:S(2)}) collective-permute-start(f32[136,128]{1,0:T(8,128)S(1)} %shard_map.65.refs_0_), channel_id=1, source_target_pairs={{0,8},{4,12},{8,0},{12,4},{1,9},{5,13},{9,1},{13,5},{2,10},{6,14},... | collective-permute-start | bytes 208904 | tf_op jit(solution)/shard_map/ppermute | solution.py:33
  61.6 5.7 %collective-permute-start.5 = (f32[136,128]{1,0:T(8,128)S(1)}, f32[136,128]{1,0:T(8,128)S(1)}, u32[]{:S(2)}, u32[]{:S(2)}) collective-permute-start(f32[136,128]{1,0:T(8,128)S(1)} %shard_map.65.refs_0_), channel_id=1, source_target_pairs={{0,12},{4,0},{8,4},{12,8},{1,13},{5,1},{9,5},{13,9},{2,14},{6,2},{... | collective-permute-start | bytes 208904 | tf_op jit(solution)/shard_map/ppermute | solution.py:33
  62.1 12.2 %collective-permute-start.6 = (f32[136,128]{1,0:T(8,128)S(1)}, f32[136,128]{1,0:T(8,128)S(1)}, u32[]{:S(2)}, u32[]{:S(2)}) collective-permute-start(f32[136,128]{1,0:T(8,128)S(1)} %shard_map.65.refs_0_), channel_id=1, source_target_pairs={{0,1},{1,0},{2,3},{3,2},{4,5},{5,4},{6,7},{7,6},{8,9},{9,8},{10,11... | collective-permute-start | bytes 208904 | tf_op jit(solution)/shard_map/ppermute | solution.py:33
  65.7 8.5 %collective-permute-start.7 = (f32[136,128]{1,0:T(8,128)S(1)}, f32[136,128]{1,0:T(8,128)S(1)}, u32[]{:S(2)}, u32[]{:S(2)}) collective-permute-start(f32[136,128]{1,0:T(8,128)S(1)} %collective-permute-done.3.refs_1_), channel_id=1, source_target_pairs={{0,1},{1,0},{2,3},{3,2},{4,5},{5,4},{6,7},{7,6},{8,9},{9,8},{10,11... | collective-permute-start | bytes 208904 | tf_op jit(solution)/shard_map/ppermute | solution.py:33
  67.3 7.0 %collective-permute-start.8 = (f32[136,128]{1,0:T(8,128)S(1)}, f32[136,128]{1,0:T(8,128)S(1)}, u32[]{:S(2)}, u32[]{:S(2)}) collective-permute-start(f32[136,128]{1,0:T(8,128)S(1)} %collective-permute-done.4.refs_2_), channel_id=1, source_target_pairs={{0,1},{1,0},{2,3},{3,2},{4,5},{5,4},{6,7},{7,6},{8,9},{9,8},{10,11... | collective-permute-start | bytes 208904 | tf_op jit(solution)/shard_map/ppermute | solution.py:33
  67.3 7.0 %collective-permute-start.9 = (f32[136,128]{1,0:T(8,128)S(1)}, f32[136,128]{1,0:T(8,128)S(1)}, u32[]{:S(2)}, u32[]{:S(2)}) collective-permute-start(f32[136,128]{1,0:T(8,128)S(1)} %collective-permute-done.5.refs_3_), channel_id=1, source_target_pairs={{0,1},{1,0},{2,3},{3,2},{4,5},{5,4},{6,7},{7,6},{8,9},{9,8},{10,11... | collective-permute-start | bytes 208904 | tf_op jit(solution)/shard_map/ppermute | solution.py:33
  67.8 1.2 %copy-start.6 = (bf16[512,1024]{1,0:T(8,128)(2,1)S(1)}, bf16[512,1024]{1,0:T(8,128)(2,1)}, u32[]{:S(2)}) copy-start(bf16[512,1024]{1,0:T(8,128)(2,1)} %all-gather.3.cloned.1.call-done) | copy-start | bytes 3145732
  76.9 8.3 %collective-permute-start.11 = (bf16[256,512]{1,0:T(8,128)(2,1)S(1)}, bf16[256,512]{1,0:T(8,128)(2,1)S(1)}, u32[]{:S(2)}, u32[]{:S(2)}) collective-permute-start(bf16[256,512]{1,0:T(8,128)(2,1)S(1)} %get-tuple-element.24), channel_id=1, source_target_pairs={{0,2},{2,0},{1,3},{3,1},{4,6},{6,4},{5,7},{7,5},{8,10},{10,8},{9,1... | collective-permute-start | bytes 786440 | tf_op jit(solution)/shard_map/ppermute | solution.py:33
Sparse Core Ops, SparseCore 0:
  32.8 31.0 all-gather.2

commit v3 on v1

--- a/solution.py
+++ b/solution.py
@@ -8,6 +8,7 @@
 
 FBLK = 128
 SLAB = FBLK + 8
+PANEL = 8
 
 damping = 0.1
 
@@ -60,47 +61,117 @@
     return first, second
 
 
-def gram_kernel(cycle, lengths, train, *slabs):
-    mine, half = lax.axis_index("dp"), lax.axis_index("rep")
+def gram_kernel(lengths, train, slabs):
+    cycle = slabs.shape[0]
+    half = lax.axis_index("rep")
     spare = lengths[...].astype(jnp.float32)
-    for shift in range(cycle):
-        owner = half * cycle + lax.rem(mine + shift, cycle)
-        start = pl.multiple_of(owner * (2 * FBLK), 2 * FBLK)
+    for target in range(cycle):
+        start = pl.multiple_of((half * cycle + target) * (2 * FBLK), 2 * FBLK)
         part = train[:, pl.ds(start, 2 * FBLK)]
         gram = lax.dot_general(part, part, (((0,), (0,)), ((), ())), preferred_element_type=jnp.float32)
         body, tail = pack(gram[:FBLK, :FBLK], gram[FBLK:, FBLK:], spare)
-        slabs[shift][pl.ds(0, FBLK), :] = body
-        slabs[shift][pl.ds(FBLK, 8), :] = tail
-
-
-def inverted(block):
+        slabs[target, pl.ds(0, FBLK), :] = body
+        slabs[target, pl.ds(FBLK, 8), :] = tail
+
+
+def thirds(value):
+    high = value.astype(jnp.bfloat16)
+    rest = value - high.astype(jnp.float32)
+    middle = rest.astype(jnp.bfloat16)
+    return high, middle, (rest - middle.astype(jnp.float32)).astype(jnp.bfloat16)
+
+
+def at_rows(panel, first):
+    pair = 2 * PANEL
+    blank = jnp.zeros((PANEL, FBLK), jnp.float32)
+    panel = panel.astype(jnp.float32)
+    piece = jnp.concatenate([panel, blank] if first % pair == 0 else [blank, panel], axis=0).astype(jnp.bfloat16)
+    before = first // pair * pair
+    pieces = [jnp.zeros((before, FBLK), jnp.bfloat16), piece, jnp.zeros((FBLK - before - pair, FBLK), jnp.bfloat16)]
+    return jnp.concatenate([piece for piece in pieces if piece.shape[0]], axis=0)
+
+
+def product(left, right, first):
+    high, middle, low = thirds(left)
+    right_high, right_middle, right_low = (at_rows(part, first) for part in thirds(right))
+    both = jnp.concatenate([right_high, right_middle], axis=1)
+    large = jnp.dot(
+        jnp.concatenate([high, middle], axis=1), jnp.concatenate([both, both], axis=0),
+        preferred_element_type=jnp.float32,
+    )
+    small = jnp.dot(
+        jnp.concatenate([high, low], axis=1), jnp.concatenate([right_low, right_high], axis=0),
+        preferred_element_type=jnp.float32,
+    )
+    return large[:, :FBLK] + (large[:, FBLK:] + small)
+
+
+def eliminated(panel, first):
+    lane = lax.broadcasted_iota(jnp.int32, (PANEL, FBLK), 1)
+    sublane = lax.broadcasted_iota(jnp.int32, (PANEL, FBLK), 0)
+    within = (lane >= first) & (lane < first + PANEL)
+    count = range(PANEL)
+
+    def across(value, row):
+        return jnp.broadcast_to(value[row:row + 1, :], (PANEL, FBLK))
+
+    columns = [jnp.broadcast_to(panel[:, first + j:first + j + 1], (PANEL, FBLK)) for j in count]
+    pivots = [[across(columns[j], i) if j >= i else None for j in count] for i in count]
+    rest = jnp.where(within, jnp.where(lane == first + sublane, 1.0, 0.0), panel)
+    lines = [across(rest, i) for i in count]
+    for i in count:
+        scale = 1.0 / pivots[i][i]
+        scaled = lines[i] * scale
+        shares = [pivots[i][j] * scale if j > i else None for j in count]
+        for m in range(i + 1, PANEL):
+            lines[m] = lines[m] - pivots[i][m] * scaled
+            for j in range(m, PANEL):
+                pivots[m][j] = pivots[m][j] - shares[m] * pivots[i][j]
+        lines[i] = scaled
+        pivots[i] = shares
+    for i in reversed(count):
+        for m in range(i):
+            lines[m] = lines[m] - pivots[m][i] * lines[i]
+    result = lines[0]
+    for i in range(1, PANEL):
+        result = jnp.where(sublane == i, lines[i], result)
+    return result
+
+
+def inverted(blocks):
     lane = square(1)
-    row8 = lax.broadcasted_iota(jnp.int32, (FBLK, FBLK), 0)
-    for k in range(FBLK):
-        column = jnp.broadcast_to(block[:, k:k + 1], (FBLK, FBLK))
-        pivot = 1.0 / column[k:k + 1, :]
-        line = jnp.where(lane[:1, :] == k, pivot, block[k:k + 1, :] * pivot)
-        rest = jnp.where(lane == k, 0.0, block) - column * line
-        block = jnp.where(row8 == k, line, rest)
-    return block
-
-
-def factor_kernel(examples, scale, *refs):
-    slabs, out = refs[:-1], refs[-1]
-    body = slabs[0][pl.ds(0, FBLK), :]
-    diagonal = slabs[0][pl.ds(FBLK, 1), :]
-    for slab in slabs[1:]:
-        body = body + slab[pl.ds(0, FBLK), :]
-        diagonal = diagonal + slab[pl.ds(FBLK, 1), :]
+    for first in range(0, FBLK, PANEL):
+        within = (lane >= first) & (lane < first + PANEL)
+        panels = [eliminated(block[first:first + PANEL, :], first) for block in blocks]
+        updates = [product(block, panel, first) for block, panel in zip(blocks, panels)]
+        rests = [jnp.where(within, 0.0, block) - update for block, update in zip(blocks, updates)]
+        blocks = [
+            jnp.concatenate(
+                [part for part in (rest[:first], panel, rest[first + PANEL:]) if part.shape[0]], axis=0
+            )
+            for rest, panel in zip(rests, panels)
+        ]
+    return blocks
+
+
+def factor_kernel(examples, scale, slabs, out):
+    copies = slabs.shape[0]
+    body = slabs[0, pl.ds(0, FBLK), :]
+    diagonal = slabs[0, pl.ds(FBLK, 1), :]
+    for index in range(1, copies):
+        body = body + slabs[index, pl.ds(0, FBLK), :]
+        diagonal = diagonal + slabs[index, pl.ds(FBLK, 1), :]
     same = square(0) == square(1)
-    results = []
+    damped = []
     for gram in unpack(body, diagonal):
         fisher = gram / examples
         trace = jnp.sum(jnp.sum(jnp.where(same, fisher, 0.0), axis=0, keepdims=True), axis=1, keepdims=True)
-        results.append(inverted(fisher + jnp.where(same, damping * (trace / FBLK), 0.0)) * scale)
-    body, tail = pack(*results)
-    out[pl.ds(0, FBLK), :] = body
-    out[pl.ds(FBLK, 8), :] = tail
+        damped.append(fisher + jnp.where(same, damping * (trace / FBLK), 0.0))
+    first, second = inverted(damped)
+    body, tail = pack(first * scale, second * scale)
+    for index in range(copies):
+        out[index, pl.ds(0, FBLK), :] = body
+        out[index, pl.ds(FBLK, 8), :] = tail
 
 
 def factors_kernel(ids, id_rows, delta_hbm, table_hbm, factor, sent, kept, delta, table, looked, sems):
@@ -156,11 +227,13 @@
     out[rows, :] = sent[rows, :] + got[rows, :]
 
 
-def queries_kernel(each, factors, slab, high_out, low_out):
+def queries_kernel(each, shift, factors, slabs, high_out, low_out):
     tokens = factors.shape[1]
     proj = factors.shape[0] - 2 * each
     queries = high_out.shape[1]
-    lengths = slab[pl.ds(FBLK + 1, 1), :]
+    cycle = slabs.shape[0]
+    source = lax.rem(lax.axis_index("dp") + cycle - shift, cycle)
+    lengths = slabs[source, pl.ds(FBLK + 1, 1), :]
     upto = jnp.where(square(0) <= square(1), 1.0, 0.0).astype(jnp.bfloat16)
     ends = lax.dot_general(
         jnp.broadcast_to(lengths, (8, queries)).astype(jnp.bfloat16), upto, (((1,), (0,)), ((), ())),
@@ -183,19 +256,17 @@
 
 
 def scores_kernel(cycle, *refs):
-    own, peers = refs[:cycle], refs[cycle:2 * cycle]
-    highs, lows = refs[2 * cycle:3 * cycle], refs[3 * cycle:4 * cycle]
-    train, sent, kept, pre = refs[4 * cycle:]
+    own, peers = refs[:2]
+    highs, lows = refs[2:2 + cycle], refs[2 + cycle:2 + 2 * cycle]
+    train, sent, kept, pre = refs[2 + 2 * cycle:]
     mine, rep, model = lax.axis_index("dp"), lax.axis_index("rep"), lax.axis_index("mp")
     queries = highs[0].shape[1]
-    for side, slabs in enumerate((own, peers)):
-        half = rep if side == 0 else 1 - rep
-        for shift in range(cycle):
-            owner = half * cycle + lax.rem(mine + cycle - shift, cycle)
-            slab = slabs[shift]
-            blocks = unpack(slab[pl.ds(0, FBLK), :], slab[pl.ds(FBLK, 1), :])
+    for half, slabs in ((rep, own), (1 - rep, peers)):
+        for owner in range(cycle):
+            blocks = unpack(slabs[owner, pl.ds(0, FBLK), :], slabs[owner, pl.ds(FBLK, 1), :])
             for index, block in enumerate(blocks):
-                rows = pl.ds(pl.multiple_of(owner * (2 * FBLK) + index * FBLK, FBLK), FBLK)
+                start = (half * cycle + owner) * (2 * FBLK) + index * FBLK
+                rows = pl.ds(pl.multiple_of(start, FBLK), FBLK)
                 high, low = halves(block)
                 right_high = jnp.concatenate([ref[rows, :] for ref in highs], axis=1)
                 right_low = jnp.concatenate([ref[rows, :] for ref in lows], axis=1)
@@ -231,14 +302,14 @@
     bf16, f32 = jnp.bfloat16, jnp.float32
 
     slabs = call(
-        functools.partial(gram_kernel, cycle),
-        [shape((SLAB, FBLK), f32)] * cycle,
+        gram_kernel,
+        shape((cycle, SLAB, FBLK), f32),
         [VMEM, VMEM],
         flops=train_rows * feat * FBLK * 2,
         moved=2 * train_rows * feat,
         vmem=16,
     )(doc_lengths, train_grads)
-    parts = [slabs[0]] + [passed_along(slabs[s], "dp", s) for s in range(1, cycle)]
+    parts = lax.all_to_all(slabs, "dp", 0, 0)
 
     sent, kept = call(
         factors_kernel,
@@ -250,7 +321,7 @@
             pltpu.VMEM((proj, tokens), f32),
             pltpu.SemaphoreType.DMA((2,)),
         ],
-        vmem=24,
+        vmem=62,
         flops=2 * tokens * width * proj,
         moved=2 * (tokens * width + proj * vocab_rows) * 2,
     )(query_ids, query_ids.reshape(tokens // FBLK, FBLK), query_delta, vocab_factor.T, output_factor.T)
@@ -265,27 +336,27 @@
     )(kept, sent, got)
     gathered = [factors] + [passed_along(factors, "dp", s) for s in range(1, cycle)]
 
-    inverse = call(
+    inverses = call(
         functools.partial(factor_kernel, train_rows * cycle, 1.0 / proj),
-        shape((SLAB, FBLK), f32),
-        [VMEM] * cycle,
+        shape((cycle, SLAB, FBLK), f32),
+        [VMEM],
         vmem=16,
         flops=10 ** 10,
         moved=10 ** 6,
-    )(*parts)
-    inverses = [inverse] + [passed_along(inverse, "dp", s) for s in range(1, cycle)]
-    peers = [passed_along(slab, "rep", 1) for slab in inverses]
+    )(parts)
+    inverses = lax.all_to_all(inverses, "dp", 0, 0)
+    peers = passed_along(inverses, "rep", 1)
 
     highs, lows = [], []
     for s in range(cycle):
         high, low = call(
-            functools.partial(queries_kernel, each),
+            functools.partial(queries_kernel, each, s),
             [shape((feat, queries), bf16)] * 2,
             [VMEM, VMEM],
             vmem=24,
             flops=2 * feat * tokens * queries,
             moved=6 * feat * queries,
-        )(gathered[s], parts[s])
+        )(gathered[s], parts)
         highs.append(high)
         lows.append(low)
 
@@ -293,12 +364,12 @@
     outgoing, own = call(
         functools.partial(scores_kernel, cycle),
         [shape((half_rows, cycle * queries), bf16)] * 2,
-        [VMEM] * (4 * cycle + 1),
+        [VMEM] * (2 * cycle + 3),
         [pltpu.VMEM((feat, cycle * queries), bf16)],
         vmem=32,
         flops=2 * train_rows * feat * cycle * queries,
         moved=8 * feat * queries * cycle,
-    )(*inverses, *peers, *highs, *lows, train_grads)
+    )(inverses, peers, *highs, *lows, train_grads)
     incoming = passed_along(outgoing, "mp", 1)
     total = (own.astype(f32) + incoming.astype(f32)).astype(bf16)
     return total.reshape(half_rows, cycle, 1, queries)

time: 74.2 us -> 85.1 us (1.15)
  the two profiles are of different devices: /device:TPU:0 before, /device:TPU:10 now
where the time goes in v3:
time: 85.1 us; the launch traced here: 84.7 us
  Pallas kernels  29.2 us (34%)
  waiting for transfers between devices  27.2 us (32%)
  blocking collectives  12.8 us (15%)
  starting transfers between devices  10.5 us (12%)
  local copies, waits for them, and re-layouts  4.87 us (6%)
    ppermute x6, waiting for transfers between devices, passed_along(): lax.ppermute(shard, axis, [(i, (i + by) % size) for i in range(size)])  27.2 us
    all_to_all x1, blocking collectives, split_over_blocks(): parts = lax.all_to_all(slabs, 'dp', 0, 0)  12.8 us
    pallas_call x1, Pallas kernels, split_over_blocks(): call(factors_kernel, [shape((2 * each + proj, tokens), bf16), shape((each...  12.3 us
    pallas_call x1, Pallas kernels, split_over_blocks(): call(functools.partial(factor_kernel, train_rows * cycle, 1.0 / proj), sh...  7.28 us
    pallas_call x4, Pallas kernels, split_over_blocks(): call(functools.partial(queries_kernel, each, s), [shape((feat, queries),...  6.56 us
    ppermute x6, starting transfers between devices, passed_along(): lax.ppermute(shard, axis, [(i, (i + by) % size) for i in range(size)])  5.59 us
    all_to_all x1, starting transfers between devices, split_over_blocks(): inverses = lax.all_to_all(inverses, 'dp', 0, 0)  4.92 us
    unnamed x10, local copies, waits for them, and re-layouts  4.11 us
  transfers between devices with their start and end apart: 7, of which 5 were waited for; matrix products, arithmetic and copies ran while one was open for 0% of the time, Pallas kernels for 22%

profile of v3, /device:TPU:10, one launch (start us, length us, event | category | flops | bytes accessed | tf_op | source)
XLA Modules:
  0.0 84.7 jit_solution(8523302619113182045)
XLA Ops:
  0.0 0.0 copy-start
  0.0 1.6 %copy-done = bf16[512,2048]{1,0:T(8,128)(2,1)S(1)} copy-done((bf16[512,2048]{1,0:T(8,128)(2,1)S(1)}, bf16[512,2048]{1,0:T(8,128)(2,1)}, u32[]{:S(2)}) %copy-start) | copy-done | bytes 2097176
  1.6 0.0 copy-start.4
  1.6 0.7 copy-done.4
  2.2 0.5 shard_map.64
  2.8 12.8 %all_to_all.10.slabs = f32[4,136,128]{2,1,0:T(8,128)S(1)} all-to-all(f32[4,136,128]{2,1,0:T(8,128)S(1)} %shard_map.64), channel_id=1, replica_groups=mesh['groups'=2,'dp'=4,'mp'=2,'rep'=2] {'dp'}, dimensions={0} | all-to-all | bytes 557056 | tf_op jit(solution)/shard_map/all_to_all | solution.py:312
  15.6 7.3 %shard_map.65 = f32[4,136,128]{2,1,0:T(8,128)} custom-call(f32[4,136,128]{2,1,0:T(8,128)S(1)} %all_to_all.10.slabs), custom_call_target="tpu_custom_call" | custom-call | flops 10000000000 | bytes 1000000 | tf_op jit(solution)/shard_map/pallas_call | solution.py:339
  22.9 4.9 %all-to-all-start.1 = ((f32[4,136,128]{2,1,0:T(8,128)}), f32[4,136,128]{2,1,0:T(8,128)S(1)}, u32[]{:S(2)}, u32[]{:S(2)}) async-start(f32[4,136,128]{2,1,0:T(8,128)} %shard_map.65), calls=%async_computation.1 | async-start | bytes 557056 | tf_op jit(solution)/shard_map/all_to_all | solution.py:347
  27.8 12.3 %shard_map.66 = (bf16[128,1024]{1,0:T(8,128)(2,1)}, f32[32,1024]{1,0:T(8,128)}) custom-call(s32[1024]{0:T(1024)} %ids.1, s32[8,128]{1,0:T(8,128)} %bitcast.6, bf16[1024,2048]{1,0:T(8,128)(2,1)} %delta_hbm.1, bf16[64,64128]{1,0:T(8,128)(2,1)} %bitcast.4, bf16[64,2048]{1,0:T(8,128)(2,1)} %bitcast.5), custom_call_target="tpu_custom_call" | custom-call | flops 268435456 | bytes 24805376 | tf_op jit(solution)/shard_map/pallas_call | solution.py:314
  40.1 0.6 collective-permute-start.1
  40.7 6.1 %collective-permute-done.1.got = bf16[128,1024]{1,0:T(8,128)(2,1)S(1)} collective-permute-done((bf16[128,1024]{1,0:T(8,128)(2,1)}, bf16[128,1024]{1,0:T(8,128)(2,1)S(1)}, u32[]{:S(2)}, u32[]{:S(2)}) %collective-permute-start.1) | collective-permute-done | bytes 262176 | tf_op jit(solution)/shard_map/ppermute | solution.py:33
  46.8 0.0 copy-start.2
  46.8 0.9 %copy-done.2 = bf16[128,1024]{1,0:T(8,128)(2,1)S(1)} copy-done((bf16[128,1024]{1,0:T(8,128)(2,1)S(1)}, bf16[128,1024]{1,0:T(8,128)(2,1)}, u32[]{:S(2)}) %copy-start.2) | copy-done | bytes 262168
  47.7 0.0 copy-start.3
  47.7 0.9 %copy-done.3 = f32[32,1024]{1,0:T(8,128)S(1)} copy-done((f32[32,1024]{1,0:T(8,128)S(1)}, f32[32,1024]{1,0:T(8,128)}, u32[]{:S(2)}) %copy-start.3) | copy-done | bytes 131096
  48.7 0.0 copy-start.1
  48.7 1.5 %collective-permute-start.2 = (bf16[128,1024]{1,0:T(8,128)(2,1)S(1)}, bf16[128,1024]{1,0:T(8,128)(2,1)}, u32[]{:S(2)}, u32[]{:S(2)}) collective-permute-start(bf16[128,1024]{1,0:T(8,128)(2,1)S(1)} %shard_map.67.factors), channel_id=1, source_target_pairs={{0,4},{4,8},{8,12},{12,0},{1,5},{5,9},{9,13},{13,1},{2,6},{6,10},{... | collective-permute-start | bytes 786440 | tf_op jit(solution)/shard_map/ppermute | solution.py:33
  50.2 1.1 %collective-permute-start.3 = (bf16[128,1024]{1,0:T(8,128)(2,1)S(1)}, bf16[128,1024]{1,0:T(8,128)(2,1)S(1)}, u32[]{:S(2)}, u32[]{:S(2)}) collective-permute-start(bf16[128,1024]{1,0:T(8,128)(2,1)S(1)} %shard_map.67.factors), channel_id=1, source_target_pairs={{0,8},{4,12},{8,0},{12,4},{1,9},{5,13},{9,1},{13,5},{2,10},{6,14},... | collective-permute-start | bytes 786440 | tf_op jit(solution)/shard_map/ppermute | solution.py:33
  51.3 1.9 %collective-permute-start.4 = (bf16[128,1024]{1,0:T(8,128)(2,1)S(1)}, bf16[128,1024]{1,0:T(8,128)(2,1)S(1)}, u32[]{:S(2)}, u32[]{:S(2)}) collective-permute-start(bf16[128,1024]{1,0:T(8,128)(2,1)S(1)} %shard_map.67.factors), channel_id=1, source_target_pairs={{0,12},{4,0},{8,4},{12,8},{1,13},{5,1},{9,5},{13,9},{2,14},{6,2},{... | collective-permute-start | bytes 786440 | tf_op jit(solution)/shard_map/ppermute | solution.py:33
  53.1 0.0 all-to-all-done.1.refs_0_
  53.1 0.0 collective-permute-start
  53.1 1.4 %shard_map.68 = (bf16[2048,128]{1,0:T(8,128)(2,1)S(1)}, bf16[2048,128]{1,0:T(8,128)(2,1)S(1)}) custom-call(bf16[128,1024]{1,0:T(8,128)(2,1)S(1)} %shard_map.67.factors, f32[4,136,128]{2,1,0:T(8,128)S(1)} %all_to_all.10.slabs), custom_call_target="tpu_custom_call" | custom-call | flops 536870912 | bytes 1572864 | tf_op jit(solution)/shard_map/pallas_call | solution.py:352
  54.6 12.3 %collective-permute-done.2.factors = bf16[128,1024]{1,0:T(8,128)(2,1)} collective-permute-done((bf16[128,1024]{1,0:T(8,128)(2,1)S(1)}, bf16[128,1024]{1,0:T(8,128)(2,1)}, u32[]{:S(2)}, u32[]{:S(2)}) %collective-permute-start.2) | collective-permute-done | bytes 262176 | tf_op jit(solution)/shard_map/ppermute | solution.py:33
  66.9 2.4 %shard_map.69 = (bf16[2048,128]{1,0:T(8,128)(2,1)S(1)}, bf16[2048,128]{1,0:T(8,128)(2,1)S(1)}) custom-call(bf16[128,1024]{1,0:T(8,128)(2,1)} %collective-permute-done.2.factors, f32[4,136,128]{2,1,0:T(8,128)S(1)} %all_to_all.10.slabs), custom_call_target="tpu_custom_call" | custom-call | flops 536870912 | bytes 1572864 | tf_op jit(solution)/shard_map/pallas_call | solution.py:352
  69.2 0.5 collective-permute-done.3.factors
  69.7 1.4 %shard_map.70 = (bf16[2048,128]{1,0:T(8,128)(2,1)S(1)}, bf16[2048,128]{1,0:T(8,128)(2,1)S(1)}) custom-call(bf16[128,1024]{1,0:T(8,128)(2,1)S(1)} %collective-permute-done.3.factors, f32[4,136,128]{2,1,0:T(8,128)S(1)} %all_to_all.10.slabs), custom_call_target="tpu_custom_call" | custom-call | flops 536870912 | bytes 1572864 | tf_op jit(solution)/shard_map/pallas_call | solution.py:352
  71.1 0.6 collective-permute-done.4.factors
  71.7 1.4 %shard_map.71 = (bf16[2048,128]{1,0:T(8,128)(2,1)S(1)}, bf16[2048,128]{1,0:T(8,128)(2,1)S(1)}) custom-call(bf16[128,1024]{1,0:T(8,128)(2,1)S(1)} %collective-permute-done.4.factors, f32[4,136,128]{2,1,0:T(8,128)S(1)} %all_to_all.10.slabs), custom_call_target="tpu_custom_call" | custom-call | flops 536870912 | bytes 1572864 | tf_op jit(solution)/shard_map/pallas_call | solution.py:352
  73.1 0.0 collective-permute-done.refs_1_
  73.1 0.0 copy-done.1
  73.1 2.5 %shard_map.72 = (bf16[256,512]{1,0:T(8,128)(2,1)S(1)}, bf16[256,512]{1,0:T(8,128)(2,1)S(1)}) custom-call(f32[4,136,128]{2,1,0:T(8,128)S(1)} %all-to-all-done.1.refs_0_, f32[4,136,128]{2,1,0:T(8,128)S(1)} %collective-permute-done.refs_1_, bf16[2048,128]{1,0:T(8,128)(2,1)S(1)} %get-tuple-element.19.refs_2_, bf16[2048,128]{1,0:T(8,128)(2,1)S(1)} %get-tuple-element.20.refs_3_, ...), custom_call_target="tpu_custom_call" | custom-call | flops 1073741824 | bytes 8388608 | tf_op jit(solution)/shard_map/pallas_call | solution.py:364
  75.6 0.6 collective-permute-start.5
  76.2 7.7 %collective-permute-done.5 = bf16[256,512]{1,0:T(8,128)(2,1)S(1)} collective-permute-done((bf16[256,512]{1,0:T(8,128)(2,1)S(1)}, bf16[256,512]{1,0:T(8,128)(2,1)S(1)}, u32[]{:S(2)}, u32[]{:S(2)}) %collective-permute-start.5) | collective-permute-done | bytes 262176 | tf_op jit(solution)/shard_map/ppermute | solution.py:33
  83.9 0.1 add_convert_fusion
  84.0 0.8 reshape.7
  (1 shorter events, 0.0 us)
Async XLA Ops:
  0.0 1.6 %copy-start = (bf16[512,2048]{1,0:T(8,128)(2,1)S(1)}, bf16[512,2048]{1,0:T(8,128)(2,1)}, u32[]{:S(2)}) copy-start(bf16[512,2048]{1,0:T(8,128)(2,1)} %refs_10_.1) | copy-start | bytes 6291460
  1.6 0.7 copy-start.4
  22.9 30.3 %all-to-all-start.1 = ((f32[4,136,128]{2,1,0:T(8,128)}), f32[4,136,128]{2,1,0:T(8,128)S(1)}, u32[]{:S(2)}, u32[]{:S(2)}) async-start(f32[4,136,128]{2,1,0:T(8,128)} %shard_map.65), calls=%async_computation.1 | async-start | bytes 557056 | tf_op jit(solution)/shard_map/all_to_all | solution.py:347
  40.1 6.6 %collective-permute-start.1 = (bf16[128,1024]{1,0:T(8,128)(2,1)}, bf16[128,1024]{1,0:T(8,128)(2,1)S(1)}, u32[]{:S(2)}, u32[]{:S(2)}) collective-permute-start(bf16[128,1024]{1,0:T(8,128)(2,1)} %get-tuple-element.18.sent), channel_id=1, source_target_pairs={{0,2},{2,0},{1,3},{3,1},{4,6},{6,4},{5,7},{7,5},{8,10},{10,8},{9,1... | collective-permute-start | bytes 786440 | tf_op jit(solution)/shard_map/ppermute | solution.py:33
  46.8 1.0 %copy-start.2 = (bf16[128,1024]{1,0:T(8,128)(2,1)S(1)}, bf16[128,1024]{1,0:T(8,128)(2,1)}, u32[]{:S(2)}) copy-start(bf16[128,1024]{1,0:T(8,128)(2,1)} %get-tuple-element.18.sent) | copy-start | bytes 786436
  47.7 0.9 %copy-start.3 = (f32[32,1024]{1,0:T(8,128)S(1)}, f32[32,1024]{1,0:T(8,128)}, u32[]{:S(2)}) copy-start(f32[32,1024]{1,0:T(8,128)} %get-tuple-element.17.kept) | copy-start | bytes 393220
  48.7 24.4 %copy-start.1 = (bf16[512,2048]{1,0:T(8,128)(2,1)S(1)}, bf16[512,2048]{1,0:T(8,128)(2,1)}, u32[]{:S(2)}) copy-start(bf16[512,2048]{1,0:T(8,128)(2,1)} %refs_10_.1) | copy-start | bytes 6291460
  48.7 18.2 %collective-permute-start.2 = (bf16[128,1024]{1,0:T(8,128)(2,1)S(1)}, bf16[128,1024]{1,0:T(8,128)(2,1)}, u32[]{:S(2)}, u32[]{:S(2)}) collective-permute-start(bf16[128,1024]{1,0:T(8,128)(2,1)S(1)} %shard_map.67.factors), channel_id=1, source_target_pairs={{0,4},{4,8},{8,12},{12,0},{1,5},{5,9},{9,13},{13,1},{2,6},{6,10},{... | collective-permute-start | bytes 786440 | tf_op jit(solution)/shard_map/ppermute | solution.py:33
  50.2 19.5 %collective-permute-start.3 = (bf16[128,1024]{1,0:T(8,128)(2,1)S(1)}, bf16[128,1024]{1,0:T(8,128)(2,1)S(1)}, u32[]{:S(2)}, u32[]{:S(2)}) collective-permute-start(bf16[128,1024]{1,0:T(8,128)(2,1)S(1)} %shard_map.67.factors), channel_id=1, source_target_pairs={{0,8},{4,12},{8,0},{12,4},{1,9},{5,13},{9,1},{13,5},{2,10},{6,14},... | collective-permute-start | bytes 786440 | tf_op jit(solution)/shard_map/ppermute | solution.py:33
  51.3 20.4 %collective-permute-start.4 = (bf16[128,1024]{1,0:T(8,128)(2,1)S(1)}, bf16[128,1024]{1,0:T(8,128)(2,1)S(1)}, u32[]{:S(2)}, u32[]{:S(2)}) collective-permute-start(bf16[128,1024]{1,0:T(8,128)(2,1)S(1)} %shard_map.67.factors), channel_id=1, source_target_pairs={{0,12},{4,0},{8,4},{12,8},{1,13},{5,1},{9,5},{13,9},{2,14},{6,2},{... | collective-permute-start | bytes 786440 | tf_op jit(solution)/shard_map/ppermute | solution.py:33
  53.1 20.0 %collective-permute-start = (f32[4,136,128]{2,1,0:T(8,128)S(1)}, f32[4,136,128]{2,1,0:T(8,128)S(1)}, u32[]{:S(2)}, u32[]{:S(2)}) collective-permute-start(f32[4,136,128]{2,1,0:T(8,128)S(1)} %all-to-all-done.1.refs_0_), channel_id=1, source_target_pairs={{0,1},{1,0},{2,3},{3,2},{4,5},{5,4},{6,7},{7,6},{8,9},{9,8},{10,11... | collective-permute-start | bytes 835592 | tf_op jit(solution)/shard_map/ppermute | solution.py:33
  75.6 8.3 %collective-permute-start.5 = (bf16[256,512]{1,0:T(8,128)(2,1)S(1)}, bf16[256,512]{1,0:T(8,128)(2,1)S(1)}, u32[]{:S(2)}, u32[]{:S(2)}) collective-permute-start(bf16[256,512]{1,0:T(8,128)(2,1)S(1)} %get-tuple-element.28), channel_id=1, source_target_pairs={{0,2},{2,0},{1,3},{3,1},{4,6},{6,4},{5,7},{7,5},{8,10},{10,8},{9,1... | collective-permute-start | bytes 786440 | tf_op jit(solution)/shard_map/ppermute | solution.py:33

commit v4 on v3

--- a/solution.py
+++ b/solution.py
@@ -9,6 +9,7 @@
 FBLK = 128
 SLAB = FBLK + 8
 PANEL = 8
+COPIES = 4
 
 damping = 0.1
 
@@ -61,17 +62,18 @@
     return first, second
 
 
-def gram_kernel(lengths, train, slabs):
-    cycle = slabs.shape[0]
-    half = lax.axis_index("rep")
+def grams(lengths, train, slabs):
+    cycle = len(slabs)
+    mine, half = lax.axis_index("dp"), lax.axis_index("rep")
     spare = lengths[...].astype(jnp.float32)
-    for target in range(cycle):
-        start = pl.multiple_of((half * cycle + target) * (2 * FBLK), 2 * FBLK)
+    for shift, slab in enumerate(slabs):
+        owner = half * cycle + lax.rem(mine + shift, cycle)
+        start = pl.multiple_of(owner * (2 * FBLK), 2 * FBLK)
         part = train[:, pl.ds(start, 2 * FBLK)]
         gram = lax.dot_general(part, part, (((0,), (0,)), ((), ())), preferred_element_type=jnp.float32)
         body, tail = pack(gram[:FBLK, :FBLK], gram[FBLK:, FBLK:], spare)
-        slabs[target, pl.ds(0, FBLK), :] = body
-        slabs[target, pl.ds(FBLK, 8), :] = tail
+        slab[pl.ds(0, FBLK), :] = body
+        slab[pl.ds(FBLK, 8), :] = tail
 
 
 def thirds(value):
@@ -154,13 +156,13 @@
     return blocks
 
 
-def factor_kernel(examples, scale, slabs, out):
-    copies = slabs.shape[0]
-    body = slabs[0, pl.ds(0, FBLK), :]
-    diagonal = slabs[0, pl.ds(FBLK, 1), :]
-    for index in range(1, copies):
-        body = body + slabs[index, pl.ds(0, FBLK), :]
-        diagonal = diagonal + slabs[index, pl.ds(FBLK, 1), :]
+def factor_kernel(examples, scale, *refs):
+    slabs, out = refs[:-2], refs[-1]
+    body = slabs[0][pl.ds(0, FBLK), :]
+    diagonal = slabs[0][pl.ds(FBLK, 1), :]
+    for slab in slabs[1:]:
+        body = body + slab[pl.ds(0, FBLK), :]
+        diagonal = diagonal + slab[pl.ds(FBLK, 1), :]
     same = square(0) == square(1)
     damped = []
     for gram in unpack(body, diagonal):
@@ -169,33 +171,52 @@
         damped.append(fisher + jnp.where(same, damping * (trace / FBLK), 0.0))
     first, second = inverted(damped)
     body, tail = pack(first * scale, second * scale)
-    for index in range(copies):
-        out[index, pl.ds(0, FBLK), :] = body
-        out[index, pl.ds(FBLK, 8), :] = tail
-
-
-def factors_kernel(ids, id_rows, delta_hbm, table_hbm, factor, sent, kept, delta, table, looked, sems):
+    out[pl.ds(0, FBLK), :] = body
+    out[pl.ds(FBLK, 8), :] = tail
+
+
+def first_kernel(ids_hbm, id_rows_hbm, delta_hbm, table_hbm, factor_hbm, lengths_hbm, train_hbm, sent, kept, *refs):
+    slabs, (ids, id_rows, delta, table, factor, lengths, train, looked, sems) = refs[:-9], refs[-9:]
     model = lax.axis_index("mp")
-    vocab_rows = table.shape[1]
-    tokens, width = delta.shape
-    proj = factor.shape[0]
+    proj, vocab_rows = table.shape
+    tokens = delta.shape[0]
     each = proj // lax.axis_size("mp")
-    get_delta = pltpu.make_async_copy(delta_hbm, delta, sems.at[0])
-    get_table = pltpu.make_async_copy(table_hbm, table, sems.at[1])
-    get_delta.start()
-    get_table.start()
-    get_delta.wait()
-    output = lax.dot_general(
-        delta[...], factor[...], (((1,), (1,)), ((), ())), preferred_element_type=jnp.float32
-    )
-    looked[pl.ds(0, proj), :] = output.T
+    small = [
+        pltpu.make_async_copy(source, target, sems.at[0, index])
+        for index, (source, target) in enumerate((
+            (factor_hbm, factor), (lengths_hbm, lengths), (train_hbm, train), (ids_hbm, ids), (id_rows_hbm, id_rows),
+        ))
+    ]
+    tall, wide = tokens // COPIES, proj // COPIES
+    get_delta = [
+        pltpu.make_async_copy(delta_hbm.at[rows], delta.at[rows], sems.at[1, index])
+        for index in range(COPIES) for rows in (pl.ds(index * tall, tall),)
+    ]
+    get_table = [
+        pltpu.make_async_copy(table_hbm.at[rows], table.at[rows], sems.at[2, index])
+        for index in range(COPIES) for rows in (pl.ds(index * wide, wide),)
+    ]
+    for copy in small[:2] + get_delta + small[2:] + get_table:
+        copy.start()
+    small[0].wait()
+    for index, copy in enumerate(get_delta):
+        copy.wait()
+        rows = pl.ds(index * tall, tall)
+        output = lax.dot_general(
+            delta[rows, :], factor[...], (((1,), (1,)), ((), ())), preferred_element_type=jnp.float32
+        )
+        looked[:, rows] = output.T
     mine = looked[pl.ds(pl.multiple_of(model * each, each), each), :]
     other = looked[pl.ds(pl.multiple_of((1 - model) * each, each), each), :]
     kept[...] = mine
     high, low = halves(other)
     sent[pl.ds(0, each), :] = high
     sent[pl.ds(each, each), :] = low
-    get_table.wait()
+    for copy in small[1:3]:
+        copy.wait()
+    grams(lengths, train, slabs)
+    for copy in small[3:] + get_table:
+        copy.wait()
     lanes = lax.broadcasted_iota(jnp.int32, (proj, FBLK), 1)
     first = model * vocab_rows
 
@@ -227,13 +248,11 @@
     out[rows, :] = sent[rows, :] + got[rows, :]
 
 
-def queries_kernel(each, shift, factors, slabs, high_out, low_out):
+def queries_kernel(each, factors, slab, high_out, low_out):
     tokens = factors.shape[1]
     proj = factors.shape[0] - 2 * each
     queries = high_out.shape[1]
-    cycle = slabs.shape[0]
-    source = lax.rem(lax.axis_index("dp") + cycle - shift, cycle)
-    lengths = slabs[source, pl.ds(FBLK + 1, 1), :]
+    lengths = slab[pl.ds(FBLK + 1, 1), :]
     upto = jnp.where(square(0) <= square(1), 1.0, 0.0).astype(jnp.bfloat16)
     ends = lax.dot_general(
         jnp.broadcast_to(lengths, (8, queries)).astype(jnp.bfloat16), upto, (((1,), (0,)), ((), ())),
@@ -255,18 +274,18 @@
         low_out[pl.ds(start * proj, step * proj), :] = low
 
 
-def scores_kernel(cycle, *refs):
-    own, peers = refs[:2]
-    highs, lows = refs[2:2 + cycle], refs[2 + cycle:2 + 2 * cycle]
-    train, sent, kept, pre = refs[2 + 2 * cycle:]
+def scores_kernel(cycle, count, *refs):
+    own, peers = refs[:cycle], refs[cycle:2 * cycle]
+    highs, lows = refs[2 * cycle:2 * cycle + count], refs[2 * cycle + count:2 * cycle + 2 * count]
+    train, sent, kept, pre = refs[2 * cycle + 2 * count:]
     mine, rep, model = lax.axis_index("dp"), lax.axis_index("rep"), lax.axis_index("mp")
-    queries = highs[0].shape[1]
     for half, slabs in ((rep, own), (1 - rep, peers)):
-        for owner in range(cycle):
-            blocks = unpack(slabs[owner, pl.ds(0, FBLK), :], slabs[owner, pl.ds(FBLK, 1), :])
+        for shift in range(cycle):
+            owner = half * cycle + lax.rem(mine + cycle - shift, cycle)
+            slab = slabs[shift]
+            blocks = unpack(slab[pl.ds(0, FBLK), :], slab[pl.ds(FBLK, 1), :])
             for index, block in enumerate(blocks):
-                start = (half * cycle + owner) * (2 * FBLK) + index * FBLK
-                rows = pl.ds(pl.multiple_of(start, FBLK), FBLK)
+                rows = pl.ds(pl.multiple_of(owner * (2 * FBLK) + index * FBLK, FBLK), FBLK)
                 high, low = halves(block)
                 right_high = jnp.concatenate([ref[rows, :] for ref in highs], axis=1)
                 right_low = jnp.concatenate([ref[rows, :] for ref in lows], axis=1)
@@ -279,12 +298,24 @@
     half_rows = sent.shape[0]
     for out, which in ((sent, 1 - model), (kept, model)):
         rows = pl.ds(pl.multiple_of(which * half_rows, half_rows), half_rows)
-        scores = jnp.dot(train[rows, :], pre[...], preferred_element_type=jnp.float32).astype(jnp.bfloat16)
-        for shift in range(cycle):
-            source = lax.rem(mine + cycle - shift, cycle)
-            out[:, pl.ds(pl.multiple_of(source * queries, queries), queries)] = (
-                scores[:, shift * queries:(shift + 1) * queries]
-            )
+        out[...] = jnp.dot(train[rows, :], pre[...], preferred_element_type=jnp.float32).astype(jnp.bfloat16)
+
+
+def total_kernel(cycle, count, *refs):
+    pieces, out = refs[:-1], refs[-1]
+    mine = lax.axis_index("dp")
+    sums = []
+    for kept, got in zip(pieces[::2], pieces[1::2]):
+        both = kept[...].astype(jnp.float32) + got[...].astype(jnp.float32)
+        sums += [both[:, index * FBLK:(index + 1) * FBLK] for index in range(count)]
+    placed = []
+    for source in range(cycle):
+        shift = lax.rem(mine + cycle - source, cycle)
+        value = sums[0]
+        for index in range(1, cycle):
+            value = jnp.where(shift == index, sums[index], value)
+        placed.append(value)
+    out[...] = jnp.stack(placed, axis=1).astype(jnp.bfloat16)
 
 
 def shape(dims, dtype):
@@ -301,31 +332,31 @@
     queries = doc_lengths.shape[1]
     bf16, f32 = jnp.bfloat16, jnp.float32
 
-    slabs = call(
-        gram_kernel,
-        shape((cycle, SLAB, FBLK), f32),
-        [VMEM, VMEM],
-        flops=train_rows * feat * FBLK * 2,
-        moved=2 * train_rows * feat,
-        vmem=16,
-    )(doc_lengths, train_grads)
-    parts = lax.all_to_all(slabs, "dp", 0, 0)
-
-    sent, kept = call(
-        factors_kernel,
-        [shape((2 * each + proj, tokens), bf16), shape((each, tokens), f32)],
-        [SMEM, VMEM, HBM, HBM, VMEM],
+    sent, kept, *slabs = call(
+        first_kernel,
+        [shape((2 * each + proj, tokens), bf16), shape((each, tokens), f32)] + [shape((SLAB, FBLK), f32)] * cycle,
+        [HBM] * 7,
         [
+            pltpu.SMEM((tokens,), jnp.int32),
+            pltpu.VMEM((tokens // FBLK, FBLK), jnp.int32),
             pltpu.VMEM((tokens, width), bf16),
             pltpu.VMEM((proj, vocab_rows), bf16),
+            pltpu.VMEM((proj, width), bf16),
+            pltpu.VMEM((1, queries), jnp.int32),
+            pltpu.VMEM((train_rows, feat), bf16),
             pltpu.VMEM((proj, tokens), f32),
-            pltpu.SemaphoreType.DMA((2,)),
+            pltpu.SemaphoreType.DMA((3, 8)),
         ],
         vmem=62,
         flops=2 * tokens * width * proj,
         moved=2 * (tokens * width + proj * vocab_rows) * 2,
-    )(query_ids, query_ids.reshape(tokens // FBLK, FBLK), query_delta, vocab_factor.T, output_factor.T)
+    )(
+        query_ids, query_ids.reshape(tokens // FBLK, FBLK), query_delta, vocab_factor.T, output_factor.T,
+        doc_lengths, train_grads,
+    )
     got = passed_along(sent, "mp", 1)
+    parts = [slabs[0]] + [passed_along(slabs[s], "dp", s) for s in range(1, cycle)]
+
     factors = call(
         merge_kernel,
         shape(sent.shape, bf16),
@@ -336,43 +367,53 @@
     )(kept, sent, got)
     gathered = [factors] + [passed_along(factors, "dp", s) for s in range(1, cycle)]
 
-    inverses = call(
+    inverse = call(
         functools.partial(factor_kernel, train_rows * cycle, 1.0 / proj),
-        shape((cycle, SLAB, FBLK), f32),
-        [VMEM],
+        shape((SLAB, FBLK), f32),
+        [VMEM] * cycle + [HBM],
         vmem=16,
         flops=10 ** 10,
         moved=10 ** 6,
-    )(parts)
-    inverses = lax.all_to_all(inverses, "dp", 0, 0)
-    peers = passed_along(inverses, "rep", 1)
+    )(*parts, factors)
+    inverses = [inverse] + [passed_along(inverse, "dp", s) for s in range(1, cycle)]
+    peers = [passed_along(slab, "rep", 1) for slab in inverses]
 
     highs, lows = [], []
     for s in range(cycle):
         high, low = call(
-            functools.partial(queries_kernel, each, s),
+            functools.partial(queries_kernel, each),
             [shape((feat, queries), bf16)] * 2,
             [VMEM, VMEM],
             vmem=24,
             flops=2 * feat * tokens * queries,
             moved=6 * feat * queries,
-        )(gathered[s], parts)
+        )(gathered[s], parts[s])
         highs.append(high)
         lows.append(low)
 
     half_rows = train_rows // lax.axis_size("mp")
-    outgoing, own = call(
-        functools.partial(scores_kernel, cycle),
-        [shape((half_rows, cycle * queries), bf16)] * 2,
-        [VMEM] * (2 * cycle + 3),
-        [pltpu.VMEM((feat, cycle * queries), bf16)],
-        vmem=32,
-        flops=2 * train_rows * feat * cycle * queries,
-        moved=8 * feat * queries * cycle,
-    )(inverses, peers, *highs, *lows, train_grads)
-    incoming = passed_along(outgoing, "mp", 1)
-    total = (own.astype(f32) + incoming.astype(f32)).astype(bf16)
-    return total.reshape(half_rows, cycle, 1, queries)
+    count = cycle // 2
+    pieces = []
+    for start in range(0, cycle, count):
+        outgoing, own = call(
+            functools.partial(scores_kernel, cycle, count),
+            [shape((half_rows, count * queries), bf16)] * 2,
+            [VMEM] * (2 * cycle + 2 * count + 1),
+            [pltpu.VMEM((feat, count * queries), bf16)],
+            vmem=24,
+            flops=2 * train_rows * feat * count * queries,
+            moved=8 * feat * queries * count,
+        )(*inverses, *peers, *highs[start:start + count], *lows[start:start + count], train_grads)
+        pieces += [own, passed_along(outgoing, "mp", 1)]
+    total = call(
+        functools.partial(total_kernel, cycle, count),
+        shape((half_rows, cycle, queries), bf16),
+        [VMEM] * len(pieces),
+        vmem=16,
+        flops=half_rows * cycle * queries,
+        moved=6 * half_rows * cycle * queries,
+    )(*pieces)
+    return total[:, :, None, :]
 
 
 def doc_matrix(lengths_row, count):

time: 85.1 us -> 72 us (0.85)
  the two profiles are of different devices: /device:TPU:10 before, /device:TPU:0 now
where the time goes in v4:
time: 72 us; the launch traced here: 70.9 us
  starting transfers between devices  29.6 us (41%)
  Pallas kernels  28.9 us (40%)
  waiting for transfers between devices  9.54 us (13%)
  local copies, waits for them, and re-layouts  2.74 us (4%)
    ppermute x16, starting transfers between devices, passed_along(): lax.ppermute(shard, axis, [(i, (i + by) % size) for i in range(size)])  29.6 us
    pallas_call x1, Pallas kernels, split_over_blocks(): call(first_kernel, [shape((2 * each + proj, tokens), bf16), shape((each,...  12.4 us
    ppermute x16, waiting for transfers between devices, passed_along(): lax.ppermute(shard, axis, [(i, (i + by) % size) for i in range(size)])  9.54 us
    pallas_call x1, Pallas kernels, split_over_blocks(): call(functools.partial(factor_kernel, train_rows * cycle, 1.0 / proj), sh...  6.58 us
    pallas_call x4, Pallas kernels, split_over_blocks(): call(functools.partial(queries_kernel, each), [shape((feat, queries), bf1...  5.63 us
    pallas_call x2, Pallas kernels, split_over_blocks(): call(functools.partial(scores_kernel, cycle, count), [shape((half_rows, c...  3 us
    unnamed x10, local copies, waits for them, and re-layouts  2.74 us
  transfers between devices with their start and end apart: 16, of which 5 were waited for; matrix products, arithmetic and copies ran while one was open for 0% of the time, Pallas kernels for 22%

profile of v4, /device:TPU:0, one launch (start us, length us, event | category | flops | bytes accessed | tf_op | source)
XLA Modules:
  0.0 70.9 jit_solution(12202432342144687904)
XLA Ops:
  0.0 12.4 %shard_map.64 = (bf16[128,1024]{1,0:T(8,128)(2,1)}, f32[32,1024]{1,0:T(8,128)}, f32[136,128]{1,0:T(8,128)}, f32[136,128]{1,0:T(8,128)}, f32[136,128]{1,0:T(8,128)}, /*index=5*/f32[136,128]{1,0:T(8,128)}) custom-call(s32[1024]{0:T(1024)} %ids_hbm.1, s32[8,128]{1,0:T(8,128)} %bitcast.8, bf16[1024,2048]{1,0:T(8,128)(2,1)} %delta_hbm.1, ...), custom_call_target="tpu_custom_call" | custom-call | flops 268435456 | bytes 24805376 | tf_op jit(solution)/shard_map/pallas_call | solution.py:335
  12.4 3.0 %collective-permute-start.3 = (bf16[128,1024]{1,0:T(8,128)(2,1)}, bf16[128,1024]{1,0:T(8,128)(2,1)S(1)}, u32[]{:S(2)}, u32[]{:S(2)}) collective-permute-start(bf16[128,1024]{1,0:T(8,128)(2,1)} %get-tuple-element.28.sent), channel_id=1, source_target_pairs={{0,2},{2,0},{1,3},{3,1},{4,6},{6,4},{5,7},{7,5},{8,10},{10,8},{9,1... | collective-permute-start | bytes 786440 | tf_op jit(solution)/shard_map/ppermute | solution.py:34
  15.4 1.6 %collective-permute-start = (f32[136,128]{1,0:T(8,128)}, f32[136,128]{1,0:T(8,128)S(1)}, u32[]{:S(2)}, u32[]{:S(2)}) collective-permute-start(f32[136,128]{1,0:T(8,128)} %get-tuple-element.24), channel_id=1, source_target_pairs={{0,4},{4,8},{8,12},{12,0},{1,5},{5,9},{9,13},{13,1},{2,6},{6,10},{... | collective-permute-start | bytes 208904 | tf_op jit(solution)/shard_map/ppermute | solution.py:34
  17.0 2.6 %collective-permute-start.1 = (f32[136,128]{1,0:T(8,128)}, f32[136,128]{1,0:T(8,128)S(1)}, u32[]{:S(2)}, u32[]{:S(2)}) collective-permute-start(f32[136,128]{1,0:T(8,128)} %get-tuple-element.25), channel_id=1, source_target_pairs={{0,8},{4,12},{8,0},{12,4},{1,9},{5,13},{9,1},{13,5},{2,10},{6,14},... | collective-permute-start | bytes 208904 | tf_op jit(solution)/shard_map/ppermute | solution.py:34
  19.6 1.3 %collective-permute-start.2 = (f32[136,128]{1,0:T(8,128)}, f32[136,128]{1,0:T(8,128)S(1)}, u32[]{:S(2)}, u32[]{:S(2)}) collective-permute-start(f32[136,128]{1,0:T(8,128)} %get-tuple-element.26), channel_id=1, source_target_pairs={{0,12},{4,0},{8,4},{12,8},{1,13},{5,1},{9,5},{13,9},{2,14},{6,2},{... | collective-permute-start | bytes 208904 | tf_op jit(solution)/shard_map/ppermute | solution.py:34
  20.9 1.0 %collective-permute-done.3.got = bf16[128,1024]{1,0:T(8,128)(2,1)S(1)} collective-permute-done((bf16[128,1024]{1,0:T(8,128)(2,1)}, bf16[128,1024]{1,0:T(8,128)(2,1)S(1)}, u32[]{:S(2)}, u32[]{:S(2)}) %collective-permute-start.3) | collective-permute-done | bytes 262176 | tf_op jit(solution)/shard_map/ppermute | solution.py:34
  21.9 0.9 %copy-done.1 = bf16[128,1024]{1,0:T(8,128)(2,1)S(1)} copy-done((bf16[128,1024]{1,0:T(8,128)(2,1)S(1)}, bf16[128,1024]{1,0:T(8,128)(2,1)}, u32[]{:S(2)}) %copy-start.1) | copy-done | bytes 262168
  22.9 0.9 %copy-done.2 = f32[32,1024]{1,0:T(8,128)S(1)} copy-done((f32[32,1024]{1,0:T(8,128)S(1)}, f32[32,1024]{1,0:T(8,128)}, u32[]{:S(2)}) %copy-start.2) | copy-done | bytes 131096
  23.9 2.9 %collective-permute-start.13 = (bf16[128,1024]{1,0:T(8,128)(2,1)S(1)}, bf16[128,1024]{1,0:T(8,128)(2,1)S(1)}, u32[]{:S(2)}, u32[]{:S(2)}) collective-permute-start(bf16[128,1024]{1,0:T(8,128)(2,1)S(1)} %shard_map.65.refs_4_.factors), channel_id=1, source_target_pairs={{0,8},{4,12},{8,0},{12,4},{1,9},{5,13},{9,1},{13,5},{2,10},{6,14},... | collective-permute-start | bytes 786440 | tf_op jit(solution)/shard_map/ppermute | solution.py:34
  26.7 1.3 %collective-permute-start.14 = (bf16[128,1024]{1,0:T(8,128)(2,1)S(1)}, bf16[128,1024]{1,0:T(8,128)(2,1)S(1)}, u32[]{:S(2)}, u32[]{:S(2)}) collective-permute-start(bf16[128,1024]{1,0:T(8,128)(2,1)S(1)} %shard_map.65.refs_4_.factors), channel_id=1, source_target_pairs={{0,12},{4,0},{8,4},{12,8},{1,13},{5,1},{9,5},{13,9},{2,14},{6,2},{... | collective-permute-start | bytes 786440 | tf_op jit(solution)/shard_map/ppermute | solution.py:34
  28.1 0.0 collective-permute-done.refs_1_.slab
  28.1 0.0 collective-permute-done.1.refs_2_.slab
  28.1 0.0 collective-permute-done.2.refs_3_.slab
  28.1 0.0 copy-start.3
  28.1 0.9 %copy-done.3 = f32[136,128]{1,0:T(8,128)S(1)} copy-done((f32[136,128]{1,0:T(8,128)S(1)}, f32[136,128]{1,0:T(8,128)}, u32[]{:S(2)}) %copy-start.3) | copy-done | bytes 69656
  29.0 6.6 %shard_map.66.refs_0_ = f32[136,128]{1,0:T(8,128)S(1)} custom-call(f32[136,128]{1,0:T(8,128)S(1)} %copy-done.3, f32[136,128]{1,0:T(8,128)S(1)} %collective-permute-done.refs_1_.slab, f32[136,128]{1,0:T(8,128)S(1)} %collective-permute-done.1.refs_2_.slab, f32[136,128]{1,0:T(8,128)S(1)} %collective-permute-done.2.refs_3_.slab, ...), custom_call_target="tpu_custom_call" | custom-call | flops 10000000000 | bytes 1000000 | tf_op jit(solution)/shard_map/pallas_call | solution.py:370
  35.6 0.0 copy-start
  35.6 0.3 collective-permute-start.6
  35.8 1.8 %collective-permute-start.11 = (bf16[128,1024]{1,0:T(8,128)(2,1)S(1)}, bf16[128,1024]{1,0:T(8,128)(2,1)S(1)}, u32[]{:S(2)}, u32[]{:S(2)}) collective-permute-start(bf16[128,1024]{1,0:T(8,128)(2,1)S(1)} %shard_map.65.refs_4_.factors), channel_id=1, source_target_pairs={{0,4},{4,8},{8,12},{12,0},{1,5},{5,9},{9,13},{13,1},{2,6},{6,10},{... | collective-permute-start | bytes 786440 | tf_op jit(solution)/shard_map/ppermute | solution.py:34
  37.7 0.7 collective-permute-start.4
  38.3 2.7 %collective-permute-done.6.refs_3_ = f32[136,128]{1,0:T(8,128)S(1)} collective-permute-done((f32[136,128]{1,0:T(8,128)S(1)}, f32[136,128]{1,0:T(8,128)S(1)}, u32[]{:S(2)}, u32[]{:S(2)}) %collective-permute-start.6) | collective-permute-done | bytes 69664 | tf_op jit(solution)/shard_map/ppermute | solution.py:34
  41.0 11.3 %collective-permute-start.5 = (f32[136,128]{1,0:T(8,128)S(1)}, f32[136,128]{1,0:T(8,128)S(1)}, u32[]{:S(2)}, u32[]{:S(2)}) collective-permute-start(f32[136,128]{1,0:T(8,128)S(1)} %shard_map.66.refs_0_), channel_id=1, source_target_pairs={{0,8},{4,12},{8,0},{12,4},{1,9},{5,13},{9,1},{13,5},{2,10},{6,14},... | collective-permute-start | bytes 208904 | tf_op jit(solution)/shard_map/ppermute | solution.py:34
  52.2 0.0 copy-done.4
  52.2 1.4 %shard_map.67 = (bf16[2048,128]{1,0:T(8,128)(2,1)S(1)}, bf16[2048,128]{1,0:T(8,128)(2,1)S(1)}) custom-call(bf16[128,1024]{1,0:T(8,128)(2,1)S(1)} %shard_map.65.refs_4_.factors, f32[136,128]{1,0:T(8,128)S(1)} %copy-done.4), custom_call_target="tpu_custom_call" | custom-call | flops 536870912 | bytes 1572864 | tf_op jit(solution)/shard_map/pallas_call | solution.py:383
  53.7 0.0 collective-permute-done.4.refs_1_
  53.7 0.1 collective-permute-start.7
  53.7 0.8 %collective-permute-done.5.refs_2_ = f32[136,128]{1,0:T(8,128)S(1)} collective-permute-done((f32[136,128]{1,0:T(8,128)S(1)}, f32[136,128]{1,0:T(8,128)S(1)}, u32[]{:S(2)}, u32[]{:S(2)}) %collective-permute-start.5) | collective-permute-done | bytes 69664 | tf_op jit(solution)/shard_map/ppermute | solution.py:34
  54.5 0.0 collective-permute-start.10
  54.5 0.0 collective-permute-done.13.factors
  54.5 0.5 collective-permute-start.8
  55.0 0.0 collective-permute-done.14.factors
  55.0 0.1 collective-permute-start.9
  55.1 1.4 %shard_map.70 = (bf16[2048,128]{1,0:T(8,128)(2,1)S(1)}, bf16[2048,128]{1,0:T(8,128)(2,1)S(1)}) custom-call(bf16[128,1024]{1,0:T(8,128)(2,1)S(1)} %collective-permute-done.13.factors, f32[136,128]{1,0:T(8,128)S(1)} %collective-permute-done.1.refs_2_.slab), custom_call_target="tpu_custom_call" | custom-call | flops 536870912 | bytes 1572864 | tf_op jit(solution)/shard_map/pallas_call | solution.py:383
  56.5 1.4 %shard_map.71 = (bf16[2048,128]{1,0:T(8,128)(2,1)S(1)}, bf16[2048,128]{1,0:T(8,128)(2,1)S(1)}) custom-call(bf16[128,1024]{1,0:T(8,128)(2,1)S(1)} %collective-permute-done.14.factors, f32[136,128]{1,0:T(8,128)S(1)} %collective-permute-done.2.refs_3_.slab), custom_call_target="tpu_custom_call" | custom-call | flops 536870912 | bytes 1572864 | tf_op jit(solution)/shard_map/pallas_call | solution.py:383
  57.9 0.0 collective-permute-done.7.refs_4_
  57.9 0.0 collective-permute-done.10.refs_7_
  58.0 0.0 collective-permute-done.8.refs_5_
  58.0 0.0 collective-permute-done.9.refs_6_
  58.0 0.0 copy-done
  58.0 1.5 %shard_map.72 = (bf16[256,256]{1,0:T(8,128)(2,1)S(1)}, bf16[256,256]{1,0:T(8,128)(2,1)S(1)}) custom-call(f32[136,128]{1,0:T(8,128)S(1)} %shard_map.66.refs_0_, f32[136,128]{1,0:T(8,128)S(1)} %collective-permute-done.4.refs_1_, f32[136,128]{1,0:T(8,128)S(1)} %collective-permute-done.5.refs_2_, f32[136,128]{1,0:T(8,128)S(1)} %collective-permute-done.6.refs_3_, ...), custom_call_target="tpu_custom_call" | custom-call | flops 536870912 | bytes 4194304 | tf_op jit(solution)/shard_map/pallas_call | solution.py:398
  59.5 1.6 %collective-permute-start.15 = (bf16[256,256]{1,0:T(8,128)(2,1)S(1)}, bf16[256,256]{1,0:T(8,128)(2,1)S(1)}, u32[]{:S(2)}, u32[]{:S(2)}) collective-permute-start(bf16[256,256]{1,0:T(8,128)(2,1)S(1)} %get-tuple-element.40), channel_id=1, source_target_pairs={{0,2},{2,0},{1,3},{3,1},{4,6},{6,4},{5,7},{7,5},{8,10},{10,8},{9,1... | collective-permute-start | bytes 393224 | tf_op jit(solution)/shard_map/ppermute | solution.py:34
  61.1 0.0 collective-permute-done.11.factors
  61.1 1.4 %shard_map.68 = (bf16[2048,128]{1,0:T(8,128)(2,1)S(1)}, bf16[2048,128]{1,0:T(8,128)(2,1)S(1)}) custom-call(bf16[128,1024]{1,0:T(8,128)(2,1)S(1)} %collective-permute-done.11.factors, f32[136,128]{1,0:T(8,128)S(1)} %collective-permute-done.refs_1_.slab), custom_call_target="tpu_custom_call" | custom-call | flops 536870912 | bytes 1572864 | tf_op jit(solution)/shard_map/pallas_call | solution.py:383
  62.5 1.5 %shard_map.69 = (bf16[256,256]{1,0:T(8,128)(2,1)S(1)}, bf16[256,256]{1,0:T(8,128)(2,1)S(1)}) custom-call(f32[136,128]{1,0:T(8,128)S(1)} %shard_map.66.refs_0_, f32[136,128]{1,0:T(8,128)S(1)} %collective-permute-done.4.refs_1_, f32[136,128]{1,0:T(8,128)S(1)} %collective-permute-done.5.refs_2_, f32[136,128]{1,0:T(8,128)S(1)} %collective-permute-done.6.refs_3_, ...), custom_call_target="tpu_custom_call" | custom-call | flops 536870912 | bytes 4194304 | tf_op jit(solution)/shard_map/pallas_call | solution.py:398
  64.0 0.6 collective-permute-start.12
  64.6 0.8 %collective-permute-done.15.refs_3_ = bf16[256,256]{1,0:T(8,128)(2,1)S(1)} collective-permute-done((bf16[256,256]{1,0:T(8,128)(2,1)S(1)}, bf16[256,256]{1,0:T(8,128)(2,1)S(1)}, u32[]{:S(2)}, u32[]{:S(2)}) %collective-permute-start.15) | collective-permute-done | bytes 131104 | tf_op jit(solution)/shard_map/ppermute | solution.py:34
  65.4 4.2 %collective-permute-done.12.refs_1_ = bf16[256,256]{1,0:T(8,128)(2,1)S(1)} collective-permute-done((bf16[256,256]{1,0:T(8,128)(2,1)S(1)}, bf16[256,256]{1,0:T(8,128)(2,1)S(1)}, u32[]{:S(2)}, u32[]{:S(2)}) %collective-permute-start.12) | collective-permute-done | bytes 131104 | tf_op jit(solution)/shard_map/ppermute | solution.py:34
  69.6 1.3 %shard_map.73 = bf16[256,4,128]{2,1,0:T(4,128)(2,1)} custom-call(bf16[256,256]{1,0:T(8,128)(2,1)S(1)} %get-tuple-element.33.refs_0_, bf16[256,256]{1,0:T(8,128)(2,1)S(1)} %collective-permute-done.12.refs_1_, bf16[256,256]{1,0:T(8,128)(2,1)S(1)} %get-tuple-element.39.refs_2_, bf16[256,256]{1,0:T(8,128)(2,1)S(1)} %collective-permute-done.15.refs_3_), custom_call_target="tpu_custom_call" | custom-call | flops 131072 | bytes 786432 | tf_op jit(solution)/shard_map/pallas_call | solution.py:408
  (4 shorter events, 0.0 us)
Async XLA Ops:
  12.4 9.5 %collective-permute-start.3 = (bf16[128,1024]{1,0:T(8,128)(2,1)}, bf16[128,1024]{1,0:T(8,128)(2,1)S(1)}, u32[]{:S(2)}, u32[]{:S(2)}) collective-permute-start(bf16[128,1024]{1,0:T(8,128)(2,1)} %get-tuple-element.28.sent), channel_id=1, source_target_pairs={{0,2},{2,0},{1,3},{3,1},{4,6},{6,4},{5,7},{7,5},{8,10},{10,8},{9,1... | collective-permute-start | bytes 786440 | tf_op jit(solution)/shard_map/ppermute | solution.py:34
  15.4 12.7 %collective-permute-start = (f32[136,128]{1,0:T(8,128)}, f32[136,128]{1,0:T(8,128)S(1)}, u32[]{:S(2)}, u32[]{:S(2)}) collective-permute-start(f32[136,128]{1,0:T(8,128)} %get-tuple-element.24), channel_id=1, source_target_pairs={{0,4},{4,8},{8,12},{12,0},{1,5},{5,9},{9,13},{13,1},{2,6},{6,10},{... | collective-permute-start | bytes 208904 | tf_op jit(solution)/shard_map/ppermute | solution.py:34
  17.0 11.1 %collective-permute-start.1 = (f32[136,128]{1,0:T(8,128)}, f32[136,128]{1,0:T(8,128)S(1)}, u32[]{:S(2)}, u32[]{:S(2)}) collective-permute-start(f32[136,128]{1,0:T(8,128)} %get-tuple-element.25), channel_id=1, source_target_pairs={{0,8},{4,12},{8,0},{12,4},{1,9},{5,13},{9,1},{13,5},{2,10},{6,14},... | collective-permute-start | bytes 208904 | tf_op jit(solution)/shard_map/ppermute | solution.py:34
  19.6 8.5 %collective-permute-start.2 = (f32[136,128]{1,0:T(8,128)}, f32[136,128]{1,0:T(8,128)S(1)}, u32[]{:S(2)}, u32[]{:S(2)}) collective-permute-start(f32[136,128]{1,0:T(8,128)} %get-tuple-element.26), channel_id=1, source_target_pairs={{0,12},{4,0},{8,4},{12,8},{1,13},{5,1},{9,5},{13,9},{2,14},{6,2},{... | collective-permute-start | bytes 208904 | tf_op jit(solution)/shard_map/ppermute | solution.py:34
  21.9 1.0 %copy-start.1 = (bf16[128,1024]{1,0:T(8,128)(2,1)S(1)}, bf16[128,1024]{1,0:T(8,128)(2,1)}, u32[]{:S(2)}) copy-start(bf16[128,1024]{1,0:T(8,128)(2,1)} %get-tuple-element.28.sent) | copy-start | bytes 786436
  22.9 0.9 %copy-start.2 = (f32[32,1024]{1,0:T(8,128)S(1)}, f32[32,1024]{1,0:T(8,128)}, u32[]{:S(2)}) copy-start(f32[32,1024]{1,0:T(8,128)} %get-tuple-element.27.kept) | copy-start | bytes 393220
  23.9 30.7 %collective-permute-start.13 = (bf16[128,1024]{1,0:T(8,128)(2,1)S(1)}, bf16[128,1024]{1,0:T(8,128)(2,1)S(1)}, u32[]{:S(2)}, u32[]{:S(2)}) collective-permute-start(bf16[128,1024]{1,0:T(8,128)(2,1)S(1)} %shard_map.65.refs_4_.factors), channel_id=1, source_target_pairs={{0,8},{4,12},{8,0},{12,4},{1,9},{5,13},{9,1},{13,5},{2,10},{6,14},... | collective-permute-start | bytes 786440 | tf_op jit(solution)/shard_map/ppermute | solution.py:34
  26.7 28.3 %collective-permute-start.14 = (bf16[128,1024]{1,0:T(8,128)(2,1)S(1)}, bf16[128,1024]{1,0:T(8,128)(2,1)S(1)}, u32[]{:S(2)}, u32[]{:S(2)}) collective-permute-start(bf16[128,1024]{1,0:T(8,128)(2,1)S(1)} %shard_map.65.refs_4_.factors), channel_id=1, source_target_pairs={{0,12},{4,0},{8,4},{12,8},{1,13},{5,1},{9,5},{13,9},{2,14},{6,2},{... | collective-permute-start | bytes 786440 | tf_op jit(solution)/shard_map/ppermute | solution.py:34
  28.1 0.9 %copy-start.3 = (f32[136,128]{1,0:T(8,128)S(1)}, f32[136,128]{1,0:T(8,128)}, u32[]{:S(2)}) copy-start(f32[136,128]{1,0:T(8,128)} %get-tuple-element.23.refs_0_.slab) | copy-start | bytes 208900
  29.0 23.3 %copy-start.4 = (f32[136,128]{1,0:T(8,128)S(1)}, f32[136,128]{1,0:T(8,128)}, u32[]{:S(2)}) copy-start(f32[136,128]{1,0:T(8,128)} %get-tuple-element.23.refs_0_.slab) | copy-start | bytes 208900
  35.6 22.4 %copy-start = (bf16[512,2048]{1,0:T(8,128)(2,1)S(1)}, bf16[512,2048]{1,0:T(8,128)(2,1)}, u32[]{:S(2)}) copy-start(bf16[512,2048]{1,0:T(8,128)(2,1)} %refs_12_.3) | copy-start | bytes 6291460
  35.6 5.4 %collective-permute-start.6 = (f32[136,128]{1,0:T(8,128)S(1)}, f32[136,128]{1,0:T(8,128)S(1)}, u32[]{:S(2)}, u32[]{:S(2)}) collective-permute-start(f32[136,128]{1,0:T(8,128)S(1)} %shard_map.66.refs_0_), channel_id=1, source_target_pairs={{0,12},{4,0},{8,4},{12,8},{1,13},{5,1},{9,5},{13,9},{2,14},{6,2},{... | collective-permute-start | bytes 208904 | tf_op jit(solution)/shard_map/ppermute | solution.py:34
  35.8 25.3 %collective-permute-start.11 = (bf16[128,1024]{1,0:T(8,128)(2,1)S(1)}, bf16[128,1024]{1,0:T(8,128)(2,1)S(1)}, u32[]{:S(2)}, u32[]{:S(2)}) collective-permute-start(bf16[128,1024]{1,0:T(8,128)(2,1)S(1)} %shard_map.65.refs_4_.factors), channel_id=1, source_target_pairs={{0,4},{4,8},{8,12},{12,0},{1,5},{5,9},{9,13},{13,1},{2,6},{6,10},{... | collective-permute-start | bytes 786440 | tf_op jit(solution)/shard_map/ppermute | solution.py:34
  37.7 16.0 %collective-permute-start.4 = (f32[136,128]{1,0:T(8,128)S(1)}, f32[136,128]{1,0:T(8,128)S(1)}, u32[]{:S(2)}, u32[]{:S(2)}) collective-permute-start(f32[136,128]{1,0:T(8,128)S(1)} %shard_map.66.refs_0_), channel_id=1, source_target_pairs={{0,4},{4,8},{8,12},{12,0},{1,5},{5,9},{9,13},{13,1},{2,6},{6,10},{... | collective-permute-start | bytes 208904 | tf_op jit(solution)/shard_map/ppermute | solution.py:34
  41.0 13.5 %collective-permute-start.5 = (f32[136,128]{1,0:T(8,128)S(1)}, f32[136,128]{1,0:T(8,128)S(1)}, u32[]{:S(2)}, u32[]{:S(2)}) collective-permute-start(f32[136,128]{1,0:T(8,128)S(1)} %shard_map.66.refs_0_), channel_id=1, source_target_pairs={{0,8},{4,12},{8,0},{12,4},{1,9},{5,13},{9,1},{13,5},{2,10},{6,14},... | collective-permute-start | bytes 208904 | tf_op jit(solution)/shard_map/ppermute | solution.py:34
  53.7 4.3 %collective-permute-start.7 = (f32[136,128]{1,0:T(8,128)S(1)}, f32[136,128]{1,0:T(8,128)S(1)}, u32[]{:S(2)}, u32[]{:S(2)}) collective-permute-start(f32[136,128]{1,0:T(8,128)S(1)} %shard_map.66.refs_0_), channel_id=1, source_target_pairs={{0,1},{1,0},{2,3},{3,2},{4,5},{5,4},{6,7},{7,6},{8,9},{9,8},{10,11... | collective-permute-start | bytes 208904 | tf_op jit(solution)/shard_map/ppermute | solution.py:34
  54.5 3.4 %collective-permute-start.10 = (f32[136,128]{1,0:T(8,128)S(1)}, f32[136,128]{1,0:T(8,128)S(1)}, u32[]{:S(2)}, u32[]{:S(2)}) collective-permute-start(f32[136,128]{1,0:T(8,128)S(1)} %collective-permute-done.6.refs_3_), channel_id=1, source_target_pairs={{0,1},{1,0},{2,3},{3,2},{4,5},{5,4},{6,7},{7,6},{8,9},{9,8},{10,11... | collective-permute-start | bytes 208904 | tf_op jit(solution)/shard_map/ppermute | solution.py:34
  54.5 3.4 %collective-permute-start.8 = (f32[136,128]{1,0:T(8,128)S(1)}, f32[136,128]{1,0:T(8,128)S(1)}, u32[]{:S(2)}, u32[]{:S(2)}) collective-permute-start(f32[136,128]{1,0:T(8,128)S(1)} %collective-permute-done.4.refs_1_), channel_id=1, source_target_pairs={{0,1},{1,0},{2,3},{3,2},{4,5},{5,4},{6,7},{7,6},{8,9},{9,8},{10,11... | collective-permute-start | bytes 208904 | tf_op jit(solution)/shard_map/ppermute | solution.py:34
  55.0 2.9 %collective-permute-start.9 = (f32[136,128]{1,0:T(8,128)S(1)}, f32[136,128]{1,0:T(8,128)S(1)}, u32[]{:S(2)}, u32[]{:S(2)}) collective-permute-start(f32[136,128]{1,0:T(8,128)S(1)} %collective-permute-done.5.refs_2_), channel_id=1, source_target_pairs={{0,1},{1,0},{2,3},{3,2},{4,5},{5,4},{6,7},{7,6},{8,9},{9,8},{10,11... | collective-permute-start | bytes 208904 | tf_op jit(solution)/shard_map/ppermute | solution.py:34
  59.5 5.9 %collective-permute-start.15 = (bf16[256,256]{1,0:T(8,128)(2,1)S(1)}, bf16[256,256]{1,0:T(8,128)(2,1)S(1)}, u32[]{:S(2)}, u32[]{:S(2)}) collective-permute-start(bf16[256,256]{1,0:T(8,128)(2,1)S(1)} %get-tuple-element.40), channel_id=1, source_target_pairs={{0,2},{2,0},{1,3},{3,1},{4,6},{6,4},{5,7},{7,5},{8,10},{10,8},{9,1... | collective-permute-start | bytes 393224 | tf_op jit(solution)/shard_map/ppermute | solution.py:34
  64.0 5.6 %collective-permute-start.12 = (bf16[256,256]{1,0:T(8,128)(2,1)S(1)}, bf16[256,256]{1,0:T(8,128)(2,1)S(1)}, u32[]{:S(2)}, u32[]{:S(2)}) collective-permute-start(bf16[256,256]{1,0:T(8,128)(2,1)S(1)} %get-tuple-element.34), channel_id=1, source_target_pairs={{0,2},{2,0},{1,3},{3,1},{4,6},{6,4},{5,7},{7,5},{8,10},{10,8},{9,1... | collective-permute-start | bytes 393224 | tf_op jit(solution)/shard_map/ppermute | solution.py:34

commit v5 on v4

--- a/solution.py
+++ b/solution.py
@@ -175,8 +175,9 @@
     out[pl.ds(FBLK, 8), :] = tail
 
 
-def first_kernel(ids_hbm, id_rows_hbm, delta_hbm, table_hbm, factor_hbm, lengths_hbm, train_hbm, sent, kept, *refs):
-    slabs, (ids, id_rows, delta, table, factor, lengths, train, looked, sems) = refs[:-9], refs[-9:]
+def first_kernel(id_rows_hbm, delta_hbm, table_hbm, factor_hbm, lengths_hbm, train_hbm, sent, own, *refs):
+    slabs, refs = refs[:-10], refs[-10:]
+    id_rows, places, reads, delta, table, factor, lengths, train, looked, sems = refs
     model = lax.axis_index("mp")
     proj, vocab_rows = table.shape
     tokens = delta.shape[0]
@@ -184,7 +185,7 @@
     small = [
         pltpu.make_async_copy(source, target, sems.at[0, index])
         for index, (source, target) in enumerate((
-            (factor_hbm, factor), (lengths_hbm, lengths), (train_hbm, train), (ids_hbm, ids), (id_rows_hbm, id_rows),
+            (id_rows_hbm, id_rows), (factor_hbm, factor), (lengths_hbm, lengths), (train_hbm, train),
         ))
     ]
     tall, wide = tokens // COPIES, proj // COPIES
@@ -196,9 +197,18 @@
         pltpu.make_async_copy(table_hbm.at[rows], table.at[rows], sems.at[2, index])
         for index in range(COPIES) for rows in (pl.ds(index * wide, wide),)
     ]
-    for copy in small[:2] + get_delta + small[2:] + get_table:
+    for copy in small[:3] + get_delta + small[3:] + get_table:
         copy.start()
     small[0].wait()
+    local = id_rows[...] - model * vocab_rows
+    owned = (local >= 0) & (local < vocab_rows)
+    local = jnp.where(owned, local, 0)
+    low = FBLK - 1
+    roll = (lax.broadcasted_iota(jnp.int32, local.shape, 1) - local) & low
+    places[...] = (local & ~low) | roll
+    fetch = pltpu.make_async_copy(places, reads, sems.at[0, 4])
+    fetch.start()
+    small[1].wait()
     for index, copy in enumerate(get_delta):
         copy.wait()
         rows = pl.ds(index * tall, tall)
@@ -208,47 +218,50 @@
         looked[:, rows] = output.T
     mine = looked[pl.ds(pl.multiple_of(model * each, each), each), :]
     other = looked[pl.ds(pl.multiple_of((1 - model) * each, each), each), :]
-    kept[...] = mine
-    high, low = halves(other)
-    sent[pl.ds(0, each), :] = high
-    sent[pl.ds(each, each), :] = low
-    for copy in small[1:3]:
+    for target, value in ((own, mine), (sent, other)):
+        high, rest = halves(value)
+        target[pl.ds(0, each), :] = high
+        target[pl.ds(each, each), :] = rest
+    for copy in small[2:]:
         copy.wait()
     grams(lengths, train, slabs)
-    for copy in small[3:] + get_table:
+    fetch.wait()
+    for copy in get_table:
         copy.wait()
     lanes = lax.broadcasted_iota(jnp.int32, (proj, FBLK), 1)
-    first = model * vocab_rows
+    places[...] = owned.astype(jnp.int32)
 
     def group(g, carry):
         gathered = jnp.zeros((proj, FBLK), jnp.bfloat16)
-        base = g * FBLK
         for j in range(FBLK):
-            local = ids[base + j] - first
-            local = jnp.where((local >= 0) & (local < vocab_rows), local, 0)
-            block = table[:, pl.ds(pl.multiple_of((local >> 7) * FBLK, FBLK), FBLK)]
-            gathered = jnp.where(lanes == j, pltpu.roll(block, (j - local) & (FBLK - 1), 1), gathered)
-        local = id_rows[pl.ds(g, 1), :] - first
-        owned = (local >= 0) & (local < vocab_rows)
-        spread = jnp.where(owned, 1.0, 0.0)
-        gathered = (gathered.astype(jnp.float32) * spread).astype(jnp.bfloat16)
-        sent[pl.ds(2 * each, proj), pl.ds(pl.multiple_of(base, FBLK), FBLK)] = gathered
+            place = reads[g, j]
+            block = table[:, pl.ds(pl.multiple_of(place & ~low, FBLK), FBLK)]
+            gathered = jnp.where(lanes == j, pltpu.roll(block, place & low, 1), gathered)
+        held = places[pl.ds(g, 1), :].astype(jnp.float32)
+        gathered = (gathered.astype(jnp.float32) * held).astype(jnp.bfloat16)
+        columns = pl.ds(pl.multiple_of(g * FBLK, FBLK), FBLK)
+        sent[pl.ds(2 * each, proj), columns] = gathered
+        own[pl.ds(2 * each, proj), columns] = gathered
         return carry
 
     lax.fori_loop(0, tokens // FBLK, group, 0)
 
 
-def merge_kernel(kept, sent, got, out):
-    each = kept.shape[0]
-    received = got[pl.ds(0, each), :].astype(jnp.float32) + got[pl.ds(each, each), :].astype(jnp.float32)
-    high, low = halves(kept[...] + received)
+def merge_kernel(each, own, got, out):
+    def value(ref):
+        return ref[pl.ds(0, each), :].astype(jnp.float32) + ref[pl.ds(each, each), :].astype(jnp.float32)
+
+    high, low = halves(value(own) + value(got))
     out[pl.ds(0, each), :] = high
     out[pl.ds(each, each), :] = low
     rows = pl.ds(2 * each, out.shape[0] - 2 * each)
-    out[rows, :] = sent[rows, :] + got[rows, :]
-
-
-def queries_kernel(each, factors, slab, high_out, low_out):
+    out[rows, :] = own[rows, :] + got[rows, :]
+
+
+def queries_kernel(each, factors, slab, *refs):
+    after, high_out, low_out, again = refs if len(refs) == 4 else (None, *refs, None)
+    if again is not None:
+        again[...] = factors[...]
     tokens = factors.shape[1]
     proj = factors.shape[0] - 2 * each
     queries = high_out.shape[1]
@@ -301,13 +314,14 @@
         out[...] = jnp.dot(train[rows, :], pre[...], preferred_element_type=jnp.float32).astype(jnp.bfloat16)
 
 
-def total_kernel(cycle, count, *refs):
+def total_kernel(order, *refs):
     pieces, out = refs[:-1], refs[-1]
-    mine = lax.axis_index("dp")
-    sums = []
+    mine, cycle = lax.axis_index("dp"), len(order)
+    sums = {}
     for kept, got in zip(pieces[::2], pieces[1::2]):
         both = kept[...].astype(jnp.float32) + got[...].astype(jnp.float32)
-        sums += [both[:, index * FBLK:(index + 1) * FBLK] for index in range(count)]
+        for index in range(both.shape[1] // FBLK):
+            sums[order[len(sums)]] = both[:, index * FBLK:(index + 1) * FBLK]
     placed = []
     for source in range(cycle):
         shift = lax.rem(mine + cycle - source, cycle)
@@ -332,13 +346,14 @@
     queries = doc_lengths.shape[1]
     bf16, f32 = jnp.bfloat16, jnp.float32
 
-    sent, kept, *slabs = call(
+    sent, own, *slabs = call(
         first_kernel,
-        [shape((2 * each + proj, tokens), bf16), shape((each, tokens), f32)] + [shape((SLAB, FBLK), f32)] * cycle,
-        [HBM] * 7,
+        [shape((2 * each + proj, tokens), bf16)] * 2 + [shape((SLAB, FBLK), f32)] * cycle,
+        [HBM] * 6,
         [
-            pltpu.SMEM((tokens,), jnp.int32),
             pltpu.VMEM((tokens // FBLK, FBLK), jnp.int32),
+            pltpu.VMEM((tokens // FBLK, FBLK), jnp.int32),
+            pltpu.SMEM((tokens // FBLK, FBLK), jnp.int32),
             pltpu.VMEM((tokens, width), bf16),
             pltpu.VMEM((proj, vocab_rows), bf16),
             pltpu.VMEM((proj, width), bf16),
@@ -351,21 +366,22 @@
         flops=2 * tokens * width * proj,
         moved=2 * (tokens * width + proj * vocab_rows) * 2,
     )(
-        query_ids, query_ids.reshape(tokens // FBLK, FBLK), query_delta, vocab_factor.T, output_factor.T,
+        query_ids.reshape(tokens // FBLK, FBLK), query_delta, vocab_factor.T, output_factor.T,
         doc_lengths, train_grads,
     )
     got = passed_along(sent, "mp", 1)
     parts = [slabs[0]] + [passed_along(slabs[s], "dp", s) for s in range(1, cycle)]
 
     factors = call(
-        merge_kernel,
+        functools.partial(merge_kernel, each),
         shape(sent.shape, bf16),
-        [VMEM, VMEM, VMEM],
+        [VMEM, VMEM],
         vmem=16,
         flops=tokens * each,
         moved=8 * tokens * each * 4,
-    )(kept, sent, got)
-    gathered = [factors] + [passed_along(factors, "dp", s) for s in range(1, cycle)]
+    )(own, got)
+    late = cycle // 2
+    gathered = [factors] + [passed_along(factors, "dp", s) if s != late else None for s in range(1, cycle)]
 
     inverse = call(
         functools.partial(factor_kernel, train_rows * cycle, 1.0 / proj),
@@ -378,24 +394,25 @@
     inverses = [inverse] + [passed_along(inverse, "dp", s) for s in range(1, cycle)]
     peers = [passed_along(slab, "rep", 1) for slab in inverses]
 
-    highs, lows = [], []
-    for s in range(cycle):
-        high, low = call(
+    highs, lows = {}, {}
+    for s in sorted(range(cycle), key=lambda shift: (shift == late, shift)):
+        first = s == 0
+        highs[s], lows[s], *again = call(
             functools.partial(queries_kernel, each),
-            [shape((feat, queries), bf16)] * 2,
-            [VMEM, VMEM],
+            [shape((feat, queries), bf16)] * 2 + [shape(factors.shape, bf16)] * first,
+            [VMEM, VMEM] + [HBM] * first,
             vmem=24,
             flops=2 * feat * tokens * queries,
             moved=6 * feat * queries,
-        )(gathered[s], parts[s])
-        highs.append(high)
-        lows.append(low)
+        )(gathered[s], parts[s], *[inverse] * first)
+        if first:
+            gathered[late] = passed_along(again[0], "dp", late)
 
     half_rows = train_rows // lax.axis_size("mp")
-    count = cycle // 2
-    pieces = []
-    for start in range(0, cycle, count):
-        outgoing, own = call(
+    pieces, order = [], []
+    for chosen in ([s for s in range(cycle) if s != late], [late]):
+        count = len(chosen)
+        outgoing, kept = call(
             functools.partial(scores_kernel, cycle, count),
             [shape((half_rows, count * queries), bf16)] * 2,
             [VMEM] * (2 * cycle + 2 * count + 1),
@@ -403,10 +420,11 @@
             vmem=24,
             flops=2 * train_rows * feat * count * queries,
             moved=8 * feat * queries * count,
-        )(*inverses, *peers, *highs[start:start + count], *lows[start:start + count], train_grads)
-        pieces += [own, passed_along(outgoing, "mp", 1)]
+        )(*inverses, *peers, *[highs[s] for s in chosen], *[lows[s] for s in chosen], train_grads)
+        pieces += [kept, passed_along(outgoing, "mp", 1)]
+        order += chosen
     total = call(
-        functools.partial(total_kernel, cycle, count),
+        functools.partial(total_kernel, order),
         shape((half_rows, cycle, queries), bf16),
         [VMEM] * len(pieces),
         vmem=16,

time: 72 us -> 65.2 us (0.906); the launches traced: 70.9 us -> 65 us
  starting transfers between devices: 29.6 us -> 20.3 us
  waiting for transfers between devices: 9.54 us -> 13.6 us
  local copies, waits for them, and re-layouts: 2.74 us -> 1.83 us
    ppermute x16, starting transfers between devices: 29.6 us -> 20.3 us  [passed_along(): lax.ppermute(shard, axis, [(i, (i + by) % size) for i in range(size)])]
    ppermute x16, waiting for transfers between devices: 9.54 us -> 13.6 us  [passed_along(): lax.ppermute(shard, axis, [(i, (i + by) % size) for i in range(size)])]
    unnamed x10 -> x6, local copies, waits for them, and re-layouts: 2.74 us -> 1.83 us
    pallas_call x2, Pallas kernels: 3 us -> 3.89 us  [split_over_blocks(): call(functools.partial(scores_kernel, cycle, count), [shape((half_rows, c...]
  transfers between devices with their start and end apart: 16 -> 16, of which waited for: 5 -> 4; matrix products, arithmetic and copies ran while one was open for 0% -> 0% of each run, Pallas kernels for 22% -> 25%
where the time goes in v5:
time: 65.2 us; the launch traced here: 65 us
  Pallas kernels  29.1 us (45%)
  starting transfers between devices  20.3 us (31%)
  waiting for transfers between devices  13.6 us (21%)
  local copies, waits for them, and re-layouts  1.83 us (3%)
    ppermute x16, starting transfers between devices, passed_along(): lax.ppermute(shard, axis, [(i, (i + by) % size) for i in range(size)])  20.3 us
    ppermute x16, waiting for transfers between devices, passed_along(): lax.ppermute(shard, axis, [(i, (i + by) % size) for i in range(size)])  13.6 us
    pallas_call x1, Pallas kernels, split_over_blocks(): call(first_kernel, [shape((2 * each + proj, tokens), bf16)] * 2 + [shape(...  11.7 us
    pallas_call x1, Pallas kernels, split_over_blocks(): call(functools.partial(factor_kernel, train_rows * cycle, 1.0 / proj), sh...  6.57 us
    pallas_call x4, Pallas kernels, split_over_blocks(): call(functools.partial(queries_kernel, each), [shape((feat, queries), bf1...  5.63 us
    pallas_call x2, Pallas kernels, split_over_blocks(): call(functools.partial(scores_kernel, cycle, count), [shape((half_rows, c...  3.89 us
    unnamed x6, local copies, waits for them, and re-layouts  1.83 us
  transfers between devices with their start and end apart: 16, of which 4 were waited for; matrix products, arithmetic and copies ran while one was open for 0% of the time, Pallas kernels for 25%

profile of v5, /device:TPU:0, one launch (start us, length us, event | category | flops | bytes accessed | tf_op | source)
XLA Modules:
  0.0 65.0 jit_solution(17175153139616979439)
XLA Ops:
  0.0 11.7 %shard_map.64 = (bf16[128,1024]{1,0:T(8,128)(2,1)}, bf16[128,1024]{1,0:T(8,128)(2,1)}, f32[136,128]{1,0:T(8,128)}, f32[136,128]{1,0:T(8,128)}, f32[136,128]{1,0:T(8,128)}, /*index=5*/f32[136,128]{1,0:T(8,128)}) custom-call(s32[8,128]{1,0:T(8,128)} %bitcast.8, bf16[1024,2048]{1,0:T(8,128)(2,1)} %delta_hbm.1, bf16[64,64128]{1,0:T(8,128)(2,1)} %bitcast.6, ...), custom_call_target="tpu_custom_call" | custom-call | flops 268435456 | bytes 24805376 | tf_op jit(solution)/shard_map/pallas_call | solution.py:349
  11.7 3.0 %collective-permute-start.3 = (bf16[128,1024]{1,0:T(8,128)(2,1)}, bf16[128,1024]{1,0:T(8,128)(2,1)S(1)}, u32[]{:S(2)}, u32[]{:S(2)}) collective-permute-start(bf16[128,1024]{1,0:T(8,128)(2,1)} %get-tuple-element.29), channel_id=1, source_target_pairs={{0,2},{2,0},{1,3},{3,1},{4,6},{6,4},{5,7},{7,5},{8,10},{10,8},{9,1... | collective-permute-start | bytes 786440 | tf_op jit(solution)/shard_map/ppermute | solution.py:34
  14.7 1.6 %collective-permute-start = (f32[136,128]{1,0:T(8,128)}, f32[136,128]{1,0:T(8,128)S(1)}, u32[]{:S(2)}, u32[]{:S(2)}) collective-permute-start(f32[136,128]{1,0:T(8,128)} %get-tuple-element.25), channel_id=1, source_target_pairs={{0,4},{4,8},{8,12},{12,0},{1,5},{5,9},{9,13},{13,1},{2,6},{6,10},{... | collective-permute-start | bytes 208904 | tf_op jit(solution)/shard_map/ppermute | solution.py:34
  16.3 2.6 %collective-permute-start.1 = (f32[136,128]{1,0:T(8,128)}, f32[136,128]{1,0:T(8,128)S(1)}, u32[]{:S(2)}, u32[]{:S(2)}) collective-permute-start(f32[136,128]{1,0:T(8,128)} %get-tuple-element.26), channel_id=1, source_target_pairs={{0,8},{4,12},{8,0},{12,4},{1,9},{5,13},{9,1},{13,5},{2,10},{6,14},... | collective-permute-start | bytes 208904 | tf_op jit(solution)/shard_map/ppermute | solution.py:34
  18.9 1.4 %collective-permute-start.2 = (f32[136,128]{1,0:T(8,128)}, f32[136,128]{1,0:T(8,128)S(1)}, u32[]{:S(2)}, u32[]{:S(2)}) collective-permute-start(f32[136,128]{1,0:T(8,128)} %get-tuple-element.27), channel_id=1, source_target_pairs={{0,12},{4,0},{8,4},{12,8},{1,13},{5,1},{9,5},{13,9},{2,14},{6,2},{... | collective-permute-start | bytes 208904 | tf_op jit(solution)/shard_map/ppermute | solution.py:34
  20.2 1.0 %collective-permute-done.3.got = bf16[128,1024]{1,0:T(8,128)(2,1)S(1)} collective-permute-done((bf16[128,1024]{1,0:T(8,128)(2,1)}, bf16[128,1024]{1,0:T(8,128)(2,1)S(1)}, u32[]{:S(2)}, u32[]{:S(2)}) %collective-permute-start.3) | collective-permute-done | bytes 262176 | tf_op jit(solution)/shard_map/ppermute | solution.py:34
  21.2 0.0 copy-start.1
  21.2 0.9 %copy-done.1 = bf16[128,1024]{1,0:T(8,128)(2,1)S(1)} copy-done((bf16[128,1024]{1,0:T(8,128)(2,1)S(1)}, bf16[128,1024]{1,0:T(8,128)(2,1)}, u32[]{:S(2)}) %copy-start.1) | copy-done | bytes 262168
  22.2 0.1 shard_map.65.refs_4_.factors
  22.2 1.9 %collective-permute-start.11 = (bf16[128,1024]{1,0:T(8,128)(2,1)S(1)}, bf16[128,1024]{1,0:T(8,128)(2,1)S(1)}, u32[]{:S(2)}, u32[]{:S(2)}) collective-permute-start(bf16[128,1024]{1,0:T(8,128)(2,1)S(1)} %shard_map.65.refs_4_.factors), channel_id=1, source_target_pairs={{0,4},{4,8},{8,12},{12,0},{1,5},{5,9},{9,13},{13,1},{2,6},{6,10},{... | collective-permute-start | bytes 786440 | tf_op jit(solution)/shard_map/ppermute | solution.py:34
  24.1 2.1 %collective-permute-start.12 = (bf16[128,1024]{1,0:T(8,128)(2,1)S(1)}, bf16[128,1024]{1,0:T(8,128)(2,1)S(1)}, u32[]{:S(2)}, u32[]{:S(2)}) collective-permute-start(bf16[128,1024]{1,0:T(8,128)(2,1)S(1)} %shard_map.65.refs_4_.factors), channel_id=1, source_target_pairs={{0,12},{4,0},{8,4},{12,8},{1,13},{5,1},{9,5},{13,9},{2,14},{6,2},{... | collective-permute-start | bytes 786440 | tf_op jit(solution)/shard_map/ppermute | solution.py:34
  26.2 0.0 collective-permute-done.refs_1_.slab
  26.2 0.0 collective-permute-done.1.refs_2_.slab
  26.2 0.0 collective-permute-done.2.refs_3_.slab
  26.2 0.0 copy-start.2
  26.2 0.9 %copy-done.2 = f32[136,128]{1,0:T(8,128)S(1)} copy-done((f32[136,128]{1,0:T(8,128)S(1)}, f32[136,128]{1,0:T(8,128)}, u32[]{:S(2)}) %copy-start.2) | copy-done | bytes 69656
  27.1 6.6 %shard_map.66.refs_0_ = f32[136,128]{1,0:T(8,128)S(1)} custom-call(f32[136,128]{1,0:T(8,128)S(1)} %copy-done.2, f32[136,128]{1,0:T(8,128)S(1)} %collective-permute-done.refs_1_.slab, f32[136,128]{1,0:T(8,128)S(1)} %collective-permute-done.1.refs_2_.slab, f32[136,128]{1,0:T(8,128)S(1)} %collective-permute-done.2.refs_3_.slab, ...), custom_call_target="tpu_custom_call" | custom-call | flops 10000000000 | bytes 1000000 | tf_op jit(solution)/shard_map/pallas_call | solution.py:386
  33.7 0.0 copy-start
  33.7 2.0 %collective-permute-start.6 = (f32[136,128]{1,0:T(8,128)S(1)}, f32[136,128]{1,0:T(8,128)S(1)}, u32[]{:S(2)}, u32[]{:S(2)}) collective-permute-start(f32[136,128]{1,0:T(8,128)S(1)} %shard_map.66.refs_0_), channel_id=1, source_target_pairs={{0,12},{4,0},{8,4},{12,8},{1,13},{5,1},{9,5},{13,9},{2,14},{6,2},{... | collective-permute-start | bytes 208904 | tf_op jit(solution)/shard_map/ppermute | solution.py:34
  35.7 0.1 collective-permute-start.4
  35.8 0.9 %collective-permute-start.5 = (f32[136,128]{1,0:T(8,128)S(1)}, f32[136,128]{1,0:T(8,128)S(1)}, u32[]{:S(2)}, u32[]{:S(2)}) collective-permute-start(f32[136,128]{1,0:T(8,128)S(1)} %shard_map.66.refs_0_), channel_id=1, source_target_pairs={{0,8},{4,12},{8,0},{12,4},{1,9},{5,13},{9,1},{13,5},{2,10},{6,14},... | collective-permute-start | bytes 208904 | tf_op jit(solution)/shard_map/ppermute | solution.py:34
  36.7 1.4 %shard_map.67 = (bf16[2048,128]{1,0:T(8,128)(2,1)S(1)}, bf16[2048,128]{1,0:T(8,128)(2,1)S(1)}, bf16[128,1024]{1,0:T(8,128)(2,1)S(1)}) custom-call(bf16[128,1024]{1,0:T(8,128)(2,1)S(1)} %shard_map.65.refs_4_.factors, f32[136,128]{1,0:T(8,128)S(1)} %copy-done.2, f32[136,128]{1,0:T(8,128)S(1)} %shard_map.66.refs_0_), custom_call_target="tpu_custom_call" | custom-call | flops 536870912 | bytes 1572864 | tf_op jit(solution)/shard_map/pallas_call | solution.py:400
  38.1 0.0 collective-permute-done.6.refs_3_
  38.1 2.0 %collective-permute-start.14 = (bf16[128,1024]{1,0:T(8,128)(2,1)S(1)}, bf16[128,1024]{1,0:T(8,128)(2,1)S(1)}, u32[]{:S(2)}, u32[]{:S(2)}) collective-permute-start(bf16[128,1024]{1,0:T(8,128)(2,1)S(1)} %get-tuple-element.38), channel_id=1, source_target_pairs={{0,8},{4,12},{8,0},{12,4},{1,9},{5,13},{9,1},{13,5},{2,10},{6,14},... | collective-permute-start | bytes 786440 | tf_op jit(solution)/shard_map/ppermute | solution.py:34
  40.2 1.7 %collective-permute-done.4.refs_1_ = f32[136,128]{1,0:T(8,128)S(1)} collective-permute-done((f32[136,128]{1,0:T(8,128)S(1)}, f32[136,128]{1,0:T(8,128)S(1)}, u32[]{:S(2)}, u32[]{:S(2)}) %collective-permute-start.4) | collective-permute-done | bytes 69664 | tf_op jit(solution)/shard_map/ppermute | solution.py:34
  41.9 0.0 collective-permute-start.7
  41.9 7.1 %collective-permute-done.5.refs_2_ = f32[136,128]{1,0:T(8,128)S(1)} collective-permute-done((f32[136,128]{1,0:T(8,128)S(1)}, f32[136,128]{1,0:T(8,128)S(1)}, u32[]{:S(2)}, u32[]{:S(2)}) %collective-permute-start.5) | collective-permute-done | bytes 69664 | tf_op jit(solution)/shard_map/ppermute | solution.py:34
  49.0 0.0 collective-permute-start.10
  49.0 0.0 collective-permute-done.11.factors
  49.0 0.5 collective-permute-start.8
  49.5 0.0 collective-permute-done.12.factors
  49.5 0.1 collective-permute-start.9
  49.6 1.4 %shard_map.68 = (bf16[2048,128]{1,0:T(8,128)(2,1)S(1)}, bf16[2048,128]{1,0:T(8,128)(2,1)S(1)}) custom-call(bf16[128,1024]{1,0:T(8,128)(2,1)S(1)} %collective-permute-done.11.factors, f32[136,128]{1,0:T(8,128)S(1)} %collective-permute-done.refs_1_.slab), custom_call_target="tpu_custom_call" | custom-call | flops 536870912 | bytes 1572864 | tf_op jit(solution)/shard_map/pallas_call | solution.py:400
  51.0 1.4 %shard_map.69 = (bf16[2048,128]{1,0:T(8,128)(2,1)S(1)}, bf16[2048,128]{1,0:T(8,128)(2,1)S(1)}) custom-call(bf16[128,1024]{1,0:T(8,128)(2,1)S(1)} %collective-permute-done.12.factors, f32[136,128]{1,0:T(8,128)S(1)} %collective-permute-done.2.refs_3_.slab), custom_call_target="tpu_custom_call" | custom-call | flops 536870912 | bytes 1572864 | tf_op jit(solution)/shard_map/pallas_call | solution.py:400
  52.4 0.0 collective-permute-done.7.refs_4_
  52.4 0.0 collective-permute-done.10.refs_7_
  52.4 0.0 collective-permute-done.8.refs_5_
  52.4 0.0 collective-permute-done.9.refs_6_
  52.4 0.0 copy-done
  52.4 2.5 %shard_map.70 = (bf16[256,384]{1,0:T(8,128)(2,1)S(1)}, bf16[256,384]{1,0:T(8,128)(2,1)S(1)}) custom-call(f32[136,128]{1,0:T(8,128)S(1)} %shard_map.66.refs_0_, f32[136,128]{1,0:T(8,128)S(1)} %collective-permute-done.4.refs_1_, f32[136,128]{1,0:T(8,128)S(1)} %collective-permute-done.5.refs_2_, f32[136,128]{1,0:T(8,128)S(1)} %collective-permute-done.6.refs_3_, ...), custom_call_target="tpu_custom_call" | custom-call | flops 805306368 | bytes 6291456 | tf_op jit(solution)/shard_map/pallas_call | solution.py:415
  55.0 1.6 %collective-permute-start.13 = (bf16[256,384]{1,0:T(8,128)(2,1)S(1)}, bf16[256,384]{1,0:T(8,128)(2,1)S(1)}, u32[]{:S(2)}, u32[]{:S(2)}) collective-permute-start(bf16[256,384]{1,0:T(8,128)(2,1)S(1)} %get-tuple-element.37), channel_id=1, source_target_pairs={{0,2},{2,0},{1,3},{3,1},{4,6},{6,4},{5,7},{7,5},{8,10},{10,8},{9,1... | collective-permute-start | bytes 589832 | tf_op jit(solution)/shard_map/ppermute | solution.py:34
  56.6 0.0 collective-permute-done.14.factors
  56.6 1.4 %shard_map.71 = (bf16[2048,128]{1,0:T(8,128)(2,1)S(1)}, bf16[2048,128]{1,0:T(8,128)(2,1)S(1)}) custom-call(bf16[128,1024]{1,0:T(8,128)(2,1)S(1)} %collective-permute-done.14.factors, f32[136,128]{1,0:T(8,128)S(1)} %collective-permute-done.1.refs_2_.slab), custom_call_target="tpu_custom_call" | custom-call | flops 536870912 | bytes 1572864 | tf_op jit(solution)/shard_map/pallas_call | solution.py:400
  58.0 1.3 %shard_map.72 = (bf16[256,128]{1,0:T(8,128)(2,1)S(1)}, bf16[256,128]{1,0:T(8,128)(2,1)S(1)}) custom-call(f32[136,128]{1,0:T(8,128)S(1)} %shard_map.66.refs_0_, f32[136,128]{1,0:T(8,128)S(1)} %collective-permute-done.4.refs_1_, f32[136,128]{1,0:T(8,128)S(1)} %collective-permute-done.5.refs_2_, f32[136,128]{1,0:T(8,128)S(1)} %collective-permute-done.6.refs_3_, ...), custom_call_target="tpu_custom_call" | custom-call | flops 268435456 | bytes 2097152 | tf_op jit(solution)/shard_map/pallas_call | solution.py:415
  59.4 0.5 collective-permute-start.15
  59.9 3.8 %collective-permute-done.15.refs_3_ = bf16[256,128]{1,0:T(8,128)(2,1)S(1)} collective-permute-done((bf16[256,128]{1,0:T(8,128)(2,1)S(1)}, bf16[256,128]{1,0:T(8,128)(2,1)S(1)}, u32[]{:S(2)}, u32[]{:S(2)}) %collective-permute-start.15) | collective-permute-done | bytes 65568 | tf_op jit(solution)/shard_map/ppermute | solution.py:34
  63.7 0.0 collective-permute-done.13.refs_1_
  63.7 1.3 %shard_map.73 = bf16[256,4,128]{2,1,0:T(4,128)(2,1)} custom-call(bf16[256,384]{1,0:T(8,128)(2,1)S(1)} %get-tuple-element.36.refs_0_, bf16[256,384]{1,0:T(8,128)(2,1)S(1)} %collective-permute-done.13.refs_1_, bf16[256,128]{1,0:T(8,128)(2,1)S(1)} %get-tuple-element.41.refs_2_, bf16[256,128]{1,0:T(8,128)(2,1)S(1)} %collective-permute-done.15.refs_3_), custom_call_target="tpu_custom_call" | custom-call | flops 131072 | bytes 786432 | tf_op jit(solution)/shard_map/pallas_call | solution.py:426
Async XLA Ops:
  11.7 9.5 %collective-permute-start.3 = (bf16[128,1024]{1,0:T(8,128)(2,1)}, bf16[128,1024]{1,0:T(8,128)(2,1)S(1)}, u32[]{:S(2)}, u32[]{:S(2)}) collective-permute-start(bf16[128,1024]{1,0:T(8,128)(2,1)} %get-tuple-element.29), channel_id=1, source_target_pairs={{0,2},{2,0},{1,3},{3,1},{4,6},{6,4},{5,7},{7,5},{8,10},{10,8},{9,1... | collective-permute-start | bytes 786440 | tf_op jit(solution)/shard_map/ppermute | solution.py:34
  14.7 11.5 %collective-permute-start = (f32[136,128]{1,0:T(8,128)}, f32[136,128]{1,0:T(8,128)S(1)}, u32[]{:S(2)}, u32[]{:S(2)}) collective-permute-start(f32[136,128]{1,0:T(8,128)} %get-tuple-element.25), channel_id=1, source_target_pairs={{0,4},{4,8},{8,12},{12,0},{1,5},{5,9},{9,13},{13,1},{2,6},{6,10},{... | collective-permute-start | bytes 208904 | tf_op jit(solution)/shard_map/ppermute | solution.py:34
  16.3 9.9 %collective-permute-start.1 = (f32[136,128]{1,0:T(8,128)}, f32[136,128]{1,0:T(8,128)S(1)}, u32[]{:S(2)}, u32[]{:S(2)}) collective-permute-start(f32[136,128]{1,0:T(8,128)} %get-tuple-element.26), channel_id=1, source_target_pairs={{0,8},{4,12},{8,0},{12,4},{1,9},{5,13},{9,1},{13,5},{2,10},{6,14},... | collective-permute-start | bytes 208904 | tf_op jit(solution)/shard_map/ppermute | solution.py:34
  18.9 7.3 %collective-permute-start.2 = (f32[136,128]{1,0:T(8,128)}, f32[136,128]{1,0:T(8,128)S(1)}, u32[]{:S(2)}, u32[]{:S(2)}) collective-permute-start(f32[136,128]{1,0:T(8,128)} %get-tuple-element.27), channel_id=1, source_target_pairs={{0,12},{4,0},{8,4},{12,8},{1,13},{5,1},{9,5},{13,9},{2,14},{6,2},{... | collective-permute-start | bytes 208904 | tf_op jit(solution)/shard_map/ppermute | solution.py:34
  21.2 1.0 %copy-start.1 = (bf16[128,1024]{1,0:T(8,128)(2,1)S(1)}, bf16[128,1024]{1,0:T(8,128)(2,1)}, u32[]{:S(2)}) copy-start(bf16[128,1024]{1,0:T(8,128)(2,1)} %get-tuple-element.28.own) | copy-start | bytes 786436
  22.2 26.8 %collective-permute-start.11 = (bf16[128,1024]{1,0:T(8,128)(2,1)S(1)}, bf16[128,1024]{1,0:T(8,128)(2,1)S(1)}, u32[]{:S(2)}, u32[]{:S(2)}) collective-permute-start(bf16[128,1024]{1,0:T(8,128)(2,1)S(1)} %shard_map.65.refs_4_.factors), channel_id=1, source_target_pairs={{0,4},{4,8},{8,12},{12,0},{1,5},{5,9},{9,13},{13,1},{2,6},{6,10},{... | collective-permute-start | bytes 786440 | tf_op jit(solution)/shard_map/ppermute | solution.py:34
  24.1 25.4 %collective-permute-start.12 = (bf16[128,1024]{1,0:T(8,128)(2,1)S(1)}, bf16[128,1024]{1,0:T(8,128)(2,1)S(1)}, u32[]{:S(2)}, u32[]{:S(2)}) collective-permute-start(bf16[128,1024]{1,0:T(8,128)(2,1)S(1)} %shard_map.65.refs_4_.factors), channel_id=1, source_target_pairs={{0,12},{4,0},{8,4},{12,8},{1,13},{5,1},{9,5},{13,9},{2,14},{6,2},{... | collective-permute-start | bytes 786440 | tf_op jit(solution)/shard_map/ppermute | solution.py:34
  26.2 0.9 %copy-start.2 = (f32[136,128]{1,0:T(8,128)S(1)}, f32[136,128]{1,0:T(8,128)}, u32[]{:S(2)}) copy-start(f32[136,128]{1,0:T(8,128)} %get-tuple-element.24.refs_0_.slab) | copy-start | bytes 208900
  33.7 18.8 %copy-start = (bf16[512,2048]{1,0:T(8,128)(2,1)S(1)}, bf16[512,2048]{1,0:T(8,128)(2,1)}, u32[]{:S(2)}) copy-start(bf16[512,2048]{1,0:T(8,128)(2,1)} %refs_10_.1) | copy-start | bytes 6291460
  33.7 4.4 %collective-permute-start.6 = (f32[136,128]{1,0:T(8,128)S(1)}, f32[136,128]{1,0:T(8,128)S(1)}, u32[]{:S(2)}, u32[]{:S(2)}) collective-permute-start(f32[136,128]{1,0:T(8,128)S(1)} %shard_map.66.refs_0_), channel_id=1, source_target_pairs={{0,12},{4,0},{8,4},{12,8},{1,13},{5,1},{9,5},{13,9},{2,14},{6,2},{... | collective-permute-start | bytes 208904 | tf_op jit(solution)/shard_map/ppermute | solution.py:34
  35.7 6.2 %collective-permute-start.4 = (f32[136,128]{1,0:T(8,128)S(1)}, f32[136,128]{1,0:T(8,128)S(1)}, u32[]{:S(2)}, u32[]{:S(2)}) collective-permute-start(f32[136,128]{1,0:T(8,128)S(1)} %shard_map.66.refs_0_), channel_id=1, source_target_pairs={{0,4},{4,8},{8,12},{12,0},{1,5},{5,9},{9,13},{13,1},{2,6},{6,10},{... | collective-permute-start | bytes 208904 | tf_op jit(solution)/shard_map/ppermute | solution.py:34
  35.8 13.2 %collective-permute-start.5 = (f32[136,128]{1,0:T(8,128)S(1)}, f32[136,128]{1,0:T(8,128)S(1)}, u32[]{:S(2)}, u32[]{:S(2)}) collective-permute-start(f32[136,128]{1,0:T(8,128)S(1)} %shard_map.66.refs_0_), channel_id=1, source_target_pairs={{0,8},{4,12},{8,0},{12,4},{1,9},{5,13},{9,1},{13,5},{2,10},{6,14},... | collective-permute-start | bytes 208904 | tf_op jit(solution)/shard_map/ppermute | solution.py:34
  38.1 18.5 %collective-permute-start.14 = (bf16[128,1024]{1,0:T(8,128)(2,1)S(1)}, bf16[128,1024]{1,0:T(8,128)(2,1)S(1)}, u32[]{:S(2)}, u32[]{:S(2)}) collective-permute-start(bf16[128,1024]{1,0:T(8,128)(2,1)S(1)} %get-tuple-element.38), channel_id=1, source_target_pairs={{0,8},{4,12},{8,0},{12,4},{1,9},{5,13},{9,1},{13,5},{2,10},{6,14},... | collective-permute-start | bytes 786440 | tf_op jit(solution)/shard_map/ppermute | solution.py:34
  41.9 10.5 %collective-permute-start.7 = (f32[136,128]{1,0:T(8,128)S(1)}, f32[136,128]{1,0:T(8,128)S(1)}, u32[]{:S(2)}, u32[]{:S(2)}) collective-permute-start(f32[136,128]{1,0:T(8,128)S(1)} %shard_map.66.refs_0_), channel_id=1, source_target_pairs={{0,1},{1,0},{2,3},{3,2},{4,5},{5,4},{6,7},{7,6},{8,9},{9,8},{10,11... | collective-permute-start | bytes 208904 | tf_op jit(solution)/shard_map/ppermute | solution.py:34
  49.0 3.4 %collective-permute-start.10 = (f32[136,128]{1,0:T(8,128)S(1)}, f32[136,128]{1,0:T(8,128)S(1)}, u32[]{:S(2)}, u32[]{:S(2)}) collective-permute-start(f32[136,128]{1,0:T(8,128)S(1)} %collective-permute-done.6.refs_3_), channel_id=1, source_target_pairs={{0,1},{1,0},{2,3},{3,2},{4,5},{5,4},{6,7},{7,6},{8,9},{9,8},{10,11... | collective-permute-start | bytes 208904 | tf_op jit(solution)/shard_map/ppermute | solution.py:34
  49.0 3.4 %collective-permute-start.8 = (f32[136,128]{1,0:T(8,128)S(1)}, f32[136,128]{1,0:T(8,128)S(1)}, u32[]{:S(2)}, u32[]{:S(2)}) collective-permute-start(f32[136,128]{1,0:T(8,128)S(1)} %collective-permute-done.4.refs_1_), channel_id=1, source_target_pairs={{0,1},{1,0},{2,3},{3,2},{4,5},{5,4},{6,7},{7,6},{8,9},{9,8},{10,11... | collective-permute-start | bytes 208904 | tf_op jit(solution)/shard_map/ppermute | solution.py:34
  49.5 2.9 %collective-permute-start.9 = (f32[136,128]{1,0:T(8,128)S(1)}, f32[136,128]{1,0:T(8,128)S(1)}, u32[]{:S(2)}, u32[]{:S(2)}) collective-permute-start(f32[136,128]{1,0:T(8,128)S(1)} %collective-permute-done.5.refs_2_), channel_id=1, source_target_pairs={{0,1},{1,0},{2,3},{3,2},{4,5},{5,4},{6,7},{7,6},{8,9},{9,8},{10,11... | collective-permute-start | bytes 208904 | tf_op jit(solution)/shard_map/ppermute | solution.py:34
  55.0 8.7 %collective-permute-start.13 = (bf16[256,384]{1,0:T(8,128)(2,1)S(1)}, bf16[256,384]{1,0:T(8,128)(2,1)S(1)}, u32[]{:S(2)}, u32[]{:S(2)}) collective-permute-start(bf16[256,384]{1,0:T(8,128)(2,1)S(1)} %get-tuple-element.37), channel_id=1, source_target_pairs={{0,2},{2,0},{1,3},{3,1},{4,6},{6,4},{5,7},{7,5},{8,10},{10,8},{9,1... | collective-permute-start | bytes 589832 | tf_op jit(solution)/shard_map/ppermute | solution.py:34
  59.4 4.3 %collective-permute-start.15 = (bf16[256,128]{1,0:T(8,128)(2,1)S(1)}, bf16[256,128]{1,0:T(8,128)(2,1)S(1)}, u32[]{:S(2)}, u32[]{:S(2)}) collective-permute-start(bf16[256,128]{1,0:T(8,128)(2,1)S(1)} %get-tuple-element.42), channel_id=1, source_target_pairs={{0,2},{2,0},{1,3},{3,1},{4,6},{6,4},{5,7},{7,5},{8,10},{10,8},{9,1... | collective-permute-start | bytes 196616 | tf_op jit(solution)/shard_map/ppermute | solution.py:34

commit v6 on v5

--- a/solution.py
+++ b/solution.py
@@ -9,7 +9,7 @@
 FBLK = 128
 SLAB = FBLK + 8
 PANEL = 8
-COPIES = 4
+ROWS = 16
 
 damping = 0.1
 
@@ -182,24 +182,25 @@
     proj, vocab_rows = table.shape
     tokens = delta.shape[0]
     each = proj // lax.axis_size("mp")
-    small = [
+    groups = tokens // FBLK
+    get_ids, get_factor, get_lengths, get_train = (
         pltpu.make_async_copy(source, target, sems.at[0, index])
         for index, (source, target) in enumerate((
             (id_rows_hbm, id_rows), (factor_hbm, factor), (lengths_hbm, lengths), (train_hbm, train),
         ))
+    )
+    get_table = [
+        pltpu.make_async_copy(table_hbm.at[rows], table.at[rows], sems.at[1, index])
+        for index in range(proj // ROWS) for rows in (pl.ds(index * ROWS, ROWS),)
     ]
-    tall, wide = tokens // COPIES, proj // COPIES
-    get_delta = [
-        pltpu.make_async_copy(delta_hbm.at[rows], delta.at[rows], sems.at[1, index])
-        for index in range(COPIES) for rows in (pl.ds(index * tall, tall),)
-    ]
-    get_table = [
-        pltpu.make_async_copy(table_hbm.at[rows], table.at[rows], sems.at[2, index])
-        for index in range(COPIES) for rows in (pl.ds(index * wide, wide),)
-    ]
-    for copy in small[:3] + get_delta + small[3:] + get_table:
+
+    def get_delta(g):
+        rows = pl.ds(pl.multiple_of(g * FBLK, FBLK), FBLK)
+        return pltpu.make_async_copy(delta_hbm.at[rows], delta.at[rows], sems.at[2, g])
+
+    for copy in (get_ids, get_lengths, get_train, *get_table, get_factor, *(get_delta(g) for g in range(groups))):
         copy.start()
-    small[0].wait()
+    get_ids.wait()
     local = id_rows[...] - model * vocab_rows
     owned = (local >= 0) & (local < vocab_rows)
     local = jnp.where(owned, local, 0)
@@ -208,43 +209,45 @@
     places[...] = (local & ~low) | roll
     fetch = pltpu.make_async_copy(places, reads, sems.at[0, 4])
     fetch.start()
-    small[1].wait()
-    for index, copy in enumerate(get_delta):
+    get_lengths.wait()
+    get_train.wait()
+    grams(lengths, train, slabs)
+    fetch.wait()
+    places[...] = owned.astype(jnp.int32)
+    for copy in get_table:
         copy.wait()
-        rows = pl.ds(index * tall, tall)
+    get_factor.wait()
+    lanes = lax.broadcasted_iota(jnp.int32, (ROWS, FBLK), 1)
+
+    def group(g, carry):
+        columns = pl.ds(pl.multiple_of(g * FBLK, FBLK), FBLK)
+        get_delta(g).wait()
         output = lax.dot_general(
-            delta[rows, :], factor[...], (((1,), (1,)), ((), ())), preferred_element_type=jnp.float32
+            delta[columns, :], factor[...], (((1,), (1,)), ((), ())), preferred_element_type=jnp.float32
         )
-        looked[:, rows] = output.T
+        looked[:, columns] = output.T
+        gathered = [jnp.zeros((ROWS, FBLK), jnp.bfloat16) for _ in range(proj // ROWS)]
+        for j in range(FBLK):
+            place = reads[g, j]
+            start, by, here = pl.multiple_of(place & ~low, FBLK), place & low, lanes == j
+            for index in range(proj // ROWS):
+                block = table[pl.ds(index * ROWS, ROWS), pl.ds(start, FBLK)]
+                gathered[index] = jnp.where(here, pltpu.roll(block, by, 1), gathered[index])
+        held = places[pl.ds(g, 1), :].astype(jnp.float32)
+        for index, value in enumerate(gathered):
+            value = (value.astype(jnp.float32) * held).astype(jnp.bfloat16)
+            rows = pl.ds(2 * each + index * ROWS, ROWS)
+            sent[rows, columns] = value
+            own[rows, columns] = value
+        return carry
+
+    lax.fori_loop(0, groups, group, 0)
     mine = looked[pl.ds(pl.multiple_of(model * each, each), each), :]
     other = looked[pl.ds(pl.multiple_of((1 - model) * each, each), each), :]
     for target, value in ((own, mine), (sent, other)):
         high, rest = halves(value)
         target[pl.ds(0, each), :] = high
         target[pl.ds(each, each), :] = rest
-    for copy in small[2:]:
-        copy.wait()
-    grams(lengths, train, slabs)
-    fetch.wait()
-    for copy in get_table:
-        copy.wait()
-    lanes = lax.broadcasted_iota(jnp.int32, (proj, FBLK), 1)
-    places[...] = owned.astype(jnp.int32)
-
-    def group(g, carry):
-        gathered = jnp.zeros((proj, FBLK), jnp.bfloat16)
-        for j in range(FBLK):
-            place = reads[g, j]
-            block = table[:, pl.ds(pl.multiple_of(place & ~low, FBLK), FBLK)]
-            gathered = jnp.where(lanes == j, pltpu.roll(block, place & low, 1), gathered)
-        held = places[pl.ds(g, 1), :].astype(jnp.float32)
-        gathered = (gathered.astype(jnp.float32) * held).astype(jnp.bfloat16)
-        columns = pl.ds(pl.multiple_of(g * FBLK, FBLK), FBLK)
-        sent[pl.ds(2 * each, proj), columns] = gathered
-        own[pl.ds(2 * each, proj), columns] = gathered
-        return carry
-
-    lax.fori_loop(0, tokens // FBLK, group, 0)
 
 
 def merge_kernel(each, own, got, out):
@@ -258,14 +261,23 @@
     out[rows, :] = own[rows, :] + got[rows, :]
 
 
-def queries_kernel(each, factors, slab, *refs):
-    after, high_out, low_out, again = refs if len(refs) == 4 else (None, *refs, None)
-    if again is not None:
-        again[...] = factors[...]
-    tokens = factors.shape[1]
-    proj = factors.shape[0] - 2 * each
+def queries_kernel(each, source_of, choose, count, *refs):
+    factor_refs, slabs, (high_out, low_out) = refs[:count], refs[count:count + 4], refs[-2:]
+    mine = lax.axis_index("dp")
+    tokens = factor_refs[0].shape[1]
+    proj = factor_refs[0].shape[0] - 2 * each
     queries = high_out.shape[1]
-    lengths = slab[pl.ds(FBLK + 1, 1), :]
+
+    def part(rows):
+        value = factor_refs[0][rows, :].astype(jnp.float32)
+        if count == 2:
+            value = jnp.where(choose(mine), factor_refs[1][rows, :].astype(jnp.float32), value)
+        return value
+
+    shift = lax.rem(mine + len(slabs) - source_of(mine), len(slabs))
+    lengths = slabs[0][pl.ds(FBLK + 1, 1), :]
+    for index in range(1, len(slabs)):
+        lengths = jnp.where(shift == index, slabs[index][pl.ds(FBLK + 1, 1), :], lengths)
     upto = jnp.where(square(0) <= square(1), 1.0, 0.0).astype(jnp.bfloat16)
     ends = lax.dot_general(
         jnp.broadcast_to(lengths, (8, queries)).astype(jnp.bfloat16), upto, (((1,), (0,)), ((), ())),
@@ -274,8 +286,8 @@
     starts = ends - lengths
     place = lax.broadcasted_iota(jnp.int32, (tokens, queries), 0).astype(jnp.float32)
     inside = jnp.where((place >= starts) & (place < ends), 1.0, 0.0).astype(jnp.bfloat16)
-    output = factors[pl.ds(0, each), :].astype(jnp.float32) + factors[pl.ds(each, each), :].astype(jnp.float32)
-    inputs = factors[pl.ds(2 * each, proj), :].astype(jnp.float32)
+    output = part(pl.ds(0, each)) + part(pl.ds(each, each))
+    inputs = part(pl.ds(2 * each, proj))
     step = 8
     for start in range(0, each, step):
         grads = jnp.concatenate(
@@ -314,20 +326,18 @@
         out[...] = jnp.dot(train[rows, :], pre[...], preferred_element_type=jnp.float32).astype(jnp.bfloat16)
 
 
-def total_kernel(order, *refs):
+def total_kernel(sources, *refs):
     pieces, out = refs[:-1], refs[-1]
-    mine, cycle = lax.axis_index("dp"), len(order)
-    sums = {}
+    mine = lax.axis_index("dp")
+    sums = []
     for kept, got in zip(pieces[::2], pieces[1::2]):
         both = kept[...].astype(jnp.float32) + got[...].astype(jnp.float32)
-        for index in range(both.shape[1] // FBLK):
-            sums[order[len(sums)]] = both[:, index * FBLK:(index + 1) * FBLK]
+        sums += [both[:, start:start + FBLK] for start in range(0, both.shape[1], FBLK)]
     placed = []
-    for source in range(cycle):
-        shift = lax.rem(mine + cycle - source, cycle)
+    for source in range(len(sums)):
         value = sums[0]
-        for index in range(1, cycle):
-            value = jnp.where(shift == index, sums[index], value)
+        for index in range(1, len(sums)):
+            value = jnp.where(sources[index](mine) == source, sums[index], value)
         placed.append(value)
     out[...] = jnp.stack(placed, axis=1).astype(jnp.bfloat16)
 
@@ -380,8 +390,18 @@
         flops=tokens * each,
         moved=8 * tokens * each * 4,
     )(own, got)
-    late = cycle // 2
-    gathered = [factors] + [passed_along(factors, "dp", s) if s != late else None for s in range(1, cycle)]
+    last = cycle - 1
+    from_two = passed_along(factors, "dp", 2)
+    from_below = lax.ppermute(factors, "dp", [(i, i + 1) for i in range(last)])
+    from_above = lax.ppermute(factors, "dp", [(i + 1, i) for i in range(last)])
+    from_far = lax.ppermute(from_two, "dp", [(1, 0), (last - 1, last)])
+    sources = (
+        (lambda d: d, None, (factors,)),
+        (lambda d: jnp.where(d == 0, 1, d - 1), lambda d: d == 0, (from_below, from_above)),
+        (lambda d: lax.rem(d + 2, cycle), None, (from_two,)),
+        (lambda d: jnp.where(d == 0, last, jnp.where(d == last, 0, d + 1)), lambda d: (d == 0) | (d == last),
+         (from_above, from_far)),
+    )
 
     inverse = call(
         functools.partial(factor_kernel, train_rows * cycle, 1.0 / proj),
@@ -394,24 +414,24 @@
     inverses = [inverse] + [passed_along(inverse, "dp", s) for s in range(1, cycle)]
     peers = [passed_along(slab, "rep", 1) for slab in inverses]
 
-    highs, lows = {}, {}
-    for s in sorted(range(cycle), key=lambda shift: (shift == late, shift)):
-        first = s == 0
-        highs[s], lows[s], *again = call(
-            functools.partial(queries_kernel, each),
-            [shape((feat, queries), bf16)] * 2 + [shape(factors.shape, bf16)] * first,
-            [VMEM, VMEM] + [HBM] * first,
+    highs, lows = [], []
+    for index, (source_of, choose, arrays) in enumerate(sources):
+        before = [inverse] if index == 0 else []
+        high, low = call(
+            functools.partial(queries_kernel, each, source_of, choose, len(arrays)),
+            [shape((feat, queries), bf16)] * 2,
+            [VMEM] * (len(arrays) + cycle) + [HBM] * len(before),
             vmem=24,
             flops=2 * feat * tokens * queries,
             moved=6 * feat * queries,
-        )(gathered[s], parts[s], *[inverse] * first)
-        if first:
-            gathered[late] = passed_along(again[0], "dp", late)
+        )(*arrays, *parts, *before)
+        highs.append(high)
+        lows.append(low)
 
     half_rows = train_rows // lax.axis_size("mp")
-    pieces, order = [], []
-    for chosen in ([s for s in range(cycle) if s != late], [late]):
-        count = len(chosen)
+    pieces = []
+    for chosen in (slice(0, last), slice(last, cycle)):
+        count = len(highs[chosen])
         outgoing, kept = call(
             functools.partial(scores_kernel, cycle, count),
             [shape((half_rows, count * queries), bf16)] * 2,
@@ -420,11 +440,10 @@
             vmem=24,
             flops=2 * train_rows * feat * count * queries,
             moved=8 * feat * queries * count,
-        )(*inverses, *peers, *[highs[s] for s in chosen], *[lows[s] for s in chosen], train_grads)
+        )(*inverses, *peers, *highs[chosen], *lows[chosen], train_grads)
         pieces += [kept, passed_along(outgoing, "mp", 1)]
-        order += chosen
     total = call(
-        functools.partial(total_kernel, order),
+        functools.partial(total_kernel, [source_of for source_of, _, _ in sources]),
         shape((half_rows, cycle, queries), bf16),
         [VMEM] * len(pieces),
         vmem=16,
@@ -495,6 +514,7 @@
     owners = lax.axis_size("dp") * lax.axis_size("rep")
     fits = (
         train_grads.shape[1] == 2 * FBLK * owners
+        and lax.axis_size("dp") == 4
         and lax.axis_size("mp") == 2
         and lax.axis_size("rep") == 2
         and doc_lengths.shape[1] == FBLK

time: 65.2 us -> 66 us (1.012)
  starting transfers between devices: 20.3 us -> 29.2 us
  waiting for transfers between devices: 13.6 us -> 5.99 us
    ppermute x16 -> x14, waiting for transfers between devices: 13.6 us -> 5.98 us  [passed_along(): lax.ppermute(shard, axis, [(i, (i + by) % size) for i in range(size)])]
    ppermute x0 -> x3, starting transfers between devices: none -> 7.3 us  [the longest x1 4.56 us: split_over_blocks(): from_below = lax.ppermute(factors, 'dp', [(i, i + 1) for i in range(last)])]
    ppermute x16 -> x14, starting transfers between devices: 20.3 us -> 21.9 us  [passed_along(): lax.ppermute(shard, axis, [(i, (i + by) % size) for i in range(size)])]
    unnamed x6 -> x8, local copies, waits for them, and re-layouts: 1.83 us -> 1.84 us
  transfers between devices with their start and end apart: 16 -> 17, of which waited for: 4 -> 4; matrix products, arithmetic and copies ran while one was open for 0% -> 0% of each run, Pallas kernels for 25% -> 25%
where the time goes in v6:
time: 66 us; the launch traced here: 65.7 us
  starting transfers between devices  29.2 us (44%)
  Pallas kernels  28.5 us (43%)
  waiting for transfers between devices  5.99 us (9%)
  local copies, waits for them, and re-layouts  1.84 us (3%)
    ppermute x14, starting transfers between devices, passed_along(): lax.ppermute(shard, axis, [(i, (i + by) % size) for i in range(size)])  21.9 us
    pallas_call x1, Pallas kernels, split_over_blocks(): call(first_kernel, [shape((2 * each + proj, tokens), bf16)] * 2 + [shape(...  11.1 us
    pallas_call x1, Pallas kernels, split_over_blocks(): call(functools.partial(factor_kernel, train_rows * cycle, 1.0 / proj), sh...  6.57 us
    ppermute x14, waiting for transfers between devices, passed_along(): lax.ppermute(shard, axis, [(i, (i + by) % size) for i in range(size)])  5.98 us
    pallas_call x4, Pallas kernels, split_over_blocks(): call(functools.partial(queries_kernel, each, source_of, choose, len(array...  5.65 us
    ppermute x1, starting transfers between devices, split_over_blocks(): from_below = lax.ppermute(factors, 'dp', [(i, i + 1) for i in range(last)])  4.56 us
    pallas_call x2, Pallas kernels, split_over_blocks(): call(functools.partial(scores_kernel, cycle, count), [shape((half_rows, c...  3.91 us
    unnamed x8, local copies, waits for them, and re-layouts  1.84 us
  transfers between devices with their start and end apart: 17, of which 4 were waited for; matrix products, arithmetic and copies ran while one was open for 0% of the time, Pallas kernels for 25%

profile of v6, /device:TPU:0, one launch (start us, length us, event | category | flops | bytes accessed | tf_op | source)
XLA Modules:
  0.0 65.7 jit_solution(12450453616787301380)
XLA Ops:
  0.0 11.1 %shard_map.64 = (bf16[128,1024]{1,0:T(8,128)(2,1)}, bf16[128,1024]{1,0:T(8,128)(2,1)}, f32[136,128]{1,0:T(8,128)}, f32[136,128]{1,0:T(8,128)}, f32[136,128]{1,0:T(8,128)}, /*index=5*/f32[136,128]{1,0:T(8,128)}) custom-call(s32[8,128]{1,0:T(8,128)} %bitcast.8, bf16[1024,2048]{1,0:T(8,128)(2,1)} %delta_hbm.1, bf16[64,64128]{1,0:T(8,128)(2,1)} %bitcast.6, ...), custom_call_target="tpu_custom_call" | custom-call | flops 268435456 | bytes 24805376 | tf_op jit(solution)/shard_map/pallas_call | solution.py:359
  11.1 3.0 %collective-permute-start.3 = (bf16[128,1024]{1,0:T(8,128)(2,1)}, bf16[128,1024]{1,0:T(8,128)(2,1)S(1)}, u32[]{:S(2)}, u32[]{:S(2)}) collective-permute-start(bf16[128,1024]{1,0:T(8,128)(2,1)} %get-tuple-element.28), channel_id=1, source_target_pairs={{0,2},{2,0},{1,3},{3,1},{4,6},{6,4},{5,7},{7,5},{8,10},{10,8},{9,1... | collective-permute-start | bytes 786440 | tf_op jit(solution)/shard_map/ppermute | solution.py:34
  14.1 1.6 %collective-permute-start = (f32[136,128]{1,0:T(8,128)}, f32[136,128]{1,0:T(8,128)S(1)}, u32[]{:S(2)}, u32[]{:S(2)}) collective-permute-start(f32[136,128]{1,0:T(8,128)} %get-tuple-element.24), channel_id=1, source_target_pairs={{0,4},{4,8},{8,12},{12,0},{1,5},{5,9},{9,13},{13,1},{2,6},{6,10},{... | collective-permute-start | bytes 208904 | tf_op jit(solution)/shard_map/ppermute | solution.py:34
  15.7 2.6 %collective-permute-start.1 = (f32[136,128]{1,0:T(8,128)}, f32[136,128]{1,0:T(8,128)S(1)}, u32[]{:S(2)}, u32[]{:S(2)}) collective-permute-start(f32[136,128]{1,0:T(8,128)} %get-tuple-element.25), channel_id=1, source_target_pairs={{0,8},{4,12},{8,0},{12,4},{1,9},{5,13},{9,1},{13,5},{2,10},{6,14},... | collective-permute-start | bytes 208904 | tf_op jit(solution)/shard_map/ppermute | solution.py:34
  18.3 1.3 %collective-permute-start.2 = (f32[136,128]{1,0:T(8,128)}, f32[136,128]{1,0:T(8,128)S(1)}, u32[]{:S(2)}, u32[]{:S(2)}) collective-permute-start(f32[136,128]{1,0:T(8,128)} %get-tuple-element.26), channel_id=1, source_target_pairs={{0,12},{4,0},{8,4},{12,8},{1,13},{5,1},{9,5},{13,9},{2,14},{6,2},{... | collective-permute-start | bytes 208904 | tf_op jit(solution)/shard_map/ppermute | solution.py:34
  19.6 1.0 %collective-permute-done.3.got = bf16[128,1024]{1,0:T(8,128)(2,1)S(1)} collective-permute-done((bf16[128,1024]{1,0:T(8,128)(2,1)}, bf16[128,1024]{1,0:T(8,128)(2,1)S(1)}, u32[]{:S(2)}, u32[]{:S(2)}) %collective-permute-start.3) | collective-permute-done | bytes 262176 | tf_op jit(solution)/shard_map/ppermute | solution.py:34
  20.6 0.9 %copy-done.1 = bf16[128,1024]{1,0:T(8,128)(2,1)S(1)} copy-done((bf16[128,1024]{1,0:T(8,128)(2,1)S(1)}, bf16[128,1024]{1,0:T(8,128)(2,1)}, u32[]{:S(2)}) %copy-start.1) | copy-done | bytes 262168
  21.6 0.1 shard_map.65.refs_4_.refs_0_
  21.6 2.9 %collective-permute-start.13 = (bf16[128,1024]{1,0:T(8,128)(2,1)S(1)}, bf16[128,1024]{1,0:T(8,128)(2,1)S(1)}, u32[]{:S(2)}, u32[]{:S(2)}) collective-permute-start(bf16[128,1024]{1,0:T(8,128)(2,1)S(1)} %shard_map.65.refs_4_.refs_0_), channel_id=1, source_target_pairs={{0,8},{4,12},{8,0},{12,4},{1,9},{5,13},{9,1},{13,5},{2,10},{6,14},... | collective-permute-start | bytes 786440 | tf_op jit(solution)/shard_map/ppermute | solution.py:34
  24.5 1.3 %collective-permute-start.12 = (bf16[128,1024]{1,0:T(8,128)(2,1)S(1)}, bf16[128,1024]{1,0:T(8,128)(2,1)S(1)}, u32[]{:S(2)}, u32[]{:S(2)}) collective-permute-start(bf16[128,1024]{1,0:T(8,128)(2,1)S(1)} %shard_map.65.refs_4_.refs_0_), channel_id=1, source_target_pairs={{4,0},{8,4},{12,8},{5,1},{9,5},{13,9},{6,2},{10,6},{14,10},{7,3},{... | collective-permute-start | bytes 786440 | tf_op jit(solution)/shard_map/ppermute | solution.py:396
  25.8 0.0 collective-permute-done.refs_1_.refs_2_.refs_3_
  25.8 4.6 %collective-permute-start.11 = (bf16[128,1024]{1,0:T(8,128)(2,1)S(1)}, bf16[128,1024]{1,0:T(8,128)(2,1)S(1)}, u32[]{:S(2)}, u32[]{:S(2)}) collective-permute-start(bf16[128,1024]{1,0:T(8,128)(2,1)S(1)} %shard_map.65.refs_4_.refs_0_), channel_id=1, source_target_pairs={{0,4},{4,8},{8,12},{1,5},{5,9},{9,13},{2,6},{6,10},{10,14},{3,7},{... | collective-permute-start | bytes 786440 | tf_op jit(solution)/shard_map/ppermute | solution.py:395
  30.4 0.0 collective-permute-done.1.refs_2_.refs_3_.refs_4_
  30.4 0.0 collective-permute-done.2.refs_3_.refs_4_.refs_5_
  30.4 0.0 copy-start.2
  30.4 0.9 %copy-done.2 = f32[136,128]{1,0:T(8,128)S(1)} copy-done((f32[136,128]{1,0:T(8,128)S(1)}, f32[136,128]{1,0:T(8,128)}, u32[]{:S(2)}) %copy-start.2) | copy-done | bytes 69656
  31.3 6.6 %shard_map.66.refs_5_.refs_0_ = f32[136,128]{1,0:T(8,128)S(1)} custom-call(f32[136,128]{1,0:T(8,128)S(1)} %copy-done.2, f32[136,128]{1,0:T(8,128)S(1)} %collective-permute-done.refs_1_.refs_2_.refs_3_, f32[136,128]{1,0:T(8,128)S(1)} %collective-permute-done.1.refs_2_.refs_3_.refs_4_, f32[136,128]{1,0:T(8,128)S(1)} %collective-permute-done.2.refs_3_.refs_4_.refs_5_, ...), custom_call_target="tpu_custom_call" | custom-call | flops 10000000000 | bytes 1000000 | tf_op jit(solution)/shard_map/pallas_call | solution.py:406
  37.9 0.0 copy-start
  37.9 0.1 collective-permute-start.6
  37.9 3.0 %collective-permute-start.5 = (f32[136,128]{1,0:T(8,128)S(1)}, f32[136,128]{1,0:T(8,128)S(1)}, u32[]{:S(2)}, u32[]{:S(2)}) collective-permute-start(f32[136,128]{1,0:T(8,128)S(1)} %shard_map.66.refs_5_.refs_0_), channel_id=1, source_target_pairs={{0,8},{4,12},{8,0},{12,4},{1,9},{5,13},{9,1},{13,5},{2,10},{6,14},... | collective-permute-start | bytes 208904 | tf_op jit(solution)/shard_map/ppermute | solution.py:34
  40.9 1.3 %collective-permute-done.6.refs_3_ = f32[136,128]{1,0:T(8,128)S(1)} collective-permute-done((f32[136,128]{1,0:T(8,128)S(1)}, f32[136,128]{1,0:T(8,128)S(1)}, u32[]{:S(2)}, u32[]{:S(2)}) %collective-permute-start.6) | collective-permute-done | bytes 69664 | tf_op jit(solution)/shard_map/ppermute | solution.py:34
  42.2 4.2 %collective-permute-start.4 = (f32[136,128]{1,0:T(8,128)S(1)}, f32[136,128]{1,0:T(8,128)S(1)}, u32[]{:S(2)}, u32[]{:S(2)}) collective-permute-start(f32[136,128]{1,0:T(8,128)S(1)} %shard_map.66.refs_5_.refs_0_), channel_id=1, source_target_pairs={{0,4},{4,8},{8,12},{12,0},{1,5},{5,9},{9,13},{13,1},{2,6},{6,10},{... | collective-permute-start | bytes 208904 | tf_op jit(solution)/shard_map/ppermute | solution.py:34
  46.4 0.0 collective-permute-done.13.refs_0_
  46.4 1.5 %collective-permute-start.15 = (bf16[128,1024]{1,0:T(8,128)(2,1)S(1)}, bf16[128,1024]{1,0:T(8,128)(2,1)S(1)}, u32[]{:S(2)}, u32[]{:S(2)}) collective-permute-start(bf16[128,1024]{1,0:T(8,128)(2,1)S(1)} %collective-permute-done.13.refs_0_), channel_id=1, source_target_pairs={{4,0},{8,12},{5,1},{9,13},{6,2},{10,14},{7,3},{11,15},{20,16},{24,... | collective-permute-start | bytes 786440 | tf_op jit(solution)/shard_map/ppermute | solution.py:397
  47.9 1.4 %shard_map.67 = (bf16[2048,128]{1,0:T(8,128)(2,1)S(1)}, bf16[2048,128]{1,0:T(8,128)(2,1)S(1)}) custom-call(bf16[128,1024]{1,0:T(8,128)(2,1)S(1)} %shard_map.65.refs_4_.refs_0_, f32[136,128]{1,0:T(8,128)S(1)} %copy-done.3, f32[136,128]{1,0:T(8,128)S(1)} %collective-permute-done.refs_1_.refs_2_.refs_3_, ...), custom_call_target="tpu_custom_call" | custom-call | flops 536870912 | bytes 1572864 | tf_op jit(solution)/shard_map/pallas_call | solution.py:420
  49.3 0.0 collective-permute-done.5.refs_2_
  49.3 0.1 collective-permute-start.7
  49.4 0.0 collective-permute-done.4.refs_1_
  49.4 0.5 collective-permute-start.10
  49.9 0.0 collective-permute-done.12.refs_1_.refs_0_
  49.9 0.1 collective-permute-start.9
  50.0 0.0 collective-permute-done.11.refs_0_
  50.0 0.4 collective-permute-start.8
  50.4 1.4 %shard_map.69 = (bf16[2048,128]{1,0:T(8,128)(2,1)S(1)}, bf16[2048,128]{1,0:T(8,128)(2,1)S(1)}) custom-call(bf16[128,1024]{1,0:T(8,128)(2,1)S(1)} %collective-permute-done.13.refs_0_, f32[136,128]{1,0:T(8,128)S(1)} %copy-done.3, f32[136,128]{1,0:T(8,128)S(1)} %collective-permute-done.refs_1_.refs_2_.refs_3_, ...), custom_call_target="tpu_custom_call" | custom-call | flops 536870912 | bytes 1572864 | tf_op jit(solution)/shard_map/pallas_call | solution.py:420
  51.8 1.4 %shard_map.68 = (bf16[2048,128]{1,0:T(8,128)(2,1)S(1)}, bf16[2048,128]{1,0:T(8,128)(2,1)S(1)}) custom-call(bf16[128,1024]{1,0:T(8,128)(2,1)S(1)} %collective-permute-done.11.refs_0_, bf16[128,1024]{1,0:T(8,128)(2,1)S(1)} %collective-permute-done.12.refs_1_.refs_0_, f32[136,128]{1,0:T(8,128)S(1)} %copy-done.3, ...), custom_call_target="tpu_custom_call" | custom-call | flops 536870912 | bytes 1572864 | tf_op jit(solution)/shard_map/pallas_call | solution.py:420
  53.2 0.0 collective-permute-done.7.refs_4_
  53.3 0.0 collective-permute-done.10.refs_7_
  53.3 0.0 collective-permute-done.9.refs_6_
  53.3 0.0 collective-permute-done.8.refs_5_
  53.3 2.6 %shard_map.70 = (bf16[256,384]{1,0:T(8,128)(2,1)S(1)}, bf16[256,384]{1,0:T(8,128)(2,1)S(1)}) custom-call(f32[136,128]{1,0:T(8,128)S(1)} %shard_map.66.refs_5_.refs_0_, f32[136,128]{1,0:T(8,128)S(1)} %collective-permute-done.4.refs_1_, f32[136,128]{1,0:T(8,128)S(1)} %collective-permute-done.5.refs_2_, f32[136,128]{1,0:T(8,128)S(1)} %collective-permute-done.6.refs_3_, ...), custom_call_target="tpu_custom_call" | custom-call | flops 805306368 | bytes 6291456 | tf_op jit(solution)/shard_map/pallas_call | solution.py:435
  55.9 1.5 %collective-permute-start.14 = (bf16[256,384]{1,0:T(8,128)(2,1)S(1)}, bf16[256,384]{1,0:T(8,128)(2,1)S(1)}, u32[]{:S(2)}, u32[]{:S(2)}) collective-permute-start(bf16[256,384]{1,0:T(8,128)(2,1)S(1)} %get-tuple-element.36), channel_id=1, source_target_pairs={{0,2},{2,0},{1,3},{3,1},{4,6},{6,4},{5,7},{7,5},{8,10},{10,8},{9,1... | collective-permute-start | bytes 589832 | tf_op jit(solution)/shard_map/ppermute | solution.py:34
  57.4 0.0 collective-permute-done.15.refs_1_
  57.4 1.4 %shard_map.71 = (bf16[2048,128]{1,0:T(8,128)(2,1)S(1)}, bf16[2048,128]{1,0:T(8,128)(2,1)S(1)}) custom-call(bf16[128,1024]{1,0:T(8,128)(2,1)S(1)} %collective-permute-done.12.refs_1_.refs_0_, bf16[128,1024]{1,0:T(8,128)(2,1)S(1)} %collective-permute-done.15.refs_1_, f32[136,128]{1,0:T(8,128)S(1)} %copy-done.3, ...), custom_call_target="tpu_custom_call" | custom-call | flops 536870912 | bytes 1572864 | tf_op jit(solution)/shard_map/pallas_call | solution.py:420
  58.8 1.3 %shard_map.72 = (bf16[256,128]{1,0:T(8,128)(2,1)S(1)}, bf16[256,128]{1,0:T(8,128)(2,1)S(1)}) custom-call(f32[136,128]{1,0:T(8,128)S(1)} %shard_map.66.refs_5_.refs_0_, f32[136,128]{1,0:T(8,128)S(1)} %collective-permute-done.4.refs_1_, f32[136,128]{1,0:T(8,128)S(1)} %collective-permute-done.5.refs_2_, f32[136,128]{1,0:T(8,128)S(1)} %collective-permute-done.6.refs_3_, ...), custom_call_target="tpu_custom_call" | custom-call | flops 268435456 | bytes 2097152 | tf_op jit(solution)/shard_map/pallas_call | solution.py:435
  60.1 0.7 %collective-permute-start.16 = (bf16[256,128]{1,0:T(8,128)(2,1)S(1)}, bf16[256,128]{1,0:T(8,128)(2,1)S(1)}, u32[]{:S(2)}, u32[]{:S(2)}) collective-permute-start(bf16[256,128]{1,0:T(8,128)(2,1)S(1)} %get-tuple-element.40), channel_id=1, source_target_pairs={{0,2},{2,0},{1,3},{3,1},{4,6},{6,4},{5,7},{7,5},{8,10},{10,8},{9,1... | collective-permute-start | bytes 196616 | tf_op jit(solution)/shard_map/ppermute | solution.py:34
  60.8 2.2 %collective-permute-done.14.refs_1_ = bf16[256,384]{1,0:T(8,128)(2,1)S(1)} collective-permute-done((bf16[256,384]{1,0:T(8,128)(2,1)S(1)}, bf16[256,384]{1,0:T(8,128)(2,1)S(1)}, u32[]{:S(2)}, u32[]{:S(2)}) %collective-permute-start.14) | collective-permute-done | bytes 196640 | tf_op jit(solution)/shard_map/ppermute | solution.py:34
  63.0 1.5 %collective-permute-done.16.refs_3_ = bf16[256,128]{1,0:T(8,128)(2,1)S(1)} collective-permute-done((bf16[256,128]{1,0:T(8,128)(2,1)S(1)}, bf16[256,128]{1,0:T(8,128)(2,1)S(1)}, u32[]{:S(2)}, u32[]{:S(2)}) %collective-permute-start.16) | collective-permute-done | bytes 65568 | tf_op jit(solution)/shard_map/ppermute | solution.py:34
  64.5 1.3 %shard_map.73 = bf16[256,4,128]{2,1,0:T(4,128)(2,1)} custom-call(bf16[256,384]{1,0:T(8,128)(2,1)S(1)} %get-tuple-element.35.refs_0_, bf16[256,384]{1,0:T(8,128)(2,1)S(1)} %collective-permute-done.14.refs_1_, bf16[256,128]{1,0:T(8,128)(2,1)S(1)} %get-tuple-element.39.refs_2_, bf16[256,128]{1,0:T(8,128)(2,1)S(1)} %collective-permute-done.16.refs_3_), custom_call_target="tpu_custom_call" | custom-call | flops 131072 | bytes 786432 | tf_op jit(solution)/shard_map/pallas_call | solution.py:445
  (4 shorter events, 0.0 us)
Async XLA Ops:
  11.1 9.5 %collective-permute-start.3 = (bf16[128,1024]{1,0:T(8,128)(2,1)}, bf16[128,1024]{1,0:T(8,128)(2,1)S(1)}, u32[]{:S(2)}, u32[]{:S(2)}) collective-permute-start(bf16[128,1024]{1,0:T(8,128)(2,1)} %get-tuple-element.28), channel_id=1, source_target_pairs={{0,2},{2,0},{1,3},{3,1},{4,6},{6,4},{5,7},{7,5},{8,10},{10,8},{9,1... | collective-permute-start | bytes 786440 | tf_op jit(solution)/shard_map/ppermute | solution.py:34
  14.1 11.7 %collective-permute-start = (f32[136,128]{1,0:T(8,128)}, f32[136,128]{1,0:T(8,128)S(1)}, u32[]{:S(2)}, u32[]{:S(2)}) collective-permute-start(f32[136,128]{1,0:T(8,128)} %get-tuple-element.24), channel_id=1, source_target_pairs={{0,4},{4,8},{8,12},{12,0},{1,5},{5,9},{9,13},{13,1},{2,6},{6,10},{... | collective-permute-start | bytes 208904 | tf_op jit(solution)/shard_map/ppermute | solution.py:34
  15.7 14.7 %collective-permute-start.1 = (f32[136,128]{1,0:T(8,128)}, f32[136,128]{1,0:T(8,128)S(1)}, u32[]{:S(2)}, u32[]{:S(2)}) collective-permute-start(f32[136,128]{1,0:T(8,128)} %get-tuple-element.25), channel_id=1, source_target_pairs={{0,8},{4,12},{8,0},{12,4},{1,9},{5,13},{9,1},{13,5},{2,10},{6,14},... | collective-permute-start | bytes 208904 | tf_op jit(solution)/shard_map/ppermute | solution.py:34
  18.3 12.1 %collective-permute-start.2 = (f32[136,128]{1,0:T(8,128)}, f32[136,128]{1,0:T(8,128)S(1)}, u32[]{:S(2)}, u32[]{:S(2)}) collective-permute-start(f32[136,128]{1,0:T(8,128)} %get-tuple-element.26), channel_id=1, source_target_pairs={{0,12},{4,0},{8,4},{12,8},{1,13},{5,1},{9,5},{13,9},{2,14},{6,2},{... | collective-permute-start | bytes 208904 | tf_op jit(solution)/shard_map/ppermute | solution.py:34
  20.6 1.0 %copy-start.1 = (bf16[128,1024]{1,0:T(8,128)(2,1)S(1)}, bf16[128,1024]{1,0:T(8,128)(2,1)}, u32[]{:S(2)}) copy-start(bf16[128,1024]{1,0:T(8,128)(2,1)} %get-tuple-element.27.own) | copy-start | bytes 786436
  21.6 24.8 %collective-permute-start.13 = (bf16[128,1024]{1,0:T(8,128)(2,1)S(1)}, bf16[128,1024]{1,0:T(8,128)(2,1)S(1)}, u32[]{:S(2)}, u32[]{:S(2)}) collective-permute-start(bf16[128,1024]{1,0:T(8,128)(2,1)S(1)} %shard_map.65.refs_4_.refs_0_), channel_id=1, source_target_pairs={{0,8},{4,12},{8,0},{12,4},{1,9},{5,13},{9,1},{13,5},{2,10},{6,14},... | collective-permute-start | bytes 786440 | tf_op jit(solution)/shard_map/ppermute | solution.py:34
  24.5 25.4 %collective-permute-start.12 = (bf16[128,1024]{1,0:T(8,128)(2,1)S(1)}, bf16[128,1024]{1,0:T(8,128)(2,1)S(1)}, u32[]{:S(2)}, u32[]{:S(2)}) collective-permute-start(bf16[128,1024]{1,0:T(8,128)(2,1)S(1)} %shard_map.65.refs_4_.refs_0_), channel_id=1, source_target_pairs={{4,0},{8,4},{12,8},{5,1},{9,5},{13,9},{6,2},{10,6},{14,10},{7,3},{... | collective-permute-start | bytes 786440 | tf_op jit(solution)/shard_map/ppermute | solution.py:396
  25.8 24.2 %collective-permute-start.11 = (bf16[128,1024]{1,0:T(8,128)(2,1)S(1)}, bf16[128,1024]{1,0:T(8,128)(2,1)S(1)}, u32[]{:S(2)}, u32[]{:S(2)}) collective-permute-start(bf16[128,1024]{1,0:T(8,128)(2,1)S(1)} %shard_map.65.refs_4_.refs_0_), channel_id=1, source_target_pairs={{0,4},{4,8},{8,12},{1,5},{5,9},{9,13},{2,6},{6,10},{10,14},{3,7},{... | collective-permute-start | bytes 786440 | tf_op jit(solution)/shard_map/ppermute | solution.py:395
  30.4 0.9 %copy-start.2 = (f32[136,128]{1,0:T(8,128)S(1)}, f32[136,128]{1,0:T(8,128)}, u32[]{:S(2)}) copy-start(f32[136,128]{1,0:T(8,128)} %get-tuple-element.23.refs_0_.refs_1_.refs_2_) | copy-start | bytes 208900
  31.3 16.6 %copy-start.3 = (f32[136,128]{1,0:T(8,128)S(1)}, f32[136,128]{1,0:T(8,128)}, u32[]{:S(2)}) copy-start(f32[136,128]{1,0:T(8,128)} %get-tuple-element.23.refs_0_.refs_1_.refs_2_) | copy-start | bytes 208900
  37.9 15.4 %copy-start = (bf16[512,2048]{1,0:T(8,128)(2,1)S(1)}, bf16[512,2048]{1,0:T(8,128)(2,1)}, u32[]{:S(2)}) copy-start(bf16[512,2048]{1,0:T(8,128)(2,1)} %refs_10_.1) | copy-start | bytes 6291460
  37.9 4.4 %collective-permute-start.6 = (f32[136,128]{1,0:T(8,128)S(1)}, f32[136,128]{1,0:T(8,128)S(1)}, u32[]{:S(2)}, u32[]{:S(2)}) collective-permute-start(f32[136,128]{1,0:T(8,128)S(1)} %shard_map.66.refs_5_.refs_0_), channel_id=1, source_target_pairs={{0,12},{4,0},{8,4},{12,8},{1,13},{5,1},{9,5},{13,9},{2,14},{6,2},{... | collective-permute-start | bytes 208904 | tf_op jit(solution)/shard_map/ppermute | solution.py:34
  37.9 11.4 %collective-permute-start.5 = (f32[136,128]{1,0:T(8,128)S(1)}, f32[136,128]{1,0:T(8,128)S(1)}, u32[]{:S(2)}, u32[]{:S(2)}) collective-permute-start(f32[136,128]{1,0:T(8,128)S(1)} %shard_map.66.refs_5_.refs_0_), channel_id=1, source_target_pairs={{0,8},{4,12},{8,0},{12,4},{1,9},{5,13},{9,1},{13,5},{2,10},{6,14},... | collective-permute-start | bytes 208904 | tf_op jit(solution)/shard_map/ppermute | solution.py:34
  42.2 7.1 %collective-permute-start.4 = (f32[136,128]{1,0:T(8,128)S(1)}, f32[136,128]{1,0:T(8,128)S(1)}, u32[]{:S(2)}, u32[]{:S(2)}) collective-permute-start(f32[136,128]{1,0:T(8,128)S(1)} %shard_map.66.refs_5_.refs_0_), channel_id=1, source_target_pairs={{0,4},{4,8},{8,12},{12,0},{1,5},{5,9},{9,13},{13,1},{2,6},{6,10},{... | collective-permute-start | bytes 208904 | tf_op jit(solution)/shard_map/ppermute | solution.py:34
  46.4 11.0 %collective-permute-start.15 = (bf16[128,1024]{1,0:T(8,128)(2,1)S(1)}, bf16[128,1024]{1,0:T(8,128)(2,1)S(1)}, u32[]{:S(2)}, u32[]{:S(2)}) collective-permute-start(bf16[128,1024]{1,0:T(8,128)(2,1)S(1)} %collective-permute-done.13.refs_0_), channel_id=1, source_target_pairs={{4,0},{8,12},{5,1},{9,13},{6,2},{10,14},{7,3},{11,15},{20,16},{24,... | collective-permute-start | bytes 786440 | tf_op jit(solution)/shard_map/ppermute | solution.py:397
  49.3 3.9 %collective-permute-start.7 = (f32[136,128]{1,0:T(8,128)S(1)}, f32[136,128]{1,0:T(8,128)S(1)}, u32[]{:S(2)}, u32[]{:S(2)}) collective-permute-start(f32[136,128]{1,0:T(8,128)S(1)} %shard_map.66.refs_5_.refs_0_), channel_id=1, source_target_pairs={{0,1},{1,0},{2,3},{3,2},{4,5},{5,4},{6,7},{7,6},{8,9},{9,8},{10,11... | collective-permute-start | bytes 208904 | tf_op jit(solution)/shard_map/ppermute | solution.py:34
  49.4 3.9 %collective-permute-start.10 = (f32[136,128]{1,0:T(8,128)S(1)}, f32[136,128]{1,0:T(8,128)S(1)}, u32[]{:S(2)}, u32[]{:S(2)}) collective-permute-start(f32[136,128]{1,0:T(8,128)S(1)} %collective-permute-done.6.refs_3_), channel_id=1, source_target_pairs={{0,1},{1,0},{2,3},{3,2},{4,5},{5,4},{6,7},{7,6},{8,9},{9,8},{10,11... | collective-permute-start | bytes 208904 | tf_op jit(solution)/shard_map/ppermute | solution.py:34
  49.9 3.4 %collective-permute-start.9 = (f32[136,128]{1,0:T(8,128)S(1)}, f32[136,128]{1,0:T(8,128)S(1)}, u32[]{:S(2)}, u32[]{:S(2)}) collective-permute-start(f32[136,128]{1,0:T(8,128)S(1)} %collective-permute-done.5.refs_2_), channel_id=1, source_target_pairs={{0,1},{1,0},{2,3},{3,2},{4,5},{5,4},{6,7},{7,6},{8,9},{9,8},{10,11... | collective-permute-start | bytes 208904 | tf_op jit(solution)/shard_map/ppermute | solution.py:34
  50.0 3.3 %collective-permute-start.8 = (f32[136,128]{1,0:T(8,128)S(1)}, f32[136,128]{1,0:T(8,128)S(1)}, u32[]{:S(2)}, u32[]{:S(2)}) collective-permute-start(f32[136,128]{1,0:T(8,128)S(1)} %collective-permute-done.4.refs_1_), channel_id=1, source_target_pairs={{0,1},{1,0},{2,3},{3,2},{4,5},{5,4},{6,7},{7,6},{8,9},{9,8},{10,11... | collective-permute-start | bytes 208904 | tf_op jit(solution)/shard_map/ppermute | solution.py:34
  55.9 7.1 %collective-permute-start.14 = (bf16[256,384]{1,0:T(8,128)(2,1)S(1)}, bf16[256,384]{1,0:T(8,128)(2,1)S(1)}, u32[]{:S(2)}, u32[]{:S(2)}) collective-permute-start(bf16[256,384]{1,0:T(8,128)(2,1)S(1)} %get-tuple-element.36), channel_id=1, source_target_pairs={{0,2},{2,0},{1,3},{3,1},{4,6},{6,4},{5,7},{7,5},{8,10},{10,8},{9,1... | collective-permute-start | bytes 589832 | tf_op jit(solution)/shard_map/ppermute | solution.py:34
  60.1 4.3 %collective-permute-start.16 = (bf16[256,128]{1,0:T(8,128)(2,1)S(1)}, bf16[256,128]{1,0:T(8,128)(2,1)S(1)}, u32[]{:S(2)}, u32[]{:S(2)}) collective-permute-start(bf16[256,128]{1,0:T(8,128)(2,1)S(1)} %get-tuple-element.40), channel_id=1, source_target_pairs={{0,2},{2,0},{1,3},{3,1},{4,6},{6,4},{5,7},{7,5},{8,10},{10,8},{9,1... | collective-permute-start | bytes 196616 | tf_op jit(solution)/shard_map/ppermute | solution.py:34

commit v7 on v6

--- a/solution.py
+++ b/solution.py
@@ -62,14 +62,27 @@
     return first, second
 
 
-def grams(lengths, train, slabs):
+def gram_kernel(lengths_hbm, train_hbm, *refs):
+    slabs, (lengths, train, sems) = refs[:-3], refs[-3:]
     cycle = len(slabs)
     mine, half = lax.axis_index("dp"), lax.axis_index("rep")
+    width = 2 * FBLK
+
+    def columns(shift):
+        owner = half * cycle + lax.rem(mine + shift, cycle)
+        return pl.ds(pl.multiple_of(owner * width, width), width)
+
+    get_lengths = pltpu.make_async_copy(lengths_hbm, lengths, sems.at[cycle])
+    get_train = [
+        pltpu.make_async_copy(train_hbm.at[:, columns(shift)], train.at[shift], sems.at[shift]) for shift in range(cycle)
+    ]
+    for copy in (get_lengths, *get_train):
+        copy.start()
+    get_lengths.wait()
     spare = lengths[...].astype(jnp.float32)
     for shift, slab in enumerate(slabs):
-        owner = half * cycle + lax.rem(mine + shift, cycle)
-        start = pl.multiple_of(owner * (2 * FBLK), 2 * FBLK)
-        part = train[:, pl.ds(start, 2 * FBLK)]
+        get_train[shift].wait()
+        part = train[shift]
         gram = lax.dot_general(part, part, (((0,), (0,)), ((), ())), preferred_element_type=jnp.float32)
         body, tail = pack(gram[:FBLK, :FBLK], gram[FBLK:, FBLK:], spare)
         slab[pl.ds(0, FBLK), :] = body
@@ -157,7 +170,7 @@
 
 
 def factor_kernel(examples, scale, *refs):
-    slabs, out = refs[:-2], refs[-1]
+    slabs, out = refs[:-1], refs[-1]
     body = slabs[0][pl.ds(0, FBLK), :]
     diagonal = slabs[0][pl.ds(FBLK, 1), :]
     for slab in slabs[1:]:
@@ -175,20 +188,15 @@
     out[pl.ds(FBLK, 8), :] = tail
 
 
-def first_kernel(id_rows_hbm, delta_hbm, table_hbm, factor_hbm, lengths_hbm, train_hbm, sent, own, *refs):
-    slabs, refs = refs[:-10], refs[-10:]
-    id_rows, places, reads, delta, table, factor, lengths, train, looked, sems = refs
+def tokens_kernel(id_rows_hbm, delta_hbm, table_hbm, factor_hbm, after, sent, own, *refs):
+    id_rows, places, reads, delta, table, factor, looked, sems = refs
     model = lax.axis_index("mp")
     proj, vocab_rows = table.shape
     tokens = delta.shape[0]
     each = proj // lax.axis_size("mp")
     groups = tokens // FBLK
-    get_ids, get_factor, get_lengths, get_train = (
-        pltpu.make_async_copy(source, target, sems.at[0, index])
-        for index, (source, target) in enumerate((
-            (id_rows_hbm, id_rows), (factor_hbm, factor), (lengths_hbm, lengths), (train_hbm, train),
-        ))
-    )
+    get_ids = pltpu.make_async_copy(id_rows_hbm, id_rows, sems.at[0, 0])
+    get_factor = pltpu.make_async_copy(factor_hbm, factor, sems.at[0, 1])
     get_table = [
         pltpu.make_async_copy(table_hbm.at[rows], table.at[rows], sems.at[1, index])
         for index in range(proj // ROWS) for rows in (pl.ds(index * ROWS, ROWS),)
@@ -198,7 +206,7 @@
         rows = pl.ds(pl.multiple_of(g * FBLK, FBLK), FBLK)
         return pltpu.make_async_copy(delta_hbm.at[rows], delta.at[rows], sems.at[2, g])
 
-    for copy in (get_ids, get_lengths, get_train, *get_table, get_factor, *(get_delta(g) for g in range(groups))):
+    for copy in (get_ids, *get_table, get_factor, *(get_delta(g) for g in range(groups))):
         copy.start()
     get_ids.wait()
     local = id_rows[...] - model * vocab_rows
@@ -207,11 +215,8 @@
     low = FBLK - 1
     roll = (lax.broadcasted_iota(jnp.int32, local.shape, 1) - local) & low
     places[...] = (local & ~low) | roll
-    fetch = pltpu.make_async_copy(places, reads, sems.at[0, 4])
+    fetch = pltpu.make_async_copy(places, reads, sems.at[0, 2])
     fetch.start()
-    get_lengths.wait()
-    get_train.wait()
-    grams(lengths, train, slabs)
     fetch.wait()
     places[...] = owned.astype(jnp.int32)
     for copy in get_table:
@@ -250,7 +255,7 @@
         target[pl.ds(each, each), :] = rest
 
 
-def merge_kernel(each, own, got, out):
+def merge_kernel(each, own, got, after, out):
     def value(ref):
         return ref[pl.ds(0, each), :].astype(jnp.float32) + ref[pl.ds(each, each), :].astype(jnp.float32)
 
@@ -262,7 +267,7 @@
 
 
 def queries_kernel(each, source_of, choose, count, *refs):
-    factor_refs, slabs, (high_out, low_out) = refs[:count], refs[count:count + 4], refs[-2:]
+    factor_refs, slabs, (high_out, low_out) = refs[:count], refs[count:-2], refs[-2:]
     mine = lax.axis_index("dp")
     tokens = factor_refs[0].shape[1]
     proj = factor_refs[0].shape[0] - 2 * each
@@ -356,10 +361,25 @@
     queries = doc_lengths.shape[1]
     bf16, f32 = jnp.bfloat16, jnp.float32
 
-    sent, own, *slabs = call(
-        first_kernel,
-        [shape((2 * each + proj, tokens), bf16)] * 2 + [shape((SLAB, FBLK), f32)] * cycle,
-        [HBM] * 6,
+    slabs = call(
+        gram_kernel,
+        [shape((SLAB, FBLK), f32)] * cycle,
+        [HBM] * 2,
+        [
+            pltpu.VMEM((1, queries), jnp.int32),
+            pltpu.VMEM((cycle, train_rows, 2 * FBLK), bf16),
+            pltpu.SemaphoreType.DMA((cycle + 1,)),
+        ],
+        vmem=62,
+        flops=train_rows * feat * FBLK * 2,
+        moved=train_rows * feat,
+    )(doc_lengths, train_grads)
+    parts = [slabs[0]] + [passed_along(slabs[s], "dp", s) for s in range(1, cycle)]
+
+    sent, own = call(
+        tokens_kernel,
+        [shape((2 * each + proj, tokens), bf16)] * 2,
+        [HBM] * 5,
         [
             pltpu.VMEM((tokens // FBLK, FBLK), jnp.int32),
             pltpu.VMEM((tokens // FBLK, FBLK), jnp.int32),
@@ -367,29 +387,34 @@
             pltpu.VMEM((tokens, width), bf16),
             pltpu.VMEM((proj, vocab_rows), bf16),
             pltpu.VMEM((proj, width), bf16),
-            pltpu.VMEM((1, queries), jnp.int32),
-            pltpu.VMEM((train_rows, feat), bf16),
             pltpu.VMEM((proj, tokens), f32),
             pltpu.SemaphoreType.DMA((3, 8)),
         ],
         vmem=62,
         flops=2 * tokens * width * proj,
         moved=2 * (tokens * width + proj * vocab_rows) * 2,
-    )(
-        query_ids.reshape(tokens // FBLK, FBLK), query_delta, vocab_factor.T, output_factor.T,
-        doc_lengths, train_grads,
-    )
+    )(query_ids.reshape(tokens // FBLK, FBLK), query_delta, vocab_factor.T, output_factor.T, slabs[0])
     got = passed_along(sent, "mp", 1)
-    parts = [slabs[0]] + [passed_along(slabs[s], "dp", s) for s in range(1, cycle)]
+
+    inverse = call(
+        functools.partial(factor_kernel, train_rows * cycle, 1.0 / proj),
+        shape((SLAB, FBLK), f32),
+        [VMEM] * cycle,
+        vmem=16,
+        flops=10 ** 10,
+        moved=10 ** 6,
+    )(*parts)
+    inverses = [inverse] + [passed_along(inverse, "dp", s) for s in range(1, cycle)]
+    peers = [passed_along(slab, "rep", 1) for slab in inverses]
 
     factors = call(
         functools.partial(merge_kernel, each),
         shape(sent.shape, bf16),
-        [VMEM, VMEM],
+        [VMEM, VMEM, HBM],
         vmem=16,
         flops=tokens * each,
         moved=8 * tokens * each * 4,
-    )(own, got)
+    )(own, got, inverse)
     last = cycle - 1
     from_two = passed_along(factors, "dp", 2)
     from_below = lax.ppermute(factors, "dp", [(i, i + 1) for i in range(last)])
@@ -403,28 +428,16 @@
          (from_above, from_far)),
     )
 
-    inverse = call(
-        functools.partial(factor_kernel, train_rows * cycle, 1.0 / proj),
-        shape((SLAB, FBLK), f32),
-        [VMEM] * cycle + [HBM],
-        vmem=16,
-        flops=10 ** 10,
-        moved=10 ** 6,
-    )(*parts, factors)
-    inverses = [inverse] + [passed_along(inverse, "dp", s) for s in range(1, cycle)]
-    peers = [passed_along(slab, "rep", 1) for slab in inverses]
-
     highs, lows = [], []
     for index, (source_of, choose, arrays) in enumerate(sources):
-        before = [inverse] if index == 0 else []
         high, low = call(
             functools.partial(queries_kernel, each, source_of, choose, len(arrays)),
             [shape((feat, queries), bf16)] * 2,
-            [VMEM] * (len(arrays) + cycle) + [HBM] * len(before),
+            [VMEM] * (len(arrays) + cycle),
             vmem=24,
             flops=2 * feat * tokens * queries,
             moved=6 * feat * queries,
-        )(*arrays, *parts, *before)
+        )(*arrays, *parts)
         highs.append(high)
         lows.append(low)
 

time: 66 us -> 72.3 us (1.095)
  waiting for transfers between devices: 5.99 us -> 11.3 us
  Pallas kernels: 28.5 us -> 30.7 us
  local copies, waits for them, and re-layouts: 1.84 us -> 0.01 us
    ppermute x14, waiting for transfers between devices: 5.98 us -> 11.3 us  [passed_along(): lax.ppermute(shard, axis, [(i, (i + by) % size) for i in range(size)])]
    pallas_call x1 -> x2, Pallas kernels: 11.1 us -> 13.3 us  [the longest x1 10.4 us: split_over_blocks(): call(tokens_kernel, [shape((2 * each + proj, tokens), bf16)] * 2, [HBM] *...]
    unnamed x8 -> x6, local copies, waits for them, and re-layouts: 1.84 us -> 0.01 us
  transfers between devices with their start and end apart: 17 -> 17, of which waited for: 4 -> 3; matrix products, arithmetic and copies ran while one was open for 0% -> 0% of each run, Pallas kernels for 25% -> 37%
where the time goes in v7:
time: 72.3 us; the launch traced here: 72.1 us
  Pallas kernels  30.7 us (42%)
  starting transfers between devices  29.9 us (41%)
  waiting for transfers between devices  11.3 us (16%)
    ppermute x14, starting transfers between devices, passed_along(): lax.ppermute(shard, axis, [(i, (i + by) % size) for i in range(size)])  22.5 us
    ppermute x14, waiting for transfers between devices, passed_along(): lax.ppermute(shard, axis, [(i, (i + by) % size) for i in range(size)])  11.3 us
    pallas_call x1, Pallas kernels, split_over_blocks(): call(tokens_kernel, [shape((2 * each + proj, tokens), bf16)] * 2, [HBM] *...  10.4 us
    pallas_call x1, Pallas kernels, split_over_blocks(): call(functools.partial(factor_kernel, train_rows * cycle, 1.0 / proj), sh...  6.58 us
    pallas_call x4, Pallas kernels, split_over_blocks(): call(functools.partial(queries_kernel, each, source_of, choose, len(array...  5.65 us
    ppermute x1, starting transfers between devices, split_over_blocks(): from_below = lax.ppermute(factors, 'dp', [(i, i + 1) for i in range(last)])  4.56 us
    pallas_call x2, Pallas kernels, split_over_blocks(): call(functools.partial(scores_kernel, cycle, count), [shape((half_rows, c...  3.9 us
    pallas_call x1, Pallas kernels, split_over_blocks(): call(gram_kernel, [shape((SLAB, FBLK), f32)] * cycle, [HBM] * 2, [pltpu.V...  2.9 us
  transfers between devices with their start and end apart: 17, of which 3 were waited for; matrix products, arithmetic and copies ran while one was open for 0% of the time, Pallas kernels for 37%

profile of v7, /device:TPU:0, one launch (start us, length us, event | category | flops | bytes accessed | tf_op | source)
XLA Modules:
  0.0 72.1 jit_solution(14338017096742025177)
XLA Ops:
  0.0 2.9 %shard_map.64 = (f32[136,128]{1,0:T(8,128)}, f32[136,128]{1,0:T(8,128)}, f32[136,128]{1,0:T(8,128)}, f32[136,128]{1,0:T(8,128)}) custom-call(s32[1,128]{1,0:T(1,128)} %lengths_hbm.1, bf16[512,2048]{1,0:T(8,128)(2,1)} %refs_10_.1), custom_call_target="tpu_custom_call" | custom-call | flops 268435456 | bytes 1048576 | tf_op jit(solution)/shard_map/pallas_call | solution.py:364
  2.9 3.1 %collective-permute-start = (f32[136,128]{1,0:T(8,128)}, f32[136,128]{1,0:T(8,128)S(1)}, u32[]{:S(2)}, u32[]{:S(2)}) collective-permute-start(f32[136,128]{1,0:T(8,128)} %get-tuple-element.24), channel_id=1, source_target_pairs={{0,4},{4,8},{8,12},{12,0},{1,5},{5,9},{9,13},{13,1},{2,6},{6,10},{... | collective-permute-start | bytes 208904 | tf_op jit(solution)/shard_map/ppermute | solution.py:34
  6.0 2.6 %collective-permute-start.1 = (f32[136,128]{1,0:T(8,128)}, f32[136,128]{1,0:T(8,128)S(1)}, u32[]{:S(2)}, u32[]{:S(2)}) collective-permute-start(f32[136,128]{1,0:T(8,128)} %get-tuple-element.25), channel_id=1, source_target_pairs={{0,8},{4,12},{8,0},{12,4},{1,9},{5,13},{9,1},{13,5},{2,10},{6,14},... | collective-permute-start | bytes 208904 | tf_op jit(solution)/shard_map/ppermute | solution.py:34
  8.6 1.3 %collective-permute-start.2 = (f32[136,128]{1,0:T(8,128)}, f32[136,128]{1,0:T(8,128)S(1)}, u32[]{:S(2)}, u32[]{:S(2)}) collective-permute-start(f32[136,128]{1,0:T(8,128)} %get-tuple-element.26), channel_id=1, source_target_pairs={{0,12},{4,0},{8,4},{12,8},{1,13},{5,1},{9,5},{13,9},{2,14},{6,2},{... | collective-permute-start | bytes 208904 | tf_op jit(solution)/shard_map/ppermute | solution.py:34
  9.9 10.4 %shard_map.66 = (bf16[128,1024]{1,0:T(8,128)(2,1)}, bf16[128,1024]{1,0:T(8,128)(2,1)}) custom-call(s32[8,128]{1,0:T(8,128)} %bitcast.8, bf16[1024,2048]{1,0:T(8,128)(2,1)} %delta_hbm.1, bf16[64,64128]{1,0:T(8,128)(2,1)} %bitcast.6, bf16[64,2048]{1,0:T(8,128)(2,1)} %bitcast.7, f32[136,128]{1,0:T(8,128)} %get-tuple-element.23.refs_0_.after.refs_1_.refs_2_), custom_call_target="tpu_custom_call" | custom-call | flops 268435456 | bytes 24805376 | tf_op jit(solution)/shard_map/pallas_call | solution.py:379
  20.3 0.0 copy-start.1
  20.3 1.6 %collective-permute-start.10 = (bf16[128,1024]{1,0:T(8,128)(2,1)}, bf16[128,1024]{1,0:T(8,128)(2,1)S(1)}, u32[]{:S(2)}, u32[]{:S(2)}) collective-permute-start(bf16[128,1024]{1,0:T(8,128)(2,1)} %get-tuple-element.28), channel_id=1, source_target_pairs={{0,2},{2,0},{1,3},{3,1},{4,6},{6,4},{5,7},{7,5},{8,10},{10,8},{9,1... | collective-permute-start | bytes 786440 | tf_op jit(solution)/shard_map/ppermute | solution.py:34
  21.9 0.0 collective-permute-done.refs_1_.refs_2_.refs_3_
  21.9 0.0 collective-permute-done.1.refs_2_.refs_3_.refs_4_
  21.9 0.0 collective-permute-done.2.refs_3_.refs_4_.refs_5_
  21.9 0.0 copy-done.2
  21.9 6.6 %shard_map.65.after.refs_0_ = f32[136,128]{1,0:T(8,128)S(1)} custom-call(f32[136,128]{1,0:T(8,128)S(1)} %copy-done.2, f32[136,128]{1,0:T(8,128)S(1)} %collective-permute-done.refs_1_.refs_2_.refs_3_, f32[136,128]{1,0:T(8,128)S(1)} %collective-permute-done.1.refs_2_.refs_3_.refs_4_, f32[136,128]{1,0:T(8,128)S(1)} %collective-permute-done.2.refs_3_.refs_4_.refs_5_), custom_call_target="tpu_custom_call" | custom-call | flops 10000000000 | bytes 1000000 | tf_op jit(solution)/shard_map/pallas_call | solution.py:399
  28.5 0.0 copy-start
  28.5 0.0 collective-permute-done.10.got
  28.5 0.1 shard_map.67.refs_0_
  28.6 0.4 collective-permute-start.13
  29.0 1.4 %collective-permute-start.12 = (bf16[128,1024]{1,0:T(8,128)(2,1)S(1)}, bf16[128,1024]{1,0:T(8,128)(2,1)S(1)}, u32[]{:S(2)}, u32[]{:S(2)}) collective-permute-start(bf16[128,1024]{1,0:T(8,128)(2,1)S(1)} %shard_map.67.refs_0_), channel_id=1, source_target_pairs={{4,0},{8,4},{12,8},{5,1},{9,5},{13,9},{6,2},{10,6},{14,10},{7,3},{... | collective-permute-start | bytes 786440 | tf_op jit(solution)/shard_map/ppermute | solution.py:421
  30.4 4.6 %collective-permute-start.11 = (bf16[128,1024]{1,0:T(8,128)(2,1)S(1)}, bf16[128,1024]{1,0:T(8,128)(2,1)S(1)}, u32[]{:S(2)}, u32[]{:S(2)}) collective-permute-start(bf16[128,1024]{1,0:T(8,128)(2,1)S(1)} %shard_map.67.refs_0_), channel_id=1, source_target_pairs={{0,4},{4,8},{8,12},{1,5},{5,9},{9,13},{2,6},{6,10},{10,14},{3,7},{... | collective-permute-start | bytes 786440 | tf_op jit(solution)/shard_map/ppermute | solution.py:420
  35.0 1.3 %collective-permute-start.5 = (f32[136,128]{1,0:T(8,128)S(1)}, f32[136,128]{1,0:T(8,128)S(1)}, u32[]{:S(2)}, u32[]{:S(2)}) collective-permute-start(f32[136,128]{1,0:T(8,128)S(1)} %shard_map.65.after.refs_0_), channel_id=1, source_target_pairs={{0,12},{4,0},{8,4},{12,8},{1,13},{5,1},{9,5},{13,9},{2,14},{6,2},{... | collective-permute-start | bytes 208904 | tf_op jit(solution)/shard_map/ppermute | solution.py:34
  36.3 1.3 %collective-permute-start.4 = (f32[136,128]{1,0:T(8,128)S(1)}, f32[136,128]{1,0:T(8,128)S(1)}, u32[]{:S(2)}, u32[]{:S(2)}) collective-permute-start(f32[136,128]{1,0:T(8,128)S(1)} %shard_map.65.after.refs_0_), channel_id=1, source_target_pairs={{0,8},{4,12},{8,0},{12,4},{1,9},{5,13},{9,1},{13,5},{2,10},{6,14},... | collective-permute-start | bytes 208904 | tf_op jit(solution)/shard_map/ppermute | solution.py:34
  37.6 7.8 %collective-permute-done.5.refs_3_ = f32[136,128]{1,0:T(8,128)S(1)} collective-permute-done((f32[136,128]{1,0:T(8,128)S(1)}, f32[136,128]{1,0:T(8,128)S(1)}, u32[]{:S(2)}, u32[]{:S(2)}) %collective-permute-start.5) | collective-permute-done | bytes 69664 | tf_op jit(solution)/shard_map/ppermute | solution.py:34
  45.4 7.6 %collective-permute-start.3 = (f32[136,128]{1,0:T(8,128)S(1)}, f32[136,128]{1,0:T(8,128)S(1)}, u32[]{:S(2)}, u32[]{:S(2)}) collective-permute-start(f32[136,128]{1,0:T(8,128)S(1)} %shard_map.65.after.refs_0_), channel_id=1, source_target_pairs={{0,4},{4,8},{8,12},{12,0},{1,5},{5,9},{9,13},{13,1},{2,6},{6,10},{... | collective-permute-start | bytes 208904 | tf_op jit(solution)/shard_map/ppermute | solution.py:34
  53.1 0.0 collective-permute-done.13.refs_0_
  53.1 1.5 %collective-permute-start.15 = (bf16[128,1024]{1,0:T(8,128)(2,1)S(1)}, bf16[128,1024]{1,0:T(8,128)(2,1)S(1)}, u32[]{:S(2)}, u32[]{:S(2)}) collective-permute-start(bf16[128,1024]{1,0:T(8,128)(2,1)S(1)} %collective-permute-done.13.refs_0_), channel_id=1, source_target_pairs={{4,0},{8,12},{5,1},{9,13},{6,2},{10,14},{7,3},{11,15},{20,16},{24,... | collective-permute-start | bytes 786440 | tf_op jit(solution)/shard_map/ppermute | solution.py:422
  54.5 1.4 %shard_map.68 = (bf16[2048,128]{1,0:T(8,128)(2,1)S(1)}, bf16[2048,128]{1,0:T(8,128)(2,1)S(1)}) custom-call(bf16[128,1024]{1,0:T(8,128)(2,1)S(1)} %shard_map.67.refs_0_, f32[136,128]{1,0:T(8,128)S(1)} %copy-done.2, f32[136,128]{1,0:T(8,128)S(1)} %collective-permute-done.refs_1_.refs_2_.refs_3_, f32[136,128]{1,0:T(8,128)S(1)} %collective-permute-done.1.refs_2_.refs_3_.refs_4_, ...), custom_call_target="tpu_custom_call" | custom-call | flops 536870912 | bytes 1572864 | tf_op jit(solution)/shard_map/pallas_call | solution.py:433
  55.9 0.0 collective-permute-done.4.refs_2_
  56.0 0.1 collective-permute-start.6
  56.0 0.0 collective-permute-done.3.refs_1_
  56.0 0.5 collective-permute-start.9
  56.5 0.0 collective-permute-done.12.refs_1_.refs_0_
  56.5 0.1 collective-permute-start.8
  56.6 0.0 collective-permute-done.11.refs_0_
  56.6 0.4 collective-permute-start.7
  57.1 1.4 %shard_map.70 = (bf16[2048,128]{1,0:T(8,128)(2,1)S(1)}, bf16[2048,128]{1,0:T(8,128)(2,1)S(1)}) custom-call(bf16[128,1024]{1,0:T(8,128)(2,1)S(1)} %collective-permute-done.13.refs_0_, f32[136,128]{1,0:T(8,128)S(1)} %copy-done.2, f32[136,128]{1,0:T(8,128)S(1)} %collective-permute-done.refs_1_.refs_2_.refs_3_, ...), custom_call_target="tpu_custom_call" | custom-call | flops 536870912 | bytes 1572864 | tf_op jit(solution)/shard_map/pallas_call | solution.py:433
  58.5 1.4 %shard_map.69 = (bf16[2048,128]{1,0:T(8,128)(2,1)S(1)}, bf16[2048,128]{1,0:T(8,128)(2,1)S(1)}) custom-call(bf16[128,1024]{1,0:T(8,128)(2,1)S(1)} %collective-permute-done.11.refs_0_, bf16[128,1024]{1,0:T(8,128)(2,1)S(1)} %collective-permute-done.12.refs_1_.refs_0_, f32[136,128]{1,0:T(8,128)S(1)} %copy-done.2, ...), custom_call_target="tpu_custom_call" | custom-call | flops 536870912 | bytes 1572864 | tf_op jit(solution)/shard_map/pallas_call | solution.py:433
  59.9 0.0 collective-permute-done.6.refs_4_
  59.9 0.0 collective-permute-done.9.refs_7_
  59.9 0.0 collective-permute-done.8.refs_6_
  59.9 0.0 collective-permute-done.7.refs_5_
  59.9 2.6 %shard_map.71 = (bf16[256,384]{1,0:T(8,128)(2,1)S(1)}, bf16[256,384]{1,0:T(8,128)(2,1)S(1)}) custom-call(f32[136,128]{1,0:T(8,128)S(1)} %shard_map.65.after.refs_0_, f32[136,128]{1,0:T(8,128)S(1)} %collective-permute-done.3.refs_1_, f32[136,128]{1,0:T(8,128)S(1)} %collective-permute-done.4.refs_2_, f32[136,128]{1,0:T(8,128)S(1)} %collective-permute-done.5.refs_3_, ...), custom_call_target="tpu_custom_call" | custom-call | flops 805306368 | bytes 6291456 | tf_op jit(solution)/shard_map/pallas_call | solution.py:448
  62.5 0.6 collective-permute-start.14
  63.1 0.0 collective-permute-done.15.refs_1_
  63.1 1.4 %shard_map.72 = (bf16[2048,128]{1,0:T(8,128)(2,1)S(1)}, bf16[2048,128]{1,0:T(8,128)(2,1)S(1)}) custom-call(bf16[128,1024]{1,0:T(8,128)(2,1)S(1)} %collective-permute-done.12.refs_1_.refs_0_, bf16[128,1024]{1,0:T(8,128)(2,1)S(1)} %collective-permute-done.15.refs_1_, f32[136,128]{1,0:T(8,128)S(1)} %copy-done.2, ...), custom_call_target="tpu_custom_call" | custom-call | flops 536870912 | bytes 1572864 | tf_op jit(solution)/shard_map/pallas_call | solution.py:433
  64.5 1.3 %shard_map.73 = (bf16[256,128]{1,0:T(8,128)(2,1)S(1)}, bf16[256,128]{1,0:T(8,128)(2,1)S(1)}) custom-call(f32[136,128]{1,0:T(8,128)S(1)} %shard_map.65.after.refs_0_, f32[136,128]{1,0:T(8,128)S(1)} %collective-permute-done.3.refs_1_, f32[136,128]{1,0:T(8,128)S(1)} %collective-permute-done.4.refs_2_, f32[136,128]{1,0:T(8,128)S(1)} %collective-permute-done.5.refs_3_, ...), custom_call_target="tpu_custom_call" | custom-call | flops 268435456 | bytes 2097152 | tf_op jit(solution)/shard_map/pallas_call | solution.py:448
  65.8 1.6 %collective-permute-start.16 = (bf16[256,128]{1,0:T(8,128)(2,1)S(1)}, bf16[256,128]{1,0:T(8,128)(2,1)S(1)}, u32[]{:S(2)}, u32[]{:S(2)}) collective-permute-start(bf16[256,128]{1,0:T(8,128)(2,1)S(1)} %get-tuple-element.40), channel_id=1, source_target_pairs={{0,2},{2,0},{1,3},{3,1},{4,6},{6,4},{5,7},{7,5},{8,10},{10,8},{9,1... | collective-permute-start | bytes 196616 | tf_op jit(solution)/shard_map/ppermute | solution.py:34
  67.4 2.7 %collective-permute-done.14.refs_1_ = bf16[256,384]{1,0:T(8,128)(2,1)S(1)} collective-permute-done((bf16[256,384]{1,0:T(8,128)(2,1)S(1)}, bf16[256,384]{1,0:T(8,128)(2,1)S(1)}, u32[]{:S(2)}, u32[]{:S(2)}) %collective-permute-start.14) | collective-permute-done | bytes 196640 | tf_op jit(solution)/shard_map/ppermute | solution.py:34
  70.2 0.7 collective-permute-done.16.refs_3_
  70.9 1.3 %shard_map.74 = bf16[256,4,128]{2,1,0:T(4,128)(2,1)} custom-call(bf16[256,384]{1,0:T(8,128)(2,1)S(1)} %get-tuple-element.35.refs_0_, bf16[256,384]{1,0:T(8,128)(2,1)S(1)} %collective-permute-done.14.refs_1_, bf16[256,128]{1,0:T(8,128)(2,1)S(1)} %get-tuple-element.39.refs_2_, bf16[256,128]{1,0:T(8,128)(2,1)S(1)} %collective-permute-done.16.refs_3_), custom_call_target="tpu_custom_call" | custom-call | flops 131072 | bytes 786432 | tf_op jit(solution)/shard_map/pallas_call | solution.py:458
  (3 shorter events, 0.0 us)
Async XLA Ops:
  2.9 19.0 %collective-permute-start = (f32[136,128]{1,0:T(8,128)}, f32[136,128]{1,0:T(8,128)S(1)}, u32[]{:S(2)}, u32[]{:S(2)}) collective-permute-start(f32[136,128]{1,0:T(8,128)} %get-tuple-element.24), channel_id=1, source_target_pairs={{0,4},{4,8},{8,12},{12,0},{1,5},{5,9},{9,13},{13,1},{2,6},{6,10},{... | collective-permute-start | bytes 208904 | tf_op jit(solution)/shard_map/ppermute | solution.py:34
  6.0 15.9 %collective-permute-start.1 = (f32[136,128]{1,0:T(8,128)}, f32[136,128]{1,0:T(8,128)S(1)}, u32[]{:S(2)}, u32[]{:S(2)}) collective-permute-start(f32[136,128]{1,0:T(8,128)} %get-tuple-element.25), channel_id=1, source_target_pairs={{0,8},{4,12},{8,0},{12,4},{1,9},{5,13},{9,1},{13,5},{2,10},{6,14},... | collective-permute-start | bytes 208904 | tf_op jit(solution)/shard_map/ppermute | solution.py:34
  8.6 13.3 %collective-permute-start.2 = (f32[136,128]{1,0:T(8,128)}, f32[136,128]{1,0:T(8,128)S(1)}, u32[]{:S(2)}, u32[]{:S(2)}) collective-permute-start(f32[136,128]{1,0:T(8,128)} %get-tuple-element.26), channel_id=1, source_target_pairs={{0,12},{4,0},{8,4},{12,8},{1,13},{5,1},{9,5},{13,9},{2,14},{6,2},{... | collective-permute-start | bytes 208904 | tf_op jit(solution)/shard_map/ppermute | solution.py:34
  9.9 12.0 %copy-start.2 = (f32[136,128]{1,0:T(8,128)S(1)}, f32[136,128]{1,0:T(8,128)}, u32[]{:S(2)}) copy-start(f32[136,128]{1,0:T(8,128)} %get-tuple-element.23.refs_0_.after.refs_1_.refs_2_) | copy-start | bytes 208900
  20.3 8.2 %copy-start.1 = (bf16[128,1024]{1,0:T(8,128)(2,1)S(1)}, bf16[128,1024]{1,0:T(8,128)(2,1)}, u32[]{:S(2)}) copy-start(bf16[128,1024]{1,0:T(8,128)(2,1)} %get-tuple-element.27.own) | copy-start | bytes 786436
  20.3 8.2 %collective-permute-start.10 = (bf16[128,1024]{1,0:T(8,128)(2,1)}, bf16[128,1024]{1,0:T(8,128)(2,1)S(1)}, u32[]{:S(2)}, u32[]{:S(2)}) collective-permute-start(bf16[128,1024]{1,0:T(8,128)(2,1)} %get-tuple-element.28), channel_id=1, source_target_pairs={{0,2},{2,0},{1,3},{3,1},{4,6},{6,4},{5,7},{7,5},{8,10},{10,8},{9,1... | collective-permute-start | bytes 786440 | tf_op jit(solution)/shard_map/ppermute | solution.py:34
  28.5 31.4 %copy-start = (bf16[512,2048]{1,0:T(8,128)(2,1)S(1)}, bf16[512,2048]{1,0:T(8,128)(2,1)}, u32[]{:S(2)}) copy-start(bf16[512,2048]{1,0:T(8,128)(2,1)} %refs_10_.1) | copy-start | bytes 6291460
  28.6 24.4 %collective-permute-start.13 = (bf16[128,1024]{1,0:T(8,128)(2,1)S(1)}, bf16[128,1024]{1,0:T(8,128)(2,1)S(1)}, u32[]{:S(2)}, u32[]{:S(2)}) collective-permute-start(bf16[128,1024]{1,0:T(8,128)(2,1)S(1)} %shard_map.67.refs_0_), channel_id=1, source_target_pairs={{0,8},{4,12},{8,0},{12,4},{1,9},{5,13},{9,1},{13,5},{2,10},{6,14},... | collective-permute-start | bytes 786440 | tf_op jit(solution)/shard_map/ppermute | solution.py:34
  29.0 27.5 %collective-permute-start.12 = (bf16[128,1024]{1,0:T(8,128)(2,1)S(1)}, bf16[128,1024]{1,0:T(8,128)(2,1)S(1)}, u32[]{:S(2)}, u32[]{:S(2)}) collective-permute-start(bf16[128,1024]{1,0:T(8,128)(2,1)S(1)} %shard_map.67.refs_0_), channel_id=1, source_target_pairs={{4,0},{8,4},{12,8},{5,1},{9,5},{13,9},{6,2},{10,6},{14,10},{7,3},{... | collective-permute-start | bytes 786440 | tf_op jit(solution)/shard_map/ppermute | solution.py:421
  30.4 26.2 %collective-permute-start.11 = (bf16[128,1024]{1,0:T(8,128)(2,1)S(1)}, bf16[128,1024]{1,0:T(8,128)(2,1)S(1)}, u32[]{:S(2)}, u32[]{:S(2)}) collective-permute-start(bf16[128,1024]{1,0:T(8,128)(2,1)S(1)} %shard_map.67.refs_0_), channel_id=1, source_target_pairs={{0,4},{4,8},{8,12},{1,5},{5,9},{9,13},{2,6},{6,10},{10,14},{3,7},{... | collective-permute-start | bytes 786440 | tf_op jit(solution)/shard_map/ppermute | solution.py:420
  35.0 10.4 %collective-permute-start.5 = (f32[136,128]{1,0:T(8,128)S(1)}, f32[136,128]{1,0:T(8,128)S(1)}, u32[]{:S(2)}, u32[]{:S(2)}) collective-permute-start(f32[136,128]{1,0:T(8,128)S(1)} %shard_map.65.after.refs_0_), channel_id=1, source_target_pairs={{0,12},{4,0},{8,4},{12,8},{1,13},{5,1},{9,5},{13,9},{2,14},{6,2},{... | collective-permute-start | bytes 208904 | tf_op jit(solution)/shard_map/ppermute | solution.py:34
  36.3 19.6 %collective-permute-start.4 = (f32[136,128]{1,0:T(8,128)S(1)}, f32[136,128]{1,0:T(8,128)S(1)}, u32[]{:S(2)}, u32[]{:S(2)}) collective-permute-start(f32[136,128]{1,0:T(8,128)S(1)} %shard_map.65.after.refs_0_), channel_id=1, source_target_pairs={{0,8},{4,12},{8,0},{12,4},{1,9},{5,13},{9,1},{13,5},{2,10},{6,14},... | collective-permute-start | bytes 208904 | tf_op jit(solution)/shard_map/ppermute | solution.py:34
  45.4 10.6 %collective-permute-start.3 = (f32[136,128]{1,0:T(8,128)S(1)}, f32[136,128]{1,0:T(8,128)S(1)}, u32[]{:S(2)}, u32[]{:S(2)}) collective-permute-start(f32[136,128]{1,0:T(8,128)S(1)} %shard_map.65.after.refs_0_), channel_id=1, source_target_pairs={{0,4},{4,8},{8,12},{12,0},{1,5},{5,9},{9,13},{13,1},{2,6},{6,10},{... | collective-permute-start | bytes 208904 | tf_op jit(solution)/shard_map/ppermute | solution.py:34
  53.1 10.0 %collective-permute-start.15 = (bf16[128,1024]{1,0:T(8,128)(2,1)S(1)}, bf16[128,1024]{1,0:T(8,128)(2,1)S(1)}, u32[]{:S(2)}, u32[]{:S(2)}) collective-permute-start(bf16[128,1024]{1,0:T(8,128)(2,1)S(1)} %collective-permute-done.13.refs_0_), channel_id=1, source_target_pairs={{4,0},{8,12},{5,1},{9,13},{6,2},{10,14},{7,3},{11,15},{20,16},{24,... | collective-permute-start | bytes 786440 | tf_op jit(solution)/shard_map/ppermute | solution.py:422
  56.0 3.9 %collective-permute-start.6 = (f32[136,128]{1,0:T(8,128)S(1)}, f32[136,128]{1,0:T(8,128)S(1)}, u32[]{:S(2)}, u32[]{:S(2)}) collective-permute-start(f32[136,128]{1,0:T(8,128)S(1)} %shard_map.65.after.refs_0_), channel_id=1, source_target_pairs={{0,1},{1,0},{2,3},{3,2},{4,5},{5,4},{6,7},{7,6},{8,9},{9,8},{10,11... | collective-permute-start | bytes 208904 | tf_op jit(solution)/shard_map/ppermute | solution.py:34
  56.0 3.9 %collective-permute-start.9 = (f32[136,128]{1,0:T(8,128)S(1)}, f32[136,128]{1,0:T(8,128)S(1)}, u32[]{:S(2)}, u32[]{:S(2)}) collective-permute-start(f32[136,128]{1,0:T(8,128)S(1)} %collective-permute-done.5.refs_3_), channel_id=1, source_target_pairs={{0,1},{1,0},{2,3},{3,2},{4,5},{5,4},{6,7},{7,6},{8,9},{9,8},{10,11... | collective-permute-start | bytes 208904 | tf_op jit(solution)/shard_map/ppermute | solution.py:34
  56.5 3.4 %collective-permute-start.8 = (f32[136,128]{1,0:T(8,128)S(1)}, f32[136,128]{1,0:T(8,128)S(1)}, u32[]{:S(2)}, u32[]{:S(2)}) collective-permute-start(f32[136,128]{1,0:T(8,128)S(1)} %collective-permute-done.4.refs_2_), channel_id=1, source_target_pairs={{0,1},{1,0},{2,3},{3,2},{4,5},{5,4},{6,7},{7,6},{8,9},{9,8},{10,11... | collective-permute-start | bytes 208904 | tf_op jit(solution)/shard_map/ppermute | solution.py:34
  56.6 3.3 %collective-permute-start.7 = (f32[136,128]{1,0:T(8,128)S(1)}, f32[136,128]{1,0:T(8,128)S(1)}, u32[]{:S(2)}, u32[]{:S(2)}) collective-permute-start(f32[136,128]{1,0:T(8,128)S(1)} %collective-permute-done.3.refs_1_), channel_id=1, source_target_pairs={{0,1},{1,0},{2,3},{3,2},{4,5},{5,4},{6,7},{7,6},{8,9},{9,8},{10,11... | collective-permute-start | bytes 208904 | tf_op jit(solution)/shard_map/ppermute | solution.py:34
  62.5 7.7 %collective-permute-start.14 = (bf16[256,384]{1,0:T(8,128)(2,1)S(1)}, bf16[256,384]{1,0:T(8,128)(2,1)S(1)}, u32[]{:S(2)}, u32[]{:S(2)}) collective-permute-start(bf16[256,384]{1,0:T(8,128)(2,1)S(1)} %get-tuple-element.36), channel_id=1, source_target_pairs={{0,2},{2,0},{1,3},{3,1},{4,6},{6,4},{5,7},{7,5},{8,10},{10,8},{9,1... | collective-permute-start | bytes 589832 | tf_op jit(solution)/shard_map/ppermute | solution.py:34
  65.8 5.0 %collective-permute-start.16 = (bf16[256,128]{1,0:T(8,128)(2,1)S(1)}, bf16[256,128]{1,0:T(8,128)(2,1)S(1)}, u32[]{:S(2)}, u32[]{:S(2)}) collective-permute-start(bf16[256,128]{1,0:T(8,128)(2,1)S(1)} %get-tuple-element.40), channel_id=1, source_target_pairs={{0,2},{2,0},{1,3},{3,1},{4,6},{6,4},{5,7},{7,5},{8,10},{10,8},{9,1... | collective-permute-start | bytes 196616 | tf_op jit(solution)/shard_map/ppermute | solution.py:34

commit v8 on v5

--- a/solution.py
+++ b/solution.py
@@ -9,7 +9,7 @@
 FBLK = 128
 SLAB = FBLK + 8
 PANEL = 8
-COPIES = 4
+ROWS = 16
 
 damping = 0.1
 
@@ -182,24 +182,26 @@
     proj, vocab_rows = table.shape
     tokens = delta.shape[0]
     each = proj // lax.axis_size("mp")
-    small = [
+    groups, pieces = tokens // FBLK, proj // ROWS
+    get_ids, get_factor, get_lengths, get_train = (
         pltpu.make_async_copy(source, target, sems.at[0, index])
         for index, (source, target) in enumerate((
             (id_rows_hbm, id_rows), (factor_hbm, factor), (lengths_hbm, lengths), (train_hbm, train),
         ))
+    )
+    get_table = [
+        pltpu.make_async_copy(table_hbm.at[rows], table.at[rows], sems.at[1, index])
+        for index in range(pieces) for rows in (pl.ds(index * ROWS, ROWS),)
     ]
-    tall, wide = tokens // COPIES, proj // COPIES
-    get_delta = [
-        pltpu.make_async_copy(delta_hbm.at[rows], delta.at[rows], sems.at[1, index])
-        for index in range(COPIES) for rows in (pl.ds(index * tall, tall),)
-    ]
-    get_table = [
-        pltpu.make_async_copy(table_hbm.at[rows], table.at[rows], sems.at[2, index])
-        for index in range(COPIES) for rows in (pl.ds(index * wide, wide),)
-    ]
-    for copy in small[:3] + get_delta + small[3:] + get_table:
+
+    def get_delta(g):
+        rows = pl.ds(pl.multiple_of(g * FBLK, FBLK), FBLK)
+        return pltpu.make_async_copy(delta_hbm.at[rows], delta.at[rows], sems.at[2, g])
+
+    first = (get_ids, get_table[0], get_lengths, get_train)
+    for copy in (*first, *get_table[1:], get_factor, *(get_delta(g) for g in range(groups))):
         copy.start()
-    small[0].wait()
+    get_ids.wait()
     local = id_rows[...] - model * vocab_rows
     owned = (local >= 0) & (local < vocab_rows)
     local = jnp.where(owned, local, 0)
@@ -208,43 +210,53 @@
     places[...] = (local & ~low) | roll
     fetch = pltpu.make_async_copy(places, reads, sems.at[0, 4])
     fetch.start()
-    small[1].wait()
-    for index, copy in enumerate(get_delta):
-        copy.wait()
-        rows = pl.ds(index * tall, tall)
+    fetch.wait()
+    places[...] = owned.astype(jnp.int32)
+    lanes = lax.broadcasted_iota(jnp.int32, (ROWS, FBLK), 1)
+
+    def gather(piece, g):
+        columns = pl.ds(pl.multiple_of(g * FBLK, FBLK), FBLK)
+        gathered = jnp.zeros((ROWS, FBLK), jnp.bfloat16)
+        for j in range(FBLK):
+            place = reads[g, j]
+            block = table[pl.ds(piece * ROWS, ROWS), pl.ds(pl.multiple_of(place & ~low, FBLK), FBLK)]
+            gathered = jnp.where(lanes == j, pltpu.roll(block, place & low, 1), gathered)
+        held = places[pl.ds(g, 1), :].astype(jnp.float32)
+        gathered = (gathered.astype(jnp.float32) * held).astype(jnp.bfloat16)
+        rows = pl.ds(2 * each + piece * ROWS, ROWS)
+        sent[rows, columns] = gathered
+        own[rows, columns] = gathered
+
+    def project(g):
+        columns = pl.ds(pl.multiple_of(g * FBLK, FBLK), FBLK)
+        get_delta(g).wait()
         output = lax.dot_general(
-            delta[rows, :], factor[...], (((1,), (1,)), ((), ())), preferred_element_type=jnp.float32
+            delta[columns, :], factor[...], (((1,), (1,)), ((), ())), preferred_element_type=jnp.float32
         )
-        looked[:, rows] = output.T
+        looked[:, columns] = output.T
+
+    for piece in range(pieces):
+        get_table[piece].wait()
+        if piece == 1:
+            get_lengths.wait()
+            get_train.wait()
+            grams(lengths, train, slabs)
+        if piece == pieces - 1:
+            get_factor.wait()
+
+        def group(g, carry):
+            if piece == pieces - 1:
+                project(g)
+            gather(piece, g)
+            return carry
+
+        lax.fori_loop(0, groups, group, 0)
     mine = looked[pl.ds(pl.multiple_of(model * each, each), each), :]
     other = looked[pl.ds(pl.multiple_of((1 - model) * each, each), each), :]
     for target, value in ((own, mine), (sent, other)):
         high, rest = halves(value)
         target[pl.ds(0, each), :] = high
         target[pl.ds(each, each), :] = rest
-    for copy in small[2:]:
-        copy.wait()
-    grams(lengths, train, slabs)
-    fetch.wait()
-    for copy in get_table:
-        copy.wait()
-    lanes = lax.broadcasted_iota(jnp.int32, (proj, FBLK), 1)
-    places[...] = owned.astype(jnp.int32)
-
-    def group(g, carry):
-        gathered = jnp.zeros((proj, FBLK), jnp.bfloat16)
-        for j in range(FBLK):
-            place = reads[g, j]
-            block = table[:, pl.ds(pl.multiple_of(place & ~low, FBLK), FBLK)]
-            gathered = jnp.where(lanes == j, pltpu.roll(block, place & low, 1), gathered)
-        held = places[pl.ds(g, 1), :].astype(jnp.float32)
-        gathered = (gathered.astype(jnp.float32) * held).astype(jnp.bfloat16)
-        columns = pl.ds(pl.multiple_of(g * FBLK, FBLK), FBLK)
-        sent[pl.ds(2 * each, proj), columns] = gathered
-        own[pl.ds(2 * each, proj), columns] = gathered
-        return carry
-
-    lax.fori_loop(0, tokens // FBLK, group, 0)
 
 
 def merge_kernel(each, own, got, out):
@@ -287,6 +299,10 @@
         low_out[pl.ds(start * proj, step * proj), :] = low
 
 
+def hand_kernel(slab, *refs):
+    refs[-1][...] = slab[...]
+
+
 def scores_kernel(cycle, count, *refs):
     own, peers = refs[:cycle], refs[cycle:2 * cycle]
     highs, lows = refs[2 * cycle:2 * cycle + count], refs[2 * cycle + count:2 * cycle + 2 * count]
@@ -392,8 +408,6 @@
         moved=10 ** 6,
     )(*parts, factors)
     inverses = [inverse] + [passed_along(inverse, "dp", s) for s in range(1, cycle)]
-    peers = [passed_along(slab, "rep", 1) for slab in inverses]
-
     highs, lows = {}, {}
     for s in sorted(range(cycle), key=lambda shift: (shift == late, shift)):
         first = s == 0
@@ -407,6 +421,15 @@
         )(gathered[s], parts[s], *[inverse] * first)
         if first:
             gathered[late] = passed_along(again[0], "dp", late)
+    handed = list(inverses)
+    handed[late] = call(
+        hand_kernel,
+        shape((SLAB, FBLK), f32),
+        [VMEM] + [HBM] * (cycle - 2),
+        vmem=16,
+        moved=8 * SLAB * FBLK,
+    )(inverses[late], *[highs[s] for s in range(1, cycle) if s != late])
+    peers = [passed_along(slab, "rep", 1) for slab in handed]
 
     half_rows = train_rows // lax.axis_size("mp")
     pieces, order = [], []

time: 65.2 us -> 66 us (1.012)
  waiting for transfers between devices: 13.6 us -> 10.3 us
  Pallas kernels: 29.1 us -> 31.3 us
  starting transfers between devices: 20.3 us -> 22.3 us
    ppermute x16, waiting for transfers between devices: 13.6 us -> 10.3 us  [passed_along(): lax.ppermute(shard, axis, [(i, (i + by) % size) for i in range(size)])]
    pallas_call x1, Pallas kernels: 11.7 us -> 13.9 us  [split_over_blocks(): call(first_kernel, [shape((2 * each + proj, tokens), bf16)] * 2 + [shape(...]
    ppermute x16, starting transfers between devices: 20.3 us -> 22.3 us  [passed_along(): lax.ppermute(shard, axis, [(i, (i + by) % size) for i in range(size)])]
  transfers between devices with their start and end apart: 16 -> 16, of which waited for: 4 -> 5; matrix products, arithmetic and copies ran while one was open for 0% -> 0% of each run, Pallas kernels for 25% -> 25%
where the time goes in v8:
time: 66 us; the launch traced here: 65.8 us
  Pallas kernels  31.3 us (47%)
  starting transfers between devices  22.3 us (34%)
  waiting for transfers between devices  10.3 us (16%)
  local copies, waits for them, and re-layouts  1.83 us (3%)
    ppermute x16, starting transfers between devices, passed_along(): lax.ppermute(shard, axis, [(i, (i + by) % size) for i in range(size)])  22.3 us
    pallas_call x1, Pallas kernels, split_over_blocks(): call(first_kernel, [shape((2 * each + proj, tokens), bf16)] * 2 + [shape(...  13.9 us
    ppermute x16, waiting for transfers between devices, passed_along(): lax.ppermute(shard, axis, [(i, (i + by) % size) for i in range(size)])  10.3 us
    pallas_call x1, Pallas kernels, split_over_blocks(): call(functools.partial(factor_kernel, train_rows * cycle, 1.0 / proj), sh...  6.58 us
    pallas_call x4, Pallas kernels, split_over_blocks(): call(functools.partial(queries_kernel, each), [shape((feat, queries), bf1...  5.63 us
    pallas_call x2, Pallas kernels, split_over_blocks(): call(functools.partial(scores_kernel, cycle, count), [shape((half_rows, c...  3.89 us
    unnamed x6, local copies, waits for them, and re-layouts  1.83 us
  transfers between devices with their start and end apart: 16, of which 5 were waited for; matrix products, arithmetic and copies ran while one was open for 0% of the time, Pallas kernels for 25%

profile of v8, /device:TPU:0, one launch (start us, length us, event | category | flops | bytes accessed | tf_op | source)
XLA Modules:
  0.0 65.8 jit_solution(9147822948115179911)
XLA Ops:
  0.0 13.9 %shard_map.64 = (bf16[128,1024]{1,0:T(8,128)(2,1)}, bf16[128,1024]{1,0:T(8,128)(2,1)}, f32[136,128]{1,0:T(8,128)}, f32[136,128]{1,0:T(8,128)}, f32[136,128]{1,0:T(8,128)}, /*index=5*/f32[136,128]{1,0:T(8,128)}) custom-call(s32[8,128]{1,0:T(8,128)} %bitcast.8, bf16[1024,2048]{1,0:T(8,128)(2,1)} %delta_hbm.1, bf16[64,64128]{1,0:T(8,128)(2,1)} %bitcast.6, ...), custom_call_target="tpu_custom_call" | custom-call | flops 268435456 | bytes 24805376 | tf_op jit(solution)/shard_map/pallas_call | solution.py:365
  13.9 3.0 %collective-permute-start.3 = (bf16[128,1024]{1,0:T(8,128)(2,1)}, bf16[128,1024]{1,0:T(8,128)(2,1)S(1)}, u32[]{:S(2)}, u32[]{:S(2)}) collective-permute-start(bf16[128,1024]{1,0:T(8,128)(2,1)} %get-tuple-element.29), channel_id=1, source_target_pairs={{0,2},{2,0},{1,3},{3,1},{4,6},{6,4},{5,7},{7,5},{8,10},{10,8},{9,1... | collective-permute-start | bytes 786440 | tf_op jit(solution)/shard_map/ppermute | solution.py:34
  16.9 1.6 %collective-permute-start = (f32[136,128]{1,0:T(8,128)}, f32[136,128]{1,0:T(8,128)S(1)}, u32[]{:S(2)}, u32[]{:S(2)}) collective-permute-start(f32[136,128]{1,0:T(8,128)} %get-tuple-element.25), channel_id=1, source_target_pairs={{0,4},{4,8},{8,12},{12,0},{1,5},{5,9},{9,13},{13,1},{2,6},{6,10},{... | collective-permute-start | bytes 208904 | tf_op jit(solution)/shard_map/ppermute | solution.py:34
  18.4 2.6 %collective-permute-start.1 = (f32[136,128]{1,0:T(8,128)}, f32[136,128]{1,0:T(8,128)S(1)}, u32[]{:S(2)}, u32[]{:S(2)}) collective-permute-start(f32[136,128]{1,0:T(8,128)} %get-tuple-element.26), channel_id=1, source_target_pairs={{0,8},{4,12},{8,0},{12,4},{1,9},{5,13},{9,1},{13,5},{2,10},{6,14},... | collective-permute-start | bytes 208904 | tf_op jit(solution)/shard_map/ppermute | solution.py:34
  21.0 1.3 %collective-permute-start.2 = (f32[136,128]{1,0:T(8,128)}, f32[136,128]{1,0:T(8,128)S(1)}, u32[]{:S(2)}, u32[]{:S(2)}) collective-permute-start(f32[136,128]{1,0:T(8,128)} %get-tuple-element.27), channel_id=1, source_target_pairs={{0,12},{4,0},{8,4},{12,8},{1,13},{5,1},{9,5},{13,9},{2,14},{6,2},{... | collective-permute-start | bytes 208904 | tf_op jit(solution)/shard_map/ppermute | solution.py:34
  22.4 1.0 %collective-permute-done.3.got = bf16[128,1024]{1,0:T(8,128)(2,1)S(1)} collective-permute-done((bf16[128,1024]{1,0:T(8,128)(2,1)}, bf16[128,1024]{1,0:T(8,128)(2,1)S(1)}, u32[]{:S(2)}, u32[]{:S(2)}) %collective-permute-start.3) | collective-permute-done | bytes 262176 | tf_op jit(solution)/shard_map/ppermute | solution.py:34
  23.4 0.0 copy-start.1
  23.4 0.9 %copy-done.1 = bf16[128,1024]{1,0:T(8,128)(2,1)S(1)} copy-done((bf16[128,1024]{1,0:T(8,128)(2,1)S(1)}, bf16[128,1024]{1,0:T(8,128)(2,1)}, u32[]{:S(2)}) %copy-start.1) | copy-done | bytes 262168
  24.3 0.1 shard_map.65.refs_4_.factors
  24.4 3.9 %collective-permute-start.10 = (bf16[128,1024]{1,0:T(8,128)(2,1)S(1)}, bf16[128,1024]{1,0:T(8,128)(2,1)S(1)}, u32[]{:S(2)}, u32[]{:S(2)}) collective-permute-start(bf16[128,1024]{1,0:T(8,128)(2,1)S(1)} %shard_map.65.refs_4_.factors), channel_id=1, source_target_pairs={{0,12},{4,0},{8,4},{12,8},{1,13},{5,1},{9,5},{13,9},{2,14},{6,2},{... | collective-permute-start | bytes 786440 | tf_op jit(solution)/shard_map/ppermute | solution.py:34
  28.3 0.0 collective-permute-start.9
  28.3 0.0 collective-permute-done.refs_1_.slab
  28.3 0.0 collective-permute-done.1.refs_2_.slab
  28.3 0.0 collective-permute-done.2.refs_3_.slab
  28.3 0.0 copy-start.2
  28.3 0.9 %copy-done.2 = f32[136,128]{1,0:T(8,128)S(1)} copy-done((f32[136,128]{1,0:T(8,128)S(1)}, f32[136,128]{1,0:T(8,128)}, u32[]{:S(2)}) %copy-start.2) | copy-done | bytes 69656
  29.2 6.6 %shard_map.66.refs_0_ = f32[136,128]{1,0:T(8,128)S(1)} custom-call(f32[136,128]{1,0:T(8,128)S(1)} %copy-done.2, f32[136,128]{1,0:T(8,128)S(1)} %collective-permute-done.refs_1_.slab, f32[136,128]{1,0:T(8,128)S(1)} %collective-permute-done.1.refs_2_.slab, f32[136,128]{1,0:T(8,128)S(1)} %collective-permute-done.2.refs_3_.slab, ...), custom_call_target="tpu_custom_call" | custom-call | flops 10000000000 | bytes 1000000 | tf_op jit(solution)/shard_map/pallas_call | solution.py:402
  35.8 0.0 copy-start
  35.8 3.9 %collective-permute-start.6 = (f32[136,128]{1,0:T(8,128)S(1)}, f32[136,128]{1,0:T(8,128)S(1)}, u32[]{:S(2)}, u32[]{:S(2)}) collective-permute-start(f32[136,128]{1,0:T(8,128)S(1)} %shard_map.66.refs_0_), channel_id=1, source_target_pairs={{0,12},{4,0},{8,4},{12,8},{1,13},{5,1},{9,5},{13,9},{2,14},{6,2},{... | collective-permute-start | bytes 208904 | tf_op jit(solution)/shard_map/ppermute | solution.py:34
  39.7 0.0 collective-permute-start.5
  39.7 0.6 collective-permute-start.4
  40.3 1.4 %shard_map.70 = (bf16[2048,128]{1,0:T(8,128)(2,1)S(1)}, bf16[2048,128]{1,0:T(8,128)(2,1)S(1)}, bf16[128,1024]{1,0:T(8,128)(2,1)S(1)}) custom-call(bf16[128,1024]{1,0:T(8,128)(2,1)S(1)} %shard_map.65.refs_4_.factors, f32[136,128]{1,0:T(8,128)S(1)} %copy-done.2, f32[136,128]{1,0:T(8,128)S(1)} %shard_map.66.refs_0_), custom_call_target="tpu_custom_call" | custom-call | flops 536870912 | bytes 1572864 | tf_op jit(solution)/shard_map/pallas_call | solution.py:414
  41.7 0.0 collective-permute-done.9.factors
  41.7 2.3 %collective-permute-start.14 = (bf16[128,1024]{1,0:T(8,128)(2,1)S(1)}, bf16[128,1024]{1,0:T(8,128)(2,1)S(1)}, u32[]{:S(2)}, u32[]{:S(2)}) collective-permute-start(bf16[128,1024]{1,0:T(8,128)(2,1)S(1)} %get-tuple-element.38), channel_id=1, source_target_pairs={{0,8},{4,12},{8,0},{12,4},{1,9},{5,13},{9,1},{13,5},{2,10},{6,14},... | collective-permute-start | bytes 786440 | tf_op jit(solution)/shard_map/ppermute | solution.py:34
  44.1 1.4 %shard_map.67 = (bf16[2048,128]{1,0:T(8,128)(2,1)S(1)}, bf16[2048,128]{1,0:T(8,128)(2,1)S(1)}) custom-call(bf16[128,1024]{1,0:T(8,128)(2,1)S(1)} %collective-permute-done.9.factors, f32[136,128]{1,0:T(8,128)S(1)} %collective-permute-done.refs_1_.slab), custom_call_target="tpu_custom_call" | custom-call | flops 536870912 | bytes 1572864 | tf_op jit(solution)/shard_map/pallas_call | solution.py:414
  45.5 0.0 collective-permute-done.6.refs_3_
  45.5 0.1 collective-permute-start.7
  45.6 1.0 %collective-permute-done.4.refs_1_ = f32[136,128]{1,0:T(8,128)S(1)} collective-permute-done((f32[136,128]{1,0:T(8,128)S(1)}, f32[136,128]{1,0:T(8,128)S(1)}, u32[]{:S(2)}, u32[]{:S(2)}) %collective-permute-start.4) | collective-permute-done | bytes 69664 | tf_op jit(solution)/shard_map/ppermute | solution.py:34
  46.5 0.0 collective-permute-start.12
  46.5 0.0 collective-permute-done.10.factors
  46.5 0.5 collective-permute-start.8
  47.0 1.4 %shard_map.68 = (bf16[2048,128]{1,0:T(8,128)(2,1)S(1)}, bf16[2048,128]{1,0:T(8,128)(2,1)S(1)}) custom-call(bf16[128,1024]{1,0:T(8,128)(2,1)S(1)} %collective-permute-done.10.factors, f32[136,128]{1,0:T(8,128)S(1)} %collective-permute-done.2.refs_3_.slab), custom_call_target="tpu_custom_call" | custom-call | flops 536870912 | bytes 1572864 | tf_op jit(solution)/shard_map/pallas_call | solution.py:414
  48.4 3.6 %collective-permute-done.5.slab.refs_2_ = f32[136,128]{1,0:T(8,128)S(1)} collective-permute-done((f32[136,128]{1,0:T(8,128)S(1)}, f32[136,128]{1,0:T(8,128)S(1)}, u32[]{:S(2)}, u32[]{:S(2)}) %collective-permute-start.5) | collective-permute-done | bytes 69664 | tf_op jit(solution)/shard_map/ppermute | solution.py:34
  52.0 0.0 collective-permute-start.11
  52.0 0.0 collective-permute-done.7.refs_4_
  52.1 0.0 collective-permute-done.12.refs_7_
  52.1 0.0 collective-permute-done.8.refs_5_
  52.1 1.2 %collective-permute-done.11.refs_6_ = f32[136,128]{1,0:T(8,128)S(1)} collective-permute-done((f32[136,128]{1,0:T(8,128)S(1)}, f32[136,128]{1,0:T(8,128)S(1)}, u32[]{:S(2)}, u32[]{:S(2)}) %collective-permute-start.11) | collective-permute-done | bytes 69664 | tf_op jit(solution)/shard_map/ppermute | solution.py:34
  53.3 0.0 copy-done
  53.3 2.5 %shard_map.71 = (bf16[256,384]{1,0:T(8,128)(2,1)S(1)}, bf16[256,384]{1,0:T(8,128)(2,1)S(1)}) custom-call(f32[136,128]{1,0:T(8,128)S(1)} %shard_map.66.refs_0_, f32[136,128]{1,0:T(8,128)S(1)} %collective-permute-done.4.refs_1_, f32[136,128]{1,0:T(8,128)S(1)} %collective-permute-done.5.slab.refs_2_, f32[136,128]{1,0:T(8,128)S(1)} %collective-permute-done.6.refs_3_, ...), custom_call_target="tpu_custom_call" | custom-call | flops 805306368 | bytes 6291456 | tf_op jit(solution)/shard_map/pallas_call | solution.py:438
  55.8 1.6 %collective-permute-start.13 = (bf16[256,384]{1,0:T(8,128)(2,1)S(1)}, bf16[256,384]{1,0:T(8,128)(2,1)S(1)}, u32[]{:S(2)}, u32[]{:S(2)}) collective-permute-start(bf16[256,384]{1,0:T(8,128)(2,1)S(1)} %get-tuple-element.37), channel_id=1, source_target_pairs={{0,2},{2,0},{1,3},{3,1},{4,6},{6,4},{5,7},{7,5},{8,10},{10,8},{9,1... | collective-permute-start | bytes 589832 | tf_op jit(solution)/shard_map/ppermute | solution.py:34
  57.4 0.0 collective-permute-done.14.factors
  57.4 1.4 %shard_map.72 = (bf16[2048,128]{1,0:T(8,128)(2,1)S(1)}, bf16[2048,128]{1,0:T(8,128)(2,1)S(1)}) custom-call(bf16[128,1024]{1,0:T(8,128)(2,1)S(1)} %collective-permute-done.14.factors, f32[136,128]{1,0:T(8,128)S(1)} %collective-permute-done.1.refs_2_.slab), custom_call_target="tpu_custom_call" | custom-call | flops 536870912 | bytes 1572864 | tf_op jit(solution)/shard_map/pallas_call | solution.py:414
  58.8 1.4 %shard_map.73 = (bf16[256,128]{1,0:T(8,128)(2,1)S(1)}, bf16[256,128]{1,0:T(8,128)(2,1)S(1)}) custom-call(f32[136,128]{1,0:T(8,128)S(1)} %shard_map.66.refs_0_, f32[136,128]{1,0:T(8,128)S(1)} %collective-permute-done.4.refs_1_, f32[136,128]{1,0:T(8,128)S(1)} %collective-permute-done.5.slab.refs_2_, f32[136,128]{1,0:T(8,128)S(1)} %collective-permute-done.6.refs_3_, ...), custom_call_target="tpu_custom_call" | custom-call | flops 268435456 | bytes 2097152 | tf_op jit(solution)/shard_map/pallas_call | solution.py:438
  60.2 0.9 %collective-permute-start.15 = (bf16[256,128]{1,0:T(8,128)(2,1)S(1)}, bf16[256,128]{1,0:T(8,128)(2,1)S(1)}, u32[]{:S(2)}, u32[]{:S(2)}) collective-permute-start(bf16[256,128]{1,0:T(8,128)(2,1)S(1)} %get-tuple-element.42), channel_id=1, source_target_pairs={{0,2},{2,0},{1,3},{3,1},{4,6},{6,4},{5,7},{7,5},{8,10},{10,8},{9,1... | collective-permute-start | bytes 196616 | tf_op jit(solution)/shard_map/ppermute | solution.py:34
  61.0 3.5 %collective-permute-done.15.refs_3_ = bf16[256,128]{1,0:T(8,128)(2,1)S(1)} collective-permute-done((bf16[256,128]{1,0:T(8,128)(2,1)S(1)}, bf16[256,128]{1,0:T(8,128)(2,1)S(1)}, u32[]{:S(2)}, u32[]{:S(2)}) %collective-permute-start.15) | collective-permute-done | bytes 65568 | tf_op jit(solution)/shard_map/ppermute | solution.py:34
  64.5 0.0 collective-permute-done.13.refs_1_
  64.5 1.3 %shard_map.74 = bf16[256,4,128]{2,1,0:T(4,128)(2,1)} custom-call(bf16[256,384]{1,0:T(8,128)(2,1)S(1)} %get-tuple-element.36.refs_0_, bf16[256,384]{1,0:T(8,128)(2,1)S(1)} %collective-permute-done.13.refs_1_, bf16[256,128]{1,0:T(8,128)(2,1)S(1)} %get-tuple-element.41.refs_2_, bf16[256,128]{1,0:T(8,128)(2,1)S(1)} %collective-permute-done.15.refs_3_), custom_call_target="tpu_custom_call" | custom-call | flops 131072 | bytes 786432 | tf_op jit(solution)/shard_map/pallas_call | solution.py:449
  (1 shorter events, 0.0 us)
Async XLA Ops:
  13.9 9.5 %collective-permute-start.3 = (bf16[128,1024]{1,0:T(8,128)(2,1)}, bf16[128,1024]{1,0:T(8,128)(2,1)S(1)}, u32[]{:S(2)}, u32[]{:S(2)}) collective-permute-start(bf16[128,1024]{1,0:T(8,128)(2,1)} %get-tuple-element.29), channel_id=1, source_target_pairs={{0,2},{2,0},{1,3},{3,1},{4,6},{6,4},{5,7},{7,5},{8,10},{10,8},{9,1... | collective-permute-start | bytes 786440 | tf_op jit(solution)/shard_map/ppermute | solution.py:34
  16.9 11.4 %collective-permute-start = (f32[136,128]{1,0:T(8,128)}, f32[136,128]{1,0:T(8,128)S(1)}, u32[]{:S(2)}, u32[]{:S(2)}) collective-permute-start(f32[136,128]{1,0:T(8,128)} %get-tuple-element.25), channel_id=1, source_target_pairs={{0,4},{4,8},{8,12},{12,0},{1,5},{5,9},{9,13},{13,1},{2,6},{6,10},{... | collective-permute-start | bytes 208904 | tf_op jit(solution)/shard_map/ppermute | solution.py:34
  18.4 9.9 %collective-permute-start.1 = (f32[136,128]{1,0:T(8,128)}, f32[136,128]{1,0:T(8,128)S(1)}, u32[]{:S(2)}, u32[]{:S(2)}) collective-permute-start(f32[136,128]{1,0:T(8,128)} %get-tuple-element.26), channel_id=1, source_target_pairs={{0,8},{4,12},{8,0},{12,4},{1,9},{5,13},{9,1},{13,5},{2,10},{6,14},... | collective-permute-start | bytes 208904 | tf_op jit(solution)/shard_map/ppermute | solution.py:34
  21.0 7.3 %collective-permute-start.2 = (f32[136,128]{1,0:T(8,128)}, f32[136,128]{1,0:T(8,128)S(1)}, u32[]{:S(2)}, u32[]{:S(2)}) collective-permute-start(f32[136,128]{1,0:T(8,128)} %get-tuple-element.27), channel_id=1, source_target_pairs={{0,12},{4,0},{8,4},{12,8},{1,13},{5,1},{9,5},{13,9},{2,14},{6,2},{... | collective-permute-start | bytes 208904 | tf_op jit(solution)/shard_map/ppermute | solution.py:34
  23.4 1.0 %copy-start.1 = (bf16[128,1024]{1,0:T(8,128)(2,1)S(1)}, bf16[128,1024]{1,0:T(8,128)(2,1)}, u32[]{:S(2)}) copy-start(bf16[128,1024]{1,0:T(8,128)(2,1)} %get-tuple-element.28.own) | copy-start | bytes 786436
  24.4 22.1 %collective-permute-start.10 = (bf16[128,1024]{1,0:T(8,128)(2,1)S(1)}, bf16[128,1024]{1,0:T(8,128)(2,1)S(1)}, u32[]{:S(2)}, u32[]{:S(2)}) collective-permute-start(bf16[128,1024]{1,0:T(8,128)(2,1)S(1)} %shard_map.65.refs_4_.factors), channel_id=1, source_target_pairs={{0,12},{4,0},{8,4},{12,8},{1,13},{5,1},{9,5},{13,9},{2,14},{6,2},{... | collective-permute-start | bytes 786440 | tf_op jit(solution)/shard_map/ppermute | solution.py:34
  28.3 13.4 %collective-permute-start.9 = (bf16[128,1024]{1,0:T(8,128)(2,1)S(1)}, bf16[128,1024]{1,0:T(8,128)(2,1)S(1)}, u32[]{:S(2)}, u32[]{:S(2)}) collective-permute-start(bf16[128,1024]{1,0:T(8,128)(2,1)S(1)} %shard_map.65.refs_4_.factors), channel_id=1, source_target_pairs={{0,4},{4,8},{8,12},{12,0},{1,5},{5,9},{9,13},{13,1},{2,6},{6,10},{... | collective-permute-start | bytes 786440 | tf_op jit(solution)/shard_map/ppermute | solution.py:34
  28.3 0.9 %copy-start.2 = (f32[136,128]{1,0:T(8,128)S(1)}, f32[136,128]{1,0:T(8,128)}, u32[]{:S(2)}) copy-start(f32[136,128]{1,0:T(8,128)} %get-tuple-element.24.refs_0_.slab) | copy-start | bytes 208900
  35.8 17.5 %copy-start = (bf16[512,2048]{1,0:T(8,128)(2,1)S(1)}, bf16[512,2048]{1,0:T(8,128)(2,1)}, u32[]{:S(2)}) copy-start(bf16[512,2048]{1,0:T(8,128)(2,1)} %refs_10_.1) | copy-start | bytes 6291460
  35.8 9.7 %collective-permute-start.6 = (f32[136,128]{1,0:T(8,128)S(1)}, f32[136,128]{1,0:T(8,128)S(1)}, u32[]{:S(2)}, u32[]{:S(2)}) collective-permute-start(f32[136,128]{1,0:T(8,128)S(1)} %shard_map.66.refs_0_), channel_id=1, source_target_pairs={{0,12},{4,0},{8,4},{12,8},{1,13},{5,1},{9,5},{13,9},{2,14},{6,2},{... | collective-permute-start | bytes 208904 | tf_op jit(solution)/shard_map/ppermute | solution.py:34
  39.7 12.4 %collective-permute-start.5 = (f32[136,128]{1,0:T(8,128)S(1)}, f32[136,128]{1,0:T(8,128)S(1)}, u32[]{:S(2)}, u32[]{:S(2)}) collective-permute-start(f32[136,128]{1,0:T(8,128)S(1)} %shard_map.66.refs_0_), channel_id=1, source_target_pairs={{0,8},{4,12},{8,0},{12,4},{1,9},{5,13},{9,1},{13,5},{2,10},{6,14},... | collective-permute-start | bytes 208904 | tf_op jit(solution)/shard_map/ppermute | solution.py:34
  39.7 6.9 %collective-permute-start.4 = (f32[136,128]{1,0:T(8,128)S(1)}, f32[136,128]{1,0:T(8,128)S(1)}, u32[]{:S(2)}, u32[]{:S(2)}) collective-permute-start(f32[136,128]{1,0:T(8,128)S(1)} %shard_map.66.refs_0_), channel_id=1, source_target_pairs={{0,4},{4,8},{8,12},{12,0},{1,5},{5,9},{9,13},{13,1},{2,6},{6,10},{... | collective-permute-start | bytes 208904 | tf_op jit(solution)/shard_map/ppermute | solution.py:34
  41.7 15.7 %collective-permute-start.14 = (bf16[128,1024]{1,0:T(8,128)(2,1)S(1)}, bf16[128,1024]{1,0:T(8,128)(2,1)S(1)}, u32[]{:S(2)}, u32[]{:S(2)}) collective-permute-start(bf16[128,1024]{1,0:T(8,128)(2,1)S(1)} %get-tuple-element.38), channel_id=1, source_target_pairs={{0,8},{4,12},{8,0},{12,4},{1,9},{5,13},{9,1},{13,5},{2,10},{6,14},... | collective-permute-start | bytes 786440 | tf_op jit(solution)/shard_map/ppermute | solution.py:34
  45.5 6.6 %collective-permute-start.7 = (f32[136,128]{1,0:T(8,128)S(1)}, f32[136,128]{1,0:T(8,128)S(1)}, u32[]{:S(2)}, u32[]{:S(2)}) collective-permute-start(f32[136,128]{1,0:T(8,128)S(1)} %shard_map.66.refs_0_), channel_id=1, source_target_pairs={{0,1},{1,0},{2,3},{3,2},{4,5},{5,4},{6,7},{7,6},{8,9},{9,8},{10,11... | collective-permute-start | bytes 208904 | tf_op jit(solution)/shard_map/ppermute | solution.py:34
  46.5 5.5 %collective-permute-start.12 = (f32[136,128]{1,0:T(8,128)S(1)}, f32[136,128]{1,0:T(8,128)S(1)}, u32[]{:S(2)}, u32[]{:S(2)}) collective-permute-start(f32[136,128]{1,0:T(8,128)S(1)} %collective-permute-done.6.refs_3_), channel_id=1, source_target_pairs={{0,1},{1,0},{2,3},{3,2},{4,5},{5,4},{6,7},{7,6},{8,9},{9,8},{10,11... | collective-permute-start | bytes 208904 | tf_op jit(solution)/shard_map/ppermute | solution.py:34
  46.5 5.5 %collective-permute-start.8 = (f32[136,128]{1,0:T(8,128)S(1)}, f32[136,128]{1,0:T(8,128)S(1)}, u32[]{:S(2)}, u32[]{:S(2)}) collective-permute-start(f32[136,128]{1,0:T(8,128)S(1)} %collective-permute-done.4.refs_1_), channel_id=1, source_target_pairs={{0,1},{1,0},{2,3},{3,2},{4,5},{5,4},{6,7},{7,6},{8,9},{9,8},{10,11... | collective-permute-start | bytes 208904 | tf_op jit(solution)/shard_map/ppermute | solution.py:34
  52.0 1.3 %collective-permute-start.11 = (f32[136,128]{1,0:T(8,128)S(1)}, f32[136,128]{1,0:T(8,128)S(1)}, u32[]{:S(2)}, u32[]{:S(2)}) collective-permute-start(f32[136,128]{1,0:T(8,128)S(1)} %shard_map.69), channel_id=1, source_target_pairs={{0,1},{1,0},{2,3},{3,2},{4,5},{5,4},{6,7},{7,6},{8,9},{9,8},{10,11... | collective-permute-start | bytes 208904 | tf_op jit(solution)/shard_map/ppermute | solution.py:34
  55.8 8.7 %collective-permute-start.13 = (bf16[256,384]{1,0:T(8,128)(2,1)S(1)}, bf16[256,384]{1,0:T(8,128)(2,1)S(1)}, u32[]{:S(2)}, u32[]{:S(2)}) collective-permute-start(bf16[256,384]{1,0:T(8,128)(2,1)S(1)} %get-tuple-element.37), channel_id=1, source_target_pairs={{0,2},{2,0},{1,3},{3,1},{4,6},{6,4},{5,7},{7,5},{8,10},{10,8},{9,1... | collective-permute-start | bytes 589832 | tf_op jit(solution)/shard_map/ppermute | solution.py:34
  60.2 4.3 %collective-permute-start.15 = (bf16[256,128]{1,0:T(8,128)(2,1)S(1)}, bf16[256,128]{1,0:T(8,128)(2,1)S(1)}, u32[]{:S(2)}, u32[]{:S(2)}) collective-permute-start(bf16[256,128]{1,0:T(8,128)(2,1)S(1)} %get-tuple-element.42), channel_id=1, source_target_pairs={{0,2},{2,0},{1,3},{3,1},{4,6},{6,4},{5,7},{7,5},{8,10},{10,8},{9,1... | collective-permute-start | bytes 196616 | tf_op jit(solution)/shard_map/ppermute | solution.py:34

commit v9 on v8

--- a/solution.py
+++ b/solution.py
@@ -29,9 +29,8 @@
     )
 
 
-def passed_along(shard, axis, by):
-    size = lax.axis_size(axis)
-    return lax.ppermute(shard, axis, [(i, (i + by) % size) for i in range(size)])
+def swapped(shard, axis, by):
+    return lax.ppermute(shard, axis, [(i, i ^ by) for i in range(lax.axis_size(axis))])
 
 
 def square(dim):
@@ -67,7 +66,7 @@
     mine, half = lax.axis_index("dp"), lax.axis_index("rep")
     spare = lengths[...].astype(jnp.float32)
     for shift, slab in enumerate(slabs):
-        owner = half * cycle + lax.rem(mine + shift, cycle)
+        owner = half * cycle + (mine ^ shift)
         start = pl.multiple_of(owner * (2 * FBLK), 2 * FBLK)
         part = train[:, pl.ds(start, 2 * FBLK)]
         gram = lax.dot_general(part, part, (((0,), (0,)), ((), ())), preferred_element_type=jnp.float32)
@@ -176,13 +175,13 @@
 
 
 def first_kernel(id_rows_hbm, delta_hbm, table_hbm, factor_hbm, lengths_hbm, train_hbm, sent, own, *refs):
-    slabs, refs = refs[:-10], refs[-10:]
-    id_rows, places, reads, delta, table, factor, lengths, train, looked, sems = refs
+    slabs, refs = refs[:-12], refs[-12:]
+    id_rows, starts, rolls, start_of, roll_of, delta, table, factor, lengths, train, looked, sems = refs
     model = lax.axis_index("mp")
     proj, vocab_rows = table.shape
     tokens = delta.shape[0]
     each = proj // lax.axis_size("mp")
-    groups, pieces = tokens // FBLK, proj // ROWS
+    groups = tokens // FBLK
     get_ids, get_factor, get_lengths, get_train = (
         pltpu.make_async_copy(source, target, sems.at[0, index])
         for index, (source, target) in enumerate((
@@ -191,66 +190,58 @@
     )
     get_table = [
         pltpu.make_async_copy(table_hbm.at[rows], table.at[rows], sems.at[1, index])
-        for index in range(pieces) for rows in (pl.ds(index * ROWS, ROWS),)
+        for index in range(proj // ROWS) for rows in (pl.ds(index * ROWS, ROWS),)
     ]
 
     def get_delta(g):
         rows = pl.ds(pl.multiple_of(g * FBLK, FBLK), FBLK)
         return pltpu.make_async_copy(delta_hbm.at[rows], delta.at[rows], sems.at[2, g])
 
-    first = (get_ids, get_table[0], get_lengths, get_train)
-    for copy in (*first, *get_table[1:], get_factor, *(get_delta(g) for g in range(groups))):
+    for copy in (get_ids, get_lengths, get_train, *get_table, get_factor, *(get_delta(g) for g in range(groups))):
         copy.start()
     get_ids.wait()
     local = id_rows[...] - model * vocab_rows
     owned = (local >= 0) & (local < vocab_rows)
     local = jnp.where(owned, local, 0)
     low = FBLK - 1
-    roll = (lax.broadcasted_iota(jnp.int32, local.shape, 1) - local) & low
-    places[...] = (local & ~low) | roll
-    fetch = pltpu.make_async_copy(places, reads, sems.at[0, 4])
-    fetch.start()
-    fetch.wait()
-    places[...] = owned.astype(jnp.int32)
+    starts[...] = local & ~low
+    rolls[...] = (lax.broadcasted_iota(jnp.int32, local.shape, 1) - local) & low
+    fetches = [pltpu.make_async_copy(starts, start_of, sems.at[0, 4]), pltpu.make_async_copy(rolls, roll_of, sems.at[0, 5])]
+    for fetch in fetches:
+        fetch.start()
+    get_lengths.wait()
+    get_train.wait()
+    grams(lengths, train, slabs)
+    for fetch in fetches:
+        fetch.wait()
+    starts[...] = owned.astype(jnp.int32)
+    for copy in get_table:
+        copy.wait()
+    get_factor.wait()
     lanes = lax.broadcasted_iota(jnp.int32, (ROWS, FBLK), 1)
 
-    def gather(piece, g):
-        columns = pl.ds(pl.multiple_of(g * FBLK, FBLK), FBLK)
-        gathered = jnp.zeros((ROWS, FBLK), jnp.bfloat16)
-        for j in range(FBLK):
-            place = reads[g, j]
-            block = table[pl.ds(piece * ROWS, ROWS), pl.ds(pl.multiple_of(place & ~low, FBLK), FBLK)]
-            gathered = jnp.where(lanes == j, pltpu.roll(block, place & low, 1), gathered)
-        held = places[pl.ds(g, 1), :].astype(jnp.float32)
-        gathered = (gathered.astype(jnp.float32) * held).astype(jnp.bfloat16)
-        rows = pl.ds(2 * each + piece * ROWS, ROWS)
-        sent[rows, columns] = gathered
-        own[rows, columns] = gathered
-
-    def project(g):
+    def group(g, carry):
         columns = pl.ds(pl.multiple_of(g * FBLK, FBLK), FBLK)
         get_delta(g).wait()
         output = lax.dot_general(
             delta[columns, :], factor[...], (((1,), (1,)), ((), ())), preferred_element_type=jnp.float32
         )
         looked[:, columns] = output.T
-
-    for piece in range(pieces):
-        get_table[piece].wait()
-        if piece == 1:
-            get_lengths.wait()
-            get_train.wait()
-            grams(lengths, train, slabs)
-        if piece == pieces - 1:
-            get_factor.wait()
-
-        def group(g, carry):
-            if piece == pieces - 1:
-                project(g)
-            gather(piece, g)
-            return carry
-
-        lax.fori_loop(0, groups, group, 0)
+        gathered = [jnp.zeros((ROWS, FBLK), jnp.bfloat16) for _ in range(proj // ROWS)]
+        for j in range(FBLK):
+            start, by, here = pl.multiple_of(start_of[g, j], FBLK), roll_of[g, j], lanes == j
+            for index in range(proj // ROWS):
+                block = table[pl.ds(index * ROWS, ROWS), pl.ds(start, FBLK)]
+                gathered[index] = jnp.where(here, pltpu.roll(block, by, 1), gathered[index])
+        held = starts[pl.ds(g, 1), :].astype(jnp.float32)
+        for index, value in enumerate(gathered):
+            value = (value.astype(jnp.float32) * held).astype(jnp.bfloat16)
+            rows = pl.ds(2 * each + index * ROWS, ROWS)
+            sent[rows, columns] = value
+            own[rows, columns] = value
+        return carry
+
+    lax.fori_loop(0, groups, group, 0)
     mine = looked[pl.ds(pl.multiple_of(model * each, each), each), :]
     other = looked[pl.ds(pl.multiple_of((1 - model) * each, each), each), :]
     for target, value in ((own, mine), (sent, other)):
@@ -271,9 +262,10 @@
 
 
 def queries_kernel(each, factors, slab, *refs):
-    after, high_out, low_out, again = refs if len(refs) == 4 else (None, *refs, None)
-    if again is not None:
-        again[...] = factors[...]
+    high_out, low_out = refs[-2:]
+    if len(refs) == 4:
+        source, high_out, low_out, copy = refs
+        copy[...] = source[...]
     tokens = factors.shape[1]
     proj = factors.shape[0] - 2 * each
     queries = high_out.shape[1]
@@ -310,7 +302,7 @@
     mine, rep, model = lax.axis_index("dp"), lax.axis_index("rep"), lax.axis_index("mp")
     for half, slabs in ((rep, own), (1 - rep, peers)):
         for shift in range(cycle):
-            owner = half * cycle + lax.rem(mine + cycle - shift, cycle)
+            owner = half * cycle + (mine ^ shift)
             slab = slabs[shift]
             blocks = unpack(slab[pl.ds(0, FBLK), :], slab[pl.ds(FBLK, 1), :])
             for index, block in enumerate(blocks):
@@ -340,12 +332,12 @@
             sums[order[len(sums)]] = both[:, index * FBLK:(index + 1) * FBLK]
     placed = []
     for source in range(cycle):
-        shift = lax.rem(mine + cycle - source, cycle)
+        shift = mine ^ source
         value = sums[0]
         for index in range(1, cycle):
             value = jnp.where(shift == index, sums[index], value)
         placed.append(value)
-    out[...] = jnp.stack(placed, axis=1).astype(jnp.bfloat16)
+    out[...] = jnp.concatenate(placed, axis=1).astype(jnp.bfloat16)
 
 
 def shape(dims, dtype):
@@ -369,6 +361,8 @@
         [
             pltpu.VMEM((tokens // FBLK, FBLK), jnp.int32),
             pltpu.VMEM((tokens // FBLK, FBLK), jnp.int32),
+            pltpu.VMEM((tokens // FBLK, FBLK), jnp.int32),
+            pltpu.SMEM((tokens // FBLK, FBLK), jnp.int32),
             pltpu.SMEM((tokens // FBLK, FBLK), jnp.int32),
             pltpu.VMEM((tokens, width), bf16),
             pltpu.VMEM((proj, vocab_rows), bf16),
@@ -385,8 +379,8 @@
         query_ids.reshape(tokens // FBLK, FBLK), query_delta, vocab_factor.T, output_factor.T,
         doc_lengths, train_grads,
     )
-    got = passed_along(sent, "mp", 1)
-    parts = [slabs[0]] + [passed_along(slabs[s], "dp", s) for s in range(1, cycle)]
+    got = swapped(sent, "mp", 1)
+    parts = [slabs[0]] + [swapped(slabs[s], "dp", s) for s in range(1, cycle)]
 
     factors = call(
         functools.partial(merge_kernel, each),
@@ -396,8 +390,8 @@
         flops=tokens * each,
         moved=8 * tokens * each * 4,
     )(own, got)
-    late = cycle // 2
-    gathered = [factors] + [passed_along(factors, "dp", s) if s != late else None for s in range(1, cycle)]
+    late = cycle - 1
+    gathered = [factors] + [swapped(factors, "dp", s) if s != late else None for s in range(1, cycle)]
 
     inverse = call(
         functools.partial(factor_kernel, train_rows * cycle, 1.0 / proj),
@@ -407,29 +401,29 @@
         flops=10 ** 10,
         moved=10 ** 6,
     )(*parts, factors)
-    inverses = [inverse] + [passed_along(inverse, "dp", s) for s in range(1, cycle)]
+    inverses = [inverse] + [swapped(inverse, "dp", s) for s in range(1, cycle)]
     highs, lows = {}, {}
-    for s in sorted(range(cycle), key=lambda shift: (shift == late, shift)):
-        first = s == 0
+    for s in range(cycle):
+        extra = {0: [inverse], 1: [factors]}.get(s, [])
         highs[s], lows[s], *again = call(
             functools.partial(queries_kernel, each),
-            [shape((feat, queries), bf16)] * 2 + [shape(factors.shape, bf16)] * first,
-            [VMEM, VMEM] + [HBM] * first,
+            [shape((feat, queries), bf16)] * 2 + [shape(factors.shape, bf16)] * (s == 1),
+            [VMEM, VMEM] + [HBM if s == 0 else VMEM] * len(extra),
             vmem=24,
             flops=2 * feat * tokens * queries,
             moved=6 * feat * queries,
-        )(gathered[s], parts[s], *[inverse] * first)
-        if first:
-            gathered[late] = passed_along(again[0], "dp", late)
+        )(gathered[s], parts[s], *extra)
+        if s == 1:
+            gathered[late] = swapped(again[0], "dp", late)
     handed = list(inverses)
     handed[late] = call(
         hand_kernel,
         shape((SLAB, FBLK), f32),
-        [VMEM] + [HBM] * (cycle - 2),
+        [VMEM] + [HBM] * (cycle - 1),
         vmem=16,
         moved=8 * SLAB * FBLK,
-    )(inverses[late], *[highs[s] for s in range(1, cycle) if s != late])
-    peers = [passed_along(slab, "rep", 1) for slab in handed]
+    )(inverses[late], *[highs[s] for s in range(cycle) if s != late])
+    peers = [swapped(slab, "rep", 1) for slab in handed]
 
     half_rows = train_rows // lax.axis_size("mp")
     pieces, order = [], []
@@ -444,17 +438,17 @@
             flops=2 * train_rows * feat * count * queries,
             moved=8 * feat * queries * count,
         )(*inverses, *peers, *[highs[s] for s in chosen], *[lows[s] for s in chosen], train_grads)
-        pieces += [kept, passed_along(outgoing, "mp", 1)]
+        pieces += [kept, swapped(outgoing, "mp", 1)]
         order += chosen
     total = call(
         functools.partial(total_kernel, order),
-        shape((half_rows, cycle, queries), bf16),
+        shape((half_rows, cycle * queries), bf16),
         [VMEM] * len(pieces),
         vmem=16,
         flops=half_rows * cycle * queries,
         moved=6 * half_rows * cycle * queries,
     )(*pieces)
-    return total[:, :, None, :]
+    return total.reshape(half_rows, cycle, 1, queries)
 
 
 def doc_matrix(lengths_row, count):
@@ -518,6 +512,7 @@
     owners = lax.axis_size("dp") * lax.axis_size("rep")
     fits = (
         train_grads.shape[1] == 2 * FBLK * owners
+        and lax.axis_size("dp") == 4
         and lax.axis_size("mp") == 2
         and lax.axis_size("rep") == 2
         and doc_lengths.shape[1] == FBLK

time: 66 us -> 63.5 us (0.962)
  Pallas kernels: 31.3 us -> 27.5 us
  waiting for transfers between devices: 10.3 us -> 13.5 us
  starting transfers between devices: 22.3 us -> 19.7 us
  local copies, waits for them, and re-layouts: 1.83 us -> 2.6 us
    ppermute x16, waiting for transfers between devices: 10.3 us -> 13.5 us  [swapped(): lax.ppermute(shard, axis, [(i, i ^ by) for i in range(lax.axis_size(axis))])]
    pallas_call x1, Pallas kernels: 13.9 us -> 11.2 us  [split_over_blocks(): call(first_kernel, [shape((2 * each + proj, tokens), bf16)] * 2 + [shape(...]
    ppermute x16, starting transfers between devices: 22.3 us -> 19.7 us  [swapped(): lax.ppermute(shard, axis, [(i, i ^ by) for i in range(lax.axis_size(axis))])]
    pallas_call x2, Pallas kernels: 1.27 us -> 0.13 us  [the longest x1 0.12 us: split_over_blocks(): call(functools.partial(total_kernel, order), shape((half_rows, cycle * qu...]
    reshape x0 -> x1, local copies, waits for them, and re-layouts: none -> 0.77 us  [split_over_blocks(): return total.reshape(half_rows, cycle, 1, queries)]
    unnamed x6 -> x8, local copies, waits for them, and re-layouts: 1.83 us -> 1.84 us
  transfers between devices with their start and end apart: 16 -> 16, of which waited for: 5 -> 5; matrix products, arithmetic and copies ran while one was open for 0% -> 0% of each run, Pallas kernels for 25% -> 26%
where the time goes in v9:
time: 63.5 us; the launch traced here: 63.3 us
  Pallas kernels  27.5 us (43%)
  starting transfers between devices  19.7 us (31%)
  waiting for transfers between devices  13.5 us (21%)
  local copies, waits for them, and re-layouts  2.6 us (4%)
    ppermute x16, starting transfers between devices, swapped(): lax.ppermute(shard, axis, [(i, i ^ by) for i in range(lax.axis_size(axis))])  19.7 us
    ppermute x16, waiting for transfers between devices, swapped(): lax.ppermute(shard, axis, [(i, i ^ by) for i in range(lax.axis_size(axis))])  13.5 us
    pallas_call x1, Pallas kernels, split_over_blocks(): call(first_kernel, [shape((2 * each + proj, tokens), bf16)] * 2 + [shape(...  11.2 us
    pallas_call x1, Pallas kernels, split_over_blocks(): call(functools.partial(factor_kernel, train_rows * cycle, 1.0 / proj), sh...  6.57 us
    pallas_call x4, Pallas kernels, split_over_blocks(): call(functools.partial(queries_kernel, each), [shape((feat, queries), bf1...  5.64 us
    pallas_call x2, Pallas kernels, split_over_blocks(): call(functools.partial(scores_kernel, cycle, count), [shape((half_rows, c...  3.9 us
    unnamed x8, local copies, waits for them, and re-layouts  1.84 us
  transfers between devices with their start and end apart: 16, of which 5 were waited for; matrix products, arithmetic and copies ran while one was open for 0% of the time, Pallas kernels for 26%

profile of v9, /device:TPU:0, one launch (start us, length us, event | category | flops | bytes accessed | tf_op | source)
XLA Modules:
  0.0 63.3 jit_solution(16664267886040181349)
XLA Ops:
  0.0 11.2 %shard_map.64 = (bf16[128,1024]{1,0:T(8,128)(2,1)}, bf16[128,1024]{1,0:T(8,128)(2,1)}, f32[136,128]{1,0:T(8,128)}, f32[136,128]{1,0:T(8,128)}, f32[136,128]{1,0:T(8,128)}, /*index=5*/f32[136,128]{1,0:T(8,128)}) custom-call(s32[8,128]{1,0:T(8,128)} %bitcast.6, bf16[1024,2048]{1,0:T(8,128)(2,1)} %delta_hbm.1, bf16[64,64128]{1,0:T(8,128)(2,1)} %bitcast.4, ...), custom_call_target="tpu_custom_call" | custom-call | flops 268435456 | bytes 24805376 | tf_op jit(solution)/shard_map/pallas_call | solution.py:357
  11.2 3.0 %collective-permute-start.3 = (bf16[128,1024]{1,0:T(8,128)(2,1)}, bf16[128,1024]{1,0:T(8,128)(2,1)S(1)}, u32[]{:S(2)}, u32[]{:S(2)}) collective-permute-start(bf16[128,1024]{1,0:T(8,128)(2,1)} %get-tuple-element.29), channel_id=1, source_target_pairs={{0,2},{2,0},{1,3},{3,1},{4,6},{6,4},{5,7},{7,5},{8,10},{10,8},{9,1... | collective-permute-start | bytes 786440 | tf_op jit(solution)/shard_map/ppermute | solution.py:33
  14.2 1.6 %collective-permute-start = (f32[136,128]{1,0:T(8,128)}, f32[136,128]{1,0:T(8,128)S(1)}, u32[]{:S(2)}, u32[]{:S(2)}) collective-permute-start(f32[136,128]{1,0:T(8,128)} %get-tuple-element.25), channel_id=1, source_target_pairs={{0,4},{4,0},{8,12},{12,8},{1,5},{5,1},{9,13},{13,9},{2,6},{6,2},{1... | collective-permute-start | bytes 208904 | tf_op jit(solution)/shard_map/ppermute | solution.py:33
  15.7 2.6 %collective-permute-start.1 = (f32[136,128]{1,0:T(8,128)}, f32[136,128]{1,0:T(8,128)S(1)}, u32[]{:S(2)}, u32[]{:S(2)}) collective-permute-start(f32[136,128]{1,0:T(8,128)} %get-tuple-element.26), channel_id=1, source_target_pairs={{0,8},{4,12},{8,0},{12,4},{1,9},{5,13},{9,1},{13,5},{2,10},{6,14},... | collective-permute-start | bytes 208904 | tf_op jit(solution)/shard_map/ppermute | solution.py:33
  18.3 0.2 collective-permute-start.2
  18.6 2.1 %collective-permute-done.3.got = bf16[128,1024]{1,0:T(8,128)(2,1)S(1)} collective-permute-done((bf16[128,1024]{1,0:T(8,128)(2,1)}, bf16[128,1024]{1,0:T(8,128)(2,1)S(1)}, u32[]{:S(2)}, u32[]{:S(2)}) %collective-permute-start.3) | collective-permute-done | bytes 262176 | tf_op jit(solution)/shard_map/ppermute | solution.py:33
  20.7 0.9 %copy-done.1 = bf16[128,1024]{1,0:T(8,128)(2,1)S(1)} copy-done((bf16[128,1024]{1,0:T(8,128)(2,1)S(1)}, bf16[128,1024]{1,0:T(8,128)(2,1)}, u32[]{:S(2)}) %copy-start.1) | copy-done | bytes 262168
  21.6 0.1 shard_map.65.refs_4_.factors.refs_0_
  21.7 1.9 %collective-permute-start.10 = (bf16[128,1024]{1,0:T(8,128)(2,1)S(1)}, bf16[128,1024]{1,0:T(8,128)(2,1)S(1)}, u32[]{:S(2)}, u32[]{:S(2)}) collective-permute-start(bf16[128,1024]{1,0:T(8,128)(2,1)S(1)} %shard_map.65.refs_4_.factors.refs_0_), channel_id=1, source_target_pairs={{0,4},{4,0},{8,12},{12,8},{1,5},{5,1},{9,13},{13,9},{2,6},{6,2},{1... | collective-permute-start | bytes 786440 | tf_op jit(solution)/shard_map/ppermute | solution.py:33
  23.6 2.6 %collective-permute-start.11 = (bf16[128,1024]{1,0:T(8,128)(2,1)S(1)}, bf16[128,1024]{1,0:T(8,128)(2,1)S(1)}, u32[]{:S(2)}, u32[]{:S(2)}) collective-permute-start(bf16[128,1024]{1,0:T(8,128)(2,1)S(1)} %shard_map.65.refs_4_.factors.refs_0_), channel_id=1, source_target_pairs={{0,8},{4,12},{8,0},{12,4},{1,9},{5,13},{9,1},{13,5},{2,10},{6,14},... | collective-permute-start | bytes 786440 | tf_op jit(solution)/shard_map/ppermute | solution.py:33
  26.2 0.0 collective-permute-done.refs_1_.slab
  26.2 0.0 collective-permute-done.1.refs_2_.slab
  26.2 0.0 collective-permute-done.2.refs_3_.slab
  26.2 0.0 copy-start.2
  26.2 0.9 %copy-done.2 = f32[136,128]{1,0:T(8,128)S(1)} copy-done((f32[136,128]{1,0:T(8,128)S(1)}, f32[136,128]{1,0:T(8,128)}, u32[]{:S(2)}) %copy-start.2) | copy-done | bytes 69656
  27.1 6.6 %shard_map.66.refs_0_ = f32[136,128]{1,0:T(8,128)S(1)} custom-call(f32[136,128]{1,0:T(8,128)S(1)} %copy-done.2, f32[136,128]{1,0:T(8,128)S(1)} %collective-permute-done.refs_1_.slab, f32[136,128]{1,0:T(8,128)S(1)} %collective-permute-done.1.refs_2_.slab, f32[136,128]{1,0:T(8,128)S(1)} %collective-permute-done.2.refs_3_.slab, ...), custom_call_target="tpu_custom_call" | custom-call | flops 10000000000 | bytes 1000000 | tf_op jit(solution)/shard_map/pallas_call | solution.py:396
  33.6 0.0 copy-start
  33.7 0.5 collective-permute-start.4
  34.2 0.3 collective-permute-start.5
  34.5 3.6 %collective-permute-start.6 = (f32[136,128]{1,0:T(8,128)S(1)}, f32[136,128]{1,0:T(8,128)S(1)}, u32[]{:S(2)}, u32[]{:S(2)}) collective-permute-start(f32[136,128]{1,0:T(8,128)S(1)} %shard_map.66.refs_0_), channel_id=1, source_target_pairs={{0,12},{4,8},{8,4},{12,0},{1,13},{5,9},{9,5},{13,1},{2,14},{6,10},... | collective-permute-start | bytes 208904 | tf_op jit(solution)/shard_map/ppermute | solution.py:33
  38.1 0.0 collective-permute-done.10.factors
  38.1 1.4 %shard_map.68 = (bf16[2048,128]{1,0:T(8,128)(2,1)S(1)}, bf16[2048,128]{1,0:T(8,128)(2,1)S(1)}, bf16[128,1024]{1,0:T(8,128)(2,1)S(1)}) custom-call(bf16[128,1024]{1,0:T(8,128)(2,1)S(1)} %collective-permute-done.10.factors, f32[136,128]{1,0:T(8,128)S(1)} %collective-permute-done.refs_1_.slab, bf16[128,1024]{1,0:T(8,128)(2,1)S(1)} %shard_map.65.refs_4_.factors.refs_0_), custom_call_target="tpu_custom_call" | custom-call | flops 536870912 | bytes 1572864 | tf_op jit(solution)/shard_map/pallas_call | solution.py:408
  39.5 0.5 collective-permute-start.14
  40.1 1.4 %shard_map.67 = (bf16[2048,128]{1,0:T(8,128)(2,1)S(1)}, bf16[2048,128]{1,0:T(8,128)(2,1)S(1)}) custom-call(bf16[128,1024]{1,0:T(8,128)(2,1)S(1)} %shard_map.65.refs_4_.factors.refs_0_, f32[136,128]{1,0:T(8,128)S(1)} %copy-done.3, f32[136,128]{1,0:T(8,128)S(1)} %shard_map.66.refs_0_), custom_call_target="tpu_custom_call" | custom-call | flops 536870912 | bytes 1572864 | tf_op jit(solution)/shard_map/pallas_call | solution.py:408
  41.5 0.0 collective-permute-done.4.refs_1_
  41.5 0.1 collective-permute-start.7
  41.6 6.3 %collective-permute-done.5.refs_2_ = f32[136,128]{1,0:T(8,128)S(1)} collective-permute-done((f32[136,128]{1,0:T(8,128)S(1)}, f32[136,128]{1,0:T(8,128)S(1)}, u32[]{:S(2)}, u32[]{:S(2)}) %collective-permute-start.5) | collective-permute-done | bytes 69664 | tf_op jit(solution)/shard_map/ppermute | solution.py:33
  47.9 0.0 collective-permute-start.8
  47.9 0.0 collective-permute-done.11.factors
  47.9 0.5 collective-permute-start.9
  48.4 1.4 %shard_map.69 = (bf16[2048,128]{1,0:T(8,128)(2,1)S(1)}, bf16[2048,128]{1,0:T(8,128)(2,1)S(1)}) custom-call(bf16[128,1024]{1,0:T(8,128)(2,1)S(1)} %collective-permute-done.11.factors, f32[136,128]{1,0:T(8,128)S(1)} %collective-permute-done.1.refs_2_.slab), custom_call_target="tpu_custom_call" | custom-call | flops 536870912 | bytes 1572864 | tf_op jit(solution)/shard_map/pallas_call | solution.py:408
  49.8 0.0 collective-permute-done.6.slab.refs_3_
  49.9 0.1 collective-permute-start.12
  49.9 0.0 collective-permute-done.7.refs_4_
  50.0 0.0 collective-permute-done.8.refs_5_
  50.0 0.0 collective-permute-done.9.refs_6_
  50.0 1.2 %collective-permute-done.12.refs_7_ = f32[136,128]{1,0:T(8,128)S(1)} collective-permute-done((f32[136,128]{1,0:T(8,128)S(1)}, f32[136,128]{1,0:T(8,128)S(1)}, u32[]{:S(2)}, u32[]{:S(2)}) %collective-permute-start.12) | collective-permute-done | bytes 69664 | tf_op jit(solution)/shard_map/ppermute | solution.py:33
  51.2 0.0 copy-done
  51.2 2.5 %shard_map.71 = (bf16[256,384]{1,0:T(8,128)(2,1)S(1)}, bf16[256,384]{1,0:T(8,128)(2,1)S(1)}) custom-call(f32[136,128]{1,0:T(8,128)S(1)} %shard_map.66.refs_0_, f32[136,128]{1,0:T(8,128)S(1)} %collective-permute-done.4.refs_1_, f32[136,128]{1,0:T(8,128)S(1)} %collective-permute-done.5.refs_2_, f32[136,128]{1,0:T(8,128)S(1)} %collective-permute-done.6.slab.refs_3_, ...), custom_call_target="tpu_custom_call" | custom-call | flops 805306368 | bytes 6291456 | tf_op jit(solution)/shard_map/pallas_call | solution.py:432
  53.7 1.6 %collective-permute-start.13 = (bf16[256,384]{1,0:T(8,128)(2,1)S(1)}, bf16[256,384]{1,0:T(8,128)(2,1)S(1)}, u32[]{:S(2)}, u32[]{:S(2)}) collective-permute-start(bf16[256,384]{1,0:T(8,128)(2,1)S(1)} %get-tuple-element.37), channel_id=1, source_target_pairs={{0,2},{2,0},{1,3},{3,1},{4,6},{6,4},{5,7},{7,5},{8,10},{10,8},{9,1... | collective-permute-start | bytes 589832 | tf_op jit(solution)/shard_map/ppermute | solution.py:33
  55.3 0.0 collective-permute-done.14.factors
  55.3 1.4 %shard_map.72 = (bf16[2048,128]{1,0:T(8,128)(2,1)S(1)}, bf16[2048,128]{1,0:T(8,128)(2,1)S(1)}) custom-call(bf16[128,1024]{1,0:T(8,128)(2,1)S(1)} %collective-permute-done.14.factors, f32[136,128]{1,0:T(8,128)S(1)} %collective-permute-done.2.refs_3_.slab), custom_call_target="tpu_custom_call" | custom-call | flops 536870912 | bytes 1572864 | tf_op jit(solution)/shard_map/pallas_call | solution.py:408
  56.7 1.4 %shard_map.73 = (bf16[256,128]{1,0:T(8,128)(2,1)S(1)}, bf16[256,128]{1,0:T(8,128)(2,1)S(1)}) custom-call(f32[136,128]{1,0:T(8,128)S(1)} %shard_map.66.refs_0_, f32[136,128]{1,0:T(8,128)S(1)} %collective-permute-done.4.refs_1_, f32[136,128]{1,0:T(8,128)S(1)} %collective-permute-done.5.refs_2_, f32[136,128]{1,0:T(8,128)S(1)} %collective-permute-done.6.slab.refs_3_, ...), custom_call_target="tpu_custom_call" | custom-call | flops 268435456 | bytes 2097152 | tf_op jit(solution)/shard_map/pallas_call | solution.py:432
  58.1 0.6 collective-permute-start.15
  58.7 2.2 %collective-permute-done.13.refs_1_ = bf16[256,384]{1,0:T(8,128)(2,1)S(1)} collective-permute-done((bf16[256,384]{1,0:T(8,128)(2,1)S(1)}, bf16[256,384]{1,0:T(8,128)(2,1)S(1)}, u32[]{:S(2)}, u32[]{:S(2)}) %collective-permute-start.13) | collective-permute-done | bytes 196640 | tf_op jit(solution)/shard_map/ppermute | solution.py:33
  60.9 1.6 %collective-permute-done.15.refs_3_ = bf16[256,128]{1,0:T(8,128)(2,1)S(1)} collective-permute-done((bf16[256,128]{1,0:T(8,128)(2,1)S(1)}, bf16[256,128]{1,0:T(8,128)(2,1)S(1)}, u32[]{:S(2)}, u32[]{:S(2)}) %collective-permute-start.15) | collective-permute-done | bytes 65568 | tf_op jit(solution)/shard_map/ppermute | solution.py:33
  62.4 0.1 shard_map.74
  62.5 0.8 %reshape.7 = bf16[256,4,1,128]{3,1,0,2:T(4,128)(2,1)} reshape(bf16[256,512]{1,0:T(8,128)(2,1)S(1)} %shard_map.74) | data formatting | bytes 524288 | tf_op jit(solution)/shard_map/reshape | solution.py:451
  (4 shorter events, 0.0 us)
Async XLA Ops:
  11.2 9.5 %collective-permute-start.3 = (bf16[128,1024]{1,0:T(8,128)(2,1)}, bf16[128,1024]{1,0:T(8,128)(2,1)S(1)}, u32[]{:S(2)}, u32[]{:S(2)}) collective-permute-start(bf16[128,1024]{1,0:T(8,128)(2,1)} %get-tuple-element.29), channel_id=1, source_target_pairs={{0,2},{2,0},{1,3},{3,1},{4,6},{6,4},{5,7},{7,5},{8,10},{10,8},{9,1... | collective-permute-start | bytes 786440 | tf_op jit(solution)/shard_map/ppermute | solution.py:33
  14.2 12.0 %collective-permute-start = (f32[136,128]{1,0:T(8,128)}, f32[136,128]{1,0:T(8,128)S(1)}, u32[]{:S(2)}, u32[]{:S(2)}) collective-permute-start(f32[136,128]{1,0:T(8,128)} %get-tuple-element.25), channel_id=1, source_target_pairs={{0,4},{4,0},{8,12},{12,8},{1,5},{5,1},{9,13},{13,9},{2,6},{6,2},{1... | collective-permute-start | bytes 208904 | tf_op jit(solution)/shard_map/ppermute | solution.py:33
  15.7 10.4 %collective-permute-start.1 = (f32[136,128]{1,0:T(8,128)}, f32[136,128]{1,0:T(8,128)S(1)}, u32[]{:S(2)}, u32[]{:S(2)}) collective-permute-start(f32[136,128]{1,0:T(8,128)} %get-tuple-element.26), channel_id=1, source_target_pairs={{0,8},{4,12},{8,0},{12,4},{1,9},{5,13},{9,1},{13,5},{2,10},{6,14},... | collective-permute-start | bytes 208904 | tf_op jit(solution)/shard_map/ppermute | solution.py:33
  18.3 7.9 %collective-permute-start.2 = (f32[136,128]{1,0:T(8,128)}, f32[136,128]{1,0:T(8,128)S(1)}, u32[]{:S(2)}, u32[]{:S(2)}) collective-permute-start(f32[136,128]{1,0:T(8,128)} %get-tuple-element.27), channel_id=1, source_target_pairs={{0,12},{4,8},{8,4},{12,0},{1,13},{5,9},{9,5},{13,1},{2,14},{6,10},... | collective-permute-start | bytes 208904 | tf_op jit(solution)/shard_map/ppermute | solution.py:33
  20.7 1.0 %copy-start.1 = (bf16[128,1024]{1,0:T(8,128)(2,1)S(1)}, bf16[128,1024]{1,0:T(8,128)(2,1)}, u32[]{:S(2)}) copy-start(bf16[128,1024]{1,0:T(8,128)(2,1)} %get-tuple-element.28.own) | copy-start | bytes 786436
  21.7 16.4 %collective-permute-start.10 = (bf16[128,1024]{1,0:T(8,128)(2,1)S(1)}, bf16[128,1024]{1,0:T(8,128)(2,1)S(1)}, u32[]{:S(2)}, u32[]{:S(2)}) collective-permute-start(bf16[128,1024]{1,0:T(8,128)(2,1)S(1)} %shard_map.65.refs_4_.factors.refs_0_), channel_id=1, source_target_pairs={{0,4},{4,0},{8,12},{12,8},{1,5},{5,1},{9,13},{13,9},{2,6},{6,2},{1... | collective-permute-start | bytes 786440 | tf_op jit(solution)/shard_map/ppermute | solution.py:33
  23.6 24.3 %collective-permute-start.11 = (bf16[128,1024]{1,0:T(8,128)(2,1)S(1)}, bf16[128,1024]{1,0:T(8,128)(2,1)S(1)}, u32[]{:S(2)}, u32[]{:S(2)}) collective-permute-start(bf16[128,1024]{1,0:T(8,128)(2,1)S(1)} %shard_map.65.refs_4_.factors.refs_0_), channel_id=1, source_target_pairs={{0,8},{4,12},{8,0},{12,4},{1,9},{5,13},{9,1},{13,5},{2,10},{6,14},... | collective-permute-start | bytes 786440 | tf_op jit(solution)/shard_map/ppermute | solution.py:33
  26.2 0.9 %copy-start.2 = (f32[136,128]{1,0:T(8,128)S(1)}, f32[136,128]{1,0:T(8,128)}, u32[]{:S(2)}) copy-start(f32[136,128]{1,0:T(8,128)} %get-tuple-element.24.refs_0_.slab) | copy-start | bytes 208900
  27.1 13.0 %copy-start.3 = (f32[136,128]{1,0:T(8,128)S(1)}, f32[136,128]{1,0:T(8,128)}, u32[]{:S(2)}) copy-start(f32[136,128]{1,0:T(8,128)} %get-tuple-element.24.refs_0_.slab) | copy-start | bytes 208900
  33.6 17.5 %copy-start = (bf16[512,2048]{1,0:T(8,128)(2,1)S(1)}, bf16[512,2048]{1,0:T(8,128)(2,1)}, u32[]{:S(2)}) copy-start(bf16[512,2048]{1,0:T(8,128)(2,1)} %refs_10_.1) | copy-start | bytes 6291460
  33.7 7.8 %collective-permute-start.4 = (f32[136,128]{1,0:T(8,128)S(1)}, f32[136,128]{1,0:T(8,128)S(1)}, u32[]{:S(2)}, u32[]{:S(2)}) collective-permute-start(f32[136,128]{1,0:T(8,128)S(1)} %shard_map.66.refs_0_), channel_id=1, source_target_pairs={{0,4},{4,0},{8,12},{12,8},{1,5},{5,1},{9,13},{13,9},{2,6},{6,2},{1... | collective-permute-start | bytes 208904 | tf_op jit(solution)/shard_map/ppermute | solution.py:33
  34.2 13.7 %collective-permute-start.5 = (f32[136,128]{1,0:T(8,128)S(1)}, f32[136,128]{1,0:T(8,128)S(1)}, u32[]{:S(2)}, u32[]{:S(2)}) collective-permute-start(f32[136,128]{1,0:T(8,128)S(1)} %shard_map.66.refs_0_), channel_id=1, source_target_pairs={{0,8},{4,12},{8,0},{12,4},{1,9},{5,13},{9,1},{13,5},{2,10},{6,14},... | collective-permute-start | bytes 208904 | tf_op jit(solution)/shard_map/ppermute | solution.py:33
  34.5 15.3 %collective-permute-start.6 = (f32[136,128]{1,0:T(8,128)S(1)}, f32[136,128]{1,0:T(8,128)S(1)}, u32[]{:S(2)}, u32[]{:S(2)}) collective-permute-start(f32[136,128]{1,0:T(8,128)S(1)} %shard_map.66.refs_0_), channel_id=1, source_target_pairs={{0,12},{4,8},{8,4},{12,0},{1,13},{5,9},{9,5},{13,1},{2,14},{6,10},... | collective-permute-start | bytes 208904 | tf_op jit(solution)/shard_map/ppermute | solution.py:33
  39.5 15.8 %collective-permute-start.14 = (bf16[128,1024]{1,0:T(8,128)(2,1)S(1)}, bf16[128,1024]{1,0:T(8,128)(2,1)S(1)}, u32[]{:S(2)}, u32[]{:S(2)}) collective-permute-start(bf16[128,1024]{1,0:T(8,128)(2,1)S(1)} %get-tuple-element.38), channel_id=1, source_target_pairs={{0,12},{4,8},{8,4},{12,0},{1,13},{5,9},{9,5},{13,1},{2,14},{6,10},... | collective-permute-start | bytes 786440 | tf_op jit(solution)/shard_map/ppermute | solution.py:33
  41.5 8.5 %collective-permute-start.7 = (f32[136,128]{1,0:T(8,128)S(1)}, f32[136,128]{1,0:T(8,128)S(1)}, u32[]{:S(2)}, u32[]{:S(2)}) collective-permute-start(f32[136,128]{1,0:T(8,128)S(1)} %shard_map.66.refs_0_), channel_id=1, source_target_pairs={{0,1},{1,0},{2,3},{3,2},{4,5},{5,4},{6,7},{7,6},{8,9},{9,8},{10,11... | collective-permute-start | bytes 208904 | tf_op jit(solution)/shard_map/ppermute | solution.py:33
  47.9 2.0 %collective-permute-start.8 = (f32[136,128]{1,0:T(8,128)S(1)}, f32[136,128]{1,0:T(8,128)S(1)}, u32[]{:S(2)}, u32[]{:S(2)}) collective-permute-start(f32[136,128]{1,0:T(8,128)S(1)} %collective-permute-done.4.refs_1_), channel_id=1, source_target_pairs={{0,1},{1,0},{2,3},{3,2},{4,5},{5,4},{6,7},{7,6},{8,9},{9,8},{10,11... | collective-permute-start | bytes 208904 | tf_op jit(solution)/shard_map/ppermute | solution.py:33
  47.9 2.0 %collective-permute-start.9 = (f32[136,128]{1,0:T(8,128)S(1)}, f32[136,128]{1,0:T(8,128)S(1)}, u32[]{:S(2)}, u32[]{:S(2)}) collective-permute-start(f32[136,128]{1,0:T(8,128)S(1)} %collective-permute-done.5.refs_2_), channel_id=1, source_target_pairs={{0,1},{1,0},{2,3},{3,2},{4,5},{5,4},{6,7},{7,6},{8,9},{9,8},{10,11... | collective-permute-start | bytes 208904 | tf_op jit(solution)/shard_map/ppermute | solution.py:33
  49.9 1.3 %collective-permute-start.12 = (f32[136,128]{1,0:T(8,128)S(1)}, f32[136,128]{1,0:T(8,128)S(1)}, u32[]{:S(2)}, u32[]{:S(2)}) collective-permute-start(f32[136,128]{1,0:T(8,128)S(1)} %shard_map.70), channel_id=1, source_target_pairs={{0,1},{1,0},{2,3},{3,2},{4,5},{5,4},{6,7},{7,6},{8,9},{9,8},{10,11... | collective-permute-start | bytes 208904 | tf_op jit(solution)/shard_map/ppermute | solution.py:33
  53.7 7.1 %collective-permute-start.13 = (bf16[256,384]{1,0:T(8,128)(2,1)S(1)}, bf16[256,384]{1,0:T(8,128)(2,1)S(1)}, u32[]{:S(2)}, u32[]{:S(2)}) collective-permute-start(bf16[256,384]{1,0:T(8,128)(2,1)S(1)} %get-tuple-element.37), channel_id=1, source_target_pairs={{0,2},{2,0},{1,3},{3,1},{4,6},{6,4},{5,7},{7,5},{8,10},{10,8},{9,1... | collective-permute-start | bytes 589832 | tf_op jit(solution)/shard_map/ppermute | solution.py:33
  58.1 4.3 %collective-permute-start.15 = (bf16[256,128]{1,0:T(8,128)(2,1)S(1)}, bf16[256,128]{1,0:T(8,128)(2,1)S(1)}, u32[]{:S(2)}, u32[]{:S(2)}) collective-permute-start(bf16[256,128]{1,0:T(8,128)(2,1)S(1)} %get-tuple-element.42), channel_id=1, source_target_pairs={{0,2},{2,0},{1,3},{3,1},{4,6},{6,4},{5,7},{7,5},{8,10},{10,8},{9,1... | collective-permute-start | bytes 196616 | tf_op jit(solution)/shard_map/ppermute | solution.py:33

commit v10 on v9

--- a/solution.py
+++ b/solution.py
@@ -261,7 +261,8 @@
     out[rows, :] = own[rows, :] + got[rows, :]
 
 
-def queries_kernel(each, factors, slab, *refs):
+def queries_kernel(each, ends_of, factors, slab, *refs):
+    far, refs = (refs[0], refs[1:]) if ends_of else (None, refs)
     high_out, low_out = refs[-2:]
     if len(refs) == 4:
         source, high_out, low_out, copy = refs
@@ -269,6 +270,15 @@
     tokens = factors.shape[1]
     proj = factors.shape[0] - 2 * each
     queries = high_out.shape[1]
+    mine = lax.axis_index("dp")
+
+    def part(first, count):
+        value = factors[pl.ds(first, count), :].astype(jnp.float32)
+        if ends_of:
+            at_end = (mine == 0) | (mine == ends_of - 1)
+            value = jnp.where(at_end, far[pl.ds(first, count), :].astype(jnp.float32), value)
+        return value
+
     lengths = slab[pl.ds(FBLK + 1, 1), :]
     upto = jnp.where(square(0) <= square(1), 1.0, 0.0).astype(jnp.bfloat16)
     ends = lax.dot_general(
@@ -278,8 +288,8 @@
     starts = ends - lengths
     place = lax.broadcasted_iota(jnp.int32, (tokens, queries), 0).astype(jnp.float32)
     inside = jnp.where((place >= starts) & (place < ends), 1.0, 0.0).astype(jnp.bfloat16)
-    output = factors[pl.ds(0, each), :].astype(jnp.float32) + factors[pl.ds(each, each), :].astype(jnp.float32)
-    inputs = factors[pl.ds(2 * each, proj), :].astype(jnp.float32)
+    output = part(0, each) + part(each, each)
+    inputs = part(2 * each, proj)
     step = 8
     for start in range(0, each, step):
         grads = jnp.concatenate(
@@ -402,19 +412,23 @@
         moved=10 ** 6,
     )(*parts, factors)
     inverses = [inverse] + [swapped(inverse, "dp", s) for s in range(1, cycle)]
-    highs, lows = {}, {}
+    copies = {0: [inverse], 1: [factors], 2: [gathered[2]]}
+    highs, lows, far = {}, {}, []
     for s in range(cycle):
-        extra = {0: [inverse], 1: [factors]}.get(s, [])
+        extra = copies.get(s, far)
+        copied = s in (1, 2)
         highs[s], lows[s], *again = call(
-            functools.partial(queries_kernel, each),
-            [shape((feat, queries), bf16)] * 2 + [shape(factors.shape, bf16)] * (s == 1),
+            functools.partial(queries_kernel, each, cycle if s == late else 0),
+            [shape((feat, queries), bf16)] * 2 + [shape(factors.shape, bf16)] * copied,
             [VMEM, VMEM] + [HBM if s == 0 else VMEM] * len(extra),
             vmem=24,
             flops=2 * feat * tokens * queries,
             moved=6 * feat * queries,
         )(gathered[s], parts[s], *extra)
         if s == 1:
-            gathered[late] = swapped(again[0], "dp", late)
+            gathered[late] = lax.ppermute(again[0], "dp", [(1, 2), (2, 1)])
+        if s == 2:
+            far = [lax.ppermute(again[0], "dp", [(1, 0), (2, 3)])]
     handed = list(inverses)
     handed[late] = call(
         hand_kernel,

time: 63.5 us -> 59.7 us (0.940)
  waiting for transfers between devices: 13.5 us -> 7.42 us
  starting transfers between devices: 19.7 us -> 21.8 us
    ppermute x16 -> x15, waiting for transfers between devices: 13.5 us -> 6.67 us  [swapped(): lax.ppermute(shard, axis, [(i, i ^ by) for i in range(lax.axis_size(axis))])]
    ppermute x0 -> x2, starting transfers between devices: none -> 2.15 us  [the longest x1 1.47 us: split_over_blocks(): far = [lax.ppermute(again[0], 'dp', [(1, 0), (2, 3)])]]
    ppermute x0 -> x2, waiting for transfers between devices: none -> 0.75 us  [the longest x1 0.75 us: split_over_blocks(): far = [lax.ppermute(again[0], 'dp', [(1, 0), (2, 3)])]]
    ppermute x16 -> x15, starting transfers between devices: 19.7 us -> 19.7 us  [swapped(): lax.ppermute(shard, axis, [(i, i ^ by) for i in range(lax.axis_size(axis))])]
  transfers between devices with their start and end apart: 16 -> 17, of which waited for: 5 -> 8; matrix products, arithmetic and copies ran while one was open for 0% -> 0% of each run, Pallas kernels for 26% -> 27%
where the time goes in v10:
time: 59.7 us; the launch traced here: 59.5 us
  Pallas kernels  27.5 us (46%)
  starting transfers between devices  21.8 us (37%)
  waiting for transfers between devices  7.42 us (12%)
  local copies, waits for them, and re-layouts  2.6 us (4%)
    ppermute x15, starting transfers between devices, swapped(): lax.ppermute(shard, axis, [(i, i ^ by) for i in range(lax.axis_size(axis))])  19.7 us
    pallas_call x1, Pallas kernels, split_over_blocks(): call(first_kernel, [shape((2 * each + proj, tokens), bf16)] * 2 + [shape(...  11.1 us
    ppermute x15, waiting for transfers between devices, swapped(): lax.ppermute(shard, axis, [(i, i ^ by) for i in range(lax.axis_size(axis))])  6.67 us
    pallas_call x1, Pallas kernels, split_over_blocks(): call(functools.partial(factor_kernel, train_rows * cycle, 1.0 / proj), sh...  6.57 us
    pallas_call x4, Pallas kernels, split_over_blocks(): call(functools.partial(queries_kernel, each, cycle if s == late else 0),...  5.66 us
    pallas_call x2, Pallas kernels, split_over_blocks(): call(functools.partial(scores_kernel, cycle, count), [shape((half_rows, c...  3.91 us
    unnamed x8, local copies, waits for them, and re-layouts  1.84 us
    ppermute x1, starting transfers between devices, split_over_blocks(): far = [lax.ppermute(again[0], 'dp', [(1, 0), (2, 3)])]  1.47 us
  transfers between devices with their start and end apart: 17, of which 8 were waited for; matrix products, arithmetic and copies ran while one was open for 0% of the time, Pallas kernels for 27%

profile of v10, /device:TPU:0, one launch (start us, length us, event | category | flops | bytes accessed | tf_op | source)
XLA Modules:
  0.0 59.5 jit_solution(3958273328030421557)
XLA Ops:
  0.0 11.1 %shard_map.64 = (bf16[128,1024]{1,0:T(8,128)(2,1)}, bf16[128,1024]{1,0:T(8,128)(2,1)}, f32[136,128]{1,0:T(8,128)}, f32[136,128]{1,0:T(8,128)}, f32[136,128]{1,0:T(8,128)}, /*index=5*/f32[136,128]{1,0:T(8,128)}) custom-call(s32[8,128]{1,0:T(8,128)} %bitcast.6, bf16[1024,2048]{1,0:T(8,128)(2,1)} %delta_hbm.1, bf16[64,64128]{1,0:T(8,128)(2,1)} %bitcast.4, ...), custom_call_target="tpu_custom_call" | custom-call | flops 268435456 | bytes 24805376 | tf_op jit(solution)/shard_map/pallas_call | solution.py:367
  11.2 3.0 %collective-permute-start.3 = (bf16[128,1024]{1,0:T(8,128)(2,1)}, bf16[128,1024]{1,0:T(8,128)(2,1)S(1)}, u32[]{:S(2)}, u32[]{:S(2)}) collective-permute-start(bf16[128,1024]{1,0:T(8,128)(2,1)} %get-tuple-element.30), channel_id=1, source_target_pairs={{0,2},{2,0},{1,3},{3,1},{4,6},{6,4},{5,7},{7,5},{8,10},{10,8},{9,1... | collective-permute-start | bytes 786440 | tf_op jit(solution)/shard_map/ppermute | solution.py:33
  14.2 1.6 %collective-permute-start = (f32[136,128]{1,0:T(8,128)}, f32[136,128]{1,0:T(8,128)S(1)}, u32[]{:S(2)}, u32[]{:S(2)}) collective-permute-start(f32[136,128]{1,0:T(8,128)} %get-tuple-element.26), channel_id=1, source_target_pairs={{0,4},{4,0},{8,12},{12,8},{1,5},{5,1},{9,13},{13,9},{2,6},{6,2},{1... | collective-permute-start | bytes 208904 | tf_op jit(solution)/shard_map/ppermute | solution.py:33
  15.8 2.6 %collective-permute-start.1 = (f32[136,128]{1,0:T(8,128)}, f32[136,128]{1,0:T(8,128)S(1)}, u32[]{:S(2)}, u32[]{:S(2)}) collective-permute-start(f32[136,128]{1,0:T(8,128)} %get-tuple-element.27), channel_id=1, source_target_pairs={{0,8},{4,12},{8,0},{12,4},{1,9},{5,13},{9,1},{13,5},{2,10},{6,14},... | collective-permute-start | bytes 208904 | tf_op jit(solution)/shard_map/ppermute | solution.py:33
  18.3 0.2 collective-permute-start.2
  18.6 2.1 %collective-permute-done.3.got = bf16[128,1024]{1,0:T(8,128)(2,1)S(1)} collective-permute-done((bf16[128,1024]{1,0:T(8,128)(2,1)}, bf16[128,1024]{1,0:T(8,128)(2,1)S(1)}, u32[]{:S(2)}, u32[]{:S(2)}) %collective-permute-start.3) | collective-permute-done | bytes 262176 | tf_op jit(solution)/shard_map/ppermute | solution.py:33
  20.7 0.9 %copy-done.1 = bf16[128,1024]{1,0:T(8,128)(2,1)S(1)} copy-done((bf16[128,1024]{1,0:T(8,128)(2,1)S(1)}, bf16[128,1024]{1,0:T(8,128)(2,1)}, u32[]{:S(2)}) %copy-start.1) | copy-done | bytes 262168
  21.6 0.1 shard_map.65.refs_4_.factors.refs_0_
  21.7 2.9 %collective-permute-start.11 = (bf16[128,1024]{1,0:T(8,128)(2,1)S(1)}, bf16[128,1024]{1,0:T(8,128)(2,1)S(1)}, u32[]{:S(2)}, u32[]{:S(2)}) collective-permute-start(bf16[128,1024]{1,0:T(8,128)(2,1)S(1)} %shard_map.65.refs_4_.factors.refs_0_), channel_id=1, source_target_pairs={{0,8},{4,12},{8,0},{12,4},{1,9},{5,13},{9,1},{13,5},{2,10},{6,14},... | collective-permute-start | bytes 786440 | tf_op jit(solution)/shard_map/ppermute | solution.py:33
  24.6 1.6 %collective-permute-start.10 = (bf16[128,1024]{1,0:T(8,128)(2,1)S(1)}, bf16[128,1024]{1,0:T(8,128)(2,1)S(1)}, u32[]{:S(2)}, u32[]{:S(2)}) collective-permute-start(bf16[128,1024]{1,0:T(8,128)(2,1)S(1)} %shard_map.65.refs_4_.factors.refs_0_), channel_id=1, source_target_pairs={{0,4},{4,0},{8,12},{12,8},{1,5},{5,1},{9,13},{13,9},{2,6},{6,2},{1... | collective-permute-start | bytes 786440 | tf_op jit(solution)/shard_map/ppermute | solution.py:33
  26.2 0.0 collective-permute-done.refs_1_.slab
  26.2 0.0 collective-permute-done.1.refs_2_.slab
  26.2 0.0 collective-permute-done.2.refs_3_.slab
  26.2 0.9 %copy-done.2 = f32[136,128]{1,0:T(8,128)S(1)} copy-done((f32[136,128]{1,0:T(8,128)S(1)}, f32[136,128]{1,0:T(8,128)}, u32[]{:S(2)}) %copy-start.2) | copy-done | bytes 69656
  27.1 6.6 %shard_map.66.refs_0_ = f32[136,128]{1,0:T(8,128)S(1)} custom-call(f32[136,128]{1,0:T(8,128)S(1)} %copy-done.2, f32[136,128]{1,0:T(8,128)S(1)} %collective-permute-done.refs_1_.slab, f32[136,128]{1,0:T(8,128)S(1)} %collective-permute-done.1.refs_2_.slab, f32[136,128]{1,0:T(8,128)S(1)} %collective-permute-done.2.refs_3_.slab, ...), custom_call_target="tpu_custom_call" | custom-call | flops 10000000000 | bytes 1000000 | tf_op jit(solution)/shard_map/pallas_call | solution.py:406
  33.6 0.0 copy-start
  33.7 0.1 collective-permute-start.7
  33.7 0.3 collective-permute-start.6
  34.0 1.7 %collective-permute-start.5 = (f32[136,128]{1,0:T(8,128)S(1)}, f32[136,128]{1,0:T(8,128)S(1)}, u32[]{:S(2)}, u32[]{:S(2)}) collective-permute-start(f32[136,128]{1,0:T(8,128)S(1)} %shard_map.66.refs_0_), channel_id=1, source_target_pairs={{0,8},{4,12},{8,0},{12,4},{1,9},{5,13},{9,1},{13,5},{2,10},{6,14},... | collective-permute-start | bytes 208904 | tf_op jit(solution)/shard_map/ppermute | solution.py:33
  35.7 0.6 collective-permute-done.10.factors
  36.3 1.9 %collective-permute-start.4 = (f32[136,128]{1,0:T(8,128)S(1)}, f32[136,128]{1,0:T(8,128)S(1)}, u32[]{:S(2)}, u32[]{:S(2)}) collective-permute-start(f32[136,128]{1,0:T(8,128)S(1)} %shard_map.66.refs_0_), channel_id=1, source_target_pairs={{0,4},{4,0},{8,12},{12,8},{1,5},{5,1},{9,13},{13,9},{2,6},{6,2},{1... | collective-permute-start | bytes 208904 | tf_op jit(solution)/shard_map/ppermute | solution.py:33
  38.2 1.4 %shard_map.68 = (bf16[2048,128]{1,0:T(8,128)(2,1)S(1)}, bf16[2048,128]{1,0:T(8,128)(2,1)S(1)}, bf16[128,1024]{1,0:T(8,128)(2,1)S(1)}) custom-call(bf16[128,1024]{1,0:T(8,128)(2,1)S(1)} %collective-permute-done.10.factors, f32[136,128]{1,0:T(8,128)S(1)} %collective-permute-done.refs_1_.slab, bf16[128,1024]{1,0:T(8,128)(2,1)S(1)} %shard_map.65.refs_4_.factors.refs_0_), custom_call_target="tpu_custom_call" | custom-call | flops 536870912 | bytes 1572864 | tf_op jit(solution)/shard_map/pallas_call | solution.py:420
  39.6 0.0 collective-permute-done.11.factors.refs_0_
  39.6 0.7 %collective-permute-start.14 = (bf16[128,1024]{1,0:T(8,128)(2,1)S(1)}, bf16[128,1024]{1,0:T(8,128)(2,1)S(1)}, u32[]{:S(2)}, u32[]{:S(2)}) collective-permute-start(bf16[128,1024]{1,0:T(8,128)(2,1)S(1)} %get-tuple-element.39), channel_id=1, source_target_pairs={{4,8},{8,4},{5,9},{9,5},{6,10},{10,6},{7,11},{11,7},{20,24},{24,20... | collective-permute-start | bytes 786440 | tf_op jit(solution)/shard_map/ppermute | solution.py:429
  40.3 1.4 %shard_map.69 = (bf16[2048,128]{1,0:T(8,128)(2,1)S(1)}, bf16[2048,128]{1,0:T(8,128)(2,1)S(1)}, bf16[128,1024]{1,0:T(8,128)(2,1)S(1)}) custom-call(bf16[128,1024]{1,0:T(8,128)(2,1)S(1)} %collective-permute-done.11.factors.refs_0_, f32[136,128]{1,0:T(8,128)S(1)} %collective-permute-done.1.refs_2_.slab, ...), custom_call_target="tpu_custom_call" | custom-call | flops 536870912 | bytes 1572864 | tf_op jit(solution)/shard_map/pallas_call | solution.py:420
  41.7 0.0 collective-permute-done.6.slab.refs_3_
  41.8 1.5 %collective-permute-start.15 = (bf16[128,1024]{1,0:T(8,128)(2,1)S(1)}, bf16[128,1024]{1,0:T(8,128)(2,1)S(1)}, u32[]{:S(2)}, u32[]{:S(2)}) collective-permute-start(bf16[128,1024]{1,0:T(8,128)(2,1)S(1)} %get-tuple-element.40), channel_id=1, source_target_pairs={{4,0},{8,12},{5,1},{9,13},{6,2},{10,14},{7,3},{11,15},{20,16},{24,... | collective-permute-start | bytes 786440 | tf_op jit(solution)/shard_map/ppermute | solution.py:431
  43.2 1.4 %shard_map.67 = (bf16[2048,128]{1,0:T(8,128)(2,1)S(1)}, bf16[2048,128]{1,0:T(8,128)(2,1)S(1)}) custom-call(bf16[128,1024]{1,0:T(8,128)(2,1)S(1)} %shard_map.65.refs_4_.factors.refs_0_, f32[136,128]{1,0:T(8,128)S(1)} %copy-done.3, f32[136,128]{1,0:T(8,128)S(1)} %shard_map.66.refs_0_), custom_call_target="tpu_custom_call" | custom-call | flops 536870912 | bytes 1572864 | tf_op jit(solution)/shard_map/pallas_call | solution.py:420
  44.7 0.0 collective-permute-done.5.refs_2_
  44.7 0.1 collective-permute-start.9
  44.7 0.0 collective-permute-done.4.refs_1_
  44.8 0.5 collective-permute-start.8
  45.3 0.0 collective-permute-done.7.refs_4_
  45.3 0.2 collective-permute-start.12
  45.4 0.6 collective-permute-done.9.refs_6_
  46.0 0.2 collective-permute-done.8.refs_5_
  46.2 0.4 collective-permute-done.12.refs_7_
  46.6 2.6 %shard_map.71 = (bf16[256,384]{1,0:T(8,128)(2,1)S(1)}, bf16[256,384]{1,0:T(8,128)(2,1)S(1)}) custom-call(f32[136,128]{1,0:T(8,128)S(1)} %shard_map.66.refs_0_, f32[136,128]{1,0:T(8,128)S(1)} %collective-permute-done.4.refs_1_, f32[136,128]{1,0:T(8,128)S(1)} %collective-permute-done.5.refs_2_, f32[136,128]{1,0:T(8,128)S(1)} %collective-permute-done.6.slab.refs_3_, ...), custom_call_target="tpu_custom_call" | custom-call | flops 805306368 | bytes 6291456 | tf_op jit(solution)/shard_map/pallas_call | solution.py:446
  49.2 1.6 %collective-permute-start.13 = (bf16[256,384]{1,0:T(8,128)(2,1)S(1)}, bf16[256,384]{1,0:T(8,128)(2,1)S(1)}, u32[]{:S(2)}, u32[]{:S(2)}) collective-permute-start(bf16[256,384]{1,0:T(8,128)(2,1)S(1)} %get-tuple-element.38), channel_id=1, source_target_pairs={{0,2},{2,0},{1,3},{3,1},{4,6},{6,4},{5,7},{7,5},{8,10},{10,8},{9,1... | collective-permute-start | bytes 589832 | tf_op jit(solution)/shard_map/ppermute | solution.py:33
  50.7 0.0 collective-permute-done.14.factors
  50.7 0.7 %collective-permute-done.15.refs_0_ = bf16[128,1024]{1,0:T(8,128)(2,1)S(1)} collective-permute-done((bf16[128,1024]{1,0:T(8,128)(2,1)S(1)}, bf16[128,1024]{1,0:T(8,128)(2,1)S(1)}, u32[]{:S(2)}, u32[]{:S(2)}) %collective-permute-start.15) | collective-permute-done | bytes 262176 | tf_op jit(solution)/shard_map/ppermute | solution.py:431
  51.5 1.4 %shard_map.72 = (bf16[2048,128]{1,0:T(8,128)(2,1)S(1)}, bf16[2048,128]{1,0:T(8,128)(2,1)S(1)}) custom-call(bf16[128,1024]{1,0:T(8,128)(2,1)S(1)} %collective-permute-done.14.factors, f32[136,128]{1,0:T(8,128)S(1)} %collective-permute-done.2.refs_3_.slab, bf16[128,1024]{1,0:T(8,128)(2,1)S(1)} %collective-permute-done.15.refs_0_), custom_call_target="tpu_custom_call" | custom-call | flops 536870912 | bytes 1572864 | tf_op jit(solution)/shard_map/pallas_call | solution.py:420
  52.9 1.4 %shard_map.73 = (bf16[256,128]{1,0:T(8,128)(2,1)S(1)}, bf16[256,128]{1,0:T(8,128)(2,1)S(1)}) custom-call(f32[136,128]{1,0:T(8,128)S(1)} %shard_map.66.refs_0_, f32[136,128]{1,0:T(8,128)S(1)} %collective-permute-done.4.refs_1_, f32[136,128]{1,0:T(8,128)S(1)} %collective-permute-done.5.refs_2_, f32[136,128]{1,0:T(8,128)S(1)} %collective-permute-done.6.slab.refs_3_, ...), custom_call_target="tpu_custom_call" | custom-call | flops 268435456 | bytes 2097152 | tf_op jit(solution)/shard_map/pallas_call | solution.py:446
  54.2 1.6 %collective-permute-start.16 = (bf16[256,128]{1,0:T(8,128)(2,1)S(1)}, bf16[256,128]{1,0:T(8,128)(2,1)S(1)}, u32[]{:S(2)}, u32[]{:S(2)}) collective-permute-start(bf16[256,128]{1,0:T(8,128)(2,1)S(1)} %get-tuple-element.44), channel_id=1, source_target_pairs={{0,2},{2,0},{1,3},{3,1},{4,6},{6,4},{5,7},{7,5},{8,10},{10,8},{9,1... | collective-permute-start | bytes 196616 | tf_op jit(solution)/shard_map/ppermute | solution.py:33
  55.8 0.5 collective-permute-done.13.refs_1_
  56.3 2.3 %collective-permute-done.16.refs_3_ = bf16[256,128]{1,0:T(8,128)(2,1)S(1)} collective-permute-done((bf16[256,128]{1,0:T(8,128)(2,1)S(1)}, bf16[256,128]{1,0:T(8,128)(2,1)S(1)}, u32[]{:S(2)}, u32[]{:S(2)}) %collective-permute-start.16) | collective-permute-done | bytes 65568 | tf_op jit(solution)/shard_map/ppermute | solution.py:33
  58.6 0.1 shard_map.74
  58.7 0.8 %reshape.7 = bf16[256,4,1,128]{3,1,0,2:T(4,128)(2,1)} reshape(bf16[256,512]{1,0:T(8,128)(2,1)S(1)} %shard_map.74) | data formatting | bytes 524288 | tf_op jit(solution)/shard_map/reshape | solution.py:465
  (6 shorter events, 0.0 us)
Async XLA Ops:
  11.2 9.5 %collective-permute-start.3 = (bf16[128,1024]{1,0:T(8,128)(2,1)}, bf16[128,1024]{1,0:T(8,128)(2,1)S(1)}, u32[]{:S(2)}, u32[]{:S(2)}) collective-permute-start(bf16[128,1024]{1,0:T(8,128)(2,1)} %get-tuple-element.30), channel_id=1, source_target_pairs={{0,2},{2,0},{1,3},{3,1},{4,6},{6,4},{5,7},{7,5},{8,10},{10,8},{9,1... | collective-permute-start | bytes 786440 | tf_op jit(solution)/shard_map/ppermute | solution.py:33
  14.2 12.0 %collective-permute-start = (f32[136,128]{1,0:T(8,128)}, f32[136,128]{1,0:T(8,128)S(1)}, u32[]{:S(2)}, u32[]{:S(2)}) collective-permute-start(f32[136,128]{1,0:T(8,128)} %get-tuple-element.26), channel_id=1, source_target_pairs={{0,4},{4,0},{8,12},{12,8},{1,5},{5,1},{9,13},{13,9},{2,6},{6,2},{1... | collective-permute-start | bytes 208904 | tf_op jit(solution)/shard_map/ppermute | solution.py:33
  15.8 10.4 %collective-permute-start.1 = (f32[136,128]{1,0:T(8,128)}, f32[136,128]{1,0:T(8,128)S(1)}, u32[]{:S(2)}, u32[]{:S(2)}) collective-permute-start(f32[136,128]{1,0:T(8,128)} %get-tuple-element.27), channel_id=1, source_target_pairs={{0,8},{4,12},{8,0},{12,4},{1,9},{5,13},{9,1},{13,5},{2,10},{6,14},... | collective-permute-start | bytes 208904 | tf_op jit(solution)/shard_map/ppermute | solution.py:33
  18.3 7.9 %collective-permute-start.2 = (f32[136,128]{1,0:T(8,128)}, f32[136,128]{1,0:T(8,128)S(1)}, u32[]{:S(2)}, u32[]{:S(2)}) collective-permute-start(f32[136,128]{1,0:T(8,128)} %get-tuple-element.28), channel_id=1, source_target_pairs={{0,12},{4,8},{8,4},{12,0},{1,13},{5,9},{9,5},{13,1},{2,14},{6,10},... | collective-permute-start | bytes 208904 | tf_op jit(solution)/shard_map/ppermute | solution.py:33
  20.7 1.0 %copy-start.1 = (bf16[128,1024]{1,0:T(8,128)(2,1)S(1)}, bf16[128,1024]{1,0:T(8,128)(2,1)}, u32[]{:S(2)}) copy-start(bf16[128,1024]{1,0:T(8,128)(2,1)} %get-tuple-element.29.own) | copy-start | bytes 786436
  21.7 17.9 %collective-permute-start.11 = (bf16[128,1024]{1,0:T(8,128)(2,1)S(1)}, bf16[128,1024]{1,0:T(8,128)(2,1)S(1)}, u32[]{:S(2)}, u32[]{:S(2)}) collective-permute-start(bf16[128,1024]{1,0:T(8,128)(2,1)S(1)} %shard_map.65.refs_4_.factors.refs_0_), channel_id=1, source_target_pairs={{0,8},{4,12},{8,0},{12,4},{1,9},{5,13},{9,1},{13,5},{2,10},{6,14},... | collective-permute-start | bytes 786440 | tf_op jit(solution)/shard_map/ppermute | solution.py:33
  24.6 11.7 %collective-permute-start.10 = (bf16[128,1024]{1,0:T(8,128)(2,1)S(1)}, bf16[128,1024]{1,0:T(8,128)(2,1)S(1)}, u32[]{:S(2)}, u32[]{:S(2)}) collective-permute-start(bf16[128,1024]{1,0:T(8,128)(2,1)S(1)} %shard_map.65.refs_4_.factors.refs_0_), channel_id=1, source_target_pairs={{0,4},{4,0},{8,12},{12,8},{1,5},{5,1},{9,13},{13,9},{2,6},{6,2},{1... | collective-permute-start | bytes 786440 | tf_op jit(solution)/shard_map/ppermute | solution.py:33
  26.2 0.9 %copy-start.2 = (f32[136,128]{1,0:T(8,128)S(1)}, f32[136,128]{1,0:T(8,128)}, u32[]{:S(2)}) copy-start(f32[136,128]{1,0:T(8,128)} %get-tuple-element.25.refs_0_.slab) | copy-start | bytes 208900
  27.1 16.2 %copy-start.3 = (f32[136,128]{1,0:T(8,128)S(1)}, f32[136,128]{1,0:T(8,128)}, u32[]{:S(2)}) copy-start(f32[136,128]{1,0:T(8,128)} %get-tuple-element.25.refs_0_.slab) | copy-start | bytes 208900
  33.6 12.9 %copy-start = (bf16[512,2048]{1,0:T(8,128)(2,1)S(1)}, bf16[512,2048]{1,0:T(8,128)(2,1)}, u32[]{:S(2)}) copy-start(bf16[512,2048]{1,0:T(8,128)(2,1)} %refs_10_.1) | copy-start | bytes 6291460
  33.7 11.6 %collective-permute-start.7 = (f32[136,128]{1,0:T(8,128)S(1)}, f32[136,128]{1,0:T(8,128)S(1)}, u32[]{:S(2)}, u32[]{:S(2)}) collective-permute-start(f32[136,128]{1,0:T(8,128)S(1)} %shard_map.66.refs_0_), channel_id=1, source_target_pairs={{0,1},{1,0},{2,3},{3,2},{4,5},{5,4},{6,7},{7,6},{8,9},{9,8},{10,11... | collective-permute-start | bytes 208904 | tf_op jit(solution)/shard_map/ppermute | solution.py:33
  33.7 8.0 %collective-permute-start.6 = (f32[136,128]{1,0:T(8,128)S(1)}, f32[136,128]{1,0:T(8,128)S(1)}, u32[]{:S(2)}, u32[]{:S(2)}) collective-permute-start(f32[136,128]{1,0:T(8,128)S(1)} %shard_map.66.refs_0_), channel_id=1, source_target_pairs={{0,12},{4,8},{8,4},{12,0},{1,13},{5,9},{9,5},{13,1},{2,14},{6,10},... | collective-permute-start | bytes 208904 | tf_op jit(solution)/shard_map/ppermute | solution.py:33
  34.0 10.6 %collective-permute-start.5 = (f32[136,128]{1,0:T(8,128)S(1)}, f32[136,128]{1,0:T(8,128)S(1)}, u32[]{:S(2)}, u32[]{:S(2)}) collective-permute-start(f32[136,128]{1,0:T(8,128)S(1)} %shard_map.66.refs_0_), channel_id=1, source_target_pairs={{0,8},{4,12},{8,0},{12,4},{1,9},{5,13},{9,1},{13,5},{2,10},{6,14},... | collective-permute-start | bytes 208904 | tf_op jit(solution)/shard_map/ppermute | solution.py:33
  36.3 8.5 %collective-permute-start.4 = (f32[136,128]{1,0:T(8,128)S(1)}, f32[136,128]{1,0:T(8,128)S(1)}, u32[]{:S(2)}, u32[]{:S(2)}) collective-permute-start(f32[136,128]{1,0:T(8,128)S(1)} %shard_map.66.refs_0_), channel_id=1, source_target_pairs={{0,4},{4,0},{8,12},{12,8},{1,5},{5,1},{9,13},{13,9},{2,6},{6,2},{1... | collective-permute-start | bytes 208904 | tf_op jit(solution)/shard_map/ppermute | solution.py:33
  39.6 11.1 %collective-permute-start.14 = (bf16[128,1024]{1,0:T(8,128)(2,1)S(1)}, bf16[128,1024]{1,0:T(8,128)(2,1)S(1)}, u32[]{:S(2)}, u32[]{:S(2)}) collective-permute-start(bf16[128,1024]{1,0:T(8,128)(2,1)S(1)} %get-tuple-element.39), channel_id=1, source_target_pairs={{4,8},{8,4},{5,9},{9,5},{6,10},{10,6},{7,11},{11,7},{20,24},{24,20... | collective-permute-start | bytes 786440 | tf_op jit(solution)/shard_map/ppermute | solution.py:429
  41.8 9.7 %collective-permute-start.15 = (bf16[128,1024]{1,0:T(8,128)(2,1)S(1)}, bf16[128,1024]{1,0:T(8,128)(2,1)S(1)}, u32[]{:S(2)}, u32[]{:S(2)}) collective-permute-start(bf16[128,1024]{1,0:T(8,128)(2,1)S(1)} %get-tuple-element.40), channel_id=1, source_target_pairs={{4,0},{8,12},{5,1},{9,13},{6,2},{10,14},{7,3},{11,15},{20,16},{24,... | collective-permute-start | bytes 786440 | tf_op jit(solution)/shard_map/ppermute | solution.py:431
  44.7 1.3 %collective-permute-start.9 = (f32[136,128]{1,0:T(8,128)S(1)}, f32[136,128]{1,0:T(8,128)S(1)}, u32[]{:S(2)}, u32[]{:S(2)}) collective-permute-start(f32[136,128]{1,0:T(8,128)S(1)} %collective-permute-done.5.refs_2_), channel_id=1, source_target_pairs={{0,1},{1,0},{2,3},{3,2},{4,5},{5,4},{6,7},{7,6},{8,9},{9,8},{10,11... | collective-permute-start | bytes 208904 | tf_op jit(solution)/shard_map/ppermute | solution.py:33
  44.8 1.4 %collective-permute-start.8 = (f32[136,128]{1,0:T(8,128)S(1)}, f32[136,128]{1,0:T(8,128)S(1)}, u32[]{:S(2)}, u32[]{:S(2)}) collective-permute-start(f32[136,128]{1,0:T(8,128)S(1)} %collective-permute-done.4.refs_1_), channel_id=1, source_target_pairs={{0,1},{1,0},{2,3},{3,2},{4,5},{5,4},{6,7},{7,6},{8,9},{9,8},{10,11... | collective-permute-start | bytes 208904 | tf_op jit(solution)/shard_map/ppermute | solution.py:33
  45.3 1.3 %collective-permute-start.12 = (f32[136,128]{1,0:T(8,128)S(1)}, f32[136,128]{1,0:T(8,128)S(1)}, u32[]{:S(2)}, u32[]{:S(2)}) collective-permute-start(f32[136,128]{1,0:T(8,128)S(1)} %shard_map.70), channel_id=1, source_target_pairs={{0,1},{1,0},{2,3},{3,2},{4,5},{5,4},{6,7},{7,6},{8,9},{9,8},{10,11... | collective-permute-start | bytes 208904 | tf_op jit(solution)/shard_map/ppermute | solution.py:33
  49.2 7.1 %collective-permute-start.13 = (bf16[256,384]{1,0:T(8,128)(2,1)S(1)}, bf16[256,384]{1,0:T(8,128)(2,1)S(1)}, u32[]{:S(2)}, u32[]{:S(2)}) collective-permute-start(bf16[256,384]{1,0:T(8,128)(2,1)S(1)} %get-tuple-element.38), channel_id=1, source_target_pairs={{0,2},{2,0},{1,3},{3,1},{4,6},{6,4},{5,7},{7,5},{8,10},{10,8},{9,1... | collective-permute-start | bytes 589832 | tf_op jit(solution)/shard_map/ppermute | solution.py:33
  54.2 4.3 %collective-permute-start.16 = (bf16[256,128]{1,0:T(8,128)(2,1)S(1)}, bf16[256,128]{1,0:T(8,128)(2,1)S(1)}, u32[]{:S(2)}, u32[]{:S(2)}) collective-permute-start(bf16[256,128]{1,0:T(8,128)(2,1)S(1)} %get-tuple-element.44), channel_id=1, source_target_pairs={{0,2},{2,0},{1,3},{3,1},{4,6},{6,4},{5,7},{7,5},{8,10},{10,8},{9,1... | collective-permute-start | bytes 196616 | tf_op jit(solution)/shard_map/ppermute | solution.py:33

commit v11 on v10

--- a/solution.py
+++ b/solution.py
@@ -301,8 +301,9 @@
         low_out[pl.ds(start * proj, step * proj), :] = low
 
 
-def hand_kernel(slab, *refs):
-    refs[-1][...] = slab[...]
+def hand_kernel(count, *refs):
+    for source, copy in zip(refs[:count], refs[-count:]):
+        copy[...] = source[...]
 
 
 def scores_kernel(cycle, count, *refs):
@@ -390,7 +391,14 @@
         doc_lengths, train_grads,
     )
     got = swapped(sent, "mp", 1)
-    parts = [slabs[0]] + [swapped(slabs[s], "dp", s) for s in range(1, cycle)]
+    own, kept = call(
+        functools.partial(hand_kernel, 2),
+        [shape(own.shape, bf16), shape((SLAB, FBLK), f32)],
+        [VMEM, VMEM],
+        vmem=16,
+        moved=4 * own.size,
+    )(own, slabs[0])
+    parts = [kept] + [swapped(slabs[s], "dp", s) for s in range(1, cycle)]
 
     factors = call(
         functools.partial(merge_kernel, each),
@@ -431,12 +439,12 @@
             far = [lax.ppermute(again[0], "dp", [(1, 0), (2, 3)])]
     handed = list(inverses)
     handed[late] = call(
-        hand_kernel,
+        functools.partial(hand_kernel, 1),
         shape((SLAB, FBLK), f32),
-        [VMEM] + [HBM] * (cycle - 1),
+        [VMEM] + [HBM] * (cycle - 2),
         vmem=16,
         moved=8 * SLAB * FBLK,
-    )(inverses[late], *[highs[s] for s in range(cycle) if s != late])
+    )(inverses[late], *[highs[s] for s in range(1, cycle) if s != late])
     peers = [swapped(slab, "rep", 1) for slab in handed]
 
     half_rows = train_rows // lax.axis_size("mp")

time: 59.7 us -> 59 us (0.988)
  waiting for transfers between devices: 7.42 us -> 6.06 us
  starting transfers between devices: 21.8 us -> 22.4 us
    ppermute x15, waiting for transfers between devices: 6.67 us -> 3.58 us  [swapped(): lax.ppermute(shard, axis, [(i, i ^ by) for i in range(lax.axis_size(axis))])]
    ppermute x1, waiting for transfers between devices: 0.75 us -> 2.47 us  [split_over_blocks(): far = [lax.ppermute(again[0], 'dp', [(1, 0), (2, 3)])]]
    unnamed x8 -> x6, local copies, waits for them, and re-layouts: 1.84 us -> 1.84 us
  transfers between devices with their start and end apart: 17 -> 17, of which waited for: 8 -> 4; matrix products, arithmetic and copies ran while one was open for 0% -> 0% of each run, Pallas kernels for 27% -> 28%
where the time goes in v11:
time: 59 us; the launch traced here: 58.7 us
  Pallas kernels  27.6 us (47%)
  starting transfers between devices  22.4 us (38%)
  waiting for transfers between devices  6.06 us (10%)
  local copies, waits for them, and re-layouts  2.6 us (4%)
    ppermute x15, starting transfers between devices, swapped(): lax.ppermute(shard, axis, [(i, i ^ by) for i in range(lax.axis_size(axis))])  20.2 us
    pallas_call x1, Pallas kernels, split_over_blocks(): call(first_kernel, [shape((2 * each + proj, tokens), bf16)] * 2 + [shape(...  11.2 us
    pallas_call x1, Pallas kernels, split_over_blocks(): call(functools.partial(factor_kernel, train_rows * cycle, 1.0 / proj), sh...  6.58 us
    pallas_call x4, Pallas kernels, split_over_blocks(): call(functools.partial(queries_kernel, each, cycle if s == late else 0),...  5.68 us
    pallas_call x2, Pallas kernels, split_over_blocks(): call(functools.partial(scores_kernel, cycle, count), [shape((half_rows, c...  3.93 us
    ppermute x15, waiting for transfers between devices, swapped(): lax.ppermute(shard, axis, [(i, i ^ by) for i in range(lax.axis_size(axis))])  3.58 us
    ppermute x1, waiting for transfers between devices, split_over_blocks(): far = [lax.ppermute(again[0], 'dp', [(1, 0), (2, 3)])]  2.47 us
    unnamed x6, local copies, waits for them, and re-layouts  1.84 us
  transfers between devices with their start and end apart: 17, of which 4 were waited for; matrix products, arithmetic and copies ran while one was open for 0% of the time, Pallas kernels for 28%

profile of v11, /device:TPU:0, one launch (start us, length us, event | category | flops | bytes accessed | tf_op | source)
XLA Modules:
  0.0 58.7 jit_solution(1098450886774344042)
XLA Ops:
  0.0 11.2 %shard_map.64 = (bf16[128,1024]{1,0:T(8,128)(2,1)}, bf16[128,1024]{1,0:T(8,128)(2,1)}, f32[136,128]{1,0:T(8,128)}, f32[136,128]{1,0:T(8,128)}, f32[136,128]{1,0:T(8,128)}, /*index=5*/f32[136,128]{1,0:T(8,128)}) custom-call(s32[8,128]{1,0:T(8,128)} %bitcast.6, bf16[1024,2048]{1,0:T(8,128)(2,1)} %delta_hbm.1, bf16[64,64128]{1,0:T(8,128)(2,1)} %bitcast.4, ...), custom_call_target="tpu_custom_call" | custom-call | flops 268435456 | bytes 24805376 | tf_op jit(solution)/shard_map/pallas_call | solution.py:368
  11.2 3.0 %collective-permute-start.3 = (bf16[128,1024]{1,0:T(8,128)(2,1)}, bf16[128,1024]{1,0:T(8,128)(2,1)S(1)}, u32[]{:S(2)}, u32[]{:S(2)}) collective-permute-start(bf16[128,1024]{1,0:T(8,128)(2,1)} %get-tuple-element.34), channel_id=1, source_target_pairs={{0,2},{2,0},{1,3},{3,1},{4,6},{6,4},{5,7},{7,5},{8,10},{10,8},{9,1... | collective-permute-start | bytes 786440 | tf_op jit(solution)/shard_map/ppermute | solution.py:33
  14.2 1.6 %collective-permute-start = (f32[136,128]{1,0:T(8,128)}, f32[136,128]{1,0:T(8,128)S(1)}, u32[]{:S(2)}, u32[]{:S(2)}) collective-permute-start(f32[136,128]{1,0:T(8,128)} %get-tuple-element.30), channel_id=1, source_target_pairs={{0,4},{4,0},{8,12},{12,8},{1,5},{5,1},{9,13},{13,9},{2,6},{6,2},{1... | collective-permute-start | bytes 208904 | tf_op jit(solution)/shard_map/ppermute | solution.py:33
  15.7 2.6 %collective-permute-start.1 = (f32[136,128]{1,0:T(8,128)}, f32[136,128]{1,0:T(8,128)S(1)}, u32[]{:S(2)}, u32[]{:S(2)}) collective-permute-start(f32[136,128]{1,0:T(8,128)} %get-tuple-element.31), channel_id=1, source_target_pairs={{0,8},{4,12},{8,0},{12,4},{1,9},{5,13},{9,1},{13,5},{2,10},{6,14},... | collective-permute-start | bytes 208904 | tf_op jit(solution)/shard_map/ppermute | solution.py:33
  18.3 0.2 collective-permute-start.2
  18.5 0.9 %copy-done.1 = bf16[128,1024]{1,0:T(8,128)(2,1)S(1)} copy-done((bf16[128,1024]{1,0:T(8,128)(2,1)S(1)}, bf16[128,1024]{1,0:T(8,128)(2,1)}, u32[]{:S(2)}) %copy-start.1) | copy-done | bytes 262168
  19.5 0.9 %copy-done.2 = f32[136,128]{1,0:T(8,128)S(1)} copy-done((f32[136,128]{1,0:T(8,128)S(1)}, f32[136,128]{1,0:T(8,128)}, u32[]{:S(2)}) %copy-start.2) | copy-done | bytes 69656
  20.4 0.3 collective-permute-done.3.got
  20.7 0.1 shard_map.66.refs_4_.refs_0_.factors
  20.7 1.9 %collective-permute-start.10 = (bf16[128,1024]{1,0:T(8,128)(2,1)S(1)}, bf16[128,1024]{1,0:T(8,128)(2,1)S(1)}, u32[]{:S(2)}, u32[]{:S(2)}) collective-permute-start(bf16[128,1024]{1,0:T(8,128)(2,1)S(1)} %shard_map.66.refs_4_.refs_0_.factors), channel_id=1, source_target_pairs={{0,4},{4,0},{8,12},{12,8},{1,5},{5,1},{9,13},{13,9},{2,6},{6,2},{1... | collective-permute-start | bytes 786440 | tf_op jit(solution)/shard_map/ppermute | solution.py:33
  22.6 2.6 %collective-permute-start.11 = (bf16[128,1024]{1,0:T(8,128)(2,1)S(1)}, bf16[128,1024]{1,0:T(8,128)(2,1)S(1)}, u32[]{:S(2)}, u32[]{:S(2)}) collective-permute-start(bf16[128,1024]{1,0:T(8,128)(2,1)S(1)} %shard_map.66.refs_4_.refs_0_.factors), channel_id=1, source_target_pairs={{0,8},{4,12},{8,0},{12,4},{1,9},{5,13},{9,1},{13,5},{2,10},{6,14},... | collective-permute-start | bytes 786440 | tf_op jit(solution)/shard_map/ppermute | solution.py:33
  25.2 0.0 collective-permute-done.refs_1_.slab
  25.2 0.0 collective-permute-done.1.refs_2_.slab
  25.2 0.0 collective-permute-done.2.refs_3_.slab
  25.2 6.6 %shard_map.67.refs_0_ = f32[136,128]{1,0:T(8,128)S(1)} custom-call(f32[136,128]{1,0:T(8,128)S(1)} %get-tuple-element.29.refs_0_.slab, f32[136,128]{1,0:T(8,128)S(1)} %collective-permute-done.refs_1_.slab, f32[136,128]{1,0:T(8,128)S(1)} %collective-permute-done.1.refs_2_.slab, f32[136,128]{1,0:T(8,128)S(1)} %collective-permute-done.2.refs_3_.slab, ...), custom_call_target="tpu_custom_call" | custom-call | flops 10000000000 | bytes 1000000 | tf_op jit(solution)/shard_map/pallas_call | solution.py:414
  31.8 0.0 copy-start
  31.8 1.3 %collective-permute-start.6 = (f32[136,128]{1,0:T(8,128)S(1)}, f32[136,128]{1,0:T(8,128)S(1)}, u32[]{:S(2)}, u32[]{:S(2)}) collective-permute-start(f32[136,128]{1,0:T(8,128)S(1)} %shard_map.67.refs_0_), channel_id=1, source_target_pairs={{0,12},{4,8},{8,4},{12,0},{1,13},{5,9},{9,5},{13,1},{2,14},{6,10},... | collective-permute-start | bytes 208904 | tf_op jit(solution)/shard_map/ppermute | solution.py:33
  33.1 0.4 collective-permute-start.4
  33.5 2.8 %collective-permute-start.5 = (f32[136,128]{1,0:T(8,128)S(1)}, f32[136,128]{1,0:T(8,128)S(1)}, u32[]{:S(2)}, u32[]{:S(2)}) collective-permute-start(f32[136,128]{1,0:T(8,128)S(1)} %shard_map.67.refs_0_), channel_id=1, source_target_pairs={{0,8},{4,12},{8,0},{12,4},{1,9},{5,13},{9,1},{13,5},{2,10},{6,14},... | collective-permute-start | bytes 208904 | tf_op jit(solution)/shard_map/ppermute | solution.py:33
  36.3 0.3 collective-permute-done.10.factors
  36.5 0.0 collective-permute-start.7
  36.6 1.4 %shard_map.68 = (bf16[2048,128]{1,0:T(8,128)(2,1)S(1)}, bf16[2048,128]{1,0:T(8,128)(2,1)S(1)}, bf16[128,1024]{1,0:T(8,128)(2,1)S(1)}) custom-call(bf16[128,1024]{1,0:T(8,128)(2,1)S(1)} %collective-permute-done.10.factors, f32[136,128]{1,0:T(8,128)S(1)} %collective-permute-done.refs_1_.slab, bf16[128,1024]{1,0:T(8,128)(2,1)S(1)} %shard_map.66.refs_4_.refs_0_.factors), custom_call_target="tpu_custom_call" | custom-call | flops 536870912 | bytes 1572864 | tf_op jit(solution)/shard_map/pallas_call | solution.py:428
  38.0 0.0 collective-permute-done.11.factors.refs_0_
  38.0 0.7 %collective-permute-start.14 = (bf16[128,1024]{1,0:T(8,128)(2,1)S(1)}, bf16[128,1024]{1,0:T(8,128)(2,1)S(1)}, u32[]{:S(2)}, u32[]{:S(2)}) collective-permute-start(bf16[128,1024]{1,0:T(8,128)(2,1)S(1)} %get-tuple-element.43), channel_id=1, source_target_pairs={{4,8},{8,4},{5,9},{9,5},{6,10},{10,6},{7,11},{11,7},{20,24},{24,20... | collective-permute-start | bytes 786440 | tf_op jit(solution)/shard_map/ppermute | solution.py:437
  38.7 1.4 %shard_map.69 = (bf16[2048,128]{1,0:T(8,128)(2,1)S(1)}, bf16[2048,128]{1,0:T(8,128)(2,1)S(1)}, bf16[128,1024]{1,0:T(8,128)(2,1)S(1)}) custom-call(bf16[128,1024]{1,0:T(8,128)(2,1)S(1)} %collective-permute-done.11.factors.refs_0_, f32[136,128]{1,0:T(8,128)S(1)} %collective-permute-done.1.refs_2_.slab, ...), custom_call_target="tpu_custom_call" | custom-call | flops 536870912 | bytes 1572864 | tf_op jit(solution)/shard_map/pallas_call | solution.py:428
  40.1 0.0 collective-permute-done.6.refs_0_.refs_3_
  40.1 1.5 %collective-permute-start.15 = (bf16[128,1024]{1,0:T(8,128)(2,1)S(1)}, bf16[128,1024]{1,0:T(8,128)(2,1)S(1)}, u32[]{:S(2)}, u32[]{:S(2)}) collective-permute-start(bf16[128,1024]{1,0:T(8,128)(2,1)S(1)} %get-tuple-element.44), channel_id=1, source_target_pairs={{4,0},{8,12},{5,1},{9,13},{6,2},{10,14},{7,3},{11,15},{20,16},{24,... | collective-permute-start | bytes 786440 | tf_op jit(solution)/shard_map/ppermute | solution.py:439
  41.6 0.0 collective-permute-done.4.refs_1_
  41.6 0.6 collective-permute-start.8
  42.2 0.0 collective-permute-done.5.refs_2_
  42.2 0.1 collective-permute-start.9
  42.3 0.0 collective-permute-done.7.refs_4_
  42.3 0.5 collective-permute-start.12
  42.8 1.4 %shard_map.71 = (bf16[2048,128]{1,0:T(8,128)(2,1)S(1)}, bf16[2048,128]{1,0:T(8,128)(2,1)S(1)}) custom-call(bf16[128,1024]{1,0:T(8,128)(2,1)S(1)} %shard_map.66.refs_4_.refs_0_.factors, f32[136,128]{1,0:T(8,128)S(1)} %get-tuple-element.29.refs_0_.slab, f32[136,128]{1,0:T(8,128)S(1)} %shard_map.67.refs_0_), custom_call_target="tpu_custom_call" | custom-call | flops 536870912 | bytes 1572864 | tf_op jit(solution)/shard_map/pallas_call | solution.py:428
  44.2 0.0 collective-permute-done.8.refs_5_
  44.2 0.0 collective-permute-done.9.refs_6_
  44.2 0.0 collective-permute-done.12.refs_7_
  44.2 2.6 %shard_map.72 = (bf16[256,384]{1,0:T(8,128)(2,1)S(1)}, bf16[256,384]{1,0:T(8,128)(2,1)S(1)}) custom-call(f32[136,128]{1,0:T(8,128)S(1)} %shard_map.67.refs_0_, f32[136,128]{1,0:T(8,128)S(1)} %collective-permute-done.4.refs_1_, f32[136,128]{1,0:T(8,128)S(1)} %collective-permute-done.5.refs_2_, f32[136,128]{1,0:T(8,128)S(1)} %collective-permute-done.6.refs_0_.refs_3_, ...), custom_call_target="tpu_custom_call" | custom-call | flops 805306368 | bytes 6291456 | tf_op jit(solution)/shard_map/pallas_call | solution.py:454
  46.8 1.4 %collective-permute-start.13 = (bf16[256,384]{1,0:T(8,128)(2,1)S(1)}, bf16[256,384]{1,0:T(8,128)(2,1)S(1)}, u32[]{:S(2)}, u32[]{:S(2)}) collective-permute-start(bf16[256,384]{1,0:T(8,128)(2,1)S(1)} %get-tuple-element.42), channel_id=1, source_target_pairs={{0,2},{2,0},{1,3},{3,1},{4,6},{6,4},{5,7},{7,5},{8,10},{10,8},{9,1... | collective-permute-start | bytes 589832 | tf_op jit(solution)/shard_map/ppermute | solution.py:33
  48.2 0.0 collective-permute-done.14.factors
  48.2 2.5 %collective-permute-done.15.refs_0_ = bf16[128,1024]{1,0:T(8,128)(2,1)S(1)} collective-permute-done((bf16[128,1024]{1,0:T(8,128)(2,1)S(1)}, bf16[128,1024]{1,0:T(8,128)(2,1)S(1)}, u32[]{:S(2)}, u32[]{:S(2)}) %collective-permute-start.15) | collective-permute-done | bytes 262176 | tf_op jit(solution)/shard_map/ppermute | solution.py:439
  50.7 1.4 %shard_map.73 = (bf16[2048,128]{1,0:T(8,128)(2,1)S(1)}, bf16[2048,128]{1,0:T(8,128)(2,1)S(1)}) custom-call(bf16[128,1024]{1,0:T(8,128)(2,1)S(1)} %collective-permute-done.14.factors, f32[136,128]{1,0:T(8,128)S(1)} %collective-permute-done.2.refs_3_.slab, bf16[128,1024]{1,0:T(8,128)(2,1)S(1)} %collective-permute-done.15.refs_0_), custom_call_target="tpu_custom_call" | custom-call | flops 536870912 | bytes 1572864 | tf_op jit(solution)/shard_map/pallas_call | solution.py:428
  52.1 1.4 %shard_map.74 = (bf16[256,128]{1,0:T(8,128)(2,1)S(1)}, bf16[256,128]{1,0:T(8,128)(2,1)S(1)}) custom-call(f32[136,128]{1,0:T(8,128)S(1)} %shard_map.67.refs_0_, f32[136,128]{1,0:T(8,128)S(1)} %collective-permute-done.4.refs_1_, f32[136,128]{1,0:T(8,128)S(1)} %collective-permute-done.5.refs_2_, f32[136,128]{1,0:T(8,128)S(1)} %collective-permute-done.6.refs_0_.refs_3_, ...), custom_call_target="tpu_custom_call" | custom-call | flops 268435456 | bytes 2097152 | tf_op jit(solution)/shard_map/pallas_call | solution.py:454
  53.5 1.3 %collective-permute-start.16 = (bf16[256,128]{1,0:T(8,128)(2,1)S(1)}, bf16[256,128]{1,0:T(8,128)(2,1)S(1)}, u32[]{:S(2)}, u32[]{:S(2)}) collective-permute-start(bf16[256,128]{1,0:T(8,128)(2,1)S(1)} %get-tuple-element.48), channel_id=1, source_target_pairs={{0,2},{2,0},{1,3},{3,1},{4,6},{6,4},{5,7},{7,5},{8,10},{10,8},{9,1... | collective-permute-start | bytes 196616 | tf_op jit(solution)/shard_map/ppermute | solution.py:33
  54.8 0.0 collective-permute-done.13.refs_1_
  54.8 3.0 %collective-permute-done.16.refs_3_ = bf16[256,128]{1,0:T(8,128)(2,1)S(1)} collective-permute-done((bf16[256,128]{1,0:T(8,128)(2,1)S(1)}, bf16[256,128]{1,0:T(8,128)(2,1)S(1)}, u32[]{:S(2)}, u32[]{:S(2)}) %collective-permute-start.16) | collective-permute-done | bytes 65568 | tf_op jit(solution)/shard_map/ppermute | solution.py:33
  57.8 0.1 shard_map.75
  58.0 0.8 %reshape.7 = bf16[256,4,1,128]{3,1,0,2:T(4,128)(2,1)} reshape(bf16[256,512]{1,0:T(8,128)(2,1)S(1)} %shard_map.75) | data formatting | bytes 524288 | tf_op jit(solution)/shard_map/reshape | solution.py:473
  (5 shorter events, 0.0 us)
Async XLA Ops:
  11.2 9.5 %collective-permute-start.3 = (bf16[128,1024]{1,0:T(8,128)(2,1)}, bf16[128,1024]{1,0:T(8,128)(2,1)S(1)}, u32[]{:S(2)}, u32[]{:S(2)}) collective-permute-start(bf16[128,1024]{1,0:T(8,128)(2,1)} %get-tuple-element.34), channel_id=1, source_target_pairs={{0,2},{2,0},{1,3},{3,1},{4,6},{6,4},{5,7},{7,5},{8,10},{10,8},{9,1... | collective-permute-start | bytes 786440 | tf_op jit(solution)/shard_map/ppermute | solution.py:33
  14.2 11.1 %collective-permute-start = (f32[136,128]{1,0:T(8,128)}, f32[136,128]{1,0:T(8,128)S(1)}, u32[]{:S(2)}, u32[]{:S(2)}) collective-permute-start(f32[136,128]{1,0:T(8,128)} %get-tuple-element.30), channel_id=1, source_target_pairs={{0,4},{4,0},{8,12},{12,8},{1,5},{5,1},{9,13},{13,9},{2,6},{6,2},{1... | collective-permute-start | bytes 208904 | tf_op jit(solution)/shard_map/ppermute | solution.py:33
  15.7 9.5 %collective-permute-start.1 = (f32[136,128]{1,0:T(8,128)}, f32[136,128]{1,0:T(8,128)S(1)}, u32[]{:S(2)}, u32[]{:S(2)}) collective-permute-start(f32[136,128]{1,0:T(8,128)} %get-tuple-element.31), channel_id=1, source_target_pairs={{0,8},{4,12},{8,0},{12,4},{1,9},{5,13},{9,1},{13,5},{2,10},{6,14},... | collective-permute-start | bytes 208904 | tf_op jit(solution)/shard_map/ppermute | solution.py:33
  18.3 6.9 %collective-permute-start.2 = (f32[136,128]{1,0:T(8,128)}, f32[136,128]{1,0:T(8,128)S(1)}, u32[]{:S(2)}, u32[]{:S(2)}) collective-permute-start(f32[136,128]{1,0:T(8,128)} %get-tuple-element.32), channel_id=1, source_target_pairs={{0,12},{4,8},{8,4},{12,0},{1,13},{5,9},{9,5},{13,1},{2,14},{6,10},... | collective-permute-start | bytes 208904 | tf_op jit(solution)/shard_map/ppermute | solution.py:33
  18.5 0.9 %copy-start.1 = (bf16[128,1024]{1,0:T(8,128)(2,1)S(1)}, bf16[128,1024]{1,0:T(8,128)(2,1)}, u32[]{:S(2)}) copy-start(bf16[128,1024]{1,0:T(8,128)(2,1)} %get-tuple-element.27.refs_0_) | copy-start | bytes 786436
  19.5 0.9 %copy-start.2 = (f32[136,128]{1,0:T(8,128)S(1)}, f32[136,128]{1,0:T(8,128)}, u32[]{:S(2)}) copy-start(f32[136,128]{1,0:T(8,128)} %get-tuple-element.28.refs_1_) | copy-start | bytes 208900
  20.7 15.8 %collective-permute-start.10 = (bf16[128,1024]{1,0:T(8,128)(2,1)S(1)}, bf16[128,1024]{1,0:T(8,128)(2,1)S(1)}, u32[]{:S(2)}, u32[]{:S(2)}) collective-permute-start(bf16[128,1024]{1,0:T(8,128)(2,1)S(1)} %shard_map.66.refs_4_.refs_0_.factors), channel_id=1, source_target_pairs={{0,4},{4,0},{8,12},{12,8},{1,5},{5,1},{9,13},{13,9},{2,6},{6,2},{1... | collective-permute-start | bytes 786440 | tf_op jit(solution)/shard_map/ppermute | solution.py:33
  22.6 15.4 %collective-permute-start.11 = (bf16[128,1024]{1,0:T(8,128)(2,1)S(1)}, bf16[128,1024]{1,0:T(8,128)(2,1)S(1)}, u32[]{:S(2)}, u32[]{:S(2)}) collective-permute-start(bf16[128,1024]{1,0:T(8,128)(2,1)S(1)} %shard_map.66.refs_4_.refs_0_.factors), channel_id=1, source_target_pairs={{0,8},{4,12},{8,0},{12,4},{1,9},{5,13},{9,1},{13,5},{2,10},{6,14},... | collective-permute-start | bytes 786440 | tf_op jit(solution)/shard_map/ppermute | solution.py:33
  31.8 12.4 %copy-start = (bf16[512,2048]{1,0:T(8,128)(2,1)S(1)}, bf16[512,2048]{1,0:T(8,128)(2,1)}, u32[]{:S(2)}) copy-start(bf16[512,2048]{1,0:T(8,128)(2,1)} %refs_10_.1) | copy-start | bytes 6291460
  31.8 8.3 %collective-permute-start.6 = (f32[136,128]{1,0:T(8,128)S(1)}, f32[136,128]{1,0:T(8,128)S(1)}, u32[]{:S(2)}, u32[]{:S(2)}) collective-permute-start(f32[136,128]{1,0:T(8,128)S(1)} %shard_map.67.refs_0_), channel_id=1, source_target_pairs={{0,12},{4,8},{8,4},{12,0},{1,13},{5,9},{9,5},{13,1},{2,14},{6,10},... | collective-permute-start | bytes 208904 | tf_op jit(solution)/shard_map/ppermute | solution.py:33
  33.1 8.5 %collective-permute-start.4 = (f32[136,128]{1,0:T(8,128)S(1)}, f32[136,128]{1,0:T(8,128)S(1)}, u32[]{:S(2)}, u32[]{:S(2)}) collective-permute-start(f32[136,128]{1,0:T(8,128)S(1)} %shard_map.67.refs_0_), channel_id=1, source_target_pairs={{0,4},{4,0},{8,12},{12,8},{1,5},{5,1},{9,13},{13,9},{2,6},{6,2},{1... | collective-permute-start | bytes 208904 | tf_op jit(solution)/shard_map/ppermute | solution.py:33
  33.5 8.7 %collective-permute-start.5 = (f32[136,128]{1,0:T(8,128)S(1)}, f32[136,128]{1,0:T(8,128)S(1)}, u32[]{:S(2)}, u32[]{:S(2)}) collective-permute-start(f32[136,128]{1,0:T(8,128)S(1)} %shard_map.67.refs_0_), channel_id=1, source_target_pairs={{0,8},{4,12},{8,0},{12,4},{1,9},{5,13},{9,1},{13,5},{2,10},{6,14},... | collective-permute-start | bytes 208904 | tf_op jit(solution)/shard_map/ppermute | solution.py:33
  36.5 5.7 %collective-permute-start.7 = (f32[136,128]{1,0:T(8,128)S(1)}, f32[136,128]{1,0:T(8,128)S(1)}, u32[]{:S(2)}, u32[]{:S(2)}) collective-permute-start(f32[136,128]{1,0:T(8,128)S(1)} %shard_map.67.refs_0_), channel_id=1, source_target_pairs={{0,1},{1,0},{2,3},{3,2},{4,5},{5,4},{6,7},{7,6},{8,9},{9,8},{10,11... | collective-permute-start | bytes 208904 | tf_op jit(solution)/shard_map/ppermute | solution.py:33
  38.0 10.3 %collective-permute-start.14 = (bf16[128,1024]{1,0:T(8,128)(2,1)S(1)}, bf16[128,1024]{1,0:T(8,128)(2,1)S(1)}, u32[]{:S(2)}, u32[]{:S(2)}) collective-permute-start(bf16[128,1024]{1,0:T(8,128)(2,1)S(1)} %get-tuple-element.43), channel_id=1, source_target_pairs={{4,8},{8,4},{5,9},{9,5},{6,10},{10,6},{7,11},{11,7},{20,24},{24,20... | collective-permute-start | bytes 786440 | tf_op jit(solution)/shard_map/ppermute | solution.py:437
  40.1 10.6 %collective-permute-start.15 = (bf16[128,1024]{1,0:T(8,128)(2,1)S(1)}, bf16[128,1024]{1,0:T(8,128)(2,1)S(1)}, u32[]{:S(2)}, u32[]{:S(2)}) collective-permute-start(bf16[128,1024]{1,0:T(8,128)(2,1)S(1)} %get-tuple-element.44), channel_id=1, source_target_pairs={{4,0},{8,12},{5,1},{9,13},{6,2},{10,14},{7,3},{11,15},{20,16},{24,... | collective-permute-start | bytes 786440 | tf_op jit(solution)/shard_map/ppermute | solution.py:439
  41.6 2.6 %collective-permute-start.8 = (f32[136,128]{1,0:T(8,128)S(1)}, f32[136,128]{1,0:T(8,128)S(1)}, u32[]{:S(2)}, u32[]{:S(2)}) collective-permute-start(f32[136,128]{1,0:T(8,128)S(1)} %collective-permute-done.4.refs_1_), channel_id=1, source_target_pairs={{0,1},{1,0},{2,3},{3,2},{4,5},{5,4},{6,7},{7,6},{8,9},{9,8},{10,11... | collective-permute-start | bytes 208904 | tf_op jit(solution)/shard_map/ppermute | solution.py:33
  42.2 2.0 %collective-permute-start.9 = (f32[136,128]{1,0:T(8,128)S(1)}, f32[136,128]{1,0:T(8,128)S(1)}, u32[]{:S(2)}, u32[]{:S(2)}) collective-permute-start(f32[136,128]{1,0:T(8,128)S(1)} %collective-permute-done.5.refs_2_), channel_id=1, source_target_pairs={{0,1},{1,0},{2,3},{3,2},{4,5},{5,4},{6,7},{7,6},{8,9},{9,8},{10,11... | collective-permute-start | bytes 208904 | tf_op jit(solution)/shard_map/ppermute | solution.py:33
  42.3 1.9 %collective-permute-start.12 = (f32[136,128]{1,0:T(8,128)S(1)}, f32[136,128]{1,0:T(8,128)S(1)}, u32[]{:S(2)}, u32[]{:S(2)}) collective-permute-start(f32[136,128]{1,0:T(8,128)S(1)} %shard_map.70), channel_id=1, source_target_pairs={{0,1},{1,0},{2,3},{3,2},{4,5},{5,4},{6,7},{7,6},{8,9},{9,8},{10,11... | collective-permute-start | bytes 208904 | tf_op jit(solution)/shard_map/ppermute | solution.py:33
  46.8 8.0 %collective-permute-start.13 = (bf16[256,384]{1,0:T(8,128)(2,1)S(1)}, bf16[256,384]{1,0:T(8,128)(2,1)S(1)}, u32[]{:S(2)}, u32[]{:S(2)}) collective-permute-start(bf16[256,384]{1,0:T(8,128)(2,1)S(1)} %get-tuple-element.42), channel_id=1, source_target_pairs={{0,2},{2,0},{1,3},{3,1},{4,6},{6,4},{5,7},{7,5},{8,10},{10,8},{9,1... | collective-permute-start | bytes 589832 | tf_op jit(solution)/shard_map/ppermute | solution.py:33
  53.5 4.3 %collective-permute-start.16 = (bf16[256,128]{1,0:T(8,128)(2,1)S(1)}, bf16[256,128]{1,0:T(8,128)(2,1)S(1)}, u32[]{:S(2)}, u32[]{:S(2)}) collective-permute-start(bf16[256,128]{1,0:T(8,128)(2,1)S(1)} %get-tuple-element.48), channel_id=1, source_target_pairs={{0,2},{2,0},{1,3},{3,1},{4,6},{6,4},{5,7},{7,5},{8,10},{10,8},{9,1... | collective-permute-start | bytes 196616 | tf_op jit(solution)/shard_map/ppermute | solution.py:33

commit v12 on v11

--- a/solution.py
+++ b/solution.py
@@ -306,10 +306,15 @@
         copy[...] = source[...]
 
 
+def stack_kernel(count, *refs):
+    for index, source in enumerate(refs[:count]):
+        refs[-1][index] = source[...]
+
+
 def scores_kernel(cycle, count, *refs):
-    own, peers = refs[:cycle], refs[cycle:2 * cycle]
-    highs, lows = refs[2 * cycle:2 * cycle + count], refs[2 * cycle + count:2 * cycle + 2 * count]
-    train, sent, kept, pre = refs[2 * cycle + 2 * count:]
+    own, peers, refs = refs[:cycle], [refs[cycle].at[index] for index in range(cycle)], refs[cycle + 1:]
+    highs, lows = refs[:count], refs[count:2 * count]
+    train, sent, kept, pre = refs[2 * count:]
     mine, rep, model = lax.axis_index("dp"), lax.axis_index("rep"), lax.axis_index("mp")
     for half, slabs in ((rep, own), (1 - rep, peers)):
         for shift in range(cycle):
@@ -437,15 +442,14 @@
             gathered[late] = lax.ppermute(again[0], "dp", [(1, 2), (2, 1)])
         if s == 2:
             far = [lax.ppermute(again[0], "dp", [(1, 0), (2, 3)])]
-    handed = list(inverses)
-    handed[late] = call(
-        functools.partial(hand_kernel, 1),
-        shape((SLAB, FBLK), f32),
-        [VMEM] + [HBM] * (cycle - 2),
+    stacked = call(
+        functools.partial(stack_kernel, cycle),
+        shape((cycle, SLAB, FBLK), f32),
+        [VMEM] * cycle + [HBM] * (cycle - 2),
         vmem=16,
-        moved=8 * SLAB * FBLK,
-    )(inverses[late], *[highs[s] for s in range(1, cycle) if s != late])
-    peers = [swapped(slab, "rep", 1) for slab in handed]
+        moved=8 * cycle * SLAB * FBLK,
+    )(*inverses, *[highs[s] for s in range(1, cycle) if s != late])
+    peers = swapped(stacked, "rep", 1)
 
     half_rows = train_rows // lax.axis_size("mp")
     pieces, order = [], []
@@ -454,12 +458,12 @@
         outgoing, kept = call(
             functools.partial(scores_kernel, cycle, count),
             [shape((half_rows, count * queries), bf16)] * 2,
-            [VMEM] * (2 * cycle + 2 * count + 1),
+            [VMEM] * (cycle + 2 * count + 2),
             [pltpu.VMEM((feat, count * queries), bf16)],
             vmem=24,
             flops=2 * train_rows * feat * count * queries,
             moved=8 * feat * queries * count,
-        )(*inverses, *peers, *[highs[s] for s in chosen], *[lows[s] for s in chosen], train_grads)
+        )(*inverses, peers, *[highs[s] for s in chosen], *[lows[s] for s in chosen], train_grads)
         pieces += [kept, swapped(outgoing, "mp", 1)]
         order += chosen
     total = call(

time: 59 us -> 62.4 us (1.058)
  waiting for transfers between devices: 6.06 us -> 10.3 us
  starting transfers between devices: 22.4 us -> 21.7 us
    ppermute x1, waiting for transfers between devices: 2.47 us -> 5.15 us  [split_over_blocks(): far = [lax.ppermute(again[0], 'dp', [(1, 0), (2, 3)])]]
    ppermute x15 -> x12, waiting for transfers between devices: 3.58 us -> 5.12 us  [swapped(): lax.ppermute(shard, axis, [(i, i ^ by) for i in range(lax.axis_size(axis))])]
    ppermute x15 -> x12, starting transfers between devices: 20.2 us -> 19.5 us  [swapped(): lax.ppermute(shard, axis, [(i, i ^ by) for i in range(lax.axis_size(axis))])]
  transfers between devices with their start and end apart: 17 -> 14, of which waited for: 4 -> 5; matrix products, arithmetic and copies ran while one was open for 0% -> 0% of each run, Pallas kernels for 28% -> 26%
where the time goes in v12:
time: 62.4 us; the launch traced here: 62.2 us
  Pallas kernels  27.5 us (44%)
  starting transfers between devices  21.7 us (35%)
  waiting for transfers between devices  10.3 us (17%)
  local copies, waits for them, and re-layouts  2.6 us (4%)
    ppermute x12, starting transfers between devices, swapped(): lax.ppermute(shard, axis, [(i, i ^ by) for i in range(lax.axis_size(axis))])  19.5 us
    pallas_call x1, Pallas kernels, split_over_blocks(): call(first_kernel, [shape((2 * each + proj, tokens), bf16)] * 2 + [shape(...  11.1 us
    pallas_call x1, Pallas kernels, split_over_blocks(): call(functools.partial(factor_kernel, train_rows * cycle, 1.0 / proj), sh...  6.58 us
    pallas_call x4, Pallas kernels, split_over_blocks(): call(functools.partial(queries_kernel, each, cycle if s == late else 0),...  5.65 us
    ppermute x1, waiting for transfers between devices, split_over_blocks(): far = [lax.ppermute(again[0], 'dp', [(1, 0), (2, 3)])]  5.15 us
    ppermute x12, waiting for transfers between devices, swapped(): lax.ppermute(shard, axis, [(i, i ^ by) for i in range(lax.axis_size(axis))])  5.12 us
    pallas_call x2, Pallas kernels, split_over_blocks(): call(functools.partial(scores_kernel, cycle, count), [shape((half_rows, c...  3.89 us
    unnamed x6, local copies, waits for them, and re-layouts  1.84 us
  transfers between devices with their start and end apart: 14, of which 5 were waited for; matrix products, arithmetic and copies ran while one was open for 0% of the time, Pallas kernels for 26%

profile of v12, /device:TPU:0, one launch (start us, length us, event | category | flops | bytes accessed | tf_op | source)
XLA Modules:
  0.0 62.2 jit_solution(3197155689254464843)
XLA Ops:
  0.0 11.1 %shard_map.64 = (bf16[128,1024]{1,0:T(8,128)(2,1)}, bf16[128,1024]{1,0:T(8,128)(2,1)}, f32[136,128]{1,0:T(8,128)}, f32[136,128]{1,0:T(8,128)}, f32[136,128]{1,0:T(8,128)}, /*index=5*/f32[136,128]{1,0:T(8,128)}) custom-call(s32[8,128]{1,0:T(8,128)} %bitcast.6, bf16[1024,2048]{1,0:T(8,128)(2,1)} %delta_hbm.1, bf16[64,64128]{1,0:T(8,128)(2,1)} %bitcast.4, ...), custom_call_target="tpu_custom_call" | custom-call | flops 268435456 | bytes 24805376 | tf_op jit(solution)/shard_map/pallas_call | solution.py:373
  11.2 3.0 %collective-permute-start.3 = (bf16[128,1024]{1,0:T(8,128)(2,1)}, bf16[128,1024]{1,0:T(8,128)(2,1)S(1)}, u32[]{:S(2)}, u32[]{:S(2)}) collective-permute-start(bf16[128,1024]{1,0:T(8,128)(2,1)} %get-tuple-element.34), channel_id=1, source_target_pairs={{0,2},{2,0},{1,3},{3,1},{4,6},{6,4},{5,7},{7,5},{8,10},{10,8},{9,1... | collective-permute-start | bytes 786440 | tf_op jit(solution)/shard_map/ppermute | solution.py:33
  14.2 1.6 %collective-permute-start = (f32[136,128]{1,0:T(8,128)}, f32[136,128]{1,0:T(8,128)S(1)}, u32[]{:S(2)}, u32[]{:S(2)}) collective-permute-start(f32[136,128]{1,0:T(8,128)} %get-tuple-element.30), channel_id=1, source_target_pairs={{0,4},{4,0},{8,12},{12,8},{1,5},{5,1},{9,13},{13,9},{2,6},{6,2},{1... | collective-permute-start | bytes 208904 | tf_op jit(solution)/shard_map/ppermute | solution.py:33
  15.7 2.6 %collective-permute-start.1 = (f32[136,128]{1,0:T(8,128)}, f32[136,128]{1,0:T(8,128)S(1)}, u32[]{:S(2)}, u32[]{:S(2)}) collective-permute-start(f32[136,128]{1,0:T(8,128)} %get-tuple-element.31), channel_id=1, source_target_pairs={{0,8},{4,12},{8,0},{12,4},{1,9},{5,13},{9,1},{13,5},{2,10},{6,14},... | collective-permute-start | bytes 208904 | tf_op jit(solution)/shard_map/ppermute | solution.py:33
  18.3 0.2 collective-permute-start.2
  18.6 0.0 copy-start.1
  18.6 0.9 %copy-done.1 = bf16[128,1024]{1,0:T(8,128)(2,1)S(1)} copy-done((bf16[128,1024]{1,0:T(8,128)(2,1)S(1)}, bf16[128,1024]{1,0:T(8,128)(2,1)}, u32[]{:S(2)}) %copy-start.1) | copy-done | bytes 262168
  19.5 0.0 copy-start.2
  19.5 0.9 %copy-done.2 = f32[136,128]{1,0:T(8,128)S(1)} copy-done((f32[136,128]{1,0:T(8,128)S(1)}, f32[136,128]{1,0:T(8,128)}, u32[]{:S(2)}) %copy-start.2) | copy-done | bytes 69656
  20.4 0.3 collective-permute-done.3.got
  20.7 0.1 shard_map.66.refs_4_.refs_0_.factors
  20.8 1.9 %collective-permute-start.7 = (bf16[128,1024]{1,0:T(8,128)(2,1)S(1)}, bf16[128,1024]{1,0:T(8,128)(2,1)S(1)}, u32[]{:S(2)}, u32[]{:S(2)}) collective-permute-start(bf16[128,1024]{1,0:T(8,128)(2,1)S(1)} %shard_map.66.refs_4_.refs_0_.factors), channel_id=1, source_target_pairs={{0,4},{4,0},{8,12},{12,8},{1,5},{5,1},{9,13},{13,9},{2,6},{6,2},{1... | collective-permute-start | bytes 786440 | tf_op jit(solution)/shard_map/ppermute | solution.py:33
  22.6 2.6 %collective-permute-start.8 = (bf16[128,1024]{1,0:T(8,128)(2,1)S(1)}, bf16[128,1024]{1,0:T(8,128)(2,1)S(1)}, u32[]{:S(2)}, u32[]{:S(2)}) collective-permute-start(bf16[128,1024]{1,0:T(8,128)(2,1)S(1)} %shard_map.66.refs_4_.refs_0_.factors), channel_id=1, source_target_pairs={{0,8},{4,12},{8,0},{12,4},{1,9},{5,13},{9,1},{13,5},{2,10},{6,14},... | collective-permute-start | bytes 786440 | tf_op jit(solution)/shard_map/ppermute | solution.py:33
  25.2 0.0 collective-permute-done.refs_1_.slab
  25.2 0.0 collective-permute-done.1.refs_2_.slab
  25.2 0.0 collective-permute-done.2.refs_3_.slab
  25.3 6.6 %shard_map.67.refs_0_ = f32[136,128]{1,0:T(8,128)S(1)} custom-call(f32[136,128]{1,0:T(8,128)S(1)} %get-tuple-element.29.refs_0_.slab, f32[136,128]{1,0:T(8,128)S(1)} %collective-permute-done.refs_1_.slab, f32[136,128]{1,0:T(8,128)S(1)} %collective-permute-done.1.refs_2_.slab, f32[136,128]{1,0:T(8,128)S(1)} %collective-permute-done.2.refs_3_.slab, ...), custom_call_target="tpu_custom_call" | custom-call | flops 10000000000 | bytes 1000000 | tf_op jit(solution)/shard_map/pallas_call | solution.py:419
  31.8 0.0 copy-start
  31.8 0.5 collective-permute-start.4
  32.3 1.3 %collective-permute-start.5 = (f32[136,128]{1,0:T(8,128)S(1)}, f32[136,128]{1,0:T(8,128)S(1)}, u32[]{:S(2)}, u32[]{:S(2)}) collective-permute-start(f32[136,128]{1,0:T(8,128)S(1)} %shard_map.67.refs_0_), channel_id=1, source_target_pairs={{0,8},{4,12},{8,0},{12,4},{1,9},{5,13},{9,1},{13,5},{2,10},{6,14},... | collective-permute-start | bytes 208904 | tf_op jit(solution)/shard_map/ppermute | solution.py:33
  33.7 2.6 %collective-permute-start.6 = (f32[136,128]{1,0:T(8,128)S(1)}, f32[136,128]{1,0:T(8,128)S(1)}, u32[]{:S(2)}, u32[]{:S(2)}) collective-permute-start(f32[136,128]{1,0:T(8,128)S(1)} %shard_map.67.refs_0_), channel_id=1, source_target_pairs={{0,12},{4,8},{8,4},{12,0},{1,13},{5,9},{9,5},{13,1},{2,14},{6,10},... | collective-permute-start | bytes 208904 | tf_op jit(solution)/shard_map/ppermute | solution.py:33
  36.3 0.2 collective-permute-done.7.factors
  36.5 1.4 %shard_map.68 = (bf16[2048,128]{1,0:T(8,128)(2,1)S(1)}, bf16[2048,128]{1,0:T(8,128)(2,1)S(1)}, bf16[128,1024]{1,0:T(8,128)(2,1)S(1)}) custom-call(bf16[128,1024]{1,0:T(8,128)(2,1)S(1)} %collective-permute-done.7.factors, f32[136,128]{1,0:T(8,128)S(1)} %collective-permute-done.refs_1_.slab, bf16[128,1024]{1,0:T(8,128)(2,1)S(1)} %shard_map.66.refs_4_.refs_0_.factors), custom_call_target="tpu_custom_call" | custom-call | flops 536870912 | bytes 1572864 | tf_op jit(solution)/shard_map/pallas_call | solution.py:433
  37.9 0.0 collective-permute-done.8.factors.refs_0_
  37.9 1.4 %shard_map.69 = (bf16[2048,128]{1,0:T(8,128)(2,1)S(1)}, bf16[2048,128]{1,0:T(8,128)(2,1)S(1)}, bf16[128,1024]{1,0:T(8,128)(2,1)S(1)}) custom-call(bf16[128,1024]{1,0:T(8,128)(2,1)S(1)} %collective-permute-done.8.factors.refs_0_, f32[136,128]{1,0:T(8,128)S(1)} %collective-permute-done.1.refs_2_.slab, bf16[128,1024]{1,0:T(8,128)(2,1)S(1)} %collective-permute-done.8.factors.refs_0_), custom_call_target="tpu_custom_call" | custom-call | flops 536870912 | bytes 1572864 | tf_op jit(solution)/shard_map/pallas_call | solution.py:433
  39.3 0.0 collective-permute-done.4.refs_1_
  39.3 1.9 %collective-permute-done.5.refs_2_ = f32[136,128]{1,0:T(8,128)S(1)} collective-permute-done((f32[136,128]{1,0:T(8,128)S(1)}, f32[136,128]{1,0:T(8,128)S(1)}, u32[]{:S(2)}, u32[]{:S(2)}) %collective-permute-start.5) | collective-permute-done | bytes 69664 | tf_op jit(solution)/shard_map/ppermute | solution.py:33
  41.2 0.0 collective-permute-done.6.refs_3_
  41.3 0.1 collective-permute-start.9
  41.3 0.7 %collective-permute-start.11 = (bf16[128,1024]{1,0:T(8,128)(2,1)S(1)}, bf16[128,1024]{1,0:T(8,128)(2,1)S(1)}, u32[]{:S(2)}, u32[]{:S(2)}) collective-permute-start(bf16[128,1024]{1,0:T(8,128)(2,1)S(1)} %get-tuple-element.43), channel_id=1, source_target_pairs={{4,8},{8,4},{5,9},{9,5},{6,10},{10,6},{7,11},{11,7},{20,24},{24,20... | collective-permute-start | bytes 786440 | tf_op jit(solution)/shard_map/ppermute | solution.py:442
  42.0 1.5 %collective-permute-start.12 = (bf16[128,1024]{1,0:T(8,128)(2,1)S(1)}, bf16[128,1024]{1,0:T(8,128)(2,1)S(1)}, u32[]{:S(2)}, u32[]{:S(2)}) collective-permute-start(bf16[128,1024]{1,0:T(8,128)(2,1)S(1)} %get-tuple-element.44), channel_id=1, source_target_pairs={{4,0},{8,12},{5,1},{9,13},{6,2},{10,14},{7,3},{11,15},{20,16},{24,... | collective-permute-start | bytes 786440 | tf_op jit(solution)/shard_map/ppermute | solution.py:444
  43.5 1.4 %shard_map.71 = (bf16[2048,128]{1,0:T(8,128)(2,1)S(1)}, bf16[2048,128]{1,0:T(8,128)(2,1)S(1)}) custom-call(bf16[128,1024]{1,0:T(8,128)(2,1)S(1)} %shard_map.66.refs_4_.refs_0_.factors, f32[136,128]{1,0:T(8,128)S(1)} %get-tuple-element.29.refs_0_.slab, f32[136,128]{1,0:T(8,128)S(1)} %shard_map.67.refs_0_), custom_call_target="tpu_custom_call" | custom-call | flops 536870912 | bytes 1572864 | tf_op jit(solution)/shard_map/pallas_call | solution.py:433
  44.9 0.0 collective-permute-done.9.refs_4_
  44.9 0.0 copy-done
  44.9 2.5 %shard_map.72 = (bf16[256,384]{1,0:T(8,128)(2,1)S(1)}, bf16[256,384]{1,0:T(8,128)(2,1)S(1)}) custom-call(f32[136,128]{1,0:T(8,128)S(1)} %shard_map.67.refs_0_, f32[136,128]{1,0:T(8,128)S(1)} %collective-permute-done.4.refs_1_, f32[136,128]{1,0:T(8,128)S(1)} %collective-permute-done.5.refs_2_, f32[136,128]{1,0:T(8,128)S(1)} %collective-permute-done.6.refs_3_, ...), custom_call_target="tpu_custom_call" | custom-call | flops 805306368 | bytes 6291456 | tf_op jit(solution)/shard_map/pallas_call | solution.py:458
  47.5 1.6 %collective-permute-start.10 = (bf16[256,384]{1,0:T(8,128)(2,1)S(1)}, bf16[256,384]{1,0:T(8,128)(2,1)S(1)}, u32[]{:S(2)}, u32[]{:S(2)}) collective-permute-start(bf16[256,384]{1,0:T(8,128)(2,1)S(1)} %get-tuple-element.42), channel_id=1, source_target_pairs={{0,2},{2,0},{1,3},{3,1},{4,6},{6,4},{5,7},{7,5},{8,10},{10,8},{9,1... | collective-permute-start | bytes 589832 | tf_op jit(solution)/shard_map/ppermute | solution.py:33
  49.0 0.0 collective-permute-done.11.factors
  49.0 5.2 %collective-permute-done.12.refs_0_ = bf16[128,1024]{1,0:T(8,128)(2,1)S(1)} collective-permute-done((bf16[128,1024]{1,0:T(8,128)(2,1)S(1)}, bf16[128,1024]{1,0:T(8,128)(2,1)S(1)}, u32[]{:S(2)}, u32[]{:S(2)}) %collective-permute-start.12) | collective-permute-done | bytes 262176 | tf_op jit(solution)/shard_map/ppermute | solution.py:444
  54.2 1.4 %shard_map.73 = (bf16[2048,128]{1,0:T(8,128)(2,1)S(1)}, bf16[2048,128]{1,0:T(8,128)(2,1)S(1)}) custom-call(bf16[128,1024]{1,0:T(8,128)(2,1)S(1)} %collective-permute-done.11.factors, f32[136,128]{1,0:T(8,128)S(1)} %collective-permute-done.2.refs_3_.slab, bf16[128,1024]{1,0:T(8,128)(2,1)S(1)} %collective-permute-done.12.refs_0_), custom_call_target="tpu_custom_call" | custom-call | flops 536870912 | bytes 1572864 | tf_op jit(solution)/shard_map/pallas_call | solution.py:433
  55.6 1.4 %shard_map.74 = (bf16[256,128]{1,0:T(8,128)(2,1)S(1)}, bf16[256,128]{1,0:T(8,128)(2,1)S(1)}) custom-call(f32[136,128]{1,0:T(8,128)S(1)} %shard_map.67.refs_0_, f32[136,128]{1,0:T(8,128)S(1)} %collective-permute-done.4.refs_1_, f32[136,128]{1,0:T(8,128)S(1)} %collective-permute-done.5.refs_2_, f32[136,128]{1,0:T(8,128)S(1)} %collective-permute-done.6.refs_3_, ...), custom_call_target="tpu_custom_call" | custom-call | flops 268435456 | bytes 2097152 | tf_op jit(solution)/shard_map/pallas_call | solution.py:458
  57.0 1.6 %collective-permute-start.13 = (bf16[256,128]{1,0:T(8,128)(2,1)S(1)}, bf16[256,128]{1,0:T(8,128)(2,1)S(1)}, u32[]{:S(2)}, u32[]{:S(2)}) collective-permute-start(bf16[256,128]{1,0:T(8,128)(2,1)S(1)} %get-tuple-element.48), channel_id=1, source_target_pairs={{0,2},{2,0},{1,3},{3,1},{4,6},{6,4},{5,7},{7,5},{8,10},{10,8},{9,1... | collective-permute-start | bytes 196616 | tf_op jit(solution)/shard_map/ppermute | solution.py:33
  58.5 2.8 %collective-permute-done.13.refs_3_ = bf16[256,128]{1,0:T(8,128)(2,1)S(1)} collective-permute-done((bf16[256,128]{1,0:T(8,128)(2,1)S(1)}, bf16[256,128]{1,0:T(8,128)(2,1)S(1)}, u32[]{:S(2)}, u32[]{:S(2)}) %collective-permute-start.13) | collective-permute-done | bytes 65568 | tf_op jit(solution)/shard_map/ppermute | solution.py:33
  61.3 0.0 collective-permute-done.10.refs_1_
  61.3 0.1 shard_map.75
  61.4 0.8 %reshape.7 = bf16[256,4,1,128]{3,1,0,2:T(4,128)(2,1)} reshape(bf16[256,512]{1,0:T(8,128)(2,1)S(1)} %shard_map.75) | data formatting | bytes 524288 | tf_op jit(solution)/shard_map/reshape | solution.py:477
  (2 shorter events, 0.0 us)
Async XLA Ops:
  11.2 9.5 %collective-permute-start.3 = (bf16[128,1024]{1,0:T(8,128)(2,1)}, bf16[128,1024]{1,0:T(8,128)(2,1)S(1)}, u32[]{:S(2)}, u32[]{:S(2)}) collective-permute-start(bf16[128,1024]{1,0:T(8,128)(2,1)} %get-tuple-element.34), channel_id=1, source_target_pairs={{0,2},{2,0},{1,3},{3,1},{4,6},{6,4},{5,7},{7,5},{8,10},{10,8},{9,1... | collective-permute-start | bytes 786440 | tf_op jit(solution)/shard_map/ppermute | solution.py:33
  14.2 11.1 %collective-permute-start = (f32[136,128]{1,0:T(8,128)}, f32[136,128]{1,0:T(8,128)S(1)}, u32[]{:S(2)}, u32[]{:S(2)}) collective-permute-start(f32[136,128]{1,0:T(8,128)} %get-tuple-element.30), channel_id=1, source_target_pairs={{0,4},{4,0},{8,12},{12,8},{1,5},{5,1},{9,13},{13,9},{2,6},{6,2},{1... | collective-permute-start | bytes 208904 | tf_op jit(solution)/shard_map/ppermute | solution.py:33
  15.7 9.5 %collective-permute-start.1 = (f32[136,128]{1,0:T(8,128)}, f32[136,128]{1,0:T(8,128)S(1)}, u32[]{:S(2)}, u32[]{:S(2)}) collective-permute-start(f32[136,128]{1,0:T(8,128)} %get-tuple-element.31), channel_id=1, source_target_pairs={{0,8},{4,12},{8,0},{12,4},{1,9},{5,13},{9,1},{13,5},{2,10},{6,14},... | collective-permute-start | bytes 208904 | tf_op jit(solution)/shard_map/ppermute | solution.py:33
  18.3 6.9 %collective-permute-start.2 = (f32[136,128]{1,0:T(8,128)}, f32[136,128]{1,0:T(8,128)S(1)}, u32[]{:S(2)}, u32[]{:S(2)}) collective-permute-start(f32[136,128]{1,0:T(8,128)} %get-tuple-element.32), channel_id=1, source_target_pairs={{0,12},{4,8},{8,4},{12,0},{1,13},{5,9},{9,5},{13,1},{2,14},{6,10},... | collective-permute-start | bytes 208904 | tf_op jit(solution)/shard_map/ppermute | solution.py:33
  18.6 0.9 %copy-start.1 = (bf16[128,1024]{1,0:T(8,128)(2,1)S(1)}, bf16[128,1024]{1,0:T(8,128)(2,1)}, u32[]{:S(2)}) copy-start(bf16[128,1024]{1,0:T(8,128)(2,1)} %get-tuple-element.27.refs_0_) | copy-start | bytes 786436
  19.5 0.9 %copy-start.2 = (f32[136,128]{1,0:T(8,128)S(1)}, f32[136,128]{1,0:T(8,128)}, u32[]{:S(2)}) copy-start(f32[136,128]{1,0:T(8,128)} %get-tuple-element.28.refs_1_) | copy-start | bytes 208900
  20.8 15.7 %collective-permute-start.7 = (bf16[128,1024]{1,0:T(8,128)(2,1)S(1)}, bf16[128,1024]{1,0:T(8,128)(2,1)S(1)}, u32[]{:S(2)}, u32[]{:S(2)}) collective-permute-start(bf16[128,1024]{1,0:T(8,128)(2,1)S(1)} %shard_map.66.refs_4_.refs_0_.factors), channel_id=1, source_target_pairs={{0,4},{4,0},{8,12},{12,8},{1,5},{5,1},{9,13},{13,9},{2,6},{6,2},{1... | collective-permute-start | bytes 786440 | tf_op jit(solution)/shard_map/ppermute | solution.py:33
  22.6 15.3 %collective-permute-start.8 = (bf16[128,1024]{1,0:T(8,128)(2,1)S(1)}, bf16[128,1024]{1,0:T(8,128)(2,1)S(1)}, u32[]{:S(2)}, u32[]{:S(2)}) collective-permute-start(bf16[128,1024]{1,0:T(8,128)(2,1)S(1)} %shard_map.66.refs_4_.refs_0_.factors), channel_id=1, source_target_pairs={{0,8},{4,12},{8,0},{12,4},{1,9},{5,13},{9,1},{13,5},{2,10},{6,14},... | collective-permute-start | bytes 786440 | tf_op jit(solution)/shard_map/ppermute | solution.py:33
  31.8 13.1 %copy-start = (bf16[512,2048]{1,0:T(8,128)(2,1)S(1)}, bf16[512,2048]{1,0:T(8,128)(2,1)}, u32[]{:S(2)}) copy-start(bf16[512,2048]{1,0:T(8,128)(2,1)} %refs_7_.1) | copy-start | bytes 6291460
  31.8 7.5 %collective-permute-start.4 = (f32[136,128]{1,0:T(8,128)S(1)}, f32[136,128]{1,0:T(8,128)S(1)}, u32[]{:S(2)}, u32[]{:S(2)}) collective-permute-start(f32[136,128]{1,0:T(8,128)S(1)} %shard_map.67.refs_0_), channel_id=1, source_target_pairs={{0,4},{4,0},{8,12},{12,8},{1,5},{5,1},{9,13},{13,9},{2,6},{6,2},{1... | collective-permute-start | bytes 208904 | tf_op jit(solution)/shard_map/ppermute | solution.py:33
  32.3 8.9 %collective-permute-start.5 = (f32[136,128]{1,0:T(8,128)S(1)}, f32[136,128]{1,0:T(8,128)S(1)}, u32[]{:S(2)}, u32[]{:S(2)}) collective-permute-start(f32[136,128]{1,0:T(8,128)S(1)} %shard_map.67.refs_0_), channel_id=1, source_target_pairs={{0,8},{4,12},{8,0},{12,4},{1,9},{5,13},{9,1},{13,5},{2,10},{6,14},... | collective-permute-start | bytes 208904 | tf_op jit(solution)/shard_map/ppermute | solution.py:33
  33.7 7.6 %collective-permute-start.6 = (f32[136,128]{1,0:T(8,128)S(1)}, f32[136,128]{1,0:T(8,128)S(1)}, u32[]{:S(2)}, u32[]{:S(2)}) collective-permute-start(f32[136,128]{1,0:T(8,128)S(1)} %shard_map.67.refs_0_), channel_id=1, source_target_pairs={{0,12},{4,8},{8,4},{12,0},{1,13},{5,9},{9,5},{13,1},{2,14},{6,10},... | collective-permute-start | bytes 208904 | tf_op jit(solution)/shard_map/ppermute | solution.py:33
  41.3 3.7 %collective-permute-start.9 = (f32[4,136,128]{2,1,0:T(8,128)S(1)}, f32[4,136,128]{2,1,0:T(8,128)S(1)}, u32[]{:S(2)}, u32[]{:S(2)}) collective-permute-start(f32[4,136,128]{2,1,0:T(8,128)S(1)} %shard_map.70), channel_id=1, source_target_pairs={{0,1},{1,0},{2,3},{3,2},{4,5},{5,4},{6,7},{7,6},{8,9},{9,8},{10,11... | collective-permute-start | bytes 835592 | tf_op jit(solution)/shard_map/ppermute | solution.py:33
  41.3 7.7 %collective-permute-start.11 = (bf16[128,1024]{1,0:T(8,128)(2,1)S(1)}, bf16[128,1024]{1,0:T(8,128)(2,1)S(1)}, u32[]{:S(2)}, u32[]{:S(2)}) collective-permute-start(bf16[128,1024]{1,0:T(8,128)(2,1)S(1)} %get-tuple-element.43), channel_id=1, source_target_pairs={{4,8},{8,4},{5,9},{9,5},{6,10},{10,6},{7,11},{11,7},{20,24},{24,20... | collective-permute-start | bytes 786440 | tf_op jit(solution)/shard_map/ppermute | solution.py:442
  42.0 12.2 %collective-permute-start.12 = (bf16[128,1024]{1,0:T(8,128)(2,1)S(1)}, bf16[128,1024]{1,0:T(8,128)(2,1)S(1)}, u32[]{:S(2)}, u32[]{:S(2)}) collective-permute-start(bf16[128,1024]{1,0:T(8,128)(2,1)S(1)} %get-tuple-element.44), channel_id=1, source_target_pairs={{4,0},{8,12},{5,1},{9,13},{6,2},{10,14},{7,3},{11,15},{20,16},{24,... | collective-permute-start | bytes 786440 | tf_op jit(solution)/shard_map/ppermute | solution.py:444
  47.5 13.8 %collective-permute-start.10 = (bf16[256,384]{1,0:T(8,128)(2,1)S(1)}, bf16[256,384]{1,0:T(8,128)(2,1)S(1)}, u32[]{:S(2)}, u32[]{:S(2)}) collective-permute-start(bf16[256,384]{1,0:T(8,128)(2,1)S(1)} %get-tuple-element.42), channel_id=1, source_target_pairs={{0,2},{2,0},{1,3},{3,1},{4,6},{6,4},{5,7},{7,5},{8,10},{10,8},{9,1... | collective-permute-start | bytes 589832 | tf_op jit(solution)/shard_map/ppermute | solution.py:33
  57.0 4.3 %collective-permute-start.13 = (bf16[256,128]{1,0:T(8,128)(2,1)S(1)}, bf16[256,128]{1,0:T(8,128)(2,1)S(1)}, u32[]{:S(2)}, u32[]{:S(2)}) collective-permute-start(bf16[256,128]{1,0:T(8,128)(2,1)S(1)} %get-tuple-element.48), channel_id=1, source_target_pairs={{0,2},{2,0},{1,3},{3,1},{4,6},{6,4},{5,7},{7,5},{8,10},{10,8},{9,1... | collective-permute-start | bytes 196616 | tf_op jit(solution)/shard_map/ppermute | solution.py:33

commit v13 on v11

--- a/solution.py
+++ b/solution.py
@@ -438,13 +438,13 @@
         if s == 2:
             far = [lax.ppermute(again[0], "dp", [(1, 0), (2, 3)])]
     handed = list(inverses)
-    handed[late] = call(
-        functools.partial(hand_kernel, 1),
-        shape((SLAB, FBLK), f32),
-        [VMEM] + [HBM] * (cycle - 2),
+    handed[0], handed[late] = call(
+        functools.partial(hand_kernel, 2),
+        [shape((SLAB, FBLK), f32)] * 2,
+        [VMEM] * 2 + [HBM] * (cycle - 2),
         vmem=16,
-        moved=8 * SLAB * FBLK,
-    )(inverses[late], *[highs[s] for s in range(1, cycle) if s != late])
+        moved=16 * SLAB * FBLK,
+    )(inverse, inverses[late], *[highs[s] for s in range(1, cycle) if s != late])
     peers = [swapped(slab, "rep", 1) for slab in handed]
 
     half_rows = train_rows // lax.axis_size("mp")

time: 59 us -> 61 us (1.034)
  waiting for transfers between devices: 6.06 us -> 9.19 us
  starting transfers between devices: 22.4 us -> 21.3 us
    ppermute x1, waiting for transfers between devices: 2.47 us -> 4.15 us  [split_over_blocks(): far = [lax.ppermute(again[0], 'dp', [(1, 0), (2, 3)])]]
    ppermute x15, waiting for transfers between devices: 3.58 us -> 5.04 us  [swapped(): lax.ppermute(shard, axis, [(i, i ^ by) for i in range(lax.axis_size(axis))])]
    ppermute x15, starting transfers between devices: 20.2 us -> 19.2 us  [swapped(): lax.ppermute(shard, axis, [(i, i ^ by) for i in range(lax.axis_size(axis))])]
  transfers between devices with their start and end apart: 17 -> 17, of which waited for: 4 -> 4; matrix products, arithmetic and copies ran while one was open for 0% -> 0% of each run, Pallas kernels for 28% -> 27%
where the time goes in v13:
time: 61 us; the launch traced here: 60.8 us
  Pallas kernels  27.5 us (45%)
  starting transfers between devices  21.3 us (35%)
  waiting for transfers between devices  9.19 us (15%)
  local copies, waits for them, and re-layouts  2.6 us (4%)
    ppermute x15, starting transfers between devices, swapped(): lax.ppermute(shard, axis, [(i, i ^ by) for i in range(lax.axis_size(axis))])  19.2 us
    pallas_call x1, Pallas kernels, split_over_blocks(): call(first_kernel, [shape((2 * each + proj, tokens), bf16)] * 2 + [shape(...  11.2 us
    pallas_call x1, Pallas kernels, split_over_blocks(): call(functools.partial(factor_kernel, train_rows * cycle, 1.0 / proj), sh...  6.58 us
    pallas_call x4, Pallas kernels, split_over_blocks(): call(functools.partial(queries_kernel, each, cycle if s == late else 0),...  5.66 us
    ppermute x15, waiting for transfers between devices, swapped(): lax.ppermute(shard, axis, [(i, i ^ by) for i in range(lax.axis_size(axis))])  5.04 us
    ppermute x1, waiting for transfers between devices, split_over_blocks(): far = [lax.ppermute(again[0], 'dp', [(1, 0), (2, 3)])]  4.15 us
    pallas_call x2, Pallas kernels, split_over_blocks(): call(functools.partial(scores_kernel, cycle, count), [shape((half_rows, c...  3.9 us
    unnamed x6, local copies, waits for them, and re-layouts  1.84 us
  transfers between devices with their start and end apart: 17, of which 4 were waited for; matrix products, arithmetic and copies ran while one was open for 0% of the time, Pallas kernels for 27%

profile of v13, /device:TPU:0, one launch (start us, length us, event | category | flops | bytes accessed | tf_op | source)
XLA Modules:
  0.0 60.8 jit_solution(8498965989157512881)
XLA Ops:
  0.0 11.2 %shard_map.64 = (bf16[128,1024]{1,0:T(8,128)(2,1)}, bf16[128,1024]{1,0:T(8,128)(2,1)}, f32[136,128]{1,0:T(8,128)}, f32[136,128]{1,0:T(8,128)}, f32[136,128]{1,0:T(8,128)}, /*index=5*/f32[136,128]{1,0:T(8,128)}) custom-call(s32[8,128]{1,0:T(8,128)} %bitcast.6, bf16[1024,2048]{1,0:T(8,128)(2,1)} %delta_hbm.1, bf16[64,64128]{1,0:T(8,128)(2,1)} %bitcast.4, ...), custom_call_target="tpu_custom_call" | custom-call | flops 268435456 | bytes 24805376 | tf_op jit(solution)/shard_map/pallas_call | solution.py:368
  11.2 3.0 %collective-permute-start.3 = (bf16[128,1024]{1,0:T(8,128)(2,1)}, bf16[128,1024]{1,0:T(8,128)(2,1)S(1)}, u32[]{:S(2)}, u32[]{:S(2)}) collective-permute-start(bf16[128,1024]{1,0:T(8,128)(2,1)} %get-tuple-element.36), channel_id=1, source_target_pairs={{0,2},{2,0},{1,3},{3,1},{4,6},{6,4},{5,7},{7,5},{8,10},{10,8},{9,1... | collective-permute-start | bytes 786440 | tf_op jit(solution)/shard_map/ppermute | solution.py:33
  14.2 1.6 %collective-permute-start = (f32[136,128]{1,0:T(8,128)}, f32[136,128]{1,0:T(8,128)S(1)}, u32[]{:S(2)}, u32[]{:S(2)}) collective-permute-start(f32[136,128]{1,0:T(8,128)} %get-tuple-element.32), channel_id=1, source_target_pairs={{0,4},{4,0},{8,12},{12,8},{1,5},{5,1},{9,13},{13,9},{2,6},{6,2},{1... | collective-permute-start | bytes 208904 | tf_op jit(solution)/shard_map/ppermute | solution.py:33
  15.7 2.6 %collective-permute-start.1 = (f32[136,128]{1,0:T(8,128)}, f32[136,128]{1,0:T(8,128)S(1)}, u32[]{:S(2)}, u32[]{:S(2)}) collective-permute-start(f32[136,128]{1,0:T(8,128)} %get-tuple-element.33), channel_id=1, source_target_pairs={{0,8},{4,12},{8,0},{12,4},{1,9},{5,13},{9,1},{13,5},{2,10},{6,14},... | collective-permute-start | bytes 208904 | tf_op jit(solution)/shard_map/ppermute | solution.py:33
  18.3 0.2 collective-permute-start.2
  18.5 0.9 %copy-done.1 = bf16[128,1024]{1,0:T(8,128)(2,1)S(1)} copy-done((bf16[128,1024]{1,0:T(8,128)(2,1)S(1)}, bf16[128,1024]{1,0:T(8,128)(2,1)}, u32[]{:S(2)}) %copy-start.1) | copy-done | bytes 262168
  19.5 0.9 %copy-done.2 = f32[136,128]{1,0:T(8,128)S(1)} copy-done((f32[136,128]{1,0:T(8,128)S(1)}, f32[136,128]{1,0:T(8,128)}, u32[]{:S(2)}) %copy-start.2) | copy-done | bytes 69656
  20.4 0.3 collective-permute-done.3.got
  20.7 0.1 shard_map.66.refs_4_.refs_0_.factors
  20.8 1.9 %collective-permute-start.7 = (bf16[128,1024]{1,0:T(8,128)(2,1)S(1)}, bf16[128,1024]{1,0:T(8,128)(2,1)S(1)}, u32[]{:S(2)}, u32[]{:S(2)}) collective-permute-start(bf16[128,1024]{1,0:T(8,128)(2,1)S(1)} %shard_map.66.refs_4_.refs_0_.factors), channel_id=1, source_target_pairs={{0,4},{4,0},{8,12},{12,8},{1,5},{5,1},{9,13},{13,9},{2,6},{6,2},{1... | collective-permute-start | bytes 786440 | tf_op jit(solution)/shard_map/ppermute | solution.py:33
  22.7 2.6 %collective-permute-start.8 = (bf16[128,1024]{1,0:T(8,128)(2,1)S(1)}, bf16[128,1024]{1,0:T(8,128)(2,1)S(1)}, u32[]{:S(2)}, u32[]{:S(2)}) collective-permute-start(bf16[128,1024]{1,0:T(8,128)(2,1)S(1)} %shard_map.66.refs_4_.refs_0_.factors), channel_id=1, source_target_pairs={{0,8},{4,12},{8,0},{12,4},{1,9},{5,13},{9,1},{13,5},{2,10},{6,14},... | collective-permute-start | bytes 786440 | tf_op jit(solution)/shard_map/ppermute | solution.py:33
  25.2 0.0 collective-permute-done.refs_1_.slab
  25.2 0.0 collective-permute-done.1.refs_2_.slab
  25.2 0.0 collective-permute-done.2.refs_3_.slab
  25.3 6.6 %shard_map.67.refs_0_ = f32[136,128]{1,0:T(8,128)S(1)} custom-call(f32[136,128]{1,0:T(8,128)S(1)} %get-tuple-element.31.refs_0_.slab, f32[136,128]{1,0:T(8,128)S(1)} %collective-permute-done.refs_1_.slab, f32[136,128]{1,0:T(8,128)S(1)} %collective-permute-done.1.refs_2_.slab, f32[136,128]{1,0:T(8,128)S(1)} %collective-permute-done.2.refs_3_.slab, ...), custom_call_target="tpu_custom_call" | custom-call | flops 10000000000 | bytes 1000000 | tf_op jit(solution)/shard_map/pallas_call | solution.py:414
  31.8 0.0 copy-start
  31.8 0.5 collective-permute-start.4
  32.3 2.0 %collective-permute-start.6 = (f32[136,128]{1,0:T(8,128)S(1)}, f32[136,128]{1,0:T(8,128)S(1)}, u32[]{:S(2)}, u32[]{:S(2)}) collective-permute-start(f32[136,128]{1,0:T(8,128)S(1)} %shard_map.67.refs_0_), channel_id=1, source_target_pairs={{0,12},{4,8},{8,4},{12,0},{1,13},{5,9},{9,5},{13,1},{2,14},{6,10},... | collective-permute-start | bytes 208904 | tf_op jit(solution)/shard_map/ppermute | solution.py:33
  34.4 1.0 %collective-permute-start.5 = (f32[136,128]{1,0:T(8,128)S(1)}, f32[136,128]{1,0:T(8,128)S(1)}, u32[]{:S(2)}, u32[]{:S(2)}) collective-permute-start(f32[136,128]{1,0:T(8,128)S(1)} %shard_map.67.refs_0_), channel_id=1, source_target_pairs={{0,8},{4,12},{8,0},{12,4},{1,9},{5,13},{9,1},{13,5},{2,10},{6,14},... | collective-permute-start | bytes 208904 | tf_op jit(solution)/shard_map/ppermute | solution.py:33
  35.4 1.9 %collective-permute-done.4.refs_1_ = f32[136,128]{1,0:T(8,128)S(1)} collective-permute-done((f32[136,128]{1,0:T(8,128)S(1)}, f32[136,128]{1,0:T(8,128)S(1)}, u32[]{:S(2)}, u32[]{:S(2)}) %collective-permute-start.4) | collective-permute-done | bytes 69664 | tf_op jit(solution)/shard_map/ppermute | solution.py:33
  37.3 0.0 collective-permute-start.10
  37.3 0.0 collective-permute-done.7.factors
  37.3 1.4 %shard_map.68 = (bf16[2048,128]{1,0:T(8,128)(2,1)S(1)}, bf16[2048,128]{1,0:T(8,128)(2,1)S(1)}, bf16[128,1024]{1,0:T(8,128)(2,1)S(1)}) custom-call(bf16[128,1024]{1,0:T(8,128)(2,1)S(1)} %collective-permute-done.7.factors, f32[136,128]{1,0:T(8,128)S(1)} %collective-permute-done.refs_1_.slab, bf16[128,1024]{1,0:T(8,128)(2,1)S(1)} %shard_map.66.refs_4_.refs_0_.factors), custom_call_target="tpu_custom_call" | custom-call | flops 536870912 | bytes 1572864 | tf_op jit(solution)/shard_map/pallas_call | solution.py:428
  38.7 0.7 %collective-permute-start.14 = (bf16[128,1024]{1,0:T(8,128)(2,1)S(1)}, bf16[128,1024]{1,0:T(8,128)(2,1)S(1)}, u32[]{:S(2)}, u32[]{:S(2)}) collective-permute-start(bf16[128,1024]{1,0:T(8,128)(2,1)S(1)} %get-tuple-element.47), channel_id=1, source_target_pairs={{4,8},{8,4},{5,9},{9,5},{6,10},{10,6},{7,11},{11,7},{20,24},{24,20... | collective-permute-start | bytes 786440 | tf_op jit(solution)/shard_map/ppermute | solution.py:437
  39.4 0.0 collective-permute-done.8.factors.refs_0_
  39.4 1.4 %shard_map.69 = (bf16[2048,128]{1,0:T(8,128)(2,1)S(1)}, bf16[2048,128]{1,0:T(8,128)(2,1)S(1)}, bf16[128,1024]{1,0:T(8,128)(2,1)S(1)}) custom-call(bf16[128,1024]{1,0:T(8,128)(2,1)S(1)} %collective-permute-done.8.factors.refs_0_, f32[136,128]{1,0:T(8,128)S(1)} %collective-permute-done.1.refs_2_.slab, bf16[128,1024]{1,0:T(8,128)(2,1)S(1)} %collective-permute-done.8.factors.refs_0_), custom_call_target="tpu_custom_call" | custom-call | flops 536870912 | bytes 1572864 | tf_op jit(solution)/shard_map/pallas_call | solution.py:428
  40.9 1.5 %collective-permute-start.15 = (bf16[128,1024]{1,0:T(8,128)(2,1)S(1)}, bf16[128,1024]{1,0:T(8,128)(2,1)S(1)}, u32[]{:S(2)}, u32[]{:S(2)}) collective-permute-start(bf16[128,1024]{1,0:T(8,128)(2,1)S(1)} %get-tuple-element.48), channel_id=1, source_target_pairs={{4,0},{8,12},{5,1},{9,13},{6,2},{10,14},{7,3},{11,15},{20,16},{24,... | collective-permute-start | bytes 786440 | tf_op jit(solution)/shard_map/ppermute | solution.py:439
  42.3 0.0 collective-permute-done.5.refs_2_
  42.4 0.6 collective-permute-start.11
  42.9 0.0 collective-permute-done.6.refs_1_.refs_3_
  42.9 0.1 collective-permute-start.12
  43.0 0.0 collective-permute-done.10.refs_5_
  43.0 0.5 collective-permute-start.9
  43.5 1.4 %shard_map.71 = (bf16[2048,128]{1,0:T(8,128)(2,1)S(1)}, bf16[2048,128]{1,0:T(8,128)(2,1)S(1)}) custom-call(bf16[128,1024]{1,0:T(8,128)(2,1)S(1)} %shard_map.66.refs_4_.refs_0_.factors, f32[136,128]{1,0:T(8,128)S(1)} %get-tuple-element.31.refs_0_.slab, f32[136,128]{1,0:T(8,128)S(1)} %shard_map.67.refs_0_), custom_call_target="tpu_custom_call" | custom-call | flops 536870912 | bytes 1572864 | tf_op jit(solution)/shard_map/pallas_call | solution.py:428
  44.9 0.0 collective-permute-done.11.refs_6_
  44.9 0.0 collective-permute-done.12.refs_7_
  45.0 0.0 collective-permute-done.9.refs_4_
  45.0 2.5 %shard_map.72 = (bf16[256,384]{1,0:T(8,128)(2,1)S(1)}, bf16[256,384]{1,0:T(8,128)(2,1)S(1)}) custom-call(f32[136,128]{1,0:T(8,128)S(1)} %shard_map.67.refs_0_, f32[136,128]{1,0:T(8,128)S(1)} %collective-permute-done.4.refs_1_, f32[136,128]{1,0:T(8,128)S(1)} %collective-permute-done.5.refs_2_, f32[136,128]{1,0:T(8,128)S(1)} %collective-permute-done.6.refs_1_.refs_3_, ...), custom_call_target="tpu_custom_call" | custom-call | flops 805306368 | bytes 6291456 | tf_op jit(solution)/shard_map/pallas_call | solution.py:454
  47.5 1.1 %collective-permute-start.13 = (bf16[256,384]{1,0:T(8,128)(2,1)S(1)}, bf16[256,384]{1,0:T(8,128)(2,1)S(1)}, u32[]{:S(2)}, u32[]{:S(2)}) collective-permute-start(bf16[256,384]{1,0:T(8,128)(2,1)S(1)} %get-tuple-element.46), channel_id=1, source_target_pairs={{0,2},{2,0},{1,3},{3,1},{4,6},{6,4},{5,7},{7,5},{8,10},{10,8},{9,1... | collective-permute-start | bytes 589832 | tf_op jit(solution)/shard_map/ppermute | solution.py:33
  48.6 0.0 collective-permute-done.14.factors
  48.6 4.1 %collective-permute-done.15.refs_0_ = bf16[128,1024]{1,0:T(8,128)(2,1)S(1)} collective-permute-done((bf16[128,1024]{1,0:T(8,128)(2,1)S(1)}, bf16[128,1024]{1,0:T(8,128)(2,1)S(1)}, u32[]{:S(2)}, u32[]{:S(2)}) %collective-permute-start.15) | collective-permute-done | bytes 262176 | tf_op jit(solution)/shard_map/ppermute | solution.py:439
  52.8 1.4 %shard_map.73 = (bf16[2048,128]{1,0:T(8,128)(2,1)S(1)}, bf16[2048,128]{1,0:T(8,128)(2,1)S(1)}) custom-call(bf16[128,1024]{1,0:T(8,128)(2,1)S(1)} %collective-permute-done.14.factors, f32[136,128]{1,0:T(8,128)S(1)} %collective-permute-done.2.refs_3_.slab, bf16[128,1024]{1,0:T(8,128)(2,1)S(1)} %collective-permute-done.15.refs_0_), custom_call_target="tpu_custom_call" | custom-call | flops 536870912 | bytes 1572864 | tf_op jit(solution)/shard_map/pallas_call | solution.py:428
  54.2 1.4 %shard_map.74 = (bf16[256,128]{1,0:T(8,128)(2,1)S(1)}, bf16[256,128]{1,0:T(8,128)(2,1)S(1)}) custom-call(f32[136,128]{1,0:T(8,128)S(1)} %shard_map.67.refs_0_, f32[136,128]{1,0:T(8,128)S(1)} %collective-permute-done.4.refs_1_, f32[136,128]{1,0:T(8,128)S(1)} %collective-permute-done.5.refs_2_, f32[136,128]{1,0:T(8,128)S(1)} %collective-permute-done.6.refs_1_.refs_3_, ...), custom_call_target="tpu_custom_call" | custom-call | flops 268435456 | bytes 2097152 | tf_op jit(solution)/shard_map/pallas_call | solution.py:454
  55.6 1.5 %collective-permute-start.16 = (bf16[256,128]{1,0:T(8,128)(2,1)S(1)}, bf16[256,128]{1,0:T(8,128)(2,1)S(1)}, u32[]{:S(2)}, u32[]{:S(2)}) collective-permute-start(bf16[256,128]{1,0:T(8,128)(2,1)S(1)} %get-tuple-element.52), channel_id=1, source_target_pairs={{0,2},{2,0},{1,3},{3,1},{4,6},{6,4},{5,7},{7,5},{8,10},{10,8},{9,1... | collective-permute-start | bytes 196616 | tf_op jit(solution)/shard_map/ppermute | solution.py:33
  57.1 0.0 collective-permute-done.13.refs_1_
  57.1 2.8 %collective-permute-done.16.refs_3_ = bf16[256,128]{1,0:T(8,128)(2,1)S(1)} collective-permute-done((bf16[256,128]{1,0:T(8,128)(2,1)S(1)}, bf16[256,128]{1,0:T(8,128)(2,1)S(1)}, u32[]{:S(2)}, u32[]{:S(2)}) %collective-permute-start.16) | collective-permute-done | bytes 65568 | tf_op jit(solution)/shard_map/ppermute | solution.py:33
  59.9 0.1 shard_map.75
  60.0 0.8 %reshape.7 = bf16[256,4,1,128]{3,1,0,2:T(4,128)(2,1)} reshape(bf16[256,512]{1,0:T(8,128)(2,1)S(1)} %shard_map.75) | data formatting | bytes 524288 | tf_op jit(solution)/shard_map/reshape | solution.py:473
  (5 shorter events, 0.0 us)
Async XLA Ops:
  11.2 9.5 %collective-permute-start.3 = (bf16[128,1024]{1,0:T(8,128)(2,1)}, bf16[128,1024]{1,0:T(8,128)(2,1)S(1)}, u32[]{:S(2)}, u32[]{:S(2)}) collective-permute-start(bf16[128,1024]{1,0:T(8,128)(2,1)} %get-tuple-element.36), channel_id=1, source_target_pairs={{0,2},{2,0},{1,3},{3,1},{4,6},{6,4},{5,7},{7,5},{8,10},{10,8},{9,1... | collective-permute-start | bytes 786440 | tf_op jit(solution)/shard_map/ppermute | solution.py:33
  14.2 11.1 %collective-permute-start = (f32[136,128]{1,0:T(8,128)}, f32[136,128]{1,0:T(8,128)S(1)}, u32[]{:S(2)}, u32[]{:S(2)}) collective-permute-start(f32[136,128]{1,0:T(8,128)} %get-tuple-element.32), channel_id=1, source_target_pairs={{0,4},{4,0},{8,12},{12,8},{1,5},{5,1},{9,13},{13,9},{2,6},{6,2},{1... | collective-permute-start | bytes 208904 | tf_op jit(solution)/shard_map/ppermute | solution.py:33
  15.7 9.5 %collective-permute-start.1 = (f32[136,128]{1,0:T(8,128)}, f32[136,128]{1,0:T(8,128)S(1)}, u32[]{:S(2)}, u32[]{:S(2)}) collective-permute-start(f32[136,128]{1,0:T(8,128)} %get-tuple-element.33), channel_id=1, source_target_pairs={{0,8},{4,12},{8,0},{12,4},{1,9},{5,13},{9,1},{13,5},{2,10},{6,14},... | collective-permute-start | bytes 208904 | tf_op jit(solution)/shard_map/ppermute | solution.py:33
  18.3 6.9 %collective-permute-start.2 = (f32[136,128]{1,0:T(8,128)}, f32[136,128]{1,0:T(8,128)S(1)}, u32[]{:S(2)}, u32[]{:S(2)}) collective-permute-start(f32[136,128]{1,0:T(8,128)} %get-tuple-element.34), channel_id=1, source_target_pairs={{0,12},{4,8},{8,4},{12,0},{1,13},{5,9},{9,5},{13,1},{2,14},{6,10},... | collective-permute-start | bytes 208904 | tf_op jit(solution)/shard_map/ppermute | solution.py:33
  18.5 0.9 %copy-start.1 = (bf16[128,1024]{1,0:T(8,128)(2,1)S(1)}, bf16[128,1024]{1,0:T(8,128)(2,1)}, u32[]{:S(2)}) copy-start(bf16[128,1024]{1,0:T(8,128)(2,1)} %get-tuple-element.29.refs_0_) | copy-start | bytes 786436
  19.5 0.9 %copy-start.2 = (f32[136,128]{1,0:T(8,128)S(1)}, f32[136,128]{1,0:T(8,128)}, u32[]{:S(2)}) copy-start(f32[136,128]{1,0:T(8,128)} %get-tuple-element.30.refs_1_) | copy-start | bytes 208900
  20.8 16.6 %collective-permute-start.7 = (bf16[128,1024]{1,0:T(8,128)(2,1)S(1)}, bf16[128,1024]{1,0:T(8,128)(2,1)S(1)}, u32[]{:S(2)}, u32[]{:S(2)}) collective-permute-start(bf16[128,1024]{1,0:T(8,128)(2,1)S(1)} %shard_map.66.refs_4_.refs_0_.factors), channel_id=1, source_target_pairs={{0,4},{4,0},{8,12},{12,8},{1,5},{5,1},{9,13},{13,9},{2,6},{6,2},{1... | collective-permute-start | bytes 786440 | tf_op jit(solution)/shard_map/ppermute | solution.py:33
  22.7 16.8 %collective-permute-start.8 = (bf16[128,1024]{1,0:T(8,128)(2,1)S(1)}, bf16[128,1024]{1,0:T(8,128)(2,1)S(1)}, u32[]{:S(2)}, u32[]{:S(2)}) collective-permute-start(bf16[128,1024]{1,0:T(8,128)(2,1)S(1)} %shard_map.66.refs_4_.refs_0_.factors), channel_id=1, source_target_pairs={{0,8},{4,12},{8,0},{12,4},{1,9},{5,13},{9,1},{13,5},{2,10},{6,14},... | collective-permute-start | bytes 786440 | tf_op jit(solution)/shard_map/ppermute | solution.py:33
  31.8 13.1 %copy-start = (bf16[512,2048]{1,0:T(8,128)(2,1)S(1)}, bf16[512,2048]{1,0:T(8,128)(2,1)}, u32[]{:S(2)}) copy-start(bf16[512,2048]{1,0:T(8,128)(2,1)} %refs_10_.1) | copy-start | bytes 6291460
  31.8 5.5 %collective-permute-start.4 = (f32[136,128]{1,0:T(8,128)S(1)}, f32[136,128]{1,0:T(8,128)S(1)}, u32[]{:S(2)}, u32[]{:S(2)}) collective-permute-start(f32[136,128]{1,0:T(8,128)S(1)} %shard_map.67.refs_0_), channel_id=1, source_target_pairs={{0,4},{4,0},{8,12},{12,8},{1,5},{5,1},{9,13},{13,9},{2,6},{6,2},{1... | collective-permute-start | bytes 208904 | tf_op jit(solution)/shard_map/ppermute | solution.py:33
  32.3 10.6 %collective-permute-start.6 = (f32[136,128]{1,0:T(8,128)S(1)}, f32[136,128]{1,0:T(8,128)S(1)}, u32[]{:S(2)}, u32[]{:S(2)}) collective-permute-start(f32[136,128]{1,0:T(8,128)S(1)} %shard_map.67.refs_0_), channel_id=1, source_target_pairs={{0,12},{4,8},{8,4},{12,0},{1,13},{5,9},{9,5},{13,1},{2,14},{6,10},... | collective-permute-start | bytes 208904 | tf_op jit(solution)/shard_map/ppermute | solution.py:33
  34.4 8.0 %collective-permute-start.5 = (f32[136,128]{1,0:T(8,128)S(1)}, f32[136,128]{1,0:T(8,128)S(1)}, u32[]{:S(2)}, u32[]{:S(2)}) collective-permute-start(f32[136,128]{1,0:T(8,128)S(1)} %shard_map.67.refs_0_), channel_id=1, source_target_pairs={{0,8},{4,12},{8,0},{12,4},{1,9},{5,13},{9,1},{13,5},{2,10},{6,14},... | collective-permute-start | bytes 208904 | tf_op jit(solution)/shard_map/ppermute | solution.py:33
  37.3 5.7 %collective-permute-start.10 = (f32[136,128]{1,0:T(8,128)S(1)}, f32[136,128]{1,0:T(8,128)S(1)}, u32[]{:S(2)}, u32[]{:S(2)}) collective-permute-start(f32[136,128]{1,0:T(8,128)S(1)} %collective-permute-done.4.refs_1_), channel_id=1, source_target_pairs={{0,1},{1,0},{2,3},{3,2},{4,5},{5,4},{6,7},{7,6},{8,9},{9,8},{10,11... | collective-permute-start | bytes 208904 | tf_op jit(solution)/shard_map/ppermute | solution.py:33
  38.7 9.9 %collective-permute-start.14 = (bf16[128,1024]{1,0:T(8,128)(2,1)S(1)}, bf16[128,1024]{1,0:T(8,128)(2,1)S(1)}, u32[]{:S(2)}, u32[]{:S(2)}) collective-permute-start(bf16[128,1024]{1,0:T(8,128)(2,1)S(1)} %get-tuple-element.47), channel_id=1, source_target_pairs={{4,8},{8,4},{5,9},{9,5},{6,10},{10,6},{7,11},{11,7},{20,24},{24,20... | collective-permute-start | bytes 786440 | tf_op jit(solution)/shard_map/ppermute | solution.py:437
  40.9 11.9 %collective-permute-start.15 = (bf16[128,1024]{1,0:T(8,128)(2,1)S(1)}, bf16[128,1024]{1,0:T(8,128)(2,1)S(1)}, u32[]{:S(2)}, u32[]{:S(2)}) collective-permute-start(bf16[128,1024]{1,0:T(8,128)(2,1)S(1)} %get-tuple-element.48), channel_id=1, source_target_pairs={{4,0},{8,12},{5,1},{9,13},{6,2},{10,14},{7,3},{11,15},{20,16},{24,... | collective-permute-start | bytes 786440 | tf_op jit(solution)/shard_map/ppermute | solution.py:439
  42.4 2.6 %collective-permute-start.11 = (f32[136,128]{1,0:T(8,128)S(1)}, f32[136,128]{1,0:T(8,128)S(1)}, u32[]{:S(2)}, u32[]{:S(2)}) collective-permute-start(f32[136,128]{1,0:T(8,128)S(1)} %collective-permute-done.5.refs_2_), channel_id=1, source_target_pairs={{0,1},{1,0},{2,3},{3,2},{4,5},{5,4},{6,7},{7,6},{8,9},{9,8},{10,11... | collective-permute-start | bytes 208904 | tf_op jit(solution)/shard_map/ppermute | solution.py:33
  42.9 2.0 %collective-permute-start.12 = (f32[136,128]{1,0:T(8,128)S(1)}, f32[136,128]{1,0:T(8,128)S(1)}, u32[]{:S(2)}, u32[]{:S(2)}) collective-permute-start(f32[136,128]{1,0:T(8,128)S(1)} %get-tuple-element.40), channel_id=1, source_target_pairs={{0,1},{1,0},{2,3},{3,2},{4,5},{5,4},{6,7},{7,6},{8,9},{9,8},{10,11... | collective-permute-start | bytes 208904 | tf_op jit(solution)/shard_map/ppermute | solution.py:33
  43.0 1.9 %collective-permute-start.9 = (f32[136,128]{1,0:T(8,128)S(1)}, f32[136,128]{1,0:T(8,128)S(1)}, u32[]{:S(2)}, u32[]{:S(2)}) collective-permute-start(f32[136,128]{1,0:T(8,128)S(1)} %get-tuple-element.39), channel_id=1, source_target_pairs={{0,1},{1,0},{2,3},{3,2},{4,5},{5,4},{6,7},{7,6},{8,9},{9,8},{10,11... | collective-permute-start | bytes 208904 | tf_op jit(solution)/shard_map/ppermute | solution.py:33
  47.5 9.6 %collective-permute-start.13 = (bf16[256,384]{1,0:T(8,128)(2,1)S(1)}, bf16[256,384]{1,0:T(8,128)(2,1)S(1)}, u32[]{:S(2)}, u32[]{:S(2)}) collective-permute-start(bf16[256,384]{1,0:T(8,128)(2,1)S(1)} %get-tuple-element.46), channel_id=1, source_target_pairs={{0,2},{2,0},{1,3},{3,1},{4,6},{6,4},{5,7},{7,5},{8,10},{10,8},{9,1... | collective-permute-start | bytes 589832 | tf_op jit(solution)/shard_map/ppermute | solution.py:33
  55.6 4.3 %collective-permute-start.16 = (bf16[256,128]{1,0:T(8,128)(2,1)S(1)}, bf16[256,128]{1,0:T(8,128)(2,1)S(1)}, u32[]{:S(2)}, u32[]{:S(2)}) collective-permute-start(bf16[256,128]{1,0:T(8,128)(2,1)S(1)} %get-tuple-element.52), channel_id=1, source_target_pairs={{0,2},{2,0},{1,3},{3,1},{4,6},{6,4},{5,7},{7,5},{8,10},{10,8},{9,1... | collective-permute-start | bytes 196616 | tf_op jit(solution)/shard_map/ppermute | solution.py:33

commit v14 on v11

--- a/solution.py
+++ b/solution.py
@@ -441,10 +441,10 @@
     handed[late] = call(
         functools.partial(hand_kernel, 1),
         shape((SLAB, FBLK), f32),
-        [VMEM] + [HBM] * (cycle - 2),
+        [VMEM] + [HBM] * (cycle - 1),
         vmem=16,
         moved=8 * SLAB * FBLK,
-    )(inverses[late], *[highs[s] for s in range(1, cycle) if s != late])
+    )(inverses[late], *[highs[s] for s in range(cycle) if s != late])
     peers = [swapped(slab, "rep", 1) for slab in handed]
 
     half_rows = train_rows // lax.axis_size("mp")

time: 59 us -> 60.8 us (1.031)
  waiting for transfers between devices: 6.06 us -> 8.15 us
    ppermute x15, waiting for transfers between devices: 3.58 us -> 5.73 us  [swapped(): lax.ppermute(shard, axis, [(i, i ^ by) for i in range(lax.axis_size(axis))])]
  transfers between devices with their start and end apart: 17 -> 17, of which waited for: 4 -> 7; matrix products, arithmetic and copies ran while one was open for 0% -> 0% of each run, Pallas kernels for 28% -> 27%
where the time goes in v14:
time: 60.8 us; the launch traced here: 60.6 us
  Pallas kernels  27.5 us (45%)
  starting transfers between devices  22.2 us (37%)
  waiting for transfers between devices  8.15 us (13%)
  local copies, waits for them, and re-layouts  2.6 us (4%)
    ppermute x15, starting transfers between devices, swapped(): lax.ppermute(shard, axis, [(i, i ^ by) for i in range(lax.axis_size(axis))])  20 us
    pallas_call x1, Pallas kernels, split_over_blocks(): call(first_kernel, [shape((2 * each + proj, tokens), bf16)] * 2 + [shape(...  11.2 us
    pallas_call x1, Pallas kernels, split_over_blocks(): call(functools.partial(factor_kernel, train_rows * cycle, 1.0 / proj), sh...  6.57 us
    ppermute x15, waiting for transfers between devices, swapped(): lax.ppermute(shard, axis, [(i, i ^ by) for i in range(lax.axis_size(axis))])  5.73 us
    pallas_call x4, Pallas kernels, split_over_blocks(): call(functools.partial(queries_kernel, each, cycle if s == late else 0),...  5.67 us
    pallas_call x2, Pallas kernels, split_over_blocks(): call(functools.partial(scores_kernel, cycle, count), [shape((half_rows, c...  3.92 us
    ppermute x1, waiting for transfers between devices, split_over_blocks(): far = [lax.ppermute(again[0], 'dp', [(1, 0), (2, 3)])]  2.42 us
    unnamed x6, local copies, waits for them, and re-layouts  1.84 us
  transfers between devices with their start and end apart: 17, of which 7 were waited for; matrix products, arithmetic and copies ran while one was open for 0% of the time, Pallas kernels for 27%

profile of v14, /device:TPU:0, one launch (start us, length us, event | category | flops | bytes accessed | tf_op | source)
XLA Modules:
  0.0 60.6 jit_solution(10013490196830892096)
XLA Ops:
  0.0 11.2 %shard_map.64 = (bf16[128,1024]{1,0:T(8,128)(2,1)}, bf16[128,1024]{1,0:T(8,128)(2,1)}, f32[136,128]{1,0:T(8,128)}, f32[136,128]{1,0:T(8,128)}, f32[136,128]{1,0:T(8,128)}, /*index=5*/f32[136,128]{1,0:T(8,128)}) custom-call(s32[8,128]{1,0:T(8,128)} %bitcast.6, bf16[1024,2048]{1,0:T(8,128)(2,1)} %delta_hbm.1, bf16[64,64128]{1,0:T(8,128)(2,1)} %bitcast.4, ...), custom_call_target="tpu_custom_call" | custom-call | flops 268435456 | bytes 24805376 | tf_op jit(solution)/shard_map/pallas_call | solution.py:368
  11.2 3.0 %collective-permute-start.3 = (bf16[128,1024]{1,0:T(8,128)(2,1)}, bf16[128,1024]{1,0:T(8,128)(2,1)S(1)}, u32[]{:S(2)}, u32[]{:S(2)}) collective-permute-start(bf16[128,1024]{1,0:T(8,128)(2,1)} %get-tuple-element.34), channel_id=1, source_target_pairs={{0,2},{2,0},{1,3},{3,1},{4,6},{6,4},{5,7},{7,5},{8,10},{10,8},{9,1... | collective-permute-start | bytes 786440 | tf_op jit(solution)/shard_map/ppermute | solution.py:33
  14.2 1.6 %collective-permute-start = (f32[136,128]{1,0:T(8,128)}, f32[136,128]{1,0:T(8,128)S(1)}, u32[]{:S(2)}, u32[]{:S(2)}) collective-permute-start(f32[136,128]{1,0:T(8,128)} %get-tuple-element.30), channel_id=1, source_target_pairs={{0,4},{4,0},{8,12},{12,8},{1,5},{5,1},{9,13},{13,9},{2,6},{6,2},{1... | collective-permute-start | bytes 208904 | tf_op jit(solution)/shard_map/ppermute | solution.py:33
  15.7 2.6 %collective-permute-start.1 = (f32[136,128]{1,0:T(8,128)}, f32[136,128]{1,0:T(8,128)S(1)}, u32[]{:S(2)}, u32[]{:S(2)}) collective-permute-start(f32[136,128]{1,0:T(8,128)} %get-tuple-element.31), channel_id=1, source_target_pairs={{0,8},{4,12},{8,0},{12,4},{1,9},{5,13},{9,1},{13,5},{2,10},{6,14},... | collective-permute-start | bytes 208904 | tf_op jit(solution)/shard_map/ppermute | solution.py:33
  18.3 0.2 collective-permute-start.2
  18.5 0.9 %copy-done.1 = bf16[128,1024]{1,0:T(8,128)(2,1)S(1)} copy-done((bf16[128,1024]{1,0:T(8,128)(2,1)S(1)}, bf16[128,1024]{1,0:T(8,128)(2,1)}, u32[]{:S(2)}) %copy-start.1) | copy-done | bytes 262168
  19.5 0.9 %copy-done.2 = f32[136,128]{1,0:T(8,128)S(1)} copy-done((f32[136,128]{1,0:T(8,128)S(1)}, f32[136,128]{1,0:T(8,128)}, u32[]{:S(2)}) %copy-start.2) | copy-done | bytes 69656
  20.4 0.3 collective-permute-done.3.got
  20.7 0.1 shard_map.66.refs_4_.factors.refs_0_
  20.7 2.9 %collective-permute-start.11 = (bf16[128,1024]{1,0:T(8,128)(2,1)S(1)}, bf16[128,1024]{1,0:T(8,128)(2,1)S(1)}, u32[]{:S(2)}, u32[]{:S(2)}) collective-permute-start(bf16[128,1024]{1,0:T(8,128)(2,1)S(1)} %shard_map.66.refs_4_.factors.refs_0_), channel_id=1, source_target_pairs={{0,8},{4,12},{8,0},{12,4},{1,9},{5,13},{9,1},{13,5},{2,10},{6,14},... | collective-permute-start | bytes 786440 | tf_op jit(solution)/shard_map/ppermute | solution.py:33
  23.7 1.6 %collective-permute-start.10 = (bf16[128,1024]{1,0:T(8,128)(2,1)S(1)}, bf16[128,1024]{1,0:T(8,128)(2,1)S(1)}, u32[]{:S(2)}, u32[]{:S(2)}) collective-permute-start(bf16[128,1024]{1,0:T(8,128)(2,1)S(1)} %shard_map.66.refs_4_.factors.refs_0_), channel_id=1, source_target_pairs={{0,4},{4,0},{8,12},{12,8},{1,5},{5,1},{9,13},{13,9},{2,6},{6,2},{1... | collective-permute-start | bytes 786440 | tf_op jit(solution)/shard_map/ppermute | solution.py:33
  25.2 0.0 collective-permute-done.refs_1_.slab
  25.2 0.0 collective-permute-done.1.refs_2_.slab
  25.2 0.0 collective-permute-done.2.refs_3_.slab
  25.3 6.6 %shard_map.67.refs_0_ = f32[136,128]{1,0:T(8,128)S(1)} custom-call(f32[136,128]{1,0:T(8,128)S(1)} %get-tuple-element.29.refs_0_.slab, f32[136,128]{1,0:T(8,128)S(1)} %collective-permute-done.refs_1_.slab, f32[136,128]{1,0:T(8,128)S(1)} %collective-permute-done.1.refs_2_.slab, f32[136,128]{1,0:T(8,128)S(1)} %collective-permute-done.2.refs_3_.slab, ...), custom_call_target="tpu_custom_call" | custom-call | flops 10000000000 | bytes 1000000 | tf_op jit(solution)/shard_map/pallas_call | solution.py:414
  31.8 0.0 copy-start
  31.8 0.1 collective-permute-start.7
  31.9 1.2 %collective-permute-start.6 = (f32[136,128]{1,0:T(8,128)S(1)}, f32[136,128]{1,0:T(8,128)S(1)}, u32[]{:S(2)}, u32[]{:S(2)}) collective-permute-start(f32[136,128]{1,0:T(8,128)S(1)} %shard_map.67.refs_0_), channel_id=1, source_target_pairs={{0,12},{4,8},{8,4},{12,0},{1,13},{5,9},{9,5},{13,1},{2,14},{6,10},... | collective-permute-start | bytes 208904 | tf_op jit(solution)/shard_map/ppermute | solution.py:33
  33.2 4.6 %collective-permute-start.5 = (f32[136,128]{1,0:T(8,128)S(1)}, f32[136,128]{1,0:T(8,128)S(1)}, u32[]{:S(2)}, u32[]{:S(2)}) collective-permute-start(f32[136,128]{1,0:T(8,128)S(1)} %shard_map.67.refs_0_), channel_id=1, source_target_pairs={{0,8},{4,12},{8,0},{12,4},{1,9},{5,13},{9,1},{13,5},{2,10},{6,14},... | collective-permute-start | bytes 208904 | tf_op jit(solution)/shard_map/ppermute | solution.py:33
  37.7 0.0 collective-permute-done.10.factors
  37.7 0.0 collective-permute-start.4
  37.7 1.4 %shard_map.69 = (bf16[2048,128]{1,0:T(8,128)(2,1)S(1)}, bf16[2048,128]{1,0:T(8,128)(2,1)S(1)}, bf16[128,1024]{1,0:T(8,128)(2,1)S(1)}) custom-call(bf16[128,1024]{1,0:T(8,128)(2,1)S(1)} %collective-permute-done.10.factors, f32[136,128]{1,0:T(8,128)S(1)} %collective-permute-done.refs_1_.slab, bf16[128,1024]{1,0:T(8,128)(2,1)S(1)} %shard_map.66.refs_4_.factors.refs_0_), custom_call_target="tpu_custom_call" | custom-call | flops 536870912 | bytes 1572864 | tf_op jit(solution)/shard_map/pallas_call | solution.py:428
  39.2 0.0 collective-permute-done.11.factors.refs_0_
  39.2 0.7 %collective-permute-start.14 = (bf16[128,1024]{1,0:T(8,128)(2,1)S(1)}, bf16[128,1024]{1,0:T(8,128)(2,1)S(1)}, u32[]{:S(2)}, u32[]{:S(2)}) collective-permute-start(bf16[128,1024]{1,0:T(8,128)(2,1)S(1)} %get-tuple-element.43), channel_id=1, source_target_pairs={{4,8},{8,4},{5,9},{9,5},{6,10},{10,6},{7,11},{11,7},{20,24},{24,20... | collective-permute-start | bytes 786440 | tf_op jit(solution)/shard_map/ppermute | solution.py:437
  39.9 1.4 %shard_map.70 = (bf16[2048,128]{1,0:T(8,128)(2,1)S(1)}, bf16[2048,128]{1,0:T(8,128)(2,1)S(1)}, bf16[128,1024]{1,0:T(8,128)(2,1)S(1)}) custom-call(bf16[128,1024]{1,0:T(8,128)(2,1)S(1)} %collective-permute-done.11.factors.refs_0_, f32[136,128]{1,0:T(8,128)S(1)} %collective-permute-done.1.refs_2_.slab, ...), custom_call_target="tpu_custom_call" | custom-call | flops 536870912 | bytes 1572864 | tf_op jit(solution)/shard_map/pallas_call | solution.py:428
  41.3 0.0 collective-permute-done.6.refs_0_.refs_3_
  41.3 1.5 %collective-permute-start.15 = (bf16[128,1024]{1,0:T(8,128)(2,1)S(1)}, bf16[128,1024]{1,0:T(8,128)(2,1)S(1)}, u32[]{:S(2)}, u32[]{:S(2)}) collective-permute-start(bf16[128,1024]{1,0:T(8,128)(2,1)S(1)} %get-tuple-element.44), channel_id=1, source_target_pairs={{4,0},{8,12},{5,1},{9,13},{6,2},{10,14},{7,3},{11,15},{20,16},{24,... | collective-permute-start | bytes 786440 | tf_op jit(solution)/shard_map/ppermute | solution.py:439
  42.8 1.4 %shard_map.68 = (bf16[2048,128]{1,0:T(8,128)(2,1)S(1)}, bf16[2048,128]{1,0:T(8,128)(2,1)S(1)}) custom-call(bf16[128,1024]{1,0:T(8,128)(2,1)S(1)} %shard_map.66.refs_4_.factors.refs_0_, f32[136,128]{1,0:T(8,128)S(1)} %get-tuple-element.29.refs_0_.slab, f32[136,128]{1,0:T(8,128)S(1)} %shard_map.67.refs_0_), custom_call_target="tpu_custom_call" | custom-call | flops 536870912 | bytes 1572864 | tf_op jit(solution)/shard_map/pallas_call | solution.py:428
  44.2 0.0 collective-permute-done.5.refs_2_
  44.2 0.1 collective-permute-start.9
  44.3 0.0 collective-permute-done.4.refs_1_
  44.3 0.5 collective-permute-start.8
  44.8 0.0 collective-permute-done.7.refs_4_
  44.8 0.2 collective-permute-start.12
  44.9 0.6 collective-permute-done.9.refs_6_
  45.5 0.2 collective-permute-done.8.refs_5_
  45.7 0.4 collective-permute-done.12.refs_7_
  46.1 2.6 %shard_map.72 = (bf16[256,384]{1,0:T(8,128)(2,1)S(1)}, bf16[256,384]{1,0:T(8,128)(2,1)S(1)}) custom-call(f32[136,128]{1,0:T(8,128)S(1)} %shard_map.67.refs_0_, f32[136,128]{1,0:T(8,128)S(1)} %collective-permute-done.4.refs_1_, f32[136,128]{1,0:T(8,128)S(1)} %collective-permute-done.5.refs_2_, f32[136,128]{1,0:T(8,128)S(1)} %collective-permute-done.6.refs_0_.refs_3_, ...), custom_call_target="tpu_custom_call" | custom-call | flops 805306368 | bytes 6291456 | tf_op jit(solution)/shard_map/pallas_call | solution.py:454
  48.7 1.5 %collective-permute-start.13 = (bf16[256,384]{1,0:T(8,128)(2,1)S(1)}, bf16[256,384]{1,0:T(8,128)(2,1)S(1)}, u32[]{:S(2)}, u32[]{:S(2)}) collective-permute-start(bf16[256,384]{1,0:T(8,128)(2,1)S(1)} %get-tuple-element.42), channel_id=1, source_target_pairs={{0,2},{2,0},{1,3},{3,1},{4,6},{6,4},{5,7},{7,5},{8,10},{10,8},{9,1... | collective-permute-start | bytes 589832 | tf_op jit(solution)/shard_map/ppermute | solution.py:33
  50.2 0.0 collective-permute-done.14.factors
  50.2 2.4 %collective-permute-done.15.refs_0_ = bf16[128,1024]{1,0:T(8,128)(2,1)S(1)} collective-permute-done((bf16[128,1024]{1,0:T(8,128)(2,1)S(1)}, bf16[128,1024]{1,0:T(8,128)(2,1)S(1)}, u32[]{:S(2)}, u32[]{:S(2)}) %collective-permute-start.15) | collective-permute-done | bytes 262176 | tf_op jit(solution)/shard_map/ppermute | solution.py:439
  52.6 1.4 %shard_map.73 = (bf16[2048,128]{1,0:T(8,128)(2,1)S(1)}, bf16[2048,128]{1,0:T(8,128)(2,1)S(1)}) custom-call(bf16[128,1024]{1,0:T(8,128)(2,1)S(1)} %collective-permute-done.14.factors, f32[136,128]{1,0:T(8,128)S(1)} %collective-permute-done.2.refs_3_.slab, bf16[128,1024]{1,0:T(8,128)(2,1)S(1)} %collective-permute-done.15.refs_0_), custom_call_target="tpu_custom_call" | custom-call | flops 536870912 | bytes 1572864 | tf_op jit(solution)/shard_map/pallas_call | solution.py:428
  54.0 1.4 %shard_map.74 = (bf16[256,128]{1,0:T(8,128)(2,1)S(1)}, bf16[256,128]{1,0:T(8,128)(2,1)S(1)}) custom-call(f32[136,128]{1,0:T(8,128)S(1)} %shard_map.67.refs_0_, f32[136,128]{1,0:T(8,128)S(1)} %collective-permute-done.4.refs_1_, f32[136,128]{1,0:T(8,128)S(1)} %collective-permute-done.5.refs_2_, f32[136,128]{1,0:T(8,128)S(1)} %collective-permute-done.6.refs_0_.refs_3_, ...), custom_call_target="tpu_custom_call" | custom-call | flops 268435456 | bytes 2097152 | tf_op jit(solution)/shard_map/pallas_call | solution.py:454
  55.4 0.1 collective-permute-start.16
  55.4 0.3 collective-permute-done.13.refs_1_
  55.7 4.0 %collective-permute-done.16.refs_3_ = bf16[256,128]{1,0:T(8,128)(2,1)S(1)} collective-permute-done((bf16[256,128]{1,0:T(8,128)(2,1)S(1)}, bf16[256,128]{1,0:T(8,128)(2,1)S(1)}, u32[]{:S(2)}, u32[]{:S(2)}) %collective-permute-start.16) | collective-permute-done | bytes 65568 | tf_op jit(solution)/shard_map/ppermute | solution.py:33
  59.7 0.1 shard_map.75
  59.8 0.8 %reshape.7 = bf16[256,4,1,128]{3,1,0,2:T(4,128)(2,1)} reshape(bf16[256,512]{1,0:T(8,128)(2,1)S(1)} %shard_map.75) | data formatting | bytes 524288 | tf_op jit(solution)/shard_map/reshape | solution.py:473
  (5 shorter events, 0.0 us)
Async XLA Ops:
  11.2 9.5 %collective-permute-start.3 = (bf16[128,1024]{1,0:T(8,128)(2,1)}, bf16[128,1024]{1,0:T(8,128)(2,1)S(1)}, u32[]{:S(2)}, u32[]{:S(2)}) collective-permute-start(bf16[128,1024]{1,0:T(8,128)(2,1)} %get-tuple-element.34), channel_id=1, source_target_pairs={{0,2},{2,0},{1,3},{3,1},{4,6},{6,4},{5,7},{7,5},{8,10},{10,8},{9,1... | collective-permute-start | bytes 786440 | tf_op jit(solution)/shard_map/ppermute | solution.py:33
  14.2 11.1 %collective-permute-start = (f32[136,128]{1,0:T(8,128)}, f32[136,128]{1,0:T(8,128)S(1)}, u32[]{:S(2)}, u32[]{:S(2)}) collective-permute-start(f32[136,128]{1,0:T(8,128)} %get-tuple-element.30), channel_id=1, source_target_pairs={{0,4},{4,0},{8,12},{12,8},{1,5},{5,1},{9,13},{13,9},{2,6},{6,2},{1... | collective-permute-start | bytes 208904 | tf_op jit(solution)/shard_map/ppermute | solution.py:33
  15.7 9.5 %collective-permute-start.1 = (f32[136,128]{1,0:T(8,128)}, f32[136,128]{1,0:T(8,128)S(1)}, u32[]{:S(2)}, u32[]{:S(2)}) collective-permute-start(f32[136,128]{1,0:T(8,128)} %get-tuple-element.31), channel_id=1, source_target_pairs={{0,8},{4,12},{8,0},{12,4},{1,9},{5,13},{9,1},{13,5},{2,10},{6,14},... | collective-permute-start | bytes 208904 | tf_op jit(solution)/shard_map/ppermute | solution.py:33
  18.3 6.9 %collective-permute-start.2 = (f32[136,128]{1,0:T(8,128)}, f32[136,128]{1,0:T(8,128)S(1)}, u32[]{:S(2)}, u32[]{:S(2)}) collective-permute-start(f32[136,128]{1,0:T(8,128)} %get-tuple-element.32), channel_id=1, source_target_pairs={{0,12},{4,8},{8,4},{12,0},{1,13},{5,9},{9,5},{13,1},{2,14},{6,10},... | collective-permute-start | bytes 208904 | tf_op jit(solution)/shard_map/ppermute | solution.py:33
  18.5 0.9 %copy-start.1 = (bf16[128,1024]{1,0:T(8,128)(2,1)S(1)}, bf16[128,1024]{1,0:T(8,128)(2,1)}, u32[]{:S(2)}) copy-start(bf16[128,1024]{1,0:T(8,128)(2,1)} %get-tuple-element.27.refs_0_) | copy-start | bytes 786436
  19.5 0.9 %copy-start.2 = (f32[136,128]{1,0:T(8,128)S(1)}, f32[136,128]{1,0:T(8,128)}, u32[]{:S(2)}) copy-start(f32[136,128]{1,0:T(8,128)} %get-tuple-element.28.refs_1_) | copy-start | bytes 208900
  20.7 18.4 %collective-permute-start.11 = (bf16[128,1024]{1,0:T(8,128)(2,1)S(1)}, bf16[128,1024]{1,0:T(8,128)(2,1)S(1)}, u32[]{:S(2)}, u32[]{:S(2)}) collective-permute-start(bf16[128,1024]{1,0:T(8,128)(2,1)S(1)} %shard_map.66.refs_4_.factors.refs_0_), channel_id=1, source_target_pairs={{0,8},{4,12},{8,0},{12,4},{1,9},{5,13},{9,1},{13,5},{2,10},{6,14},... | collective-permute-start | bytes 786440 | tf_op jit(solution)/shard_map/ppermute | solution.py:33
  23.7 14.1 %collective-permute-start.10 = (bf16[128,1024]{1,0:T(8,128)(2,1)S(1)}, bf16[128,1024]{1,0:T(8,128)(2,1)S(1)}, u32[]{:S(2)}, u32[]{:S(2)}) collective-permute-start(bf16[128,1024]{1,0:T(8,128)(2,1)S(1)} %shard_map.66.refs_4_.factors.refs_0_), channel_id=1, source_target_pairs={{0,4},{4,0},{8,12},{12,8},{1,5},{5,1},{9,13},{13,9},{2,6},{6,2},{1... | collective-permute-start | bytes 786440 | tf_op jit(solution)/shard_map/ppermute | solution.py:33
  31.8 14.3 %copy-start = (bf16[512,2048]{1,0:T(8,128)(2,1)S(1)}, bf16[512,2048]{1,0:T(8,128)(2,1)}, u32[]{:S(2)}) copy-start(bf16[512,2048]{1,0:T(8,128)(2,1)} %refs_10_.1) | copy-start | bytes 6291460
  31.8 12.9 %collective-permute-start.7 = (f32[136,128]{1,0:T(8,128)S(1)}, f32[136,128]{1,0:T(8,128)S(1)}, u32[]{:S(2)}, u32[]{:S(2)}) collective-permute-start(f32[136,128]{1,0:T(8,128)S(1)} %shard_map.67.refs_0_), channel_id=1, source_target_pairs={{0,1},{1,0},{2,3},{3,2},{4,5},{5,4},{6,7},{7,6},{8,9},{9,8},{10,11... | collective-permute-start | bytes 208904 | tf_op jit(solution)/shard_map/ppermute | solution.py:33
  31.9 9.4 %collective-permute-start.6 = (f32[136,128]{1,0:T(8,128)S(1)}, f32[136,128]{1,0:T(8,128)S(1)}, u32[]{:S(2)}, u32[]{:S(2)}) collective-permute-start(f32[136,128]{1,0:T(8,128)S(1)} %shard_map.67.refs_0_), channel_id=1, source_target_pairs={{0,12},{4,8},{8,4},{12,0},{1,13},{5,9},{9,5},{13,1},{2,14},{6,10},... | collective-permute-start | bytes 208904 | tf_op jit(solution)/shard_map/ppermute | solution.py:33
  33.2 11.0 %collective-permute-start.5 = (f32[136,128]{1,0:T(8,128)S(1)}, f32[136,128]{1,0:T(8,128)S(1)}, u32[]{:S(2)}, u32[]{:S(2)}) collective-permute-start(f32[136,128]{1,0:T(8,128)S(1)} %shard_map.67.refs_0_), channel_id=1, source_target_pairs={{0,8},{4,12},{8,0},{12,4},{1,9},{5,13},{9,1},{13,5},{2,10},{6,14},... | collective-permute-start | bytes 208904 | tf_op jit(solution)/shard_map/ppermute | solution.py:33
  37.7 6.6 %collective-permute-start.4 = (f32[136,128]{1,0:T(8,128)S(1)}, f32[136,128]{1,0:T(8,128)S(1)}, u32[]{:S(2)}, u32[]{:S(2)}) collective-permute-start(f32[136,128]{1,0:T(8,128)S(1)} %shard_map.67.refs_0_), channel_id=1, source_target_pairs={{0,4},{4,0},{8,12},{12,8},{1,5},{5,1},{9,13},{13,9},{2,6},{6,2},{1... | collective-permute-start | bytes 208904 | tf_op jit(solution)/shard_map/ppermute | solution.py:33
  39.2 11.0 %collective-permute-start.14 = (bf16[128,1024]{1,0:T(8,128)(2,1)S(1)}, bf16[128,1024]{1,0:T(8,128)(2,1)S(1)}, u32[]{:S(2)}, u32[]{:S(2)}) collective-permute-start(bf16[128,1024]{1,0:T(8,128)(2,1)S(1)} %get-tuple-element.43), channel_id=1, source_target_pairs={{4,8},{8,4},{5,9},{9,5},{6,10},{10,6},{7,11},{11,7},{20,24},{24,20... | collective-permute-start | bytes 786440 | tf_op jit(solution)/shard_map/ppermute | solution.py:437
  41.3 11.3 %collective-permute-start.15 = (bf16[128,1024]{1,0:T(8,128)(2,1)S(1)}, bf16[128,1024]{1,0:T(8,128)(2,1)S(1)}, u32[]{:S(2)}, u32[]{:S(2)}) collective-permute-start(bf16[128,1024]{1,0:T(8,128)(2,1)S(1)} %get-tuple-element.44), channel_id=1, source_target_pairs={{4,0},{8,12},{5,1},{9,13},{6,2},{10,14},{7,3},{11,15},{20,16},{24,... | collective-permute-start | bytes 786440 | tf_op jit(solution)/shard_map/ppermute | solution.py:439
  44.2 1.3 %collective-permute-start.9 = (f32[136,128]{1,0:T(8,128)S(1)}, f32[136,128]{1,0:T(8,128)S(1)}, u32[]{:S(2)}, u32[]{:S(2)}) collective-permute-start(f32[136,128]{1,0:T(8,128)S(1)} %collective-permute-done.5.refs_2_), channel_id=1, source_target_pairs={{0,1},{1,0},{2,3},{3,2},{4,5},{5,4},{6,7},{7,6},{8,9},{9,8},{10,11... | collective-permute-start | bytes 208904 | tf_op jit(solution)/shard_map/ppermute | solution.py:33
  44.3 1.4 %collective-permute-start.8 = (f32[136,128]{1,0:T(8,128)S(1)}, f32[136,128]{1,0:T(8,128)S(1)}, u32[]{:S(2)}, u32[]{:S(2)}) collective-permute-start(f32[136,128]{1,0:T(8,128)S(1)} %collective-permute-done.4.refs_1_), channel_id=1, source_target_pairs={{0,1},{1,0},{2,3},{3,2},{4,5},{5,4},{6,7},{7,6},{8,9},{9,8},{10,11... | collective-permute-start | bytes 208904 | tf_op jit(solution)/shard_map/ppermute | solution.py:33
  44.8 1.3 %collective-permute-start.12 = (f32[136,128]{1,0:T(8,128)S(1)}, f32[136,128]{1,0:T(8,128)S(1)}, u32[]{:S(2)}, u32[]{:S(2)}) collective-permute-start(f32[136,128]{1,0:T(8,128)S(1)} %shard_map.71), channel_id=1, source_target_pairs={{0,1},{1,0},{2,3},{3,2},{4,5},{5,4},{6,7},{7,6},{8,9},{9,8},{10,11... | collective-permute-start | bytes 208904 | tf_op jit(solution)/shard_map/ppermute | solution.py:33
  48.7 7.0 %collective-permute-start.13 = (bf16[256,384]{1,0:T(8,128)(2,1)S(1)}, bf16[256,384]{1,0:T(8,128)(2,1)S(1)}, u32[]{:S(2)}, u32[]{:S(2)}) collective-permute-start(bf16[256,384]{1,0:T(8,128)(2,1)S(1)} %get-tuple-element.42), channel_id=1, source_target_pairs={{0,2},{2,0},{1,3},{3,1},{4,6},{6,4},{5,7},{7,5},{8,10},{10,8},{9,1... | collective-permute-start | bytes 589832 | tf_op jit(solution)/shard_map/ppermute | solution.py:33
  55.4 4.3 %collective-permute-start.16 = (bf16[256,128]{1,0:T(8,128)(2,1)S(1)}, bf16[256,128]{1,0:T(8,128)(2,1)S(1)}, u32[]{:S(2)}, u32[]{:S(2)}) collective-permute-start(bf16[256,128]{1,0:T(8,128)(2,1)S(1)} %get-tuple-element.48), channel_id=1, source_target_pairs={{0,2},{2,0},{1,3},{3,1},{4,6},{6,4},{5,7},{7,5},{8,10},{10,8},{9,1... | collective-permute-start | bytes 196616 | tf_op jit(solution)/shard_map/ppermute | solution.py:33

commit v15 on v11

--- a/solution.py
+++ b/solution.py
@@ -309,7 +309,7 @@
 def scores_kernel(cycle, count, *refs):
     own, peers = refs[:cycle], refs[cycle:2 * cycle]
     highs, lows = refs[2 * cycle:2 * cycle + count], refs[2 * cycle + count:2 * cycle + 2 * count]
-    train, sent, kept, pre = refs[2 * cycle + 2 * count:]
+    train, sent, pre = refs[2 * cycle + 2 * count:]
     mine, rep, model = lax.axis_index("dp"), lax.axis_index("rep"), lax.axis_index("mp")
     for half, slabs in ((rep, own), (1 - rep, peers)):
         for shift in range(cycle):
@@ -328,9 +328,14 @@
                 )
                 pre[rows, :] = solved.astype(jnp.bfloat16)
     half_rows = sent.shape[0]
-    for out, which in ((sent, 1 - model), (kept, model)):
-        rows = pl.ds(pl.multiple_of(which * half_rows, half_rows), half_rows)
-        out[...] = jnp.dot(train[rows, :], pre[...], preferred_element_type=jnp.float32).astype(jnp.bfloat16)
+    rows = pl.ds(pl.multiple_of((1 - model) * half_rows, half_rows), half_rows)
+    sent[...] = jnp.dot(train[rows, :], pre[...], preferred_element_type=jnp.float32).astype(jnp.bfloat16)
+
+
+def kept_kernel(train, pre, kept):
+    half_rows = kept.shape[0]
+    rows = pl.ds(pl.multiple_of(lax.axis_index("mp") * half_rows, half_rows), half_rows)
+    kept[...] = jnp.dot(train[rows, :], pre[...], preferred_element_type=jnp.float32).astype(jnp.bfloat16)
 
 
 def total_kernel(order, *refs):
@@ -451,15 +456,22 @@
     pieces, order = [], []
     for chosen in ([s for s in range(cycle) if s != late], [late]):
         count = len(chosen)
-        outgoing, kept = call(
+        outgoing, solved = call(
             functools.partial(scores_kernel, cycle, count),
-            [shape((half_rows, count * queries), bf16)] * 2,
+            [shape((half_rows, count * queries), bf16), shape((feat, count * queries), bf16)],
             [VMEM] * (2 * cycle + 2 * count + 1),
-            [pltpu.VMEM((feat, count * queries), bf16)],
             vmem=24,
             flops=2 * train_rows * feat * count * queries,
             moved=8 * feat * queries * count,
         )(*inverses, *peers, *[highs[s] for s in chosen], *[lows[s] for s in chosen], train_grads)
+        kept = call(
+            kept_kernel,
+            shape((half_rows, count * queries), bf16),
+            [VMEM, VMEM],
+            vmem=24,
+            flops=train_rows * feat * count * queries,
+            moved=2 * feat * (half_rows + count * queries),
+        )(train_grads, solved)
         pieces += [kept, swapped(outgoing, "mp", 1)]
         order += chosen
     total = call(

time: 59 us -> 58.7 us (level)
    pallas_call x0 -> x2, Pallas kernels: none -> 1.13 us  [split_over_blocks(): call(kept_kernel, shape((half_rows, count * queries), bf16), [VMEM, VMEM]...]
    ppermute x15, waiting for transfers between devices: 3.58 us -> 2.49 us  [swapped(): lax.ppermute(shard, axis, [(i, i ^ by) for i in range(lax.axis_size(axis))])]
    pallas_call x2, Pallas kernels: 3.93 us -> 3.1 us  [split_over_blocks(): call(functools.partial(scores_kernel, cycle, count), [shape((half_rows, c...]
where the time goes in v15:
time: 58.7 us; the launch traced here: 58.5 us
  Pallas kernels  27.8 us (47%)
  starting transfers between devices  22.3 us (38%)
  waiting for transfers between devices  5.54 us (9%)
  local copies, waits for them, and re-layouts  2.6 us (4%)
    ppermute x15, starting transfers between devices, swapped(): lax.ppermute(shard, axis, [(i, i ^ by) for i in range(lax.axis_size(axis))])  20.2 us
    pallas_call x1, Pallas kernels, split_over_blocks(): call(first_kernel, [shape((2 * each + proj, tokens), bf16)] * 2 + [shape(...  11.2 us
    pallas_call x1, Pallas kernels, split_over_blocks(): call(functools.partial(factor_kernel, train_rows * cycle, 1.0 / proj), sh...  6.57 us
    pallas_call x4, Pallas kernels, split_over_blocks(): call(functools.partial(queries_kernel, each, cycle if s == late else 0),...  5.65 us
    pallas_call x2, Pallas kernels, split_over_blocks(): call(functools.partial(scores_kernel, cycle, count), [shape((half_rows, c...  3.1 us
    ppermute x1, waiting for transfers between devices, split_over_blocks(): far = [lax.ppermute(again[0], 'dp', [(1, 0), (2, 3)])]  3.05 us
    ppermute x15, waiting for transfers between devices, swapped(): lax.ppermute(shard, axis, [(i, i ^ by) for i in range(lax.axis_size(axis))])  2.49 us
    unnamed x6, local copies, waits for them, and re-layouts  1.84 us
  transfers between devices with their start and end apart: 17, of which 4 were waited for; matrix products, arithmetic and copies ran while one was open for 0% of the time, Pallas kernels for 28%

profile of v15, /device:TPU:0, one launch (start us, length us, event | category | flops | bytes accessed | tf_op | source)
XLA Modules:
  0.0 58.5 jit_solution(14229887468884536980)
XLA Ops:
  0.0 11.2 %shard_map.64 = (bf16[128,1024]{1,0:T(8,128)(2,1)}, bf16[128,1024]{1,0:T(8,128)(2,1)}, f32[136,128]{1,0:T(8,128)}, f32[136,128]{1,0:T(8,128)}, f32[136,128]{1,0:T(8,128)}, /*index=5*/f32[136,128]{1,0:T(8,128)}) custom-call(s32[8,128]{1,0:T(8,128)} %bitcast.6, bf16[1024,2048]{1,0:T(8,128)(2,1)} %delta_hbm.1, bf16[64,64128]{1,0:T(8,128)(2,1)} %bitcast.4, ...), custom_call_target="tpu_custom_call" | custom-call | flops 268435456 | bytes 24805376 | tf_op jit(solution)/shard_map/pallas_call | solution.py:373
  11.2 3.0 %collective-permute-start.3 = (bf16[128,1024]{1,0:T(8,128)(2,1)}, bf16[128,1024]{1,0:T(8,128)(2,1)S(1)}, u32[]{:S(2)}, u32[]{:S(2)}) collective-permute-start(bf16[128,1024]{1,0:T(8,128)(2,1)} %get-tuple-element.34), channel_id=1, source_target_pairs={{0,2},{2,0},{1,3},{3,1},{4,6},{6,4},{5,7},{7,5},{8,10},{10,8},{9,1... | collective-permute-start | bytes 786440 | tf_op jit(solution)/shard_map/ppermute | solution.py:33
  14.2 1.6 %collective-permute-start = (f32[136,128]{1,0:T(8,128)}, f32[136,128]{1,0:T(8,128)S(1)}, u32[]{:S(2)}, u32[]{:S(2)}) collective-permute-start(f32[136,128]{1,0:T(8,128)} %get-tuple-element.30), channel_id=1, source_target_pairs={{0,4},{4,0},{8,12},{12,8},{1,5},{5,1},{9,13},{13,9},{2,6},{6,2},{1... | collective-permute-start | bytes 208904 | tf_op jit(solution)/shard_map/ppermute | solution.py:33
  15.8 2.6 %collective-permute-start.1 = (f32[136,128]{1,0:T(8,128)}, f32[136,128]{1,0:T(8,128)S(1)}, u32[]{:S(2)}, u32[]{:S(2)}) collective-permute-start(f32[136,128]{1,0:T(8,128)} %get-tuple-element.31), channel_id=1, source_target_pairs={{0,8},{4,12},{8,0},{12,4},{1,9},{5,13},{9,1},{13,5},{2,10},{6,14},... | collective-permute-start | bytes 208904 | tf_op jit(solution)/shard_map/ppermute | solution.py:33
  18.3 0.2 collective-permute-start.2
  18.6 0.9 %copy-done.1 = bf16[128,1024]{1,0:T(8,128)(2,1)S(1)} copy-done((bf16[128,1024]{1,0:T(8,128)(2,1)S(1)}, bf16[128,1024]{1,0:T(8,128)(2,1)}, u32[]{:S(2)}) %copy-start.1) | copy-done | bytes 262168
  19.5 0.9 %copy-done.2 = f32[136,128]{1,0:T(8,128)S(1)} copy-done((f32[136,128]{1,0:T(8,128)S(1)}, f32[136,128]{1,0:T(8,128)}, u32[]{:S(2)}) %copy-start.2) | copy-done | bytes 69656
  20.4 0.3 collective-permute-done.3.got
  20.7 0.1 shard_map.66.refs_4_.refs_0_.factors
  20.8 1.9 %collective-permute-start.10 = (bf16[128,1024]{1,0:T(8,128)(2,1)S(1)}, bf16[128,1024]{1,0:T(8,128)(2,1)S(1)}, u32[]{:S(2)}, u32[]{:S(2)}) collective-permute-start(bf16[128,1024]{1,0:T(8,128)(2,1)S(1)} %shard_map.66.refs_4_.refs_0_.factors), channel_id=1, source_target_pairs={{0,4},{4,0},{8,12},{12,8},{1,5},{5,1},{9,13},{13,9},{2,6},{6,2},{1... | collective-permute-start | bytes 786440 | tf_op jit(solution)/shard_map/ppermute | solution.py:33
  22.6 2.6 %collective-permute-start.11 = (bf16[128,1024]{1,0:T(8,128)(2,1)S(1)}, bf16[128,1024]{1,0:T(8,128)(2,1)S(1)}, u32[]{:S(2)}, u32[]{:S(2)}) collective-permute-start(bf16[128,1024]{1,0:T(8,128)(2,1)S(1)} %shard_map.66.refs_4_.refs_0_.factors), channel_id=1, source_target_pairs={{0,8},{4,12},{8,0},{12,4},{1,9},{5,13},{9,1},{13,5},{2,10},{6,14},... | collective-permute-start | bytes 786440 | tf_op jit(solution)/shard_map/ppermute | solution.py:33
  25.2 0.0 collective-permute-done.refs_1_.slab
  25.2 0.0 collective-permute-done.1.refs_2_.slab
  25.2 0.0 collective-permute-done.2.refs_3_.slab
  25.2 6.6 %shard_map.67.refs_0_ = f32[136,128]{1,0:T(8,128)S(1)} custom-call(f32[136,128]{1,0:T(8,128)S(1)} %get-tuple-element.29.refs_0_.slab, f32[136,128]{1,0:T(8,128)S(1)} %collective-permute-done.refs_1_.slab, f32[136,128]{1,0:T(8,128)S(1)} %collective-permute-done.1.refs_2_.slab, f32[136,128]{1,0:T(8,128)S(1)} %collective-permute-done.2.refs_3_.slab, ...), custom_call_target="tpu_custom_call" | custom-call | flops 10000000000 | bytes 1000000 | tf_op jit(solution)/shard_map/pallas_call | solution.py:419
  31.8 0.0 copy-start
  31.8 1.3 %collective-permute-start.6 = (f32[136,128]{1,0:T(8,128)S(1)}, f32[136,128]{1,0:T(8,128)S(1)}, u32[]{:S(2)}, u32[]{:S(2)}) collective-permute-start(f32[136,128]{1,0:T(8,128)S(1)} %shard_map.67.refs_0_), channel_id=1, source_target_pairs={{0,12},{4,8},{8,4},{12,0},{1,13},{5,9},{9,5},{13,1},{2,14},{6,10},... | collective-permute-start | bytes 208904 | tf_op jit(solution)/shard_map/ppermute | solution.py:33
  33.1 0.4 collective-permute-start.4
  33.5 2.8 %collective-permute-start.5 = (f32[136,128]{1,0:T(8,128)S(1)}, f32[136,128]{1,0:T(8,128)S(1)}, u32[]{:S(2)}, u32[]{:S(2)}) collective-permute-start(f32[136,128]{1,0:T(8,128)S(1)} %shard_map.67.refs_0_), channel_id=1, source_target_pairs={{0,8},{4,12},{8,0},{12,4},{1,9},{5,13},{9,1},{13,5},{2,10},{6,14},... | collective-permute-start | bytes 208904 | tf_op jit(solution)/shard_map/ppermute | solution.py:33
  36.3 0.3 collective-permute-done.10.factors
  36.6 0.0 collective-permute-start.7
  36.6 1.4 %shard_map.68 = (bf16[2048,128]{1,0:T(8,128)(2,1)S(1)}, bf16[2048,128]{1,0:T(8,128)(2,1)S(1)}, bf16[128,1024]{1,0:T(8,128)(2,1)S(1)}) custom-call(bf16[128,1024]{1,0:T(8,128)(2,1)S(1)} %collective-permute-done.10.factors, f32[136,128]{1,0:T(8,128)S(1)} %collective-permute-done.refs_1_.slab, bf16[128,1024]{1,0:T(8,128)(2,1)S(1)} %shard_map.66.refs_4_.refs_0_.factors), custom_call_target="tpu_custom_call" | custom-call | flops 536870912 | bytes 1572864 | tf_op jit(solution)/shard_map/pallas_call | solution.py:433
  38.0 0.0 collective-permute-done.11.factors.refs_0_
  38.0 0.7 %collective-permute-start.14 = (bf16[128,1024]{1,0:T(8,128)(2,1)S(1)}, bf16[128,1024]{1,0:T(8,128)(2,1)S(1)}, u32[]{:S(2)}, u32[]{:S(2)}) collective-permute-start(bf16[128,1024]{1,0:T(8,128)(2,1)S(1)} %get-tuple-element.43), channel_id=1, source_target_pairs={{4,8},{8,4},{5,9},{9,5},{6,10},{10,6},{7,11},{11,7},{20,24},{24,20... | collective-permute-start | bytes 786440 | tf_op jit(solution)/shard_map/ppermute | solution.py:442
  38.7 1.4 %shard_map.69 = (bf16[2048,128]{1,0:T(8,128)(2,1)S(1)}, bf16[2048,128]{1,0:T(8,128)(2,1)S(1)}, bf16[128,1024]{1,0:T(8,128)(2,1)S(1)}) custom-call(bf16[128,1024]{1,0:T(8,128)(2,1)S(1)} %collective-permute-done.11.factors.refs_0_, f32[136,128]{1,0:T(8,128)S(1)} %collective-permute-done.1.refs_2_.slab, ...), custom_call_target="tpu_custom_call" | custom-call | flops 536870912 | bytes 1572864 | tf_op jit(solution)/shard_map/pallas_call | solution.py:433
  40.1 0.0 collective-permute-done.6.refs_0_.refs_3_
  40.1 1.5 %collective-permute-start.15 = (bf16[128,1024]{1,0:T(8,128)(2,1)S(1)}, bf16[128,1024]{1,0:T(8,128)(2,1)S(1)}, u32[]{:S(2)}, u32[]{:S(2)}) collective-permute-start(bf16[128,1024]{1,0:T(8,128)(2,1)S(1)} %get-tuple-element.44), channel_id=1, source_target_pairs={{4,0},{8,12},{5,1},{9,13},{6,2},{10,14},{7,3},{11,15},{20,16},{24,... | collective-permute-start | bytes 786440 | tf_op jit(solution)/shard_map/ppermute | solution.py:444
  41.6 0.0 collective-permute-done.4.refs_1_
  41.6 0.6 collective-permute-start.8
  42.2 0.0 collective-permute-done.5.refs_2_
  42.2 0.1 collective-permute-start.9
  42.3 0.0 collective-permute-done.7.refs_4_
  42.3 0.5 collective-permute-start.12
  42.8 1.4 %shard_map.71 = (bf16[2048,128]{1,0:T(8,128)(2,1)S(1)}, bf16[2048,128]{1,0:T(8,128)(2,1)S(1)}) custom-call(bf16[128,1024]{1,0:T(8,128)(2,1)S(1)} %shard_map.66.refs_4_.refs_0_.factors, f32[136,128]{1,0:T(8,128)S(1)} %get-tuple-element.29.refs_0_.slab, f32[136,128]{1,0:T(8,128)S(1)} %shard_map.67.refs_0_), custom_call_target="tpu_custom_call" | custom-call | flops 536870912 | bytes 1572864 | tf_op jit(solution)/shard_map/pallas_call | solution.py:433
  44.2 0.0 collective-permute-done.8.refs_5_
  44.2 0.0 collective-permute-done.9.refs_6_
  44.2 2.0 %shard_map.72 = (bf16[256,384]{1,0:T(8,128)(2,1)S(1)}, bf16[2048,384]{1,0:T(8,128)(2,1)S(1)}) custom-call(f32[136,128]{1,0:T(8,128)S(1)} %shard_map.67.refs_0_, f32[136,128]{1,0:T(8,128)S(1)} %collective-permute-done.4.refs_1_, f32[136,128]{1,0:T(8,128)S(1)} %collective-permute-done.5.refs_2_, f32[136,128]{1,0:T(8,128)S(1)} %collective-permute-done.6.refs_0_.refs_3_, ...), custom_call_target="tpu_custom_call" | custom-call | flops 805306368 | bytes 6291456 | tf_op jit(solution)/shard_map/pallas_call | solution.py:459
  46.3 1.4 %collective-permute-start.13 = (bf16[256,384]{1,0:T(8,128)(2,1)S(1)}, bf16[256,384]{1,0:T(8,128)(2,1)S(1)}, u32[]{:S(2)}, u32[]{:S(2)}) collective-permute-start(bf16[256,384]{1,0:T(8,128)(2,1)S(1)} %get-tuple-element.42), channel_id=1, source_target_pairs={{0,2},{2,0},{1,3},{3,1},{4,6},{6,4},{5,7},{7,5},{8,10},{10,8},{9,1... | collective-permute-start | bytes 589832 | tf_op jit(solution)/shard_map/ppermute | solution.py:33
  47.7 0.0 collective-permute-done.14.factors
  47.7 3.0 %collective-permute-done.15.refs_0_ = bf16[128,1024]{1,0:T(8,128)(2,1)S(1)} collective-permute-done((bf16[128,1024]{1,0:T(8,128)(2,1)S(1)}, bf16[128,1024]{1,0:T(8,128)(2,1)S(1)}, u32[]{:S(2)}, u32[]{:S(2)}) %collective-permute-start.15) | collective-permute-done | bytes 262176 | tf_op jit(solution)/shard_map/ppermute | solution.py:444
  50.7 1.4 %shard_map.74 = (bf16[2048,128]{1,0:T(8,128)(2,1)S(1)}, bf16[2048,128]{1,0:T(8,128)(2,1)S(1)}) custom-call(bf16[128,1024]{1,0:T(8,128)(2,1)S(1)} %collective-permute-done.14.factors, f32[136,128]{1,0:T(8,128)S(1)} %collective-permute-done.2.refs_3_.slab, bf16[128,1024]{1,0:T(8,128)(2,1)S(1)} %collective-permute-done.15.refs_0_), custom_call_target="tpu_custom_call" | custom-call | flops 536870912 | bytes 1572864 | tf_op jit(solution)/shard_map/pallas_call | solution.py:433
  52.1 1.1 %shard_map.75 = (bf16[256,128]{1,0:T(8,128)(2,1)S(1)}, bf16[2048,128]{1,0:T(8,128)(2,1)S(1)}) custom-call(f32[136,128]{1,0:T(8,128)S(1)} %shard_map.67.refs_0_, f32[136,128]{1,0:T(8,128)S(1)} %collective-permute-done.4.refs_1_, f32[136,128]{1,0:T(8,128)S(1)} %collective-permute-done.5.refs_2_, f32[136,128]{1,0:T(8,128)S(1)} %collective-permute-done.6.refs_0_.refs_3_, ...), custom_call_target="tpu_custom_call" | custom-call | flops 268435456 | bytes 2097152 | tf_op jit(solution)/shard_map/pallas_call | solution.py:459
  53.2 1.3 %collective-permute-start.16 = (bf16[256,128]{1,0:T(8,128)(2,1)S(1)}, bf16[256,128]{1,0:T(8,128)(2,1)S(1)}, u32[]{:S(2)}, u32[]{:S(2)}) collective-permute-start(bf16[256,128]{1,0:T(8,128)(2,1)S(1)} %get-tuple-element.48), channel_id=1, source_target_pairs={{0,2},{2,0},{1,3},{3,1},{4,6},{6,4},{5,7},{7,5},{8,10},{10,8},{9,1... | collective-permute-start | bytes 196616 | tf_op jit(solution)/shard_map/ppermute | solution.py:33
  54.5 0.7 %shard_map.73.refs_0_ = bf16[256,384]{1,0:T(8,128)(2,1)S(1)} custom-call(bf16[512,2048]{1,0:T(8,128)(2,1)S(1)} %copy-done, bf16[2048,384]{1,0:T(8,128)(2,1)S(1)} %get-tuple-element.41.pre), custom_call_target="tpu_custom_call" | custom-call | flops 402653184 | bytes 2621440 | tf_op jit(solution)/shard_map/pallas_call | solution.py:467
  55.2 0.4 shard_map.76.refs_2_
  55.7 1.9 %collective-permute-done.16.refs_3_ = bf16[256,128]{1,0:T(8,128)(2,1)S(1)} collective-permute-done((bf16[256,128]{1,0:T(8,128)(2,1)S(1)}, bf16[256,128]{1,0:T(8,128)(2,1)S(1)}, u32[]{:S(2)}, u32[]{:S(2)}) %collective-permute-start.16) | collective-permute-done | bytes 65568 | tf_op jit(solution)/shard_map/ppermute | solution.py:33
  57.6 0.1 shard_map.77
  57.7 0.8 %reshape.7 = bf16[256,4,1,128]{3,1,0,2:T(4,128)(2,1)} reshape(bf16[256,512]{1,0:T(8,128)(2,1)S(1)} %shard_map.77) | data formatting | bytes 524288 | tf_op jit(solution)/shard_map/reshape | solution.py:485
  (7 shorter events, 0.0 us)
Async XLA Ops:
  11.2 9.5 %collective-permute-start.3 = (bf16[128,1024]{1,0:T(8,128)(2,1)}, bf16[128,1024]{1,0:T(8,128)(2,1)S(1)}, u32[]{:S(2)}, u32[]{:S(2)}) collective-permute-start(bf16[128,1024]{1,0:T(8,128)(2,1)} %get-tuple-element.34), channel_id=1, source_target_pairs={{0,2},{2,0},{1,3},{3,1},{4,6},{6,4},{5,7},{7,5},{8,10},{10,8},{9,1... | collective-permute-start | bytes 786440 | tf_op jit(solution)/shard_map/ppermute | solution.py:33
  14.2 11.1 %collective-permute-start = (f32[136,128]{1,0:T(8,128)}, f32[136,128]{1,0:T(8,128)S(1)}, u32[]{:S(2)}, u32[]{:S(2)}) collective-permute-start(f32[136,128]{1,0:T(8,128)} %get-tuple-element.30), channel_id=1, source_target_pairs={{0,4},{4,0},{8,12},{12,8},{1,5},{5,1},{9,13},{13,9},{2,6},{6,2},{1... | collective-permute-start | bytes 208904 | tf_op jit(solution)/shard_map/ppermute | solution.py:33
  15.8 9.5 %collective-permute-start.1 = (f32[136,128]{1,0:T(8,128)}, f32[136,128]{1,0:T(8,128)S(1)}, u32[]{:S(2)}, u32[]{:S(2)}) collective-permute-start(f32[136,128]{1,0:T(8,128)} %get-tuple-element.31), channel_id=1, source_target_pairs={{0,8},{4,12},{8,0},{12,4},{1,9},{5,13},{9,1},{13,5},{2,10},{6,14},... | collective-permute-start | bytes 208904 | tf_op jit(solution)/shard_map/ppermute | solution.py:33
  18.3 6.9 %collective-permute-start.2 = (f32[136,128]{1,0:T(8,128)}, f32[136,128]{1,0:T(8,128)S(1)}, u32[]{:S(2)}, u32[]{:S(2)}) collective-permute-start(f32[136,128]{1,0:T(8,128)} %get-tuple-element.32), channel_id=1, source_target_pairs={{0,12},{4,8},{8,4},{12,0},{1,13},{5,9},{9,5},{13,1},{2,14},{6,10},... | collective-permute-start | bytes 208904 | tf_op jit(solution)/shard_map/ppermute | solution.py:33
  18.6 0.9 %copy-start.1 = (bf16[128,1024]{1,0:T(8,128)(2,1)S(1)}, bf16[128,1024]{1,0:T(8,128)(2,1)}, u32[]{:S(2)}) copy-start(bf16[128,1024]{1,0:T(8,128)(2,1)} %get-tuple-element.27.refs_0_) | copy-start | bytes 786436
  19.5 0.9 %copy-start.2 = (f32[136,128]{1,0:T(8,128)S(1)}, f32[136,128]{1,0:T(8,128)}, u32[]{:S(2)}) copy-start(f32[136,128]{1,0:T(8,128)} %get-tuple-element.28.refs_1_) | copy-start | bytes 208900
  20.8 15.8 %collective-permute-start.10 = (bf16[128,1024]{1,0:T(8,128)(2,1)S(1)}, bf16[128,1024]{1,0:T(8,128)(2,1)S(1)}, u32[]{:S(2)}, u32[]{:S(2)}) collective-permute-start(bf16[128,1024]{1,0:T(8,128)(2,1)S(1)} %shard_map.66.refs_4_.refs_0_.factors), channel_id=1, source_target_pairs={{0,4},{4,0},{8,12},{12,8},{1,5},{5,1},{9,13},{13,9},{2,6},{6,2},{1... | collective-permute-start | bytes 786440 | tf_op jit(solution)/shard_map/ppermute | solution.py:33
  22.6 15.3 %collective-permute-start.11 = (bf16[128,1024]{1,0:T(8,128)(2,1)S(1)}, bf16[128,1024]{1,0:T(8,128)(2,1)S(1)}, u32[]{:S(2)}, u32[]{:S(2)}) collective-permute-start(bf16[128,1024]{1,0:T(8,128)(2,1)S(1)} %shard_map.66.refs_4_.refs_0_.factors), channel_id=1, source_target_pairs={{0,8},{4,12},{8,0},{12,4},{1,9},{5,13},{9,1},{13,5},{2,10},{6,14},... | collective-permute-start | bytes 786440 | tf_op jit(solution)/shard_map/ppermute | solution.py:33
  31.8 12.4 %copy-start = (bf16[512,2048]{1,0:T(8,128)(2,1)S(1)}, bf16[512,2048]{1,0:T(8,128)(2,1)}, u32[]{:S(2)}) copy-start(bf16[512,2048]{1,0:T(8,128)(2,1)} %train.3) | copy-start | bytes 6291460
  31.8 8.3 %collective-permute-start.6 = (f32[136,128]{1,0:T(8,128)S(1)}, f32[136,128]{1,0:T(8,128)S(1)}, u32[]{:S(2)}, u32[]{:S(2)}) collective-permute-start(f32[136,128]{1,0:T(8,128)S(1)} %shard_map.67.refs_0_), channel_id=1, source_target_pairs={{0,12},{4,8},{8,4},{12,0},{1,13},{5,9},{9,5},{13,1},{2,14},{6,10},... | collective-permute-start | bytes 208904 | tf_op jit(solution)/shard_map/ppermute | solution.py:33
  33.1 8.5 %collective-permute-start.4 = (f32[136,128]{1,0:T(8,128)S(1)}, f32[136,128]{1,0:T(8,128)S(1)}, u32[]{:S(2)}, u32[]{:S(2)}) collective-permute-start(f32[136,128]{1,0:T(8,128)S(1)} %shard_map.67.refs_0_), channel_id=1, source_target_pairs={{0,4},{4,0},{8,12},{12,8},{1,5},{5,1},{9,13},{13,9},{2,6},{6,2},{1... | collective-permute-start | bytes 208904 | tf_op jit(solution)/shard_map/ppermute | solution.py:33
  33.5 8.7 %collective-permute-start.5 = (f32[136,128]{1,0:T(8,128)S(1)}, f32[136,128]{1,0:T(8,128)S(1)}, u32[]{:S(2)}, u32[]{:S(2)}) collective-permute-start(f32[136,128]{1,0:T(8,128)S(1)} %shard_map.67.refs_0_), channel_id=1, source_target_pairs={{0,8},{4,12},{8,0},{12,4},{1,9},{5,13},{9,1},{13,5},{2,10},{6,14},... | collective-permute-start | bytes 208904 | tf_op jit(solution)/shard_map/ppermute | solution.py:33
  36.6 5.7 %collective-permute-start.7 = (f32[136,128]{1,0:T(8,128)S(1)}, f32[136,128]{1,0:T(8,128)S(1)}, u32[]{:S(2)}, u32[]{:S(2)}) collective-permute-start(f32[136,128]{1,0:T(8,128)S(1)} %shard_map.67.refs_0_), channel_id=1, source_target_pairs={{0,1},{1,0},{2,3},{3,2},{4,5},{5,4},{6,7},{7,6},{8,9},{9,8},{10,11... | collective-permute-start | bytes 208904 | tf_op jit(solution)/shard_map/ppermute | solution.py:33
  38.0 9.7 %collective-permute-start.14 = (bf16[128,1024]{1,0:T(8,128)(2,1)S(1)}, bf16[128,1024]{1,0:T(8,128)(2,1)S(1)}, u32[]{:S(2)}, u32[]{:S(2)}) collective-permute-start(bf16[128,1024]{1,0:T(8,128)(2,1)S(1)} %get-tuple-element.43), channel_id=1, source_target_pairs={{4,8},{8,4},{5,9},{9,5},{6,10},{10,6},{7,11},{11,7},{20,24},{24,20... | collective-permute-start | bytes 786440 | tf_op jit(solution)/shard_map/ppermute | solution.py:442
  40.1 10.6 %collective-permute-start.15 = (bf16[128,1024]{1,0:T(8,128)(2,1)S(1)}, bf16[128,1024]{1,0:T(8,128)(2,1)S(1)}, u32[]{:S(2)}, u32[]{:S(2)}) collective-permute-start(bf16[128,1024]{1,0:T(8,128)(2,1)S(1)} %get-tuple-element.44), channel_id=1, source_target_pairs={{4,0},{8,12},{5,1},{9,13},{6,2},{10,14},{7,3},{11,15},{20,16},{24,... | collective-permute-start | bytes 786440 | tf_op jit(solution)/shard_map/ppermute | solution.py:444
  41.6 2.6 %collective-permute-start.8 = (f32[136,128]{1,0:T(8,128)S(1)}, f32[136,128]{1,0:T(8,128)S(1)}, u32[]{:S(2)}, u32[]{:S(2)}) collective-permute-start(f32[136,128]{1,0:T(8,128)S(1)} %collective-permute-done.4.refs_1_), channel_id=1, source_target_pairs={{0,1},{1,0},{2,3},{3,2},{4,5},{5,4},{6,7},{7,6},{8,9},{9,8},{10,11... | collective-permute-start | bytes 208904 | tf_op jit(solution)/shard_map/ppermute | solution.py:33
  42.2 2.0 %collective-permute-start.9 = (f32[136,128]{1,0:T(8,128)S(1)}, f32[136,128]{1,0:T(8,128)S(1)}, u32[]{:S(2)}, u32[]{:S(2)}) collective-permute-start(f32[136,128]{1,0:T(8,128)S(1)} %collective-permute-done.5.refs_2_), channel_id=1, source_target_pairs={{0,1},{1,0},{2,3},{3,2},{4,5},{5,4},{6,7},{7,6},{8,9},{9,8},{10,11... | collective-permute-start | bytes 208904 | tf_op jit(solution)/shard_map/ppermute | solution.py:33
  42.3 1.9 %collective-permute-start.12 = (f32[136,128]{1,0:T(8,128)S(1)}, f32[136,128]{1,0:T(8,128)S(1)}, u32[]{:S(2)}, u32[]{:S(2)}) collective-permute-start(f32[136,128]{1,0:T(8,128)S(1)} %shard_map.70), channel_id=1, source_target_pairs={{0,1},{1,0},{2,3},{3,2},{4,5},{5,4},{6,7},{7,6},{8,9},{9,8},{10,11... | collective-permute-start | bytes 208904 | tf_op jit(solution)/shard_map/ppermute | solution.py:33
  46.3 9.4 %collective-permute-start.13 = (bf16[256,384]{1,0:T(8,128)(2,1)S(1)}, bf16[256,384]{1,0:T(8,128)(2,1)S(1)}, u32[]{:S(2)}, u32[]{:S(2)}) collective-permute-start(bf16[256,384]{1,0:T(8,128)(2,1)S(1)} %get-tuple-element.42), channel_id=1, source_target_pairs={{0,2},{2,0},{1,3},{3,1},{4,6},{6,4},{5,7},{7,5},{8,10},{10,8},{9,1... | collective-permute-start | bytes 589832 | tf_op jit(solution)/shard_map/ppermute | solution.py:33
  53.2 4.3 %collective-permute-start.16 = (bf16[256,128]{1,0:T(8,128)(2,1)S(1)}, bf16[256,128]{1,0:T(8,128)(2,1)S(1)}, u32[]{:S(2)}, u32[]{:S(2)}) collective-permute-start(bf16[256,128]{1,0:T(8,128)(2,1)S(1)} %get-tuple-element.48), channel_id=1, source_target_pairs={{0,2},{2,0},{1,3},{3,1},{4,6},{6,4},{5,7},{7,5},{8,10},{10,8},{9,1... | collective-permute-start | bytes 196616 | tf_op jit(solution)/shard_map/ppermute | solution.py:33

commit v16 on v15

--- a/solution.py
+++ b/solution.py
@@ -290,7 +290,7 @@
     inside = jnp.where((place >= starts) & (place < ends), 1.0, 0.0).astype(jnp.bfloat16)
     output = part(0, each) + part(each, each)
     inputs = part(2 * each, proj)
-    step = 8
+    step = 16
     for start in range(0, each, step):
         grads = jnp.concatenate(
             [(inputs * output[r:r + 1, :]).astype(jnp.bfloat16) for r in range(start, start + step)], axis=0

time: 58.7 us -> 58.6 us (level)
  no operation moved by 1% of the time
where the time goes in v16:
time: 58.6 us; the launch traced here: 58.4 us
  Pallas kernels  27.8 us (47%)
  starting transfers between devices  22.4 us (38%)
  waiting for transfers between devices  5.45 us (9%)
  local copies, waits for them, and re-layouts  2.6 us (4%)
    ppermute x15, starting transfers between devices, swapped(): lax.ppermute(shard, axis, [(i, i ^ by) for i in range(lax.axis_size(axis))])  20.3 us
    pallas_call x1, Pallas kernels, split_over_blocks(): call(first_kernel, [shape((2 * each + proj, tokens), bf16)] * 2 + [shape(...  11.2 us
    pallas_call x1, Pallas kernels, split_over_blocks(): call(functools.partial(factor_kernel, train_rows * cycle, 1.0 / proj), sh...  6.58 us
    pallas_call x4, Pallas kernels, split_over_blocks(): call(functools.partial(queries_kernel, each, cycle if s == late else 0),...  5.61 us
    pallas_call x2, Pallas kernels, split_over_blocks(): call(functools.partial(scores_kernel, cycle, count), [shape((half_rows, c...  3.1 us
    ppermute x1, waiting for transfers between devices, split_over_blocks(): far = [lax.ppermute(again[0], 'dp', [(1, 0), (2, 3)])]  3.02 us
    ppermute x15, waiting for transfers between devices, swapped(): lax.ppermute(shard, axis, [(i, i ^ by) for i in range(lax.axis_size(axis))])  2.43 us
    unnamed x6, local copies, waits for them, and re-layouts  1.84 us
  transfers between devices with their start and end apart: 17, of which 4 were waited for; matrix products, arithmetic and copies ran while one was open for 0% of the time, Pallas kernels for 28%

profile of v16, /device:TPU:0, one launch (start us, length us, event | category | flops | bytes accessed | tf_op | source)
XLA Modules:
  0.0 58.4 jit_solution(10713700552893263471)
XLA Ops:
  0.0 11.2 %shard_map.64 = (bf16[128,1024]{1,0:T(8,128)(2,1)}, bf16[128,1024]{1,0:T(8,128)(2,1)}, f32[136,128]{1,0:T(8,128)}, f32[136,128]{1,0:T(8,128)}, f32[136,128]{1,0:T(8,128)}, /*index=5*/f32[136,128]{1,0:T(8,128)}) custom-call(s32[8,128]{1,0:T(8,128)} %bitcast.6, bf16[1024,2048]{1,0:T(8,128)(2,1)} %delta_hbm.1, bf16[64,64128]{1,0:T(8,128)(2,1)} %bitcast.4, ...), custom_call_target="tpu_custom_call" | custom-call | flops 268435456 | bytes 24805376 | tf_op jit(solution)/shard_map/pallas_call | solution.py:373
  11.2 3.0 %collective-permute-start.3 = (bf16[128,1024]{1,0:T(8,128)(2,1)}, bf16[128,1024]{1,0:T(8,128)(2,1)S(1)}, u32[]{:S(2)}, u32[]{:S(2)}) collective-permute-start(bf16[128,1024]{1,0:T(8,128)(2,1)} %get-tuple-element.34), channel_id=1, source_target_pairs={{0,2},{2,0},{1,3},{3,1},{4,6},{6,4},{5,7},{7,5},{8,10},{10,8},{9,1... | collective-permute-start | bytes 786440 | tf_op jit(solution)/shard_map/ppermute | solution.py:33
  14.2 1.6 %collective-permute-start = (f32[136,128]{1,0:T(8,128)}, f32[136,128]{1,0:T(8,128)S(1)}, u32[]{:S(2)}, u32[]{:S(2)}) collective-permute-start(f32[136,128]{1,0:T(8,128)} %get-tuple-element.30), channel_id=1, source_target_pairs={{0,4},{4,0},{8,12},{12,8},{1,5},{5,1},{9,13},{13,9},{2,6},{6,2},{1... | collective-permute-start | bytes 208904 | tf_op jit(solution)/shard_map/ppermute | solution.py:33
  15.7 2.6 %collective-permute-start.1 = (f32[136,128]{1,0:T(8,128)}, f32[136,128]{1,0:T(8,128)S(1)}, u32[]{:S(2)}, u32[]{:S(2)}) collective-permute-start(f32[136,128]{1,0:T(8,128)} %get-tuple-element.31), channel_id=1, source_target_pairs={{0,8},{4,12},{8,0},{12,4},{1,9},{5,13},{9,1},{13,5},{2,10},{6,14},... | collective-permute-start | bytes 208904 | tf_op jit(solution)/shard_map/ppermute | solution.py:33
  18.3 0.3 collective-permute-start.2
  18.6 0.9 %copy-done.1 = bf16[128,1024]{1,0:T(8,128)(2,1)S(1)} copy-done((bf16[128,1024]{1,0:T(8,128)(2,1)S(1)}, bf16[128,1024]{1,0:T(8,128)(2,1)}, u32[]{:S(2)}) %copy-start.1) | copy-done | bytes 262168
  19.5 0.9 %copy-done.2 = f32[136,128]{1,0:T(8,128)S(1)} copy-done((f32[136,128]{1,0:T(8,128)S(1)}, f32[136,128]{1,0:T(8,128)}, u32[]{:S(2)}) %copy-start.2) | copy-done | bytes 69656
  20.4 0.3 collective-permute-done.3.got
  20.7 0.1 shard_map.66.refs_4_.refs_0_.factors
  20.8 1.9 %collective-permute-start.10 = (bf16[128,1024]{1,0:T(8,128)(2,1)S(1)}, bf16[128,1024]{1,0:T(8,128)(2,1)S(1)}, u32[]{:S(2)}, u32[]{:S(2)}) collective-permute-start(bf16[128,1024]{1,0:T(8,128)(2,1)S(1)} %shard_map.66.refs_4_.refs_0_.factors), channel_id=1, source_target_pairs={{0,4},{4,0},{8,12},{12,8},{1,5},{5,1},{9,13},{13,9},{2,6},{6,2},{1... | collective-permute-start | bytes 786440 | tf_op jit(solution)/shard_map/ppermute | solution.py:33
  22.6 2.6 %collective-permute-start.11 = (bf16[128,1024]{1,0:T(8,128)(2,1)S(1)}, bf16[128,1024]{1,0:T(8,128)(2,1)S(1)}, u32[]{:S(2)}, u32[]{:S(2)}) collective-permute-start(bf16[128,1024]{1,0:T(8,128)(2,1)S(1)} %shard_map.66.refs_4_.refs_0_.factors), channel_id=1, source_target_pairs={{0,8},{4,12},{8,0},{12,4},{1,9},{5,13},{9,1},{13,5},{2,10},{6,14},... | collective-permute-start | bytes 786440 | tf_op jit(solution)/shard_map/ppermute | solution.py:33
  25.2 0.0 collective-permute-done.refs_1_.slab
  25.2 0.0 collective-permute-done.1.refs_2_.slab
  25.2 0.0 collective-permute-done.2.refs_3_.slab
  25.2 6.6 %shard_map.67.refs_0_ = f32[136,128]{1,0:T(8,128)S(1)} custom-call(f32[136,128]{1,0:T(8,128)S(1)} %get-tuple-element.29.refs_0_.slab, f32[136,128]{1,0:T(8,128)S(1)} %collective-permute-done.refs_1_.slab, f32[136,128]{1,0:T(8,128)S(1)} %collective-permute-done.1.refs_2_.slab, f32[136,128]{1,0:T(8,128)S(1)} %collective-permute-done.2.refs_3_.slab, ...), custom_call_target="tpu_custom_call" | custom-call | flops 10000000000 | bytes 1000000 | tf_op jit(solution)/shard_map/pallas_call | solution.py:419
  31.8 0.0 copy-start
  31.8 1.3 %collective-permute-start.6 = (f32[136,128]{1,0:T(8,128)S(1)}, f32[136,128]{1,0:T(8,128)S(1)}, u32[]{:S(2)}, u32[]{:S(2)}) collective-permute-start(f32[136,128]{1,0:T(8,128)S(1)} %shard_map.67.refs_0_), channel_id=1, source_target_pairs={{0,12},{4,8},{8,4},{12,0},{1,13},{5,9},{9,5},{13,1},{2,14},{6,10},... | collective-permute-start | bytes 208904 | tf_op jit(solution)/shard_map/ppermute | solution.py:33
  33.1 0.4 collective-permute-start.4
  33.5 2.8 %collective-permute-start.5 = (f32[136,128]{1,0:T(8,128)S(1)}, f32[136,128]{1,0:T(8,128)S(1)}, u32[]{:S(2)}, u32[]{:S(2)}) collective-permute-start(f32[136,128]{1,0:T(8,128)S(1)} %shard_map.67.refs_0_), channel_id=1, source_target_pairs={{0,8},{4,12},{8,0},{12,4},{1,9},{5,13},{9,1},{13,5},{2,10},{6,14},... | collective-permute-start | bytes 208904 | tf_op jit(solution)/shard_map/ppermute | solution.py:33
  36.3 0.3 collective-permute-done.10.factors
  36.5 1.4 %shard_map.68 = (bf16[2048,128]{1,0:T(8,128)(2,1)S(1)}, bf16[2048,128]{1,0:T(8,128)(2,1)S(1)}, bf16[128,1024]{1,0:T(8,128)(2,1)S(1)}) custom-call(bf16[128,1024]{1,0:T(8,128)(2,1)S(1)} %collective-permute-done.10.factors, f32[136,128]{1,0:T(8,128)S(1)} %collective-permute-done.refs_1_.slab, bf16[128,1024]{1,0:T(8,128)(2,1)S(1)} %shard_map.66.refs_4_.refs_0_.factors), custom_call_target="tpu_custom_call" | custom-call | flops 536870912 | bytes 1572864 | tf_op jit(solution)/shard_map/pallas_call | solution.py:433
  38.0 0.0 collective-permute-done.11.factors.refs_0_
  38.0 0.7 %collective-permute-start.14 = (bf16[128,1024]{1,0:T(8,128)(2,1)S(1)}, bf16[128,1024]{1,0:T(8,128)(2,1)S(1)}, u32[]{:S(2)}, u32[]{:S(2)}) collective-permute-start(bf16[128,1024]{1,0:T(8,128)(2,1)S(1)} %get-tuple-element.43), channel_id=1, source_target_pairs={{4,8},{8,4},{5,9},{9,5},{6,10},{10,6},{7,11},{11,7},{20,24},{24,20... | collective-permute-start | bytes 786440 | tf_op jit(solution)/shard_map/ppermute | solution.py:442
  38.7 1.4 %shard_map.69 = (bf16[2048,128]{1,0:T(8,128)(2,1)S(1)}, bf16[2048,128]{1,0:T(8,128)(2,1)S(1)}, bf16[128,1024]{1,0:T(8,128)(2,1)S(1)}) custom-call(bf16[128,1024]{1,0:T(8,128)(2,1)S(1)} %collective-permute-done.11.factors.refs_0_, f32[136,128]{1,0:T(8,128)S(1)} %collective-permute-done.1.refs_2_.slab, ...), custom_call_target="tpu_custom_call" | custom-call | flops 536870912 | bytes 1572864 | tf_op jit(solution)/shard_map/pallas_call | solution.py:433
  40.1 0.0 collective-permute-done.6.refs_0_.refs_3_
  40.1 1.5 %collective-permute-start.15 = (bf16[128,1024]{1,0:T(8,128)(2,1)S(1)}, bf16[128,1024]{1,0:T(8,128)(2,1)S(1)}, u32[]{:S(2)}, u32[]{:S(2)}) collective-permute-start(bf16[128,1024]{1,0:T(8,128)(2,1)S(1)} %get-tuple-element.44), channel_id=1, source_target_pairs={{4,0},{8,12},{5,1},{9,13},{6,2},{10,14},{7,3},{11,15},{20,16},{24,... | collective-permute-start | bytes 786440 | tf_op jit(solution)/shard_map/ppermute | solution.py:444
  41.6 0.0 collective-permute-done.4.refs_1_
  41.6 0.6 collective-permute-start.8
  42.1 0.0 collective-permute-done.5.refs_2_
  42.2 0.1 collective-permute-start.9
  42.2 0.0 collective-permute-done.7.refs_4_
  42.3 0.5 collective-permute-start.12
  42.7 1.4 %shard_map.71 = (bf16[2048,128]{1,0:T(8,128)(2,1)S(1)}, bf16[2048,128]{1,0:T(8,128)(2,1)S(1)}) custom-call(bf16[128,1024]{1,0:T(8,128)(2,1)S(1)} %shard_map.66.refs_4_.refs_0_.factors, f32[136,128]{1,0:T(8,128)S(1)} %get-tuple-element.29.refs_0_.slab, f32[136,128]{1,0:T(8,128)S(1)} %shard_map.67.refs_0_), custom_call_target="tpu_custom_call" | custom-call | flops 536870912 | bytes 1572864 | tf_op jit(solution)/shard_map/pallas_call | solution.py:433
  44.1 0.0 collective-permute-done.8.refs_5_
  44.2 0.0 collective-permute-done.12.refs_7_
  44.2 2.0 %shard_map.72 = (bf16[256,384]{1,0:T(8,128)(2,1)S(1)}, bf16[2048,384]{1,0:T(8,128)(2,1)S(1)}) custom-call(f32[136,128]{1,0:T(8,128)S(1)} %shard_map.67.refs_0_, f32[136,128]{1,0:T(8,128)S(1)} %collective-permute-done.4.refs_1_, f32[136,128]{1,0:T(8,128)S(1)} %collective-permute-done.5.refs_2_, f32[136,128]{1,0:T(8,128)S(1)} %collective-permute-done.6.refs_0_.refs_3_, ...), custom_call_target="tpu_custom_call" | custom-call | flops 805306368 | bytes 6291456 | tf_op jit(solution)/shard_map/pallas_call | solution.py:459
  46.2 1.5 %collective-permute-start.13 = (bf16[256,384]{1,0:T(8,128)(2,1)S(1)}, bf16[256,384]{1,0:T(8,128)(2,1)S(1)}, u32[]{:S(2)}, u32[]{:S(2)}) collective-permute-start(bf16[256,384]{1,0:T(8,128)(2,1)S(1)} %get-tuple-element.42), channel_id=1, source_target_pairs={{0,2},{2,0},{1,3},{3,1},{4,6},{6,4},{5,7},{7,5},{8,10},{10,8},{9,1... | collective-permute-start | bytes 589832 | tf_op jit(solution)/shard_map/ppermute | solution.py:33
  47.7 0.0 collective-permute-done.14.factors
  47.7 3.0 %collective-permute-done.15.refs_0_ = bf16[128,1024]{1,0:T(8,128)(2,1)S(1)} collective-permute-done((bf16[128,1024]{1,0:T(8,128)(2,1)S(1)}, bf16[128,1024]{1,0:T(8,128)(2,1)S(1)}, u32[]{:S(2)}, u32[]{:S(2)}) %collective-permute-start.15) | collective-permute-done | bytes 262176 | tf_op jit(solution)/shard_map/ppermute | solution.py:444
  50.7 1.4 %shard_map.74 = (bf16[2048,128]{1,0:T(8,128)(2,1)S(1)}, bf16[2048,128]{1,0:T(8,128)(2,1)S(1)}) custom-call(bf16[128,1024]{1,0:T(8,128)(2,1)S(1)} %collective-permute-done.14.factors, f32[136,128]{1,0:T(8,128)S(1)} %collective-permute-done.2.refs_3_.slab, bf16[128,1024]{1,0:T(8,128)(2,1)S(1)} %collective-permute-done.15.refs_0_), custom_call_target="tpu_custom_call" | custom-call | flops 536870912 | bytes 1572864 | tf_op jit(solution)/shard_map/pallas_call | solution.py:433
  52.1 1.1 %shard_map.75 = (bf16[256,128]{1,0:T(8,128)(2,1)S(1)}, bf16[2048,128]{1,0:T(8,128)(2,1)S(1)}) custom-call(f32[136,128]{1,0:T(8,128)S(1)} %shard_map.67.refs_0_, f32[136,128]{1,0:T(8,128)S(1)} %collective-permute-done.4.refs_1_, f32[136,128]{1,0:T(8,128)S(1)} %collective-permute-done.5.refs_2_, f32[136,128]{1,0:T(8,128)S(1)} %collective-permute-done.6.refs_0_.refs_3_, ...), custom_call_target="tpu_custom_call" | custom-call | flops 268435456 | bytes 2097152 | tf_op jit(solution)/shard_map/pallas_call | solution.py:459
  53.2 1.3 %collective-permute-start.16 = (bf16[256,128]{1,0:T(8,128)(2,1)S(1)}, bf16[256,128]{1,0:T(8,128)(2,1)S(1)}, u32[]{:S(2)}, u32[]{:S(2)}) collective-permute-start(bf16[256,128]{1,0:T(8,128)(2,1)S(1)} %get-tuple-element.48), channel_id=1, source_target_pairs={{0,2},{2,0},{1,3},{3,1},{4,6},{6,4},{5,7},{7,5},{8,10},{10,8},{9,1... | collective-permute-start | bytes 196616 | tf_op jit(solution)/shard_map/ppermute | solution.py:33
  54.5 0.7 %shard_map.73.refs_0_ = bf16[256,384]{1,0:T(8,128)(2,1)S(1)} custom-call(bf16[512,2048]{1,0:T(8,128)(2,1)S(1)} %copy-done, bf16[2048,384]{1,0:T(8,128)(2,1)S(1)} %get-tuple-element.41.pre), custom_call_target="tpu_custom_call" | custom-call | flops 402653184 | bytes 2621440 | tf_op jit(solution)/shard_map/pallas_call | solution.py:467
  55.2 0.4 shard_map.76.refs_2_
  55.6 0.0 collective-permute-done.13.refs_1_
  55.6 1.9 %collective-permute-done.16.refs_3_ = bf16[256,128]{1,0:T(8,128)(2,1)S(1)} collective-permute-done((bf16[256,128]{1,0:T(8,128)(2,1)S(1)}, bf16[256,128]{1,0:T(8,128)(2,1)S(1)}, u32[]{:S(2)}, u32[]{:S(2)}) %collective-permute-start.16) | collective-permute-done | bytes 65568 | tf_op jit(solution)/shard_map/ppermute | solution.py:33
  57.5 0.1 shard_map.77
  57.6 0.8 %reshape.7 = bf16[256,4,1,128]{3,1,0,2:T(4,128)(2,1)} reshape(bf16[256,512]{1,0:T(8,128)(2,1)S(1)} %shard_map.77) | data formatting | bytes 524288 | tf_op jit(solution)/shard_map/reshape | solution.py:485
  (7 shorter events, 0.0 us)
Async XLA Ops:
  11.2 9.5 %collective-permute-start.3 = (bf16[128,1024]{1,0:T(8,128)(2,1)}, bf16[128,1024]{1,0:T(8,128)(2,1)S(1)}, u32[]{:S(2)}, u32[]{:S(2)}) collective-permute-start(bf16[128,1024]{1,0:T(8,128)(2,1)} %get-tuple-element.34), channel_id=1, source_target_pairs={{0,2},{2,0},{1,3},{3,1},{4,6},{6,4},{5,7},{7,5},{8,10},{10,8},{9,1... | collective-permute-start | bytes 786440 | tf_op jit(solution)/shard_map/ppermute | solution.py:33
  14.2 11.0 %collective-permute-start = (f32[136,128]{1,0:T(8,128)}, f32[136,128]{1,0:T(8,128)S(1)}, u32[]{:S(2)}, u32[]{:S(2)}) collective-permute-start(f32[136,128]{1,0:T(8,128)} %get-tuple-element.30), channel_id=1, source_target_pairs={{0,4},{4,0},{8,12},{12,8},{1,5},{5,1},{9,13},{13,9},{2,6},{6,2},{1... | collective-permute-start | bytes 208904 | tf_op jit(solution)/shard_map/ppermute | solution.py:33
  15.7 9.5 %collective-permute-start.1 = (f32[136,128]{1,0:T(8,128)}, f32[136,128]{1,0:T(8,128)S(1)}, u32[]{:S(2)}, u32[]{:S(2)}) collective-permute-start(f32[136,128]{1,0:T(8,128)} %get-tuple-element.31), channel_id=1, source_target_pairs={{0,8},{4,12},{8,0},{12,4},{1,9},{5,13},{9,1},{13,5},{2,10},{6,14},... | collective-permute-start | bytes 208904 | tf_op jit(solution)/shard_map/ppermute | solution.py:33
  18.3 6.9 %collective-permute-start.2 = (f32[136,128]{1,0:T(8,128)}, f32[136,128]{1,0:T(8,128)S(1)}, u32[]{:S(2)}, u32[]{:S(2)}) collective-permute-start(f32[136,128]{1,0:T(8,128)} %get-tuple-element.32), channel_id=1, source_target_pairs={{0,12},{4,8},{8,4},{12,0},{1,13},{5,9},{9,5},{13,1},{2,14},{6,10},... | collective-permute-start | bytes 208904 | tf_op jit(solution)/shard_map/ppermute | solution.py:33
  18.6 0.9 %copy-start.1 = (bf16[128,1024]{1,0:T(8,128)(2,1)S(1)}, bf16[128,1024]{1,0:T(8,128)(2,1)}, u32[]{:S(2)}) copy-start(bf16[128,1024]{1,0:T(8,128)(2,1)} %get-tuple-element.27.refs_0_) | copy-start | bytes 786436
  19.5 0.9 %copy-start.2 = (f32[136,128]{1,0:T(8,128)S(1)}, f32[136,128]{1,0:T(8,128)}, u32[]{:S(2)}) copy-start(f32[136,128]{1,0:T(8,128)} %get-tuple-element.28.refs_1_) | copy-start | bytes 208900
  20.8 15.8 %collective-permute-start.10 = (bf16[128,1024]{1,0:T(8,128)(2,1)S(1)}, bf16[128,1024]{1,0:T(8,128)(2,1)S(1)}, u32[]{:S(2)}, u32[]{:S(2)}) collective-permute-start(bf16[128,1024]{1,0:T(8,128)(2,1)S(1)} %shard_map.66.refs_4_.refs_0_.factors), channel_id=1, source_target_pairs={{0,4},{4,0},{8,12},{12,8},{1,5},{5,1},{9,13},{13,9},{2,6},{6,2},{1... | collective-permute-start | bytes 786440 | tf_op jit(solution)/shard_map/ppermute | solution.py:33
  22.6 15.3 %collective-permute-start.11 = (bf16[128,1024]{1,0:T(8,128)(2,1)S(1)}, bf16[128,1024]{1,0:T(8,128)(2,1)S(1)}, u32[]{:S(2)}, u32[]{:S(2)}) collective-permute-start(bf16[128,1024]{1,0:T(8,128)(2,1)S(1)} %shard_map.66.refs_4_.refs_0_.factors), channel_id=1, source_target_pairs={{0,8},{4,12},{8,0},{12,4},{1,9},{5,13},{9,1},{13,5},{2,10},{6,14},... | collective-permute-start | bytes 786440 | tf_op jit(solution)/shard_map/ppermute | solution.py:33
  31.8 12.4 %copy-start = (bf16[512,2048]{1,0:T(8,128)(2,1)S(1)}, bf16[512,2048]{1,0:T(8,128)(2,1)}, u32[]{:S(2)}) copy-start(bf16[512,2048]{1,0:T(8,128)(2,1)} %train.3) | copy-start | bytes 6291460
  31.8 8.2 %collective-permute-start.6 = (f32[136,128]{1,0:T(8,128)S(1)}, f32[136,128]{1,0:T(8,128)S(1)}, u32[]{:S(2)}, u32[]{:S(2)}) collective-permute-start(f32[136,128]{1,0:T(8,128)S(1)} %shard_map.67.refs_0_), channel_id=1, source_target_pairs={{0,12},{4,8},{8,4},{12,0},{1,13},{5,9},{9,5},{13,1},{2,14},{6,10},... | collective-permute-start | bytes 208904 | tf_op jit(solution)/shard_map/ppermute | solution.py:33
  33.1 8.5 %collective-permute-start.4 = (f32[136,128]{1,0:T(8,128)S(1)}, f32[136,128]{1,0:T(8,128)S(1)}, u32[]{:S(2)}, u32[]{:S(2)}) collective-permute-start(f32[136,128]{1,0:T(8,128)S(1)} %shard_map.67.refs_0_), channel_id=1, source_target_pairs={{0,4},{4,0},{8,12},{12,8},{1,5},{5,1},{9,13},{13,9},{2,6},{6,2},{1... | collective-permute-start | bytes 208904 | tf_op jit(solution)/shard_map/ppermute | solution.py:33
  33.5 8.7 %collective-permute-start.5 = (f32[136,128]{1,0:T(8,128)S(1)}, f32[136,128]{1,0:T(8,128)S(1)}, u32[]{:S(2)}, u32[]{:S(2)}) collective-permute-start(f32[136,128]{1,0:T(8,128)S(1)} %shard_map.67.refs_0_), channel_id=1, source_target_pairs={{0,8},{4,12},{8,0},{12,4},{1,9},{5,13},{9,1},{13,5},{2,10},{6,14},... | collective-permute-start | bytes 208904 | tf_op jit(solution)/shard_map/ppermute | solution.py:33
  36.5 5.7 %collective-permute-start.7 = (f32[136,128]{1,0:T(8,128)S(1)}, f32[136,128]{1,0:T(8,128)S(1)}, u32[]{:S(2)}, u32[]{:S(2)}) collective-permute-start(f32[136,128]{1,0:T(8,128)S(1)} %shard_map.67.refs_0_), channel_id=1, source_target_pairs={{0,1},{1,0},{2,3},{3,2},{4,5},{5,4},{6,7},{7,6},{8,9},{9,8},{10,11... | collective-permute-start | bytes 208904 | tf_op jit(solution)/shard_map/ppermute | solution.py:33
  38.0 9.7 %collective-permute-start.14 = (bf16[128,1024]{1,0:T(8,128)(2,1)S(1)}, bf16[128,1024]{1,0:T(8,128)(2,1)S(1)}, u32[]{:S(2)}, u32[]{:S(2)}) collective-permute-start(bf16[128,1024]{1,0:T(8,128)(2,1)S(1)} %get-tuple-element.43), channel_id=1, source_target_pairs={{4,8},{8,4},{5,9},{9,5},{6,10},{10,6},{7,11},{11,7},{20,24},{24,20... | collective-permute-start | bytes 786440 | tf_op jit(solution)/shard_map/ppermute | solution.py:442
  40.1 10.6 %collective-permute-start.15 = (bf16[128,1024]{1,0:T(8,128)(2,1)S(1)}, bf16[128,1024]{1,0:T(8,128)(2,1)S(1)}, u32[]{:S(2)}, u32[]{:S(2)}) collective-permute-start(bf16[128,1024]{1,0:T(8,128)(2,1)S(1)} %get-tuple-element.44), channel_id=1, source_target_pairs={{4,0},{8,12},{5,1},{9,13},{6,2},{10,14},{7,3},{11,15},{20,16},{24,... | collective-permute-start | bytes 786440 | tf_op jit(solution)/shard_map/ppermute | solution.py:444
  41.6 2.6 %collective-permute-start.8 = (f32[136,128]{1,0:T(8,128)S(1)}, f32[136,128]{1,0:T(8,128)S(1)}, u32[]{:S(2)}, u32[]{:S(2)}) collective-permute-start(f32[136,128]{1,0:T(8,128)S(1)} %collective-permute-done.4.refs_1_), channel_id=1, source_target_pairs={{0,1},{1,0},{2,3},{3,2},{4,5},{5,4},{6,7},{7,6},{8,9},{9,8},{10,11... | collective-permute-start | bytes 208904 | tf_op jit(solution)/shard_map/ppermute | solution.py:33
  42.2 2.0 %collective-permute-start.9 = (f32[136,128]{1,0:T(8,128)S(1)}, f32[136,128]{1,0:T(8,128)S(1)}, u32[]{:S(2)}, u32[]{:S(2)}) collective-permute-start(f32[136,128]{1,0:T(8,128)S(1)} %collective-permute-done.5.refs_2_), channel_id=1, source_target_pairs={{0,1},{1,0},{2,3},{3,2},{4,5},{5,4},{6,7},{7,6},{8,9},{9,8},{10,11... | collective-permute-start | bytes 208904 | tf_op jit(solution)/shard_map/ppermute | solution.py:33
  42.3 1.9 %collective-permute-start.12 = (f32[136,128]{1,0:T(8,128)S(1)}, f32[136,128]{1,0:T(8,128)S(1)}, u32[]{:S(2)}, u32[]{:S(2)}) collective-permute-start(f32[136,128]{1,0:T(8,128)S(1)} %shard_map.70), channel_id=1, source_target_pairs={{0,1},{1,0},{2,3},{3,2},{4,5},{5,4},{6,7},{7,6},{8,9},{9,8},{10,11... | collective-permute-start | bytes 208904 | tf_op jit(solution)/shard_map/ppermute | solution.py:33
  46.2 9.4 %collective-permute-start.13 = (bf16[256,384]{1,0:T(8,128)(2,1)S(1)}, bf16[256,384]{1,0:T(8,128)(2,1)S(1)}, u32[]{:S(2)}, u32[]{:S(2)}) collective-permute-start(bf16[256,384]{1,0:T(8,128)(2,1)S(1)} %get-tuple-element.42), channel_id=1, source_target_pairs={{0,2},{2,0},{1,3},{3,1},{4,6},{6,4},{5,7},{7,5},{8,10},{10,8},{9,1... | collective-permute-start | bytes 589832 | tf_op jit(solution)/shard_map/ppermute | solution.py:33
  53.2 4.3 %collective-permute-start.16 = (bf16[256,128]{1,0:T(8,128)(2,1)S(1)}, bf16[256,128]{1,0:T(8,128)(2,1)S(1)}, u32[]{:S(2)}, u32[]{:S(2)}) collective-permute-start(bf16[256,128]{1,0:T(8,128)(2,1)S(1)} %get-tuple-element.48), channel_id=1, source_target_pairs={{0,2},{2,0},{1,3},{3,1},{4,6},{6,4},{5,7},{7,5},{8,10},{10,8},{9,1... | collective-permute-start | bytes 196616 | tf_op jit(solution)/shard_map/ppermute | solution.py:33
